TPU v7x, 128 devices: a whole 4x4x4 slice. The times are simulated.
128 devices in a mesh: panel: 2 (over x_hi), colat: 4 (over z), lon: 16 (over y, x_lo, core).
Axes of the slice: x: 4 (x_hi: 2, x_lo: 2; x = x_hi * 2 + x_lo), y: 4, z: 4, core: 2. Of those that a mesh axis runs over, the one named last changes fastest.
Arguments:
- state: float32 [4, 2, 4, 1536, 512], P(None, 'panel', None, 'lon', 'colat'), may hold values from -6 to 6
- partners: int32 [2, 4, 16, 2], P('panel', 'colat', 'lon'), may hold values from 0 to 63, as said below
- send_counts: int32 [2, 4, 16, 2], P('panel', 'colat', 'lon'), may hold values from 0 to 128
- source_cells: int32 [2, 4, 16, 256], P('panel', 'colat', 'lon'), may hold values from 0 to 12158, as said below
- weights: float32 [4, 2, 4, 16, 256], P(None, 'panel', 'colat', 'lon'), may hold values from 0 to 1, as said below
- turn_angles: float32 [2, 4, 16, 256], P('panel', 'colat', 'lon'), may hold values from -3.140625 to 3.140625
- ghost_slots: int32 [2, 4, 16, 896], P('panel', 'colat', 'lon'), may hold values from -1 to 8191, as said below
Outputs:
- new_state: float32 [4, 2, 4, 1536, 512], P(None, 'panel', None, 'lon', 'colat')
Inputs may be any that keep to these rules, and one draw needn't show every extreme that they name: `partners`: A block's slots with a positive count name distinct blocks; every live row is read by exactly one ghost position of the block that its slot names. `source_cells`: the interpolation square lies inside the block: lat offset at most 126, lon offset at most 94. Positive; the four weights of a row sum to one. `ghost_slots`: -1 exactly on the sides of a block that are not panel borders; on border sides each ghost position points to a live row of a slot that names this block; the positions of one side come in consecutive runs of rows.
All inputs are finite; a program needn't handle non-finite values.
Results may differ from a plain program's by a relative error of at most 0.00002.
Values sent between devices are 32-bit elements; how exact they have to be, the bound alone decides.
No kernel may reach another device: no remote copies, remote signals or barrier semaphores. Data moves between devices by JAX's collectives and lax.ppermute only.
A program may use at most 128 MiB of HBM per device.

v0:
```python
import math

import jax
import jax.numpy as jnp
from jax import lax
from jax.sharding import PartitionSpec as P

STEPS = 2


R_LOW = 0.7
HALF_ROOT = 0.7071067811865476


def swapped(block, axis, bit):
    count = lax.axis_size(axis)
    route = []
    for low in range(count):
        high = low | 1 << bit
        if high != low and high < count:
            route += [(low, high), (high, low)]
    return lax.ppermute(block, axis, route)


def with_halo(value, sides, width):
    for axis, dim in sides:
        count, length = (lax.axis_size(axis), value.shape[dim])
        up = [(i, (i + 1) % count) for i in range(count - 1)]
        down = [(j, i) for i, j in up]
        last = lax.slice_in_dim(value, length - width, length, axis=dim)
        first = lax.slice_in_dim(value, 0, width, axis=dim)
        before = lax.ppermute(last, axis, up)
        after = lax.ppermute(first, axis, down)
        value = jnp.concatenate([before, value, after], axis=dim)
    return value


def constants(lat_total, lon_total):
    d_theta = 0.5 * math.pi / lat_total
    d_phi = 1.5 * math.pi / lon_total
    spacing = R_LOW * min(d_theta, HALF_ROOT * d_phi)
    time_step = 0.25 * spacing
    kappa = 0.04 * spacing * spacing / time_step
    viscous = 0.06 * spacing * spacing / time_step
    return (
        d_theta,
        d_phi,
        time_step,
        kappa,
        viscous,
        0.05 / time_step,
        0.2 / time_step,
        4.0 * spacing,
    )


def spin_parts(theta, phi, is_yang, omega):
    cos_t = jnp.cos(theta)[None, :]
    sin_t = jnp.sin(theta)[None, :]
    cos_p = jnp.cos(phi)[:, None]
    sin_p = jnp.sin(phi)[:, None]
    keep = 1.0 - is_yang
    spin_r = omega * (keep * cos_t + is_yang * sin_t * sin_p)
    spin_t = omega * (is_yang * cos_t * sin_p - keep * sin_t)
    spin_p = omega * (is_yang * cos_p) + 0.0 * cos_t
    return (spin_r, spin_t, spin_p)


def rates(padded, lower, upper, radius, sin_t, cot_t, spins, consts):
    d_theta, d_phi, time_step, kappa, viscous, omega, buoyancy, radial = consts
    center = padded[..., 2:-2, 2:-2]
    lat_far_up = padded[..., 2:-2, 4:]
    lat_up = padded[..., 2:-2, 3:-1]
    lat_down = padded[..., 2:-2, 1:-3]
    lat_far_down = padded[..., 2:-2, :-4]
    lon_far_up = padded[..., 4:, 2:-2]
    lon_up = padded[..., 3:-1, 2:-2]
    lon_down = padded[..., 1:-3, 2:-2]
    lon_far_down = padded[..., :-4, 2:-2]
    lat_one = (8.0 * (lat_up - lat_down) - (lat_far_up - lat_far_down)) / (12.0 * d_theta)
    lat_two = (16.0 * (lat_up + lat_down) - (lat_far_up + lat_far_down) - 30.0 * center) / (
        12.0 * d_theta * d_theta
    )
    lon_one = (8.0 * (lon_up - lon_down) - (lon_far_up - lon_far_down)) / (12.0 * d_phi)
    lon_two = (16.0 * (lon_up + lon_down) - (lon_far_up + lon_far_down) - 30.0 * center) / (
        12.0 * d_phi * d_phi
    )
    rad_one = (upper - lower) / (2.0 * radial)
    rad_two = (upper + lower - 2.0 * center) / (radial * radial)
    inverse = 1.0 / radius
    vel_r = center[1]
    vel_t = center[2]
    vel_p = center[3]
    advect = vel_r * rad_one + vel_t * inverse * lat_one + vel_p * inverse / sin_t * lon_one
    laplace = (
        rad_two
        + 2.0 * inverse * rad_one
        + (lat_two + cot_t * lat_one) * (inverse * inverse)
        + lon_two * (inverse * inverse / (sin_t * sin_t))
    )
    spin_r, spin_t, spin_p = spins
    heat = kappa * laplace[0] - advect[0]
    rate_r = (
        viscous * laplace[1]
        - advect[1]
        + buoyancy * center[0]
        - 2.0 * (spin_t * vel_p - spin_p * vel_t)
    )
    rate_t = viscous * laplace[2] - advect[2] - 2.0 * (spin_p * vel_r - spin_r * vel_p)
    rate_p = viscous * laplace[3] - advect[3] - 2.0 * (spin_r * vel_t - spin_t * vel_r)
    return jnp.stack([heat, rate_r, rate_t, rate_p])


def turn_and_mask(value, turn, live):
    levels = value.shape[0] // 4
    cosine = jnp.cos(turn)
    sine = jnp.sin(turn)
    lat_part = value[2 * levels : 3 * levels]
    lon_part = value[3 * levels :]
    value = jnp.concatenate(
        [
            value[: 2 * levels],
            cosine * lat_part + sine * lon_part,
            cosine * lon_part - sine * lat_part,
        ],
        axis=0,
    )
    return jnp.where(live, value, 0.0)


def pack(values, targets, total):
    places = jnp.arange(total, dtype=jnp.int32)[:, None, None]
    buffer = jnp.zeros((total, values.shape[0], values.shape[2]), jnp.float32)
    for slot_number in range(values.shape[1]):
        buffer = buffer + jnp.where(
            places == targets[slot_number], values[:, slot_number][None], 0.0
        )
    return buffer


def on_device(state, partners, send_counts, source_cells, weights, turn_angles, ghost_slots):
    lat_blocks = lax.axis_size("colat")
    lon_blocks = lax.axis_size("lon")
    peers = lat_blocks * lon_blocks
    comps = state.shape[0]
    levels = state.shape[2]
    lon_cells = state.shape[3]
    lat_cells = state.shape[4]
    width = comps * levels
    capacity = source_cells.shape[-1] // partners.shape[-1]
    consts = constants(lat_cells * lat_blocks, lon_cells * lon_blocks)
    time_step = consts[2]
    panel = lax.axis_index("panel")
    is_yang = panel.astype(jnp.float32)
    theta = (
        (lax.axis_index("colat") * lat_cells + jnp.arange(lat_cells, dtype=jnp.int32)).astype(
            jnp.float32
        )
        + 0.5
    ) * consts[0] + 0.25 * math.pi
    phi = (
        (lax.axis_index("lon") * lon_cells + jnp.arange(lon_cells, dtype=jnp.int32)).astype(
            jnp.float32
        )
        + 0.5
    ) * consts[1] - 0.75 * math.pi
    sin_t = jnp.sin(theta)
    cot_t = jnp.cos(theta) / sin_t
    spins = spin_parts(theta, phi, is_yang, consts[5])
    radius = (jnp.arange(levels, dtype=jnp.int32).astype(jnp.float32) * consts[7] + R_LOW)[
        :, None, None
    ]
    targets = partners[0, 0, 0]
    sources = source_cells[0, 0, 0]
    wts = weights[:, 0, 0, 0]
    turn = turn_angles[0, 0, 0]
    live = jnp.arange(sources.shape[0], dtype=jnp.int32) % capacity < jnp.repeat(
        send_counts[0, 0, 0], capacity
    )
    slot_table = ghost_slots[0, 0, 0]
    safe = jnp.maximum(slot_table, 0)
    from_peer = safe // capacity
    from_row = safe % capacity

    def tendency(current):
        flat = current.reshape(width, lon_cells * lat_cells)
        value = (
            wts[0] * flat[:, sources]
            + wts[1] * flat[:, sources + 1]
            + wts[2] * flat[:, sources + lat_cells]
            + wts[3] * flat[:, sources + lat_cells + 1]
        )
        sent = turn_and_mask(value, turn, live).reshape(width, targets.shape[0], capacity)
        spread = lax.all_to_all(
            pack(sent, targets, peers), ("colat", "lon"), split_axis=0, concat_axis=0, tiled=True
        )
        received = swapped(spread, "panel", 0)
        ghosts = jnp.where((slot_table >= 0)[:, None], received[from_peer, :, from_row], 0.0).T
        padded = with_halo(
            current.reshape(width, lon_cells, lat_cells), (("colat", 2), ("lon", 1)), 2
        )
        north = ghosts[:, 0 : 2 * lon_cells].reshape(width, 2, lon_cells)
        south = ghosts[:, 2 * lon_cells : 4 * lon_cells].reshape(width, 2, lon_cells)
        west = ghosts[:, 4 * lon_cells : 4 * lon_cells + 2 * lat_cells].reshape(width, 2, lat_cells)
        east = ghosts[:, 4 * lon_cells + 2 * lat_cells :].reshape(width, 2, lat_cells)
        padded = padded.at[:, 2:-2, 1].add(north[:, 0]).at[:, 2:-2, 0].add(north[:, 1])
        padded = (
            padded.at[:, 2:-2, lat_cells + 2]
            .add(south[:, 0])
            .at[:, 2:-2, lat_cells + 3]
            .add(south[:, 1])
        )
        padded = padded.at[:, 1, 2:-2].add(west[:, 0]).at[:, 0, 2:-2].add(west[:, 1])
        padded = (
            padded.at[:, lon_cells + 2, 2:-2]
            .add(east[:, 0])
            .at[:, lon_cells + 3, 2:-2]
            .add(east[:, 1])
        )
        shaped = padded.reshape(comps, levels, lon_cells + 4, lat_cells + 4)
        lower = jnp.concatenate([current[:, :1], current[:, :-1]], axis=1)
        upper = jnp.concatenate([current[:, 1:], current[:, -1:]], axis=1)
        return rates(shaped, lower, upper, radius, sin_t, cot_t, spins, consts)

    current = state[:, 0]
    for sweep_index in range(STEPS):
        first = current + time_step * tendency(current)
        current = 0.5 * (current + first + time_step * tendency(first))
    return current[:, None]


def solution(mesh):
    in_specs = (
        P(None, "panel", None, "lon", "colat"),
        P("panel", "colat", "lon", None),
        P("panel", "colat", "lon", None),
        P("panel", "colat", "lon", None),
        P(None, "panel", "colat", "lon", None),
        P("panel", "colat", "lon", None),
        P("panel", "colat", "lon", None),
    )
    out_specs = P(None, "panel", None, "lon", "colat")
    return jax.shard_map(
        on_device, mesh=mesh, in_specs=in_specs, out_specs=out_specs, check_vma=False
    )
```

profile of v0, /device:TPU:1, one launch (start us, length us, event | category | flops | bytes accessed | tf_op | source)
XLA Modules:
  0.0 898.1 jit_solution(17793433414955016978)
XLA Ops:
  24.0 11.1 %all-to-all-start = ((f32[64,16,128]{2,1,0:T(8,128)}), f32[64,16,128]{2,1,0:T(8,128)}, u32[]{:S(2)}, u32[]{:S(2)}) async-start(f32[64,16,128]{2,1,0:T(8,128)} %select_add_fusion.3), calls=%async_computation | async-start | bytes 1048576 | tf_op jit(solution)/shard_map/all_to_all | solution.py:194
  71.4 34.3 %gather_fusion.4 = f32[896,16]{1,0:T(8,128)S(1)} fusion(f32[64,16,128]{1,2,0:T(8,128)} %copy.330, s32[896]{0:T(1024)S(1)} %fusion.34), kind=kCustom, calls=%fused_computation.4 | custom fusion | bytes 121856 | tf_op jit(solution)/shard_map/gather | solution.py:198
  114.0 11.5 %scatter-add.114 = f32[16,100,132]{1,0,2:T(8,128)S(1)} dynamic-update-slice(f32[16,100,132]{1,0,2:T(8,128)S(1)} %scatter-add.111, f32[16,1,128]{1,0,2:T(8,128)} %slice_add_fusion.11, s32[]{:T(128)} %constant.856.clone.1, s32[]{:T(128)} %constant.860.clone.1, s32[]{:T(128)} %constant.869.clone.1) | dynamic-update-slice | bytes 16388 | tf_op jit(solution)/shard_map/scatter-add | solution.py:213
  131.6 4.4 scatter-add.115
  142.2 11.5 %scatter-add.116 = f32[16,100,132]{1,0,2:T(8,128)S(1)} dynamic-update-slice(f32[16,100,132]{1,0,2:T(8,128)S(1)} %scatter-add.115, f32[16,1,128]{1,0,2:T(8,128)} %slice_add_fusion.10, s32[]{:T(128)} %constant.856.clone.1, s32[]{:T(128)} %constant.875.clone.1, s32[]{:T(128)} %constant.869.clone.1) | dynamic-update-slice | bytes 16388 | tf_op jit(solution)/shard_map/scatter-add | solution.py:216
  156.2 11.5 %scatter-add.119 = f32[16,100,132]{1,0,2:T(8,128)S(1)} dynamic-update-slice(f32[16,100,132]{1,0,2:T(8,128)S(1)} %scatter-add.116, f32[16,1,128]{1,0,2:T(8,128)} %slice_add_fusion.9, s32[]{:T(128)} %constant.856.clone.1, s32[]{:T(128)} %constant.876.clone.1, s32[]{:T(128)} %constant.869.clone.1) | dynamic-update-slice | bytes 16388 | tf_op jit(solution)/shard_map/scatter-add | solution.py:218
  167.7 7.1 fusion.52
  215.3 4.8 copy.358
  220.1 7.7 add.935
  255.1 16.0 %all-to-all-start.1 = ((f32[64,16,128]{2,1,0:T(8,128)}), f32[64,16,128]{2,1,0:T(8,128)}, u32[]{:S(2)}, u32[]{:S(2)}) async-start(f32[64,16,128]{2,1,0:T(8,128)} %select_add_fusion.2), calls=%async_computation.1 | async-start | bytes 1048576 | tf_op jit(solution)/shard_map/all_to_all | solution.py:194
  306.0 34.4 %gather_fusion.9 = f32[896,16]{1,0:T(8,128)S(1)} fusion(f32[64,16,128]{1,2,0:T(8,128)} %copy.365, s32[896]{0:T(1024)S(1)} %fusion.34), kind=kCustom, calls=%fused_computation.9 | custom fusion | bytes 121856 | tf_op jit(solution)/shard_map/gather | solution.py:198
  348.7 11.5 %scatter-add.126 = f32[16,100,132]{1,0,2:T(8,128)S(1)} dynamic-update-slice(f32[16,100,132]{1,0,2:T(8,128)S(1)} %scatter-add.125, f32[16,1,128]{1,0,2:T(8,128)} %slice_add_fusion.8, s32[]{:T(128)} %constant.856.clone.1, s32[]{:T(128)} %constant.860.clone.1, s32[]{:T(128)} %constant.869.clone.1) | dynamic-update-slice | bytes 16388 | tf_op jit(solution)/shard_map/scatter-add | solution.py:213
  366.3 4.4 scatter-add.129
  375.1 11.5 %scatter-add.130 = f32[16,100,132]{1,0,2:T(8,128)S(1)} dynamic-update-slice(f32[16,100,132]{1,0,2:T(8,128)S(1)} %scatter-add.129, f32[16,1,128]{1,0,2:T(8,128)} %slice_add_fusion.7, s32[]{:T(128)} %constant.856.clone.1, s32[]{:T(128)} %constant.875.clone.1, s32[]{:T(128)} %constant.869.clone.1) | dynamic-update-slice | bytes 16388 | tf_op jit(solution)/shard_map/scatter-add | solution.py:216
  390.9 11.5 %scatter-add.131 = f32[16,100,132]{1,0,2:T(8,128)S(1)} dynamic-update-slice(f32[16,100,132]{1,0,2:T(8,128)S(1)} %scatter-add.130, f32[16,1,128]{1,0,2:T(8,128)} %slice_add_fusion.6, s32[]{:T(128)} %constant.856.clone.1, s32[]{:T(128)} %constant.876.clone.1, s32[]{:T(128)} %constant.869.clone.1) | dynamic-update-slice | bytes 16388 | tf_op jit(solution)/shard_map/scatter-add | solution.py:218
  402.4 7.1 fusion.49
  454.6 9.7 %add_multiply_fusion = f32[16,12288]{0,1:T(8,128)} fusion(f32[16,12288]{0,1:T(8,128)} %copy.393, f32[16,12288]{0,1:T(8,128)} %copy.320, f32[16,12288]{0,1:T(8,128)} %add.935), kind=kLoop, calls=%fused_computation.20 | loop fusion | flops 589824 | bytes 3145728 | tf_op jit(solution)/shard_map/mul | solution.py:228
  481.7 14.5 %all-to-all-start.2 = ((f32[64,16,128]{2,1,0:T(8,128)}), f32[64,16,128]{2,1,0:T(8,128)}, u32[]{:S(2)}, u32[]{:S(2)}) async-start(f32[64,16,128]{2,1,0:T(8,128)} %select_add_fusion.1), calls=%async_computation.2 | async-start | bytes 1048576 | tf_op jit(solution)/shard_map/all_to_all | solution.py:194
  531.8 36.8 %gather_fusion.14 = f32[896,16]{1,0:T(8,128)} fusion(f32[64,16,128]{1,2,0:T(8,128)} %copy.400, s32[896]{0:T(1024)S(1)} %fusion.34), kind=kCustom, calls=%fused_computation.14 | custom fusion | bytes 121856 | tf_op jit(solution)/shard_map/gather | solution.py:198
  584.6 11.5 %scatter-add.140 = f32[16,100,132]{1,0,2:T(8,128)S(1)} dynamic-update-slice(f32[16,100,132]{1,0,2:T(8,128)S(1)} %scatter-add.139, f32[16,1,128]{1,0,2:T(8,128)} %slice_add_fusion.5, s32[]{:T(128)} %constant.856.clone.1, s32[]{:T(128)} %constant.860.clone.1, s32[]{:T(128)} %constant.869.clone.1) | dynamic-update-slice | bytes 16388 | tf_op jit(solution)/shard_map/scatter-add | solution.py:213
  603.0 4.4 scatter-add.141
  614.1 11.5 %scatter-add.144 = f32[16,100,132]{1,0,2:T(8,128)S(1)} dynamic-update-slice(f32[16,100,132]{1,0,2:T(8,128)S(1)} %scatter-add.141, f32[16,1,128]{1,0,2:T(8,128)} %slice_add_fusion.4, s32[]{:T(128)} %constant.856.clone.1, s32[]{:T(128)} %constant.875.clone.1, s32[]{:T(128)} %constant.869.clone.1) | dynamic-update-slice | bytes 16388 | tf_op jit(solution)/shard_map/scatter-add | solution.py:216
  630.7 11.5 %scatter-add.145 = f32[16,100,132]{1,0,2:T(8,128)S(1)} dynamic-update-slice(f32[16,100,132]{1,0,2:T(8,128)S(1)} %scatter-add.144, f32[16,1,128]{1,0,2:T(8,128)} %slice_add_fusion.3, s32[]{:T(128)} %constant.856.clone.1, s32[]{:T(128)} %constant.876.clone.1, s32[]{:T(128)} %constant.869.clone.1) | dynamic-update-slice | bytes 16388 | tf_op jit(solution)/shard_map/scatter-add | solution.py:218
  642.2 7.0 fusion.46
  689.6 4.8 copy.427
  694.4 7.8 add.997
  719.7 14.8 %all-to-all-start.3 = ((f32[64,16,128]{2,1,0:T(8,128)}), f32[64,16,128]{2,1,0:T(8,128)}, u32[]{:S(2)}, u32[]{:S(2)}) async-start(f32[64,16,128]{2,1,0:T(8,128)} %select_add_fusion), calls=%async_computation.3 | async-start | bytes 1048576 | tf_op jit(solution)/shard_map/all_to_all | solution.py:194
  768.1 34.4 %gather_fusion.19 = f32[896,16]{1,0:T(8,128)S(1)} fusion(f32[64,16,128]{1,2,0:T(8,128)} %copy.434, s32[896]{0:T(1024)S(1)} %fusion.34), kind=kCustom, calls=%fused_computation.19 | custom fusion | bytes 121856 | tf_op jit(solution)/shard_map/gather | solution.py:198
  807.6 10.7 %scatter-add.154 = f32[16,100,132]{1,0,2:T(8,128)S(1)} dynamic-update-slice(f32[16,100,132]{1,0,2:T(8,128)S(1)} %scatter-add.151, f32[16,1,128]{1,0,2:T(8,128)S(1)} %slice_add_fusion.2, s32[]{:T(128)} %constant.856.clone.1, s32[]{:T(128)} %constant.860.clone.1, s32[]{:T(128)} %constant.869.clone.1) | dynamic-update-slice | bytes 16388 | tf_op jit(solution)/shard_map/scatter-add | solution.py:213
  830.2 10.7 %scatter-add.156 = f32[16,100,132]{1,0,2:T(8,128)S(1)} dynamic-update-slice(f32[16,100,132]{1,0,2:T(8,128)S(1)} %scatter-add.155, f32[16,1,128]{1,0,2:T(8,128)S(1)} %slice_add_fusion.1, s32[]{:T(128)} %constant.856.clone.1, s32[]{:T(128)} %constant.875.clone.1, s32[]{:T(128)} %constant.869.clone.1) | dynamic-update-slice | bytes 16388 | tf_op jit(solution)/shard_map/scatter-add | solution.py:216
  844.2 10.7 %scatter-add.159 = f32[16,100,132]{1,0,2:T(8,128)S(1)} dynamic-update-slice(f32[16,100,132]{1,0,2:T(8,128)S(1)} %scatter-add.156, f32[16,1,128]{1,0,2:T(8,128)S(1)} %slice_add_fusion, s32[]{:T(128)} %constant.856.clone.1, s32[]{:T(128)} %constant.876.clone.1, s32[]{:T(128)} %constant.869.clone.1) | dynamic-update-slice | bytes 16388 | tf_op jit(solution)/shard_map/scatter-add | solution.py:218
  854.9 6.6 fusion.43
  (703 shorter events, 488.0 us)
Async XLA Ops:
  20.8 458.4 %copy-start.110 = (f32[1,1,1,1,256]{4,3,2,1,0:T(1,128)}, f32[1,1,1,1,256]{4,3,2,1,0:T(1,128)S(1)}, u32[]{:S(2)}) copy-start(f32[1,1,1,1,256]{4,3,2,1,0:T(1,128)S(1)} %get-tuple-element.559) | copy-start | bytes 3076
  20.8 458.4 %copy-start.112 = (f32[1,1,1,1,256]{4,3,2,1,0:T(1,128)}, f32[1,1,1,1,256]{4,3,2,1,0:T(1,128)S(1)}, u32[]{:S(2)}) copy-start(f32[1,1,1,1,256]{4,3,2,1,0:T(1,128)S(1)} %get-tuple-element.560) | copy-start | bytes 3076
  24.0 23.9 %all-to-all-start = ((f32[64,16,128]{2,1,0:T(8,128)}), f32[64,16,128]{2,1,0:T(8,128)}, u32[]{:S(2)}, u32[]{:S(2)}) async-start(f32[64,16,128]{2,1,0:T(8,128)} %select_add_fusion.3), calls=%async_computation | async-start | bytes 1048576 | tf_op jit(solution)/shard_map/all_to_all | solution.py:194
  35.8 11.3 %collective-permute-start = (f32[16,96,2]{1,0,2:T(8,128)S(1)}, f32[16,96,2]{1,0,2:T(8,128)S(1)}, u32[]{:S(2)}, u32[]{:S(2)}) collective-permute-start(f32[16,96,2]{1,0,2:T(8,128)S(1)} %get-tuple-element.471), channel_id=1, source_target_pairs={{0,16},{16,32},{32,48},{1,17},{17,33},{33,49},{2,18},{18,34},{34,5... | collective-permute-start | bytes 36872 | tf_op jit(solution)/shard_map/ppermute | solution.py:32
  39.1 8.0 collective-permute-start.1
  43.9 403.4 %copy-start.92 = (f32[96,128]{1,0:T(8,128)}, f32[96,128]{1,0:T(8,128)S(1)}, u32[]{:S(2)}) copy-start(f32[96,128]{1,0:T(8,128)S(1)} %broadcast_add_fusion) | copy-start | bytes 147460
  45.4 402.0 %copy-start.95 = (f32[96,128]{1,0:T(8,128)}, f32[96,128]{1,0:T(8,128)S(1)}, u32[]{:S(2)}) copy-start(f32[96,128]{1,0:T(8,128)S(1)} %get-tuple-element.575) | copy-start | bytes 147460
  47.9 19.9 %collective-permute-start.4 = (f32[64,16,128]{2,1,0:T(8,128)}, f32[64,16,128]{2,1,0:T(8,128)}, u32[]{:S(2)}, u32[]{:S(2)}) collective-permute-start(f32[64,16,128]{2,1,0:T(8,128)} %all-to-all-done), channel_id=1, source_target_pairs={{0,64},{64,0},{1,65},{65,1},{2,66},{66,2},{3,67},{67,3},{4,68},{68... | collective-permute-start | bytes 1572872 | tf_op jit(solution)/shard_map/ppermute | solution.py:22
  53.9 8.1 collective-permute-start.2
  57.4 6.4 collective-permute-start.3
  214.0 63.2 %copy-start.33 = (f32[4,4,96,128]{3,2,1,0:T(8,128)}, f32[4,4,96,128]{3,2,1,0:T(8,128)S(1)}, u32[]{:S(2)}) copy-start(f32[4,4,96,128]{3,2,1,0:T(8,128)S(1)} %get-tuple-element.489) | copy-start | bytes 2359300
  255.1 28.8 %all-to-all-start.1 = ((f32[64,16,128]{2,1,0:T(8,128)}), f32[64,16,128]{2,1,0:T(8,128)}, u32[]{:S(2)}, u32[]{:S(2)}) async-start(f32[64,16,128]{2,1,0:T(8,128)} %select_add_fusion.2), calls=%async_computation.1 | async-start | bytes 1048576 | tf_op jit(solution)/shard_map/all_to_all | solution.py:194
  272.6 5.8 collective-permute-start.5
  275.9 5.0 collective-permute-start.6
  283.8 18.6 %collective-permute-start.9 = (f32[64,16,128]{2,1,0:T(8,128)}, f32[64,16,128]{2,1,0:T(8,128)}, u32[]{:S(2)}, u32[]{:S(2)}) collective-permute-start(f32[64,16,128]{2,1,0:T(8,128)} %all-to-all-done.1), channel_id=1, source_target_pairs={{0,64},{64,0},{1,65},{65,1},{2,66},{66,2},{3,67},{67,3},{4,68},{68... | collective-permute-start | bytes 1572872 | tf_op jit(solution)/shard_map/ppermute | solution.py:22
  288.5 8.1 collective-permute-start.7
  292.5 5.8 collective-permute-start.8
  306.0 34.4 %copy-start.127 = (pred[896]{0:T(1024)(128)(4,1)S(1)}, pred[896]{0:T(1024)(128)(4,1)}, u32[]{:S(2)}) copy-start(pred[896]{0:T(1024)(128)(4,1)} %compare_reduce_fusion) | copy-start | bytes 2692
  481.7 27.2 %all-to-all-start.2 = ((f32[64,16,128]{2,1,0:T(8,128)}), f32[64,16,128]{2,1,0:T(8,128)}, u32[]{:S(2)}, u32[]{:S(2)}) async-start(f32[64,16,128]{2,1,0:T(8,128)} %select_add_fusion.1), calls=%async_computation.2 | async-start | bytes 1048576 | tf_op jit(solution)/shard_map/all_to_all | solution.py:194
  498.2 5.6 collective-permute-start.10
  501.5 4.9 collective-permute-start.11
  508.9 19.3 %collective-permute-start.14 = (f32[64,16,128]{2,1,0:T(8,128)}, f32[64,16,128]{2,1,0:T(8,128)}, u32[]{:S(2)}, u32[]{:S(2)}) collective-permute-start(f32[64,16,128]{2,1,0:T(8,128)} %all-to-all-done.2), channel_id=1, source_target_pairs={{0,64},{64,0},{1,65},{65,1},{2,66},{66,2},{3,67},{67,3},{4,68},{68... | collective-permute-start | bytes 1572872 | tf_op jit(solution)/shard_map/ppermute | solution.py:22
  514.5 8.1 collective-permute-start.12
  518.3 6.0 collective-permute-start.13
  531.8 36.8 %copy-start.128 = (pred[896]{0:T(1024)(128)(4,1)S(1)}, pred[896]{0:T(1024)(128)(4,1)}, u32[]{:S(2)}) copy-start(pred[896]{0:T(1024)(128)(4,1)} %compare_reduce_fusion) | copy-start | bytes 2692
  719.7 27.5 %all-to-all-start.3 = ((f32[64,16,128]{2,1,0:T(8,128)}), f32[64,16,128]{2,1,0:T(8,128)}, u32[]{:S(2)}, u32[]{:S(2)}) async-start(f32[64,16,128]{2,1,0:T(8,128)} %select_add_fusion), calls=%async_computation.3 | async-start | bytes 1048576 | tf_op jit(solution)/shard_map/all_to_all | solution.py:194
  734.6 5.9 collective-permute-start.15
  738.1 5.5 collective-permute-start.16
  747.2 18.3 %collective-permute-start.19 = (f32[64,16,128]{2,1,0:T(8,128)}, f32[64,16,128]{2,1,0:T(8,128)S(1)}, u32[]{:S(2)}, u32[]{:S(2)}) collective-permute-start(f32[64,16,128]{2,1,0:T(8,128)} %all-to-all-done.3), channel_id=1, source_target_pairs={{0,64},{64,0},{1,65},{65,1},{2,66},{66,2},{3,67},{67,3},{4,68},{68... | collective-permute-start | bytes 1572872 | tf_op jit(solution)/shard_map/ppermute | solution.py:22
  751.4 8.5 collective-permute-start.17
  754.1 7.5 collective-permute-start.18
  768.1 34.4 %copy-start.129 = (pred[896]{0:T(1024)(128)(4,1)S(1)}, pred[896]{0:T(1024)(128)(4,1)}, u32[]{:S(2)}) copy-start(pred[896]{0:T(1024)(128)(4,1)} %compare_reduce_fusion) | copy-start | bytes 2692
  (158 other events, 755.7 us)
where the time goes:
time: 914 us; the launch traced here: 898 us
  local copies, waits for them, and re-layouts  640 us (70%)
  other arithmetic  132 us (14%)
  starting transfers between devices  99.7 us (11%)
  waiting for transfers between devices  24.2 us (3%)
    unnamed x429, local copies, waits for them, and re-layouts  172 us
    gather x4, local copies, waits for them, and re-layouts, tendency(): received[from_peer, :, from_row]  140 us
    scatter-add x8, local copies, waits for them, and re-layouts, tendency(): padded = padded.at[:, lon_cells + 2, 2:-2].add(east[:, 0]).at[:, lon_cell...  90.3 us
    scatter-add x8, local copies, waits for them, and re-layouts, tendency(): padded.at[:, 1, 2:-2].add(west[:, 0]).at[:, 0, 2:-2].add(west[:, 1])  61.6 us
    all_to_all x4, starting transfers between devices, tendency(): lax.all_to_all(pack(sent, targets, peers), ('colat', 'lon'), split_axis=0...  56.4 us
    slice x4, local copies, waits for them, and re-layouts, rates(): center = padded[..., 2:-2, 2:-2]  27.8 us
    ppermute x8, starting transfers between devices, with_halo(): before = lax.ppermute(last, axis, up)  22.1 us
    add x8, other arithmetic, tendency(): padded = padded.at[:, lon_cells + 2, 2:-2].add(east[:, 0]).at[:, lon_cell...  18.4 us
  transfers between devices with their start and end apart: 24, of which 12 were waited for; matrix products, arithmetic and copies ran while one was open for 7% of the time, Pallas kernels for 0%

commit v1 on v0

v1 whole, which is shorter than its diff:
```python
import functools
import math

import jax
import jax.numpy as jnp
import numpy as np
from jax import lax
from jax.experimental import pallas as pl
from jax.experimental.pallas import tpu as pltpu
from jax.sharding import Mesh, PartitionSpec as P

STEPS = 2
R_LOW = 0.7
HALF_ROOT = 0.7071067811865476
LANES = 128
ROWS = 16
NO_KEY = 1.0e9
SWAP = [(0, 1), (1, 0)]


def constants(lat_total, lon_total):
    d_theta = 0.5 * math.pi / lat_total
    d_phi = 1.5 * math.pi / lon_total
    spacing = R_LOW * min(d_theta, HALF_ROOT * d_phi)
    time_step = 0.25 * spacing
    kappa = 0.04 * spacing * spacing / time_step
    viscous = 0.06 * spacing * spacing / time_step
    return (
        d_theta,
        d_phi,
        time_step,
        kappa,
        viscous,
        0.05 / time_step,
        0.2 / time_step,
        4.0 * spacing,
    )


def lane_ids(rows):
    return lax.broadcasted_iota(jnp.int32, (rows, LANES), 1)


def sub_ids():
    return lax.broadcasted_iota(jnp.int32, (8, LANES), 0)


def tile(ref, u):
    return ref[pl.ds(pl.multiple_of(u * ROWS, ROWS), ROWS), :]


def gather_rows(field, src, table, sent):
    lane = lane_ids(2 * ROWS)

    def one(slot, m, accs):
        cell = src[slot * LANES + m]
        lon = lax.shift_right_logical(cell, 7)
        lat = lax.bitwise_and(cell, LANES - 1)
        both = field[pl.ds(pl.multiple_of(lon * ROWS, ROWS), 2 * ROWS), :]
        both = pltpu.roll(both, lax.bitwise_and(m - lat + LANES, LANES - 1), 1)
        near, far = accs
        near = jnp.where(lane == m, both, near)
        far = jnp.where(lane == lax.bitwise_and(m + 1, LANES - 1), both, far)
        return near, far

    def body(m, accs):
        return one(0, m, accs[0:2]) + one(1, m, accs[2:4])

    zero = jnp.zeros((2 * ROWS, LANES), jnp.float32)
    accs = lax.fori_loop(0, LANES, body, (zero, zero, zero, zero), unroll=8)
    sub = sub_ids()
    for slot in range(2):
        near, far = accs[2 * slot], accs[2 * slot + 1]
        far = pltpu.roll(far, LANES - 1, 1)
        base = slot * 8
        w0 = table[base : base + 1, :]
        w1 = table[base + 1 : base + 2, :]
        w2 = table[base + 2 : base + 3, :]
        w3 = table[base + 3 : base + 4, :]
        value = w0 * near[:ROWS] + w1 * far[:ROWS] + w2 * near[ROWS:] + w3 * far[ROWS:]
        low, high = value[:8], value[8:]
        cosine = table[base + 4 : base + 5, :]
        sine = table[base + 5 : base + 6, :]
        turned = cosine * high + jnp.where(sub < 4, sine, -sine) * pltpu.roll(high, 4, 0)
        sent[slot * ROWS : slot * ROWS + 8, :] = low
        sent[slot * ROWS + 8 : slot * ROWS + 16, :] = turned
    sent[32:40, :] = table[16:24, :]


def put_edges(field, flag, lon_cells, edge_a, edge_b):
    first = field[0 : 2 * ROWS, :]
    last = field[(lon_cells - 2) * ROWS : lon_cells * ROWS, :]
    odd = flag[0] > 0
    edge_a[...] = jnp.where(odd, first, last)
    edge_b[...] = jnp.where(odd, last, first)


def strip_of(value, col):
    return pltpu.roll(value, 4 * col + 2, 1)


def start_kernel(lon_cells, state, src, table, flag, field, sent, edge_a, edge_b, strips):
    lane = lane_ids(ROWS)
    quad = lax.shift_right_logical(lane, 2)
    for block in range(lon_cells // 32):

        def body(col, acc, block=block):
            u = block * 32 + col
            low = state[pl.ds(u, 8, stride=lon_cells), :]
            high = state[pl.ds(u + 8 * lon_cells, 8, stride=lon_cells), :]
            value = jnp.concatenate([low, high], axis=0)
            field[pl.ds(pl.multiple_of(u * ROWS, ROWS), ROWS), :] = value
            return jnp.where(quad == col, strip_of(value, col), acc)

        acc = lax.fori_loop(0, 32, body, jnp.zeros((ROWS, LANES), jnp.float32), unroll=4)
        strips[block * ROWS : (block + 1) * ROWS, :] = acc
    put_edges(field, flag, lon_cells, edge_a, edge_b)
    gather_rows(field, src, table, sent)


def key_kernel(slots, keys, listed):
    lane = lane_ids(8)
    slot = slots[...]
    peer = lax.shift_right_arithmetic(slot, 7)
    shift = lax.bitwise_and(slot - lane, LANES - 1)
    key = jnp.where(slot >= 0, (peer * LANES + shift).astype(jnp.float32), NO_KEY)
    keys[...] = key

    def cond(carry):
        count, more = carry[0], carry[1]
        return jnp.logical_and(count < LANES, more > 0)

    def body(carry):
        count, _, last, found, total = carry
        now = jnp.min(jnp.where(key > last, key, NO_KEY), axis=1, keepdims=True)
        now = jnp.broadcast_to(now, (8, LANES))
        hit = now < NO_KEY
        found = jnp.where(lane == count, jnp.where(hit, now, 0.0), found)
        total = total + jnp.where(hit, 1.0, 0.0)
        more = (jnp.min(now) < NO_KEY).astype(jnp.int32)
        return count + 1, more, now, found, total

    zero = jnp.zeros((8, LANES), jnp.float32)
    out = lax.while_loop(cond, body, (jnp.int32(0), jnp.int32(1), zero - 1.0, zero, zero))
    listed[0:8, :] = out[3].astype(jnp.int32)
    listed[8:16, :] = out[4].astype(jnp.int32)


def fill_ghosts(received, keys, listed, ghosts):
    for row in range(8):
        wanted = keys[row : row + 1, :]

        def body(i, acc, row=row, wanted=wanted):
            key = listed[row, i]
            peer = lax.shift_right_logical(key, 7)
            shift = lax.bitwise_and(key, LANES - 1)
            value = pltpu.roll(tile(received, peer), lax.bitwise_and(LANES - shift, LANES - 1), 1)
            return jnp.where(wanted == key.astype(jnp.float32), value, acc)

        acc = lax.fori_loop(0, listed[8 + row, 0], body, jnp.zeros((ROWS, LANES), jnp.float32))
        ghosts[row * ROWS : (row + 1) * ROWS, :] = acc


def merge_strips(strip_a, strip_b, flag, ghosts, merged, blocks):
    lane = lane_ids(8)
    part = lax.bitwise_and(lane, 3)
    odd = flag[1] > 0
    for block in range(blocks):
        spread = lax.shift_right_logical(lane, 2) + 32 * block
        for half in range(2):
            at = block * ROWS + half * 8
            a = strip_a[at : at + 8, :]
            b = strip_b[at : at + 8, :]
            value = jnp.where(part < 2, jnp.where(odd, a, b), jnp.where(odd, b, a))
            extra = jnp.zeros((8, LANES), jnp.float32)
            for row, where in ((0, 1), (1, 0), (2, 2), (3, 3)):
                source = ghosts[row * ROWS + half * 8 : row * ROWS + half * 8 + 8, :]
                wide = jnp.take_along_axis(source, spread, axis=1)
                extra = jnp.where(part == where, wide, extra)
            merged[at : at + 8, :] = value + extra


def coefficients(geo, lon_cells, consts, coef):
    d_theta, d_phi, step, kappa, viscous, omega, buoyancy, radial = consts
    sub = sub_ids()
    low = sub < 4
    level = lax.bitwise_and(sub, 3).astype(jnp.float32)
    inverse = 1.0 / (level * radial + R_LOW)
    base = 2 * lon_cells
    sin_t = geo[base : base + 8, :]
    cos_t = geo[base + 8 : base + 16, :]
    yang = geo[base + 16 : base + 24, :]
    keep = 1.0 - yang
    over_sin = 1.0 / sin_t
    square = inverse * inverse
    advect_t = -step / (12.0 * d_theta) * inverse
    advect_p = -step / (12.0 * d_phi) * inverse * over_sin
    values = [advect_t, advect_p]
    for half in range(2):
        spread = jnp.where(low, step * kappa, step * viscous) if half == 0 else jnp.full((8, LANES), step * viscous)
        second_t = spread * square / (12.0 * d_theta * d_theta)
        first_t = spread * square * (cos_t * over_sin) / (12.0 * d_theta)
        second_p = spread * square * (over_sin * over_sin) / (12.0 * d_phi * d_phi)
        second_r = spread / (radial * radial)
        first_r = spread * inverse / radial
        middle = -30.0 * second_t - 30.0 * second_p - 2.0 * second_r
        values += [second_t, first_t, second_p, second_r, first_r, middle]
    twice = 2.0 * step * omega
    zero = jnp.zeros((8, LANES), jnp.float32)
    sign = jnp.where(low, 1.0, -1.0)
    values += [
        jnp.where(low, 0.0, step * buoyancy),
        jnp.where(low, zero, twice * keep * sin_t),
        jnp.where(low, zero, -twice * cos_t),
        jnp.where(low, 0.0, twice) + zero,
        sign * twice * keep * cos_t,
        sign * twice * sin_t,
        jnp.where(low, zero, -twice * keep * sin_t),
        jnp.where(low, zero, twice * cos_t),
        jnp.where(low, -twice, 0.0) + zero,
    ]
    for i, value in enumerate(values):
        coef[8 * i : 8 * i + 8, :] = value


def stage_kernel(
    second, final, lon_cells, consts, *refs
):
    refs = list(refs)
    field = refs.pop(0)
    origin = refs.pop(0) if second else None
    lon_a, lon_b, strip_a, strip_b, received, keys, listed, flag, geo, src, table = refs[:11]
    refs = refs[11:]
    if final:
        result = refs.pop(0)
    else:
        result, sent, edge_a, edge_b, strips = refs[:5]
        refs = refs[5:]
    ghosts, merged, coef, sides = refs

    radial = consts[7]
    coefficients(geo, lon_cells, consts, coef)
    fill_ghosts(received, keys, listed, ghosts)
    merge_strips(strip_a, strip_b, flag, ghosts, merged, lon_cells // 32)
    odd = flag[0] > 0
    before = jnp.where(odd, lon_a[...], lon_b[...])
    after = jnp.where(odd, lon_b[...], lon_a[...])
    sides[0:ROWS, :] = before[0:ROWS] + ghosts[5 * ROWS : 6 * ROWS, :]
    sides[ROWS : 2 * ROWS, :] = before[ROWS:] + ghosts[4 * ROWS : 5 * ROWS, :]
    sides[2 * ROWS : 3 * ROWS, :] = after[0:ROWS] + ghosts[6 * ROWS : 7 * ROWS, :]
    sides[3 * ROWS : 4 * ROWS, :] = after[ROWS:] + ghosts[7 * ROWS : 8 * ROWS, :]

    lane16 = lane_ids(ROWS)
    quad = lax.shift_right_logical(lane16, 2)
    sub = sub_ids()
    low = sub < 4
    level = lax.bitwise_and(sub, 3)
    top = level == 3
    bottom = level == 0
    advect_r = -consts[2] / (2.0 * radial)

    def c(i):
        return coef[8 * i : 8 * i + 8, :]

    def update(u, block, col, down2, down1, here, up1, up2):
        border = pltpu.roll(merged[block * ROWS : (block + 1) * ROWS, :], lax.bitwise_and(LANES - 2 - 4 * col, LANES - 1), 1)
        south1 = pltpu.roll(jnp.where(lane16 == LANES - 1, border, here), 1, 1)
        south2 = pltpu.roll(jnp.where(lane16 >= LANES - 2, border, here), 2, 1)
        north1 = pltpu.roll(jnp.where(lane16 == 0, border, here), LANES - 1, 1)
        north2 = pltpu.roll(jnp.where(lane16 < 2, border, here), LANES - 2, 1)
        lat_odd = 8.0 * (north1 - south1) - (north2 - south2)
        lat_even = 16.0 * (north1 + south1) - (north2 + south2)
        lon_odd = 8.0 * (up1 - down1) - (up2 - down2)
        lon_even = 16.0 * (up1 + down1) - (up2 + down2)
        v0, v1 = here[:8], here[8:]
        r0, r1 = pltpu.roll(v0, 4, 0), pltpu.roll(v1, 4, 0)
        vel_r = jnp.where(low, r0, v0)
        vel_t = jnp.where(low, v1, r1)
        vel_p = jnp.where(low, r1, v1)
        along_t = vel_t * c(0)
        along_p = vel_p * c(1)
        along_r = vel_r * advect_r
        sin_p = geo[pl.ds(u, 1), :]
        cos_p = geo[pl.ds(lon_cells + u, 1), :]
        turn0 = c(14) * r0 + (c(15) + c(16) * sin_p) * vel_p + (c(17) * cos_p) * vel_t
        turn1 = (c(18) + c(19) * sin_p) * r1 + (c(20) + c(21) * sin_p + c(22) * cos_p) * vel_r
        out = []
        for half, value, turn in ((0, v0, turn0), (1, v1, turn1)):
            at = 2 + 6 * half
            part = slice(8 * half, 8 * half + 8)
            above = jnp.where(top, value, pltpu.roll(value, 7, 0))
            below = jnp.where(bottom, value, pltpu.roll(value, 1, 0))
            change = (
                (c(at + 1) + along_t) * lat_odd[part]
                + c(at) * lat_even[part]
                + along_p * lon_odd[part]
                + c(at + 2) * lon_even[part]
                + (c(at + 4) + along_r) * (above - below)
                + c(at + 3) * (above + below)
                + c(at + 5) * value
                + turn
            )
            out.append(value + change)
        new = jnp.concatenate(out, axis=0)
        if second:
            new = 0.5 * (tile(origin, u) + new)
        return new

    def store(u, new):
        if final:
            result[pl.ds(u, 8, stride=lon_cells), :] = new[:8]
            result[pl.ds(u + 8 * lon_cells, 8, stride=lon_cells), :] = new[8:]
        else:
            result[pl.ds(pl.multiple_of(u * ROWS, ROWS), ROWS), :] = new

    def at(u):
        if u < 0:
            return sides[(u + 2) * ROWS : (u + 3) * ROWS, :]
        if u >= lon_cells:
            return sides[(u - lon_cells + 2) * ROWS : (u - lon_cells + 3) * ROWS, :]
        return field[u * ROWS : (u + 1) * ROWS, :]

    def edge(u, acc):
        block, col = divmod(u, 32)
        new = update(u, block, col, at(u - 2), at(u - 1), at(u), at(u + 1), at(u + 2))
        store(u, new)
        return acc if final else jnp.where(quad == col, strip_of(new, col), acc)

    blocks = lon_cells // 32
    for block in range(blocks):
        acc = jnp.zeros((ROWS, LANES), jnp.float32)
        first_col, last_col = 0, 32
        if block == 0:
            acc = edge(1, edge(0, acc))
            first_col = 2
        if block == blocks - 1:
            acc = edge(lon_cells - 1, edge(lon_cells - 2, acc))
            last_col = 30

        def body(col, acc, block=block):
            u = block * 32 + col
            new = update(u, block, col, tile(field, u - 2), tile(field, u - 1), tile(field, u), tile(field, u + 1), tile(field, u + 2))
            store(u, new)
            return acc if final else jnp.where(quad == col, strip_of(new, col), acc)

        acc = lax.fori_loop(first_col, last_col, body, acc, unroll=2)
        if not final:
            strips[block * ROWS : (block + 1) * ROWS, :] = acc
    if not final:
        put_edges(result, flag, lon_cells, edge_a, edge_b)
        gather_rows(result, src, table, sent)


def pairs(count, first):
    route = []
    for low in range(first, count - 1, 2):
        route += [(low, low + 1), (low + 1, low)]
    return route


def on_device(state, partners, send_counts, source_cells, weights, turn_angles, ghost_slots):
    lat_blocks = lax.axis_size("colat")
    lon_axes = ("lon_hi", "core")
    lon_blocks = lax.axis_size(lon_axes)
    peers = lat_blocks * lon_blocks
    lon_cells, lat_cells = state.shape[3], state.shape[4]
    consts = constants(lat_cells * lat_blocks, lon_cells * lon_blocks)
    core = lax.axis_index("core")
    colat = lax.axis_index("colat")
    lon = lax.axis_index(lon_axes)
    yang = lax.axis_index("panel").astype(jnp.float32)
    flag = jnp.stack([lon % 2, colat % 2]).astype(jnp.int32)

    live = jnp.arange(LANES, dtype=jnp.int32)[None, :] < send_counts[0, 0, 0][:, None]
    turn = turn_angles[0, 0, 0].reshape(2, LANES)
    wts = jnp.where(live[None], weights[:, 0, 0, 0].reshape(4, 2, LANES), 0.0)
    named = jnp.broadcast_to(partners[0, 0, 0].astype(jnp.float32)[:, None], (2, LANES))
    blank = jnp.zeros((2, LANES), jnp.float32)
    table = jnp.stack([wts[0], wts[1], wts[2], wts[3], jnp.cos(turn), jnp.sin(turn), blank, blank], axis=1)
    table = jnp.concatenate([table.reshape(16, LANES), named, jnp.zeros((6, LANES), jnp.float32)])
    src = source_cells[0, 0, 0]

    theta = ((colat * lat_cells + jnp.arange(lat_cells, dtype=jnp.int32)).astype(jnp.float32) + 0.5) * consts[0] + 0.25 * math.pi
    phi = ((lon * lon_cells + jnp.arange(lon_cells, dtype=jnp.int32)).astype(jnp.float32) + 0.5) * consts[1] - 0.75 * math.pi
    geo = jnp.concatenate(
        [
            jnp.broadcast_to((yang * jnp.sin(phi))[:, None], (lon_cells, LANES)),
            jnp.broadcast_to((yang * jnp.cos(phi))[:, None], (lon_cells, LANES)),
            jnp.broadcast_to(jnp.sin(theta)[None], (8, LANES)),
            jnp.broadcast_to(jnp.cos(theta)[None], (8, LANES)),
            jnp.broadcast_to(yang, (8, LANES)),
        ]
    )
    slot = ghost_slots[0, 0, 0]
    poles = jnp.pad(slot[: 4 * lon_cells].reshape(4, lon_cells), ((0, 0), (0, LANES - lon_cells)), constant_values=-1)
    slots = jnp.concatenate([poles, slot[4 * lon_cells :].reshape(4, LANES)])

    vmem = pl.BlockSpec(memory_space=pltpu.VMEM)
    smem = pl.BlockSpec(memory_space=pltpu.SMEM)

    def f32(*shape):
        return jax.ShapeDtypeStruct(shape, jnp.float32)

    cells = lon_cells * ROWS
    strip_rows = lon_cells // 32 * ROWS
    moving = [f32(cells, LANES), f32(40, LANES), f32(32, LANES), f32(32, LANES), f32(strip_rows, LANES)]
    params = pltpu.CompilerParams(vmem_limit_bytes=16 * 1024 * 1024)

    keys, listed = pl.pallas_call(
        key_kernel,
        out_shape=[f32(8, LANES), jax.ShapeDtypeStruct((16, LANES), jnp.int32)],
        in_specs=[vmem],
        out_specs=[vmem, vmem],
        compiler_params=params,
    )(slots)

    field, sent, edge_a, edge_b, strips = pl.pallas_call(
        functools.partial(start_kernel, lon_cells),
        out_shape=moving,
        in_specs=[vmem, smem, vmem, smem],
        out_specs=[vmem] * 5,
        compiler_params=params,
    )(state.reshape(cells, LANES), src, table, flag)

    place = jnp.arange(peers, dtype=jnp.int32)[:, None, None]

    def exchange(sent, edge_a, edge_b, strips):
        over = lax.ppermute(sent, "panel", SWAP)
        mate = lax.ppermute(over, "core", SWAP)
        buffer = jnp.zeros((peers, ROWS, LANES), jnp.float32)
        for message, own in ((over, core), (mate, 1 - core)):
            for number in range(2):
                target = message[32 + number, 0].astype(jnp.int32)
                spot = jnp.where(target % 2 == core, target - core + own, -1)
                buffer = buffer + jnp.where(place == spot, message[number * ROWS : (number + 1) * ROWS][None], 0.0)
        buffer, edge_a, edge_b, strips = lax.optimization_barrier((buffer, edge_a, edge_b, strips))
        received = lax.all_to_all(
            buffer.reshape(peers // 2, 2 * ROWS, LANES), ("colat", "lon_hi"), split_axis=0, concat_axis=0, tiled=True
        )
        lon_a = lax.ppermute(edge_a, lon_axes, pairs(lon_blocks, 0))
        lon_b = lax.ppermute(edge_b, lon_axes, pairs(lon_blocks, 1))
        strip_a = lax.ppermute(strips, "colat", pairs(lat_blocks, 0))
        strip_b = lax.ppermute(strips, "colat", pairs(lat_blocks, 1))
        return lon_a, lon_b, strip_a, strip_b, received.reshape(peers * ROWS, LANES)

    origin = field
    for number in range(2 * STEPS):
        second = number % 2 == 1
        final = number == 2 * STEPS - 1
        lon_a, lon_b, strip_a, strip_b, received = exchange(sent, edge_a, edge_b, strips)
        operands = [field] + ([origin] if second else [])
        specs = [vmem] * len(operands) + [vmem] * 5 + [vmem, smem, smem, vmem, smem, vmem]
        operands += [lon_a, lon_b, strip_a, strip_b, received, keys, listed, flag, geo, src, table]
        out = pl.pallas_call(
            functools.partial(stage_kernel, second, final, lon_cells, consts),
            out_shape=moving[:1] if final else moving,
            in_specs=specs,
            out_specs=[vmem] * (1 if final else 5),
            scratch_shapes=[
                pltpu.VMEM((8 * ROWS, LANES), jnp.float32),
                pltpu.VMEM((strip_rows, LANES), jnp.float32),
                pltpu.VMEM((8 * 23, LANES), jnp.float32),
                pltpu.VMEM((4 * ROWS, LANES), jnp.float32),
            ],
            compiler_params=params,
        )(*operands)
        if final:
            return out[0].reshape(state.shape)
        field, sent, edge_a, edge_b, strips = out
        if second:
            origin = field


def solution(mesh):
    lon = mesh.shape["lon"]
    fine = Mesh(
        mesh.devices.reshape(mesh.shape["panel"], mesh.shape["colat"], lon // 2, 2), ("panel", "colat", "lon_hi", "core")
    )
    lon_axes = ("lon_hi", "core")
    table = P("panel", "colat", lon_axes, None)
    in_specs = (
        P(None, "panel", None, lon_axes, "colat"),
        table,
        table,
        table,
        P(None, "panel", "colat", lon_axes, None),
        table,
        table,
    )
    out_specs = P(None, "panel", None, lon_axes, "colat")
    return jax.shard_map(on_device, mesh=fine, in_specs=in_specs, out_specs=out_specs, check_vma=False)
```

time: 914 us -> 184 us (0.20); the launches traced: 898 us -> 183 us
  local copies, waits for them, and re-layouts: 640 us -> 8.7 us
  other arithmetic: 132 us -> 4.96 us
  Pallas kernels: 0 us -> 59.5 us
  starting transfers between devices: 99.7 us -> 78.2 us
    gather x36 -> x0, local copies, waits for them, and re-layouts: 206 us -> none  [the longest x4 140 us: tendency(): received[from_peer, :, from_row]]
    unnamed x429 -> x18, local copies, waits for them, and re-layouts: 172 us -> 3.84 us
    scatter-add x32 -> x0, local copies, waits for them, and re-layouts: 156 us -> none  [the longest x8 90.3 us: tendency(): padded = padded.at[:, lon_cells + 2, 2:-2].add(east[:, 0]).at[:, lon_cell...]
    add x51 -> x4, other arithmetic: 71.7 us -> 4.54 us  [exchange(): buffer + jnp.where(place == spot, message[number * ROWS:(number + 1) * RO...]
    pallas_call x0 -> x6, Pallas kernels: none -> 59.5 us  [the longest x4 54 us: on_device(): pl.pallas_call(functools.partial(stage_kernel, second, final, lon_cells,...]
    slice x50 -> x20, local copies, waits for them, and re-layouts: 56.7 us -> 4.55 us  [the longest x8 4.49 us: exchange(): target = message[32 + number, 0].astype(jnp.int32)]
    all_to_all x4, starting transfers between devices: 56.4 us -> 20.9 us  [exchange(): lax.all_to_all(buffer.reshape(peers // 2, 2 * ROWS, LANES), ('colat', 'lo...]
    ppermute x12 -> x0, local copies, waits for them, and re-layouts: 26.8 us -> none  [the longest x4 13.3 us: swapped(): return lax.ppermute(block, axis, route)]
  transfers between devices with their start and end apart: 24 -> 28, of which waited for: 12 -> 15; matrix products, arithmetic and copies ran while one was open for 7% -> 0% of each run, Pallas kernels for 0% -> 0%
where the time goes in v1:
time: 184 us; the launch traced here: 183 us
  starting transfers between devices  78.2 us (42%)
  Pallas kernels  59.5 us (32%)
  waiting for transfers between devices  20.6 us (11%)
  between operations  11 us (6%)
  local copies, waits for them, and re-layouts  8.7 us (5%)
  other arithmetic  4.96 us (3%)
    pallas_call x4, Pallas kernels, on_device(): pl.pallas_call(functools.partial(stage_kernel, second, final, lon_cells,...  54 us
    all_to_all x4, starting transfers between devices, exchange(): lax.all_to_all(buffer.reshape(peers // 2, 2 * ROWS, LANES), ('colat', 'lo...  20.9 us
    ppermute x4, starting transfers between devices, exchange(): strip_a = lax.ppermute(strips, 'colat', pairs(lat_blocks, 0))  14.9 us
    ppermute x4, starting transfers between devices, exchange(): lon_b = lax.ppermute(edge_b, lon_axes, pairs(lon_blocks, 1))  11.9 us
    ppermute x4, starting transfers between devices, exchange(): mate = lax.ppermute(over, 'core', SWAP)  11.4 us
    ppermute x4, starting transfers between devices, exchange(): over = lax.ppermute(sent, 'panel', SWAP)  11.2 us
    ppermute x4, waiting for transfers between devices, exchange(): lon_b = lax.ppermute(edge_b, lon_axes, pairs(lon_blocks, 1))  8.87 us
    ppermute x4, waiting for transfers between devices, exchange(): over = lax.ppermute(sent, 'panel', SWAP)  5.98 us
  transfers between devices with their start and end apart: 28, of which 15 were waited for; matrix products, arithmetic and copies ran while one was open for 0% of the time, Pallas kernels for 0%

profile of v1, /device:TPU:1, one launch (start us, length us, event | category | flops | bytes accessed | tf_op | source)
XLA Modules:
  0.0 182.9 jit_solution(11010210883520053034)
XLA Ops:
  4.2 5.0 %shard_map.73 = (f32[1536,128]{1,0:T(8,128)S(1)}, f32[40,128]{1,0:T(8,128)S(1)}, f32[32,128]{1,0:T(8,128)S(1)}, f32[32,128]{1,0:T(8,128)S(1)}, f32[48,128]{1,0:T(8,128)S(1)}) custom-call(f32[1536,128]{1,0:T(8,128)S(1)} %bitcast.59, s32[256]{0:T(256)S(1)} %bitcast.60, f32[24,128]{1,0:T(8,128)S(1)} %maximum_maximum_fusion.table.refs_11_.refs_12_, ...), custom_call_target="tpu_custom_call" | custom-call | tf_op jit(solution)/shard_map/pallas_call | solution.py:417
  9.2 3.7 %collective-permute-start = (f32[40,128]{1,0:T(8,128)S(1)}, f32[40,128]{1,0:T(8,128)S(1)}, u32[]{:S(2)}, u32[]{:S(2)}) collective-permute-start(f32[40,128]{1,0:T(8,128)S(1)} %get-tuple-element.44), channel_id=1, source_target_pairs={{0,64},{64,0},{1,65},{65,1},{2,66},{66,2},{3,67},{67,3},{4,68},{68... | collective-permute-start | bytes 61448 | tf_op jit(solution)/shard_map/ppermute | solution.py:428
  15.9 2.0 %collective-permute-start.1 = (f32[40,128]{1,0:T(8,128)S(1)}, f32[40,128]{1,0:T(8,128)S(1)}, u32[]{:S(2)}, u32[]{:S(2)}) collective-permute-start(f32[40,128]{1,0:T(8,128)S(1)} %collective-permute-done), channel_id=1, source_target_pairs={{0,1},{1,0},{2,3},{3,2},{4,5},{5,4},{6,7},{7,6},{8,9},{9,8},{10,11... | collective-permute-start | bytes 61448 | tf_op jit(solution)/shard_map/ppermute | solution.py:429
  21.8 9.2 %all-to-all-start = ((f32[32,32,128]{2,1,0:T(8,128)}), f32[32,32,128]{2,1,0:T(8,128)S(1)}, u32[]{:S(2)}, u32[]{:S(2)}) async-start(f32[32,32,128]{2,1,0:T(8,128)} %bitcast.23), calls=%async_computation | async-start | bytes 1048576 | tf_op jit(solution)/shard_map/all_to_all | solution.py:437
  32.0 3.7 %collective-permute-start.4 = (f32[48,128]{1,0:T(8,128)S(1)}, f32[48,128]{1,0:T(8,128)S(1)}, u32[]{:S(2)}, u32[]{:S(2)}) collective-permute-start(f32[48,128]{1,0:T(8,128)S(1)} %get-tuple-element.50), channel_id=1, source_target_pairs={{0,16},{16,0},{32,48},{48,32},{1,17},{17,1},{33,49},{49,33},{2,18}... | collective-permute-start | bytes 73736 | tf_op jit(solution)/shard_map/ppermute | solution.py:442
  37.2 3.0 %collective-permute-start.3 = (f32[32,128]{1,0:T(8,128)S(1)}, f32[32,128]{1,0:T(8,128)S(1)}, u32[]{:S(2)}, u32[]{:S(2)}) collective-permute-start(f32[32,128]{1,0:T(8,128)S(1)} %get-tuple-element.49), channel_id=1, source_target_pairs={{1,2},{2,1},{3,4},{4,3},{5,6},{6,5},{7,8},{8,7},{9,10},{10,9},{11,... | collective-permute-start | bytes 49160 | tf_op jit(solution)/shard_map/ppermute | solution.py:441
  40.7 1.8 %collective-permute-done.3.refs_2_ = f32[32,128]{1,0:T(8,128)S(1)} collective-permute-done((f32[32,128]{1,0:T(8,128)S(1)}, f32[32,128]{1,0:T(8,128)S(1)}, u32[]{:S(2)}, u32[]{:S(2)}) %collective-permute-start.3) | collective-permute-done | bytes 16416 | tf_op jit(solution)/shard_map/ppermute | solution.py:441
  42.5 14.5 %shard_map.75 = (f32[1536,128]{1,0:T(8,128)S(1)}, f32[40,128]{1,0:T(8,128)S(1)}, f32[32,128]{1,0:T(8,128)S(1)}, f32[32,128]{1,0:T(8,128)S(1)}, f32[48,128]{1,0:T(8,128)S(1)}) custom-call(f32[1536,128]{1,0:T(8,128)S(1)} %get-tuple-element.43.refs_0_.refs_1_, f32[32,128]{1,0:T(8,128)S(1)} %collective-permute-done.2.refs_1_, ...), custom_call_target="tpu_custom_call" | custom-call | tf_op jit(solution)/shard_map/pallas_call | solution.py:454
  57.1 2.5 %collective-permute-start.6 = (f32[40,128]{1,0:T(8,128)S(1)}, f32[40,128]{1,0:T(8,128)S(1)}, u32[]{:S(2)}, u32[]{:S(2)}) collective-permute-start(f32[40,128]{1,0:T(8,128)S(1)} %get-tuple-element.55), channel_id=1, source_target_pairs={{0,64},{64,0},{1,65},{65,1},{2,66},{66,2},{3,67},{67,3},{4,68},{68... | collective-permute-start | bytes 61448 | tf_op jit(solution)/shard_map/ppermute | solution.py:428
  59.6 1.7 collective-permute-done.6
  63.2 3.3 %collective-permute-start.7 = (f32[40,128]{1,0:T(8,128)S(1)}, f32[40,128]{1,0:T(8,128)S(1)}, u32[]{:S(2)}, u32[]{:S(2)}) collective-permute-start(f32[40,128]{1,0:T(8,128)S(1)} %collective-permute-done.6), channel_id=1, source_target_pairs={{0,1},{1,0},{2,3},{3,2},{4,5},{5,4},{6,7},{7,6},{8,9},{9,8},{10,11... | collective-permute-start | bytes 61448 | tf_op jit(solution)/shard_map/ppermute | solution.py:429
  70.4 3.9 %all-to-all-start.1 = ((f32[32,32,128]{2,1,0:T(8,128)}), f32[32,32,128]{2,1,0:T(8,128)S(1)}, u32[]{:S(2)}, u32[]{:S(2)}) async-start(f32[32,32,128]{2,1,0:T(8,128)} %bitcast.30), calls=%async_computation.1 | async-start | bytes 1048576 | tf_op jit(solution)/shard_map/all_to_all | solution.py:437
  75.0 3.7 %collective-permute-start.10 = (f32[48,128]{1,0:T(8,128)S(1)}, f32[48,128]{1,0:T(8,128)S(1)}, u32[]{:S(2)}, u32[]{:S(2)}) collective-permute-start(f32[48,128]{1,0:T(8,128)S(1)} %get-tuple-element.61), channel_id=1, source_target_pairs={{0,16},{16,0},{32,48},{48,32},{1,17},{17,1},{33,49},{49,33},{2,18}... | collective-permute-start | bytes 73736 | tf_op jit(solution)/shard_map/ppermute | solution.py:442
  79.9 3.0 %collective-permute-start.9 = (f32[32,128]{1,0:T(8,128)S(1)}, f32[32,128]{1,0:T(8,128)S(1)}, u32[]{:S(2)}, u32[]{:S(2)}) collective-permute-start(f32[32,128]{1,0:T(8,128)S(1)} %get-tuple-element.60), channel_id=1, source_target_pairs={{1,2},{2,1},{3,4},{4,3},{5,6},{6,5},{7,8},{8,7},{9,10},{10,9},{11,... | collective-permute-start | bytes 49160 | tf_op jit(solution)/shard_map/ppermute | solution.py:441
  82.9 2.3 %collective-permute-done.9.refs_3_ = f32[32,128]{1,0:T(8,128)S(1)} collective-permute-done((f32[32,128]{1,0:T(8,128)S(1)}, f32[32,128]{1,0:T(8,128)S(1)}, u32[]{:S(2)}, u32[]{:S(2)}) %collective-permute-start.9) | collective-permute-done | bytes 16416 | tf_op jit(solution)/shard_map/ppermute | solution.py:441
  86.0 14.6 %shard_map.76 = (f32[1536,128]{1,0:T(8,128)S(1)}, f32[40,128]{1,0:T(8,128)S(1)}, f32[32,128]{1,0:T(8,128)S(1)}, f32[32,128]{1,0:T(8,128)S(1)}, f32[48,128]{1,0:T(8,128)S(1)}) custom-call(f32[1536,128]{1,0:T(8,128)S(1)} %get-tuple-element.54.refs_0_, f32[1536,128]{1,0:T(8,128)S(1)} %get-tuple-element.43.refs_0_.refs_1_, ...), custom_call_target="tpu_custom_call" | custom-call | tf_op jit(solution)/shard_map/pallas_call | solution.py:454
  100.6 2.5 %collective-permute-start.12 = (f32[40,128]{1,0:T(8,128)S(1)}, f32[40,128]{1,0:T(8,128)S(1)}, u32[]{:S(2)}, u32[]{:S(2)}) collective-permute-start(f32[40,128]{1,0:T(8,128)S(1)} %get-tuple-element.64), channel_id=1, source_target_pairs={{0,64},{64,0},{1,65},{65,1},{2,66},{66,2},{3,67},{67,3},{4,68},{68... | collective-permute-start | bytes 61448 | tf_op jit(solution)/shard_map/ppermute | solution.py:428
  103.1 1.7 collective-permute-done.12
  106.7 3.1 %collective-permute-start.13 = (f32[40,128]{1,0:T(8,128)S(1)}, f32[40,128]{1,0:T(8,128)S(1)}, u32[]{:S(2)}, u32[]{:S(2)}) collective-permute-start(f32[40,128]{1,0:T(8,128)S(1)} %collective-permute-done.12), channel_id=1, source_target_pairs={{0,1},{1,0},{2,3},{3,2},{4,5},{5,4},{6,7},{7,6},{8,9},{9,8},{10,11... | collective-permute-start | bytes 61448 | tf_op jit(solution)/shard_map/ppermute | solution.py:429
  113.7 3.9 %all-to-all-start.2 = ((f32[32,32,128]{2,1,0:T(8,128)}), f32[32,32,128]{2,1,0:T(8,128)S(1)}, u32[]{:S(2)}, u32[]{:S(2)}) async-start(f32[32,32,128]{2,1,0:T(8,128)} %bitcast.36), calls=%async_computation.2 | async-start | bytes 1048576 | tf_op jit(solution)/shard_map/all_to_all | solution.py:437
  118.3 3.7 %collective-permute-start.16 = (f32[48,128]{1,0:T(8,128)S(1)}, f32[48,128]{1,0:T(8,128)S(1)}, u32[]{:S(2)}, u32[]{:S(2)}) collective-permute-start(f32[48,128]{1,0:T(8,128)S(1)} %get-tuple-element.70), channel_id=1, source_target_pairs={{0,16},{16,0},{32,48},{48,32},{1,17},{17,1},{33,49},{49,33},{2,18}... | collective-permute-start | bytes 73736 | tf_op jit(solution)/shard_map/ppermute | solution.py:442
  123.2 3.0 %collective-permute-start.15 = (f32[32,128]{1,0:T(8,128)S(1)}, f32[32,128]{1,0:T(8,128)S(1)}, u32[]{:S(2)}, u32[]{:S(2)}) collective-permute-start(f32[32,128]{1,0:T(8,128)S(1)} %get-tuple-element.69), channel_id=1, source_target_pairs={{1,2},{2,1},{3,4},{4,3},{5,6},{6,5},{7,8},{8,7},{9,10},{10,9},{11,... | collective-permute-start | bytes 49160 | tf_op jit(solution)/shard_map/ppermute | solution.py:441
  126.2 2.3 %collective-permute-done.15.refs_2_ = f32[32,128]{1,0:T(8,128)S(1)} collective-permute-done((f32[32,128]{1,0:T(8,128)S(1)}, f32[32,128]{1,0:T(8,128)S(1)}, u32[]{:S(2)}, u32[]{:S(2)}) %collective-permute-start.15) | collective-permute-done | bytes 16416 | tf_op jit(solution)/shard_map/ppermute | solution.py:441
  129.3 14.5 %shard_map.77 = (f32[1536,128]{1,0:T(8,128)S(1)}, f32[40,128]{1,0:T(8,128)S(1)}, f32[32,128]{1,0:T(8,128)S(1)}, f32[32,128]{1,0:T(8,128)S(1)}, f32[48,128]{1,0:T(8,128)S(1)}) custom-call(f32[1536,128]{1,0:T(8,128)S(1)} %get-tuple-element.63.refs_0_.refs_1_, f32[32,128]{1,0:T(8,128)S(1)} %collective-permute-done.14.refs_1_, ...), custom_call_target="tpu_custom_call" | custom-call | tf_op jit(solution)/shard_map/pallas_call | solution.py:454
  143.8 2.5 %collective-permute-start.18 = (f32[40,128]{1,0:T(8,128)S(1)}, f32[40,128]{1,0:T(8,128)S(1)}, u32[]{:S(2)}, u32[]{:S(2)}) collective-permute-start(f32[40,128]{1,0:T(8,128)S(1)} %get-tuple-element.73), channel_id=1, source_target_pairs={{0,64},{64,0},{1,65},{65,1},{2,66},{66,2},{3,67},{67,3},{4,68},{68... | collective-permute-start | bytes 61448 | tf_op jit(solution)/shard_map/ppermute | solution.py:428
  146.4 1.7 collective-permute-done.18
  150.0 3.1 %collective-permute-start.19 = (f32[40,128]{1,0:T(8,128)S(1)}, f32[40,128]{1,0:T(8,128)S(1)}, u32[]{:S(2)}, u32[]{:S(2)}) collective-permute-start(f32[40,128]{1,0:T(8,128)S(1)} %collective-permute-done.18), channel_id=1, source_target_pairs={{0,1},{1,0},{2,3},{3,2},{4,5},{5,4},{6,7},{7,6},{8,9},{9,8},{10,11... | collective-permute-start | bytes 61448 | tf_op jit(solution)/shard_map/ppermute | solution.py:429
  156.9 3.9 %all-to-all-start.3 = ((f32[32,32,128]{2,1,0:T(8,128)}), f32[32,32,128]{2,1,0:T(8,128)S(1)}, u32[]{:S(2)}, u32[]{:S(2)}) async-start(f32[32,32,128]{2,1,0:T(8,128)} %bitcast.42), calls=%async_computation.3 | async-start | bytes 1048576 | tf_op jit(solution)/shard_map/all_to_all | solution.py:437
  161.5 3.7 %collective-permute-start.22 = (f32[48,128]{1,0:T(8,128)S(1)}, f32[48,128]{1,0:T(8,128)S(1)}, u32[]{:S(2)}, u32[]{:S(2)}) collective-permute-start(f32[48,128]{1,0:T(8,128)S(1)} %get-tuple-element.79), channel_id=1, source_target_pairs={{0,16},{16,0},{32,48},{48,32},{1,17},{17,1},{33,49},{49,33},{2,18}... | collective-permute-start | bytes 73736 | tf_op jit(solution)/shard_map/ppermute | solution.py:442
  166.4 3.0 %collective-permute-start.21 = (f32[32,128]{1,0:T(8,128)S(1)}, f32[32,128]{1,0:T(8,128)S(1)}, u32[]{:S(2)}, u32[]{:S(2)}) collective-permute-start(f32[32,128]{1,0:T(8,128)S(1)} %get-tuple-element.78), channel_id=1, source_target_pairs={{1,2},{2,1},{3,4},{4,3},{5,6},{6,5},{7,8},{8,7},{9,10},{10,9},{11,... | collective-permute-start | bytes 49160 | tf_op jit(solution)/shard_map/ppermute | solution.py:441
  169.4 2.3 %collective-permute-done.21.refs_3_ = f32[32,128]{1,0:T(8,128)S(1)} collective-permute-done((f32[32,128]{1,0:T(8,128)S(1)}, f32[32,128]{1,0:T(8,128)S(1)}, u32[]{:S(2)}, u32[]{:S(2)}) %collective-permute-start.21) | collective-permute-done | bytes 16416 | tf_op jit(solution)/shard_map/ppermute | solution.py:441
  172.6 10.3 %shard_map.78 = f32[1536,128]{1,0:T(8,128)} custom-call(f32[1536,128]{1,0:T(8,128)S(1)} %get-tuple-element.72.refs_0_, f32[1536,128]{1,0:T(8,128)S(1)} %get-tuple-element.63.refs_0_.refs_1_, f32[32,128]{1,0:T(8,128)S(1)} %collective-permute-done.20.refs_2_, f32[32,128]{1,0:T(8,128)S(1)} %collective-permute-done.21.refs_3_, ...), custom_call_target="tpu_custom_call" | custom-call | tf_op jit(solution)/shard_map/pallas_call | solution.py:454
  (102 shorter events, 28.6 us)
Async XLA Ops:
  1.5 0.7 copy-start.3
  3.0 1.1 copy-start
  9.2 4.8 %collective-permute-start = (f32[40,128]{1,0:T(8,128)S(1)}, f32[40,128]{1,0:T(8,128)S(1)}, u32[]{:S(2)}, u32[]{:S(2)}) collective-permute-start(f32[40,128]{1,0:T(8,128)S(1)} %get-tuple-element.44), channel_id=1, source_target_pairs={{0,64},{64,0},{1,65},{65,1},{2,66},{66,2},{3,67},{67,3},{4,68},{68... | collective-permute-start | bytes 61448 | tf_op jit(solution)/shard_map/ppermute | solution.py:428
  15.9 2.9 %collective-permute-start.1 = (f32[40,128]{1,0:T(8,128)S(1)}, f32[40,128]{1,0:T(8,128)S(1)}, u32[]{:S(2)}, u32[]{:S(2)}) collective-permute-start(f32[40,128]{1,0:T(8,128)S(1)} %collective-permute-done), channel_id=1, source_target_pairs={{0,1},{1,0},{2,3},{3,2},{4,5},{5,4},{6,7},{7,6},{8,9},{9,8},{10,11... | collective-permute-start | bytes 61448 | tf_op jit(solution)/shard_map/ppermute | solution.py:429
  21.8 9.2 %copy-start.2 = (s32[1,1,1,896]{3,2,1,0:T(1,128)S(1)}, s32[1,1,1,896]{3,2,1,0:T(1,128)}, u32[]{:S(2)}) copy-start(s32[1,1,1,896]{3,2,1,0:T(1,128)} %param.13) | copy-start | bytes 10756
  21.8 20.7 %all-to-all-start = ((f32[32,32,128]{2,1,0:T(8,128)}), f32[32,32,128]{2,1,0:T(8,128)S(1)}, u32[]{:S(2)}, u32[]{:S(2)}) async-start(f32[32,32,128]{2,1,0:T(8,128)} %bitcast.23), calls=%async_computation | async-start | bytes 1048576 | tf_op jit(solution)/shard_map/all_to_all | solution.py:437
  31.2 9.0 %slice-start = ((s32[1,1,1,896]{3,2,1,0:T(1,128)}), s32[1,1,1,512]{3,2,1,0:T(1,128)S(1)}, s32[]{:S(2)}) async-start(s32[1,1,1,896]{3,2,1,0:T(1,128)} %param.13), calls=%async_computation.4 | async-start | bytes 4096 | tf_op jit(solution)/shard_map/slice | solution.py:396
  31.2 11.4 %collective-permute-start.5 = (f32[48,128]{1,0:T(8,128)S(1)}, f32[48,128]{1,0:T(8,128)S(1)}, u32[]{:S(2)}, u32[]{:S(2)}) collective-permute-start(f32[48,128]{1,0:T(8,128)S(1)} %get-tuple-element.50), channel_id=1, source_target_pairs={{16,32},{32,16},{17,33},{33,17},{18,34},{34,18},{19,35},{35,19},{2... | collective-permute-start | bytes 73736 | tf_op jit(solution)/shard_map/ppermute | solution.py:443
  32.0 10.6 %collective-permute-start.4 = (f32[48,128]{1,0:T(8,128)S(1)}, f32[48,128]{1,0:T(8,128)S(1)}, u32[]{:S(2)}, u32[]{:S(2)}) collective-permute-start(f32[48,128]{1,0:T(8,128)S(1)} %get-tuple-element.50), channel_id=1, source_target_pairs={{0,16},{16,0},{32,48},{48,32},{1,17},{17,1},{33,49},{49,33},{2,18}... | collective-permute-start | bytes 73736 | tf_op jit(solution)/shard_map/ppermute | solution.py:442
  35.7 5.0 %collective-permute-start.2 = (f32[32,128]{1,0:T(8,128)S(1)}, f32[32,128]{1,0:T(8,128)S(1)}, u32[]{:S(2)}, u32[]{:S(2)}) collective-permute-start(f32[32,128]{1,0:T(8,128)S(1)} %get-tuple-element.48), channel_id=1, source_target_pairs={{0,1},{1,0},{2,3},{3,2},{4,5},{5,4},{6,7},{7,6},{8,9},{9,8},{10,11... | collective-permute-start | bytes 49160 | tf_op jit(solution)/shard_map/ppermute | solution.py:440
  37.2 5.3 %collective-permute-start.3 = (f32[32,128]{1,0:T(8,128)S(1)}, f32[32,128]{1,0:T(8,128)S(1)}, u32[]{:S(2)}, u32[]{:S(2)}) collective-permute-start(f32[32,128]{1,0:T(8,128)S(1)} %get-tuple-element.49), channel_id=1, source_target_pairs={{1,2},{2,1},{3,4},{4,3},{5,6},{6,5},{7,8},{8,7},{9,10},{10,9},{11,... | collective-permute-start | bytes 49160 | tf_op jit(solution)/shard_map/ppermute | solution.py:441
  57.1 4.2 %collective-permute-start.6 = (f32[40,128]{1,0:T(8,128)S(1)}, f32[40,128]{1,0:T(8,128)S(1)}, u32[]{:S(2)}, u32[]{:S(2)}) collective-permute-start(f32[40,128]{1,0:T(8,128)S(1)} %get-tuple-element.55), channel_id=1, source_target_pairs={{0,64},{64,0},{1,65},{65,1},{2,66},{66,2},{3,67},{67,3},{4,68},{68... | collective-permute-start | bytes 61448 | tf_op jit(solution)/shard_map/ppermute | solution.py:428
  63.2 4.1 %collective-permute-start.7 = (f32[40,128]{1,0:T(8,128)S(1)}, f32[40,128]{1,0:T(8,128)S(1)}, u32[]{:S(2)}, u32[]{:S(2)}) collective-permute-start(f32[40,128]{1,0:T(8,128)S(1)} %collective-permute-done.6), channel_id=1, source_target_pairs={{0,1},{1,0},{2,3},{3,2},{4,5},{5,4},{6,7},{7,6},{8,9},{9,8},{10,11... | collective-permute-start | bytes 61448 | tf_op jit(solution)/shard_map/ppermute | solution.py:429
  70.4 15.6 %all-to-all-start.1 = ((f32[32,32,128]{2,1,0:T(8,128)}), f32[32,32,128]{2,1,0:T(8,128)S(1)}, u32[]{:S(2)}, u32[]{:S(2)}) async-start(f32[32,32,128]{2,1,0:T(8,128)} %bitcast.30), calls=%async_computation.1 | async-start | bytes 1048576 | tf_op jit(solution)/shard_map/all_to_all | solution.py:437
  74.3 10.9 %collective-permute-start.11 = (f32[48,128]{1,0:T(8,128)S(1)}, f32[48,128]{1,0:T(8,128)S(1)}, u32[]{:S(2)}, u32[]{:S(2)}) collective-permute-start(f32[48,128]{1,0:T(8,128)S(1)} %get-tuple-element.61), channel_id=1, source_target_pairs={{16,32},{32,16},{17,33},{33,17},{18,34},{34,18},{19,35},{35,19},{2... | collective-permute-start | bytes 73736 | tf_op jit(solution)/shard_map/ppermute | solution.py:443
  75.0 10.3 %collective-permute-start.10 = (f32[48,128]{1,0:T(8,128)S(1)}, f32[48,128]{1,0:T(8,128)S(1)}, u32[]{:S(2)}, u32[]{:S(2)}) collective-permute-start(f32[48,128]{1,0:T(8,128)S(1)} %get-tuple-element.61), channel_id=1, source_target_pairs={{0,16},{16,0},{32,48},{48,32},{1,17},{17,1},{33,49},{49,33},{2,18}... | collective-permute-start | bytes 73736 | tf_op jit(solution)/shard_map/ppermute | solution.py:442
  78.7 4.2 %collective-permute-start.8 = (f32[32,128]{1,0:T(8,128)S(1)}, f32[32,128]{1,0:T(8,128)S(1)}, u32[]{:S(2)}, u32[]{:S(2)}) collective-permute-start(f32[32,128]{1,0:T(8,128)S(1)} %get-tuple-element.59), channel_id=1, source_target_pairs={{0,1},{1,0},{2,3},{3,2},{4,5},{5,4},{6,7},{7,6},{8,9},{9,8},{10,11... | collective-permute-start | bytes 49160 | tf_op jit(solution)/shard_map/ppermute | solution.py:440
  79.9 5.3 %collective-permute-start.9 = (f32[32,128]{1,0:T(8,128)S(1)}, f32[32,128]{1,0:T(8,128)S(1)}, u32[]{:S(2)}, u32[]{:S(2)}) collective-permute-start(f32[32,128]{1,0:T(8,128)S(1)} %get-tuple-element.60), channel_id=1, source_target_pairs={{1,2},{2,1},{3,4},{4,3},{5,6},{6,5},{7,8},{8,7},{9,10},{10,9},{11,... | collective-permute-start | bytes 49160 | tf_op jit(solution)/shard_map/ppermute | solution.py:441
  100.6 4.2 %collective-permute-start.12 = (f32[40,128]{1,0:T(8,128)S(1)}, f32[40,128]{1,0:T(8,128)S(1)}, u32[]{:S(2)}, u32[]{:S(2)}) collective-permute-start(f32[40,128]{1,0:T(8,128)S(1)} %get-tuple-element.64), channel_id=1, source_target_pairs={{0,64},{64,0},{1,65},{65,1},{2,66},{66,2},{3,67},{67,3},{4,68},{68... | collective-permute-start | bytes 61448 | tf_op jit(solution)/shard_map/ppermute | solution.py:428
  106.7 3.9 %collective-permute-start.13 = (f32[40,128]{1,0:T(8,128)S(1)}, f32[40,128]{1,0:T(8,128)S(1)}, u32[]{:S(2)}, u32[]{:S(2)}) collective-permute-start(f32[40,128]{1,0:T(8,128)S(1)} %collective-permute-done.12), channel_id=1, source_target_pairs={{0,1},{1,0},{2,3},{3,2},{4,5},{5,4},{6,7},{7,6},{8,9},{9,8},{10,11... | collective-permute-start | bytes 61448 | tf_op jit(solution)/shard_map/ppermute | solution.py:429
  113.7 15.6 %all-to-all-start.2 = ((f32[32,32,128]{2,1,0:T(8,128)}), f32[32,32,128]{2,1,0:T(8,128)S(1)}, u32[]{:S(2)}, u32[]{:S(2)}) async-start(f32[32,32,128]{2,1,0:T(8,128)} %bitcast.36), calls=%async_computation.2 | async-start | bytes 1048576 | tf_op jit(solution)/shard_map/all_to_all | solution.py:437
  117.6 10.9 %collective-permute-start.17 = (f32[48,128]{1,0:T(8,128)S(1)}, f32[48,128]{1,0:T(8,128)S(1)}, u32[]{:S(2)}, u32[]{:S(2)}) collective-permute-start(f32[48,128]{1,0:T(8,128)S(1)} %get-tuple-element.70), channel_id=1, source_target_pairs={{16,32},{32,16},{17,33},{33,17},{18,34},{34,18},{19,35},{35,19},{2... | collective-permute-start | bytes 73736 | tf_op jit(solution)/shard_map/ppermute | solution.py:443
  118.3 10.3 %collective-permute-start.16 = (f32[48,128]{1,0:T(8,128)S(1)}, f32[48,128]{1,0:T(8,128)S(1)}, u32[]{:S(2)}, u32[]{:S(2)}) collective-permute-start(f32[48,128]{1,0:T(8,128)S(1)} %get-tuple-element.70), channel_id=1, source_target_pairs={{0,16},{16,0},{32,48},{48,32},{1,17},{17,1},{33,49},{49,33},{2,18}... | collective-permute-start | bytes 73736 | tf_op jit(solution)/shard_map/ppermute | solution.py:442
  122.0 4.2 %collective-permute-start.14 = (f32[32,128]{1,0:T(8,128)S(1)}, f32[32,128]{1,0:T(8,128)S(1)}, u32[]{:S(2)}, u32[]{:S(2)}) collective-permute-start(f32[32,128]{1,0:T(8,128)S(1)} %get-tuple-element.68), channel_id=1, source_target_pairs={{0,1},{1,0},{2,3},{3,2},{4,5},{5,4},{6,7},{7,6},{8,9},{9,8},{10,11... | collective-permute-start | bytes 49160 | tf_op jit(solution)/shard_map/ppermute | solution.py:440
  123.2 5.3 %collective-permute-start.15 = (f32[32,128]{1,0:T(8,128)S(1)}, f32[32,128]{1,0:T(8,128)S(1)}, u32[]{:S(2)}, u32[]{:S(2)}) collective-permute-start(f32[32,128]{1,0:T(8,128)S(1)} %get-tuple-element.69), channel_id=1, source_target_pairs={{1,2},{2,1},{3,4},{4,3},{5,6},{6,5},{7,8},{8,7},{9,10},{10,9},{11,... | collective-permute-start | bytes 49160 | tf_op jit(solution)/shard_map/ppermute | solution.py:441
  143.8 4.2 %collective-permute-start.18 = (f32[40,128]{1,0:T(8,128)S(1)}, f32[40,128]{1,0:T(8,128)S(1)}, u32[]{:S(2)}, u32[]{:S(2)}) collective-permute-start(f32[40,128]{1,0:T(8,128)S(1)} %get-tuple-element.73), channel_id=1, source_target_pairs={{0,64},{64,0},{1,65},{65,1},{2,66},{66,2},{3,67},{67,3},{4,68},{68... | collective-permute-start | bytes 61448 | tf_op jit(solution)/shard_map/ppermute | solution.py:428
  150.0 3.9 %collective-permute-start.19 = (f32[40,128]{1,0:T(8,128)S(1)}, f32[40,128]{1,0:T(8,128)S(1)}, u32[]{:S(2)}, u32[]{:S(2)}) collective-permute-start(f32[40,128]{1,0:T(8,128)S(1)} %collective-permute-done.18), channel_id=1, source_target_pairs={{0,1},{1,0},{2,3},{3,2},{4,5},{5,4},{6,7},{7,6},{8,9},{9,8},{10,11... | collective-permute-start | bytes 61448 | tf_op jit(solution)/shard_map/ppermute | solution.py:429
  156.9 15.6 %all-to-all-start.3 = ((f32[32,32,128]{2,1,0:T(8,128)}), f32[32,32,128]{2,1,0:T(8,128)S(1)}, u32[]{:S(2)}, u32[]{:S(2)}) async-start(f32[32,32,128]{2,1,0:T(8,128)} %bitcast.42), calls=%async_computation.3 | async-start | bytes 1048576 | tf_op jit(solution)/shard_map/all_to_all | solution.py:437
  160.8 10.9 %collective-permute-start.23 = (f32[48,128]{1,0:T(8,128)S(1)}, f32[48,128]{1,0:T(8,128)S(1)}, u32[]{:S(2)}, u32[]{:S(2)}) collective-permute-start(f32[48,128]{1,0:T(8,128)S(1)} %get-tuple-element.79), channel_id=1, source_target_pairs={{16,32},{32,16},{17,33},{33,17},{18,34},{34,18},{19,35},{35,19},{2... | collective-permute-start | bytes 73736 | tf_op jit(solution)/shard_map/ppermute | solution.py:443
  161.5 10.3 %collective-permute-start.22 = (f32[48,128]{1,0:T(8,128)S(1)}, f32[48,128]{1,0:T(8,128)S(1)}, u32[]{:S(2)}, u32[]{:S(2)}) collective-permute-start(f32[48,128]{1,0:T(8,128)S(1)} %get-tuple-element.79), channel_id=1, source_target_pairs={{0,16},{16,0},{32,48},{48,32},{1,17},{17,1},{33,49},{49,33},{2,18}... | collective-permute-start | bytes 73736 | tf_op jit(solution)/shard_map/ppermute | solution.py:442
  165.2 4.2 %collective-permute-start.20 = (f32[32,128]{1,0:T(8,128)S(1)}, f32[32,128]{1,0:T(8,128)S(1)}, u32[]{:S(2)}, u32[]{:S(2)}) collective-permute-start(f32[32,128]{1,0:T(8,128)S(1)} %get-tuple-element.77), channel_id=1, source_target_pairs={{0,1},{1,0},{2,3},{3,2},{4,5},{5,4},{6,7},{7,6},{8,9},{9,8},{10,11... | collective-permute-start | bytes 49160 | tf_op jit(solution)/shard_map/ppermute | solution.py:440
  166.4 5.3 %collective-permute-start.21 = (f32[32,128]{1,0:T(8,128)S(1)}, f32[32,128]{1,0:T(8,128)S(1)}, u32[]{:S(2)}, u32[]{:S(2)}) collective-permute-start(f32[32,128]{1,0:T(8,128)S(1)} %get-tuple-element.78), channel_id=1, source_target_pairs={{1,2},{2,1},{3,4},{4,3},{5,6},{6,5},{7,8},{8,7},{9,10},{10,9},{11,... | collective-permute-start | bytes 49160 | tf_op jit(solution)/shard_map/ppermute | solution.py:441
  (4 other events, 2.7 us)

commit v2 on v1

--- a/solution.py
+++ b/solution.py
@@ -15,6 +15,7 @@
 LANES = 128
 ROWS = 16
 NO_KEY = 1.0e9
+GROUP = 8
 SWAP = [(0, 1), (1, 0)]
 
 
@@ -45,8 +46,14 @@
     return lax.broadcasted_iota(jnp.int32, (8, LANES), 0)
 
 
+def rows_of(u):
+    if isinstance(u, int):
+        return slice(u * ROWS, (u + 1) * ROWS)
+    return pl.ds(pl.multiple_of(u * ROWS, ROWS), ROWS)
+
+
 def tile(ref, u):
-    return ref[pl.ds(pl.multiple_of(u * ROWS, ROWS), ROWS), :]
+    return ref[rows_of(u), :]
 
 
 def gather_rows(field, src, table, sent):
@@ -263,7 +270,7 @@
         return coef[8 * i : 8 * i + 8, :]
 
     def update(u, block, col, down2, down1, here, up1, up2):
-        border = pltpu.roll(merged[block * ROWS : (block + 1) * ROWS, :], lax.bitwise_and(LANES - 2 - 4 * col, LANES - 1), 1)
+        border = pltpu.roll(tile(merged, block), lax.bitwise_and(LANES - 2 - 4 * col, LANES - 1), 1)
         south1 = pltpu.roll(jnp.where(lane16 == LANES - 1, border, here), 1, 1)
         south2 = pltpu.roll(jnp.where(lane16 >= LANES - 2, border, here), 2, 1)
         north1 = pltpu.roll(jnp.where(lane16 == 0, border, here), LANES - 1, 1)
@@ -311,7 +318,7 @@
             result[pl.ds(u, 8, stride=lon_cells), :] = new[:8]
             result[pl.ds(u + 8 * lon_cells, 8, stride=lon_cells), :] = new[8:]
         else:
-            result[pl.ds(pl.multiple_of(u * ROWS, ROWS), ROWS), :] = new
+            result[rows_of(u), :] = new
 
     def at(u):
         if u < 0:
@@ -320,35 +327,59 @@
             return sides[(u - lon_cells + 2) * ROWS : (u - lon_cells + 3) * ROWS, :]
         return field[u * ROWS : (u + 1) * ROWS, :]
 
-    def edge(u, acc):
-        block, col = divmod(u, 32)
-        new = update(u, block, col, at(u - 2), at(u - 1), at(u), at(u + 1), at(u + 2))
-        store(u, new)
-        return acc if final else jnp.where(quad == col, strip_of(new, col), acc)
-
-    blocks = lon_cells // 32
-    for block in range(blocks):
+    def group(index, block, col, tiles):
         acc = jnp.zeros((ROWS, LANES), jnp.float32)
-        first_col, last_col = 0, 32
-        if block == 0:
-            acc = edge(1, edge(0, acc))
-            first_col = 2
-        if block == blocks - 1:
-            acc = edge(lon_cells - 1, edge(lon_cells - 2, acc))
-            last_col = 30
-
-        def body(col, acc, block=block):
-            u = block * 32 + col
-            new = update(u, block, col, tile(field, u - 2), tile(field, u - 1), tile(field, u), tile(field, u + 1), tile(field, u + 2))
-            store(u, new)
-            return acc if final else jnp.where(quad == col, strip_of(new, col), acc)
-
-        acc = lax.fori_loop(first_col, last_col, body, acc, unroll=2)
+        for k in range(GROUP):
+            new = update(index + k, block, col + k, *tiles[k : k + 5])
+            store(index + k, new)
+            if not final:
+                acc = jnp.where(quad == col + k, strip_of(new, col + k), acc)
         if not final:
-            strips[block * ROWS : (block + 1) * ROWS, :] = acc
+            rows = rows_of(block)
+            mine = jnp.logical_and(quad >= col, quad < col + GROUP)
+            strips[rows, :] = jnp.where(mine, acc, strips[rows, :])
+
+    if not final:
+        strips[...] = jnp.zeros(strips.shape, jnp.float32)
+    for index in (0, lon_cells - GROUP):
+        group(index, index // 32, index % 32, [at(u) for u in range(index - 2, index + GROUP + 2)])
+
+    def body(number, carry):
+        index = number * GROUP
+        tiles = [tile(field, index + k) for k in range(-2, GROUP + 2)]
+        group(index, lax.shift_right_logical(index, 5), lax.bitwise_and(index, 31), tiles)
+        return carry
+
+    lax.fori_loop(1, lon_cells // GROUP - 1, body, 0)
     if not final:
         put_edges(result, flag, lon_cells, edge_a, edge_b)
         gather_rows(result, src, table, sent)
+
+
+def pack_kernel(message_a, message_b, flag, _, buffer, staged, sems):
+    core = flag[0]
+    copies = []
+    for number, (message, own) in enumerate(((message_a, core), (message_b, 1 - core))):
+        target0 = jnp.max(message[32:33, :]).astype(jnp.int32)
+        target1 = jnp.max(message[33:34, :]).astype(jnp.int32)
+        same = target0 == target1
+        slot0, slot1 = message[0:ROWS, :], message[ROWS : 2 * ROWS, :]
+        staged[2 * number * ROWS : (2 * number + 1) * ROWS, :] = jnp.where(same, slot0 + slot1, slot0)
+        staged[(2 * number + 1) * ROWS : (2 * number + 2) * ROWS, :] = slot1
+        for slot, target in ((0, target0), (1, target1)):
+            wanted = lax.bitwise_and(target, 1) == core
+            if slot == 1:
+                wanted = jnp.logical_and(wanted, jnp.logical_not(same))
+            place = pl.multiple_of((target - core + own) * ROWS, ROWS)
+            at = 2 * number + slot
+            copy = pltpu.make_async_copy(
+                staged.at[pl.ds(at * ROWS, ROWS), :], buffer.at[pl.ds(place, ROWS), :], sems.at[at]
+            )
+            copies.append((wanted, copy))
+    for wanted, copy in copies:
+        pl.when(wanted)(copy.start)
+    for wanted, copy in copies:
+        pl.when(wanted)(copy.wait)
 
 
 def pairs(count, first):
@@ -422,17 +453,20 @@
         compiler_params=params,
     )(state.reshape(cells, LANES), src, table, flag)
 
-    place = jnp.arange(peers, dtype=jnp.int32)[:, None, None]
-
-    def exchange(sent, edge_a, edge_b, strips):
+    hbm = pl.BlockSpec(memory_space=pl.ANY)
+
+    def exchange(buffer, sent, edge_a, edge_b, strips):
         over = lax.ppermute(sent, "panel", SWAP)
         mate = lax.ppermute(over, "core", SWAP)
-        buffer = jnp.zeros((peers, ROWS, LANES), jnp.float32)
-        for message, own in ((over, core), (mate, 1 - core)):
-            for number in range(2):
-                target = message[32 + number, 0].astype(jnp.int32)
-                spot = jnp.where(target % 2 == core, target - core + own, -1)
-                buffer = buffer + jnp.where(place == spot, message[number * ROWS : (number + 1) * ROWS][None], 0.0)
+        buffer = pl.pallas_call(
+            pack_kernel,
+            out_shape=f32(peers * ROWS, LANES),
+            in_specs=[vmem, vmem, smem, hbm],
+            out_specs=hbm,
+            scratch_shapes=[pltpu.VMEM((4 * ROWS, LANES), jnp.float32), pltpu.SemaphoreType.DMA((4,))],
+            input_output_aliases={3: 0},
+            compiler_params=params,
+        )(over, mate, flag, buffer)
         buffer, edge_a, edge_b, strips = lax.optimization_barrier((buffer, edge_a, edge_b, strips))
         received = lax.all_to_all(
             buffer.reshape(peers // 2, 2 * ROWS, LANES), ("colat", "lon_hi"), split_axis=0, concat_axis=0, tiled=True
@@ -441,13 +475,14 @@
         lon_b = lax.ppermute(edge_b, lon_axes, pairs(lon_blocks, 1))
         strip_a = lax.ppermute(strips, "colat", pairs(lat_blocks, 0))
         strip_b = lax.ppermute(strips, "colat", pairs(lat_blocks, 1))
-        return lon_a, lon_b, strip_a, strip_b, received.reshape(peers * ROWS, LANES)
+        return buffer, lon_a, lon_b, strip_a, strip_b, received.reshape(peers * ROWS, LANES)
 
     origin = field
+    buffer = jnp.zeros((peers * ROWS, LANES), jnp.float32)
     for number in range(2 * STEPS):
         second = number % 2 == 1
         final = number == 2 * STEPS - 1
-        lon_a, lon_b, strip_a, strip_b, received = exchange(sent, edge_a, edge_b, strips)
+        buffer, lon_a, lon_b, strip_a, strip_b, received = exchange(buffer, sent, edge_a, edge_b, strips)
         operands = [field] + ([origin] if second else [])
         specs = [vmem] * len(operands) + [vmem] * 5 + [vmem, smem, smem, vmem, smem, vmem]
         operands += [lon_a, lon_b, strip_a, strip_b, received, keys, listed, flag, geo, src, table]

time: 184 us -> 141 us (0.77)
  Pallas kernels: 59.5 us -> 35.5 us
  between operations: 11 us -> 0.28 us
  other arithmetic: 4.96 us -> 0.34 us
  local copies, waits for them, and re-layouts: 8.7 us -> 5.01 us
    pallas_call x4, Pallas kernels: 54 us -> 24.8 us  [on_device(): pl.pallas_call(functools.partial(stage_kernel, second, final, lon_cells,...]
    pallas_call x0 -> x4, Pallas kernels: none -> 5.24 us  [exchange(): pl.pallas_call(pack_kernel, out_shape=f32(peers * ROWS, LANES), in_specs=...]
    add x4 -> x0, other arithmetic: 4.54 us -> none  [exchange(): buffer + jnp.where(place == spot, message[number * ROWS:(number + 1) * RO...]
    slice x16 -> x0, local copies, waits for them, and re-layouts: 4.52 us -> none  [the longest x8 4.49 us: exchange(): target = message[32 + number, 0].astype(jnp.int32)]
where the time goes in v2:
time: 141 us; the launch traced here: 139 us
  starting transfers between devices  77.7 us (55%)
  Pallas kernels  35.5 us (25%)
  waiting for transfers between devices  20.7 us (15%)
  local copies, waits for them, and re-layouts  5.01 us (4%)
    pallas_call x4, Pallas kernels, on_device(): pl.pallas_call(functools.partial(stage_kernel, second, final, lon_cells,...  24.8 us
    all_to_all x4, starting transfers between devices, exchange(): lax.all_to_all(buffer.reshape(peers // 2, 2 * ROWS, LANES), ('colat', 'lo...  20.8 us
    ppermute x4, starting transfers between devices, exchange(): strip_a = lax.ppermute(strips, 'colat', pairs(lat_blocks, 0))  14.9 us
    ppermute x4, starting transfers between devices, exchange(): lon_b = lax.ppermute(edge_b, lon_axes, pairs(lon_blocks, 1))  11.9 us
    ppermute x4, starting transfers between devices, exchange(): over = lax.ppermute(sent, 'panel', SWAP)  11.2 us
    ppermute x4, starting transfers between devices, exchange(): mate = lax.ppermute(over, 'core', SWAP)  11.1 us
    ppermute x4, waiting for transfers between devices, exchange(): lon_b = lax.ppermute(edge_b, lon_axes, pairs(lon_blocks, 1))  8.87 us
    ppermute x4, waiting for transfers between devices, exchange(): over = lax.ppermute(sent, 'panel', SWAP)  6.01 us
  transfers between devices with their start and end apart: 28, of which 15 were waited for; matrix products, arithmetic and copies ran while one was open for 0% of the time, Pallas kernels for 0%

profile of v2, /device:TPU:1, one launch (start us, length us, event | category | flops | bytes accessed | tf_op | source)
XLA Modules:
  0.0 139.4 jit_solution(14749659427550808728)
XLA Ops:
  4.2 5.0 %shard_map.73 = (f32[1536,128]{1,0:T(8,128)S(1)}, f32[40,128]{1,0:T(8,128)S(1)}, f32[32,128]{1,0:T(8,128)S(1)}, f32[32,128]{1,0:T(8,128)S(1)}, f32[48,128]{1,0:T(8,128)S(1)}) custom-call(f32[1536,128]{1,0:T(8,128)S(1)} %bitcast.43, s32[256]{0:T(256)S(1)} %bitcast.44, f32[24,128]{1,0:T(8,128)S(1)} %maximum_maximum_fusion.table.refs_11_.refs_12_, ...), custom_call_target="tpu_custom_call" | custom-call | tf_op jit(solution)/shard_map/pallas_call | solution.py:448
  9.2 3.7 %collective-permute-start = (f32[40,128]{1,0:T(8,128)S(1)}, f32[40,128]{1,0:T(8,128)S(1)}, u32[]{:S(2)}, u32[]{:S(2)}) collective-permute-start(f32[40,128]{1,0:T(8,128)S(1)} %get-tuple-element.44), channel_id=1, source_target_pairs={{0,64},{64,0},{1,65},{65,1},{2,66},{66,2},{3,67},{67,3},{4,68},{68... | collective-permute-start | bytes 61448 | tf_op jit(solution)/shard_map/ppermute | solution.py:459
  14.0 2.0 %collective-permute-start.1 = (f32[40,128]{1,0:T(8,128)S(1)}, f32[40,128]{1,0:T(8,128)S(1)}, u32[]{:S(2)}, u32[]{:S(2)}) collective-permute-start(f32[40,128]{1,0:T(8,128)S(1)} %collective-permute-done.message_a), channel_id=1, source_target_pairs={{0,1},{1,0},{2,3},{3,2},{4,5},{5,4},{6,7},{7,6},{8,9},{9,8},{10,11... | collective-permute-start | bytes 61448 | tf_op jit(solution)/shard_map/ppermute | solution.py:460
  18.9 9.1 %all-to-all-start = ((f32[32,32,128]{2,1,0:T(8,128)}), f32[32,32,128]{2,1,0:T(8,128)S(1)}, u32[]{:S(2)}, u32[]{:S(2)}) async-start(f32[32,32,128]{2,1,0:T(8,128)} %bitcast.19), calls=%async_computation | async-start | bytes 1048576 | tf_op jit(solution)/shard_map/all_to_all | solution.py:471
  29.0 3.7 %collective-permute-start.4 = (f32[48,128]{1,0:T(8,128)S(1)}, f32[48,128]{1,0:T(8,128)S(1)}, u32[]{:S(2)}, u32[]{:S(2)}) collective-permute-start(f32[48,128]{1,0:T(8,128)S(1)} %get-tuple-element.50), channel_id=1, source_target_pairs={{0,16},{16,0},{32,48},{48,32},{1,17},{17,1},{33,49},{49,33},{2,18}... | collective-permute-start | bytes 73736 | tf_op jit(solution)/shard_map/ppermute | solution.py:476
  34.2 3.0 %collective-permute-start.3 = (f32[32,128]{1,0:T(8,128)S(1)}, f32[32,128]{1,0:T(8,128)S(1)}, u32[]{:S(2)}, u32[]{:S(2)}) collective-permute-start(f32[32,128]{1,0:T(8,128)S(1)} %get-tuple-element.49), channel_id=1, source_target_pairs={{1,2},{2,1},{3,4},{4,3},{5,6},{6,5},{7,8},{8,7},{9,10},{10,9},{11,... | collective-permute-start | bytes 49160 | tf_op jit(solution)/shard_map/ppermute | solution.py:475
  37.7 1.8 %collective-permute-done.3.refs_2_ = f32[32,128]{1,0:T(8,128)S(1)} collective-permute-done((f32[32,128]{1,0:T(8,128)S(1)}, f32[32,128]{1,0:T(8,128)S(1)}, u32[]{:S(2)}, u32[]{:S(2)}) %collective-permute-start.3) | collective-permute-done | bytes 16416 | tf_op jit(solution)/shard_map/ppermute | solution.py:475
  39.5 6.6 %shard_map.76 = (f32[1536,128]{1,0:T(8,128)S(1)}, f32[40,128]{1,0:T(8,128)S(1)}, f32[32,128]{1,0:T(8,128)S(1)}, f32[32,128]{1,0:T(8,128)S(1)}, f32[48,128]{1,0:T(8,128)S(1)}) custom-call(f32[1536,128]{1,0:T(8,128)S(1)} %get-tuple-element.43.refs_0_.refs_1_, f32[32,128]{1,0:T(8,128)S(1)} %collective-permute-done.2.refs_1_, ...), custom_call_target="tpu_custom_call" | custom-call | tf_op jit(solution)/shard_map/pallas_call | solution.py:489
  46.1 2.5 %collective-permute-start.6 = (f32[40,128]{1,0:T(8,128)S(1)}, f32[40,128]{1,0:T(8,128)S(1)}, u32[]{:S(2)}, u32[]{:S(2)}) collective-permute-start(f32[40,128]{1,0:T(8,128)S(1)} %get-tuple-element.55), channel_id=1, source_target_pairs={{0,64},{64,0},{1,65},{65,1},{2,66},{66,2},{3,67},{67,3},{4,68},{68... | collective-permute-start | bytes 61448 | tf_op jit(solution)/shard_map/ppermute | solution.py:459
  48.6 1.7 %collective-permute-done.6.message_a = f32[40,128]{1,0:T(8,128)S(1)} collective-permute-done((f32[40,128]{1,0:T(8,128)S(1)}, f32[40,128]{1,0:T(8,128)S(1)}, u32[]{:S(2)}, u32[]{:S(2)}) %collective-permute-start.6) | collective-permute-done | bytes 20512 | tf_op jit(solution)/shard_map/ppermute | solution.py:459
  50.3 3.2 %collective-permute-start.7 = (f32[40,128]{1,0:T(8,128)S(1)}, f32[40,128]{1,0:T(8,128)S(1)}, u32[]{:S(2)}, u32[]{:S(2)}) collective-permute-start(f32[40,128]{1,0:T(8,128)S(1)} %collective-permute-done.6.message_a), channel_id=1, source_target_pairs={{0,1},{1,0},{2,3},{3,2},{4,5},{5,4},{6,7},{7,6},{8,9},{9,8},{10,11... | collective-permute-start | bytes 61448 | tf_op jit(solution)/shard_map/ppermute | solution.py:460
  55.7 3.9 %all-to-all-start.1 = ((f32[32,32,128]{2,1,0:T(8,128)}), f32[32,32,128]{2,1,0:T(8,128)S(1)}, u32[]{:S(2)}, u32[]{:S(2)}) async-start(f32[32,32,128]{2,1,0:T(8,128)} %bitcast.22), calls=%async_computation.1 | async-start | bytes 1048576 | tf_op jit(solution)/shard_map/all_to_all | solution.py:471
  60.2 3.7 %collective-permute-start.10 = (f32[48,128]{1,0:T(8,128)S(1)}, f32[48,128]{1,0:T(8,128)S(1)}, u32[]{:S(2)}, u32[]{:S(2)}) collective-permute-start(f32[48,128]{1,0:T(8,128)S(1)} %get-tuple-element.61), channel_id=1, source_target_pairs={{0,16},{16,0},{32,48},{48,32},{1,17},{17,1},{33,49},{49,33},{2,18}... | collective-permute-start | bytes 73736 | tf_op jit(solution)/shard_map/ppermute | solution.py:476
  65.2 3.0 %collective-permute-start.9 = (f32[32,128]{1,0:T(8,128)S(1)}, f32[32,128]{1,0:T(8,128)S(1)}, u32[]{:S(2)}, u32[]{:S(2)}) collective-permute-start(f32[32,128]{1,0:T(8,128)S(1)} %get-tuple-element.60), channel_id=1, source_target_pairs={{1,2},{2,1},{3,4},{4,3},{5,6},{6,5},{7,8},{8,7},{9,10},{10,9},{11,... | collective-permute-start | bytes 49160 | tf_op jit(solution)/shard_map/ppermute | solution.py:475
  68.1 2.3 %collective-permute-done.9.refs_3_ = f32[32,128]{1,0:T(8,128)S(1)} collective-permute-done((f32[32,128]{1,0:T(8,128)S(1)}, f32[32,128]{1,0:T(8,128)S(1)}, u32[]{:S(2)}, u32[]{:S(2)}) %collective-permute-start.9) | collective-permute-done | bytes 16416 | tf_op jit(solution)/shard_map/ppermute | solution.py:475
  71.3 6.7 %shard_map.78 = (f32[1536,128]{1,0:T(8,128)S(1)}, f32[40,128]{1,0:T(8,128)S(1)}, f32[32,128]{1,0:T(8,128)S(1)}, f32[32,128]{1,0:T(8,128)S(1)}, f32[48,128]{1,0:T(8,128)S(1)}) custom-call(f32[1536,128]{1,0:T(8,128)S(1)} %get-tuple-element.54.refs_0_, f32[1536,128]{1,0:T(8,128)S(1)} %get-tuple-element.43.refs_0_.refs_1_, ...), custom_call_target="tpu_custom_call" | custom-call | tf_op jit(solution)/shard_map/pallas_call | solution.py:489
  78.0 2.5 %collective-permute-start.12 = (f32[40,128]{1,0:T(8,128)S(1)}, f32[40,128]{1,0:T(8,128)S(1)}, u32[]{:S(2)}, u32[]{:S(2)}) collective-permute-start(f32[40,128]{1,0:T(8,128)S(1)} %get-tuple-element.64), channel_id=1, source_target_pairs={{0,64},{64,0},{1,65},{65,1},{2,66},{66,2},{3,67},{67,3},{4,68},{68... | collective-permute-start | bytes 61448 | tf_op jit(solution)/shard_map/ppermute | solution.py:459
  80.5 1.7 %collective-permute-done.12.message_a = f32[40,128]{1,0:T(8,128)S(1)} collective-permute-done((f32[40,128]{1,0:T(8,128)S(1)}, f32[40,128]{1,0:T(8,128)S(1)}, u32[]{:S(2)}, u32[]{:S(2)}) %collective-permute-start.12) | collective-permute-done | bytes 20512 | tf_op jit(solution)/shard_map/ppermute | solution.py:459
  82.2 3.0 %collective-permute-start.13 = (f32[40,128]{1,0:T(8,128)S(1)}, f32[40,128]{1,0:T(8,128)S(1)}, u32[]{:S(2)}, u32[]{:S(2)}) collective-permute-start(f32[40,128]{1,0:T(8,128)S(1)} %collective-permute-done.12.message_a), channel_id=1, source_target_pairs={{0,1},{1,0},{2,3},{3,2},{4,5},{5,4},{6,7},{7,6},{8,9},{9,8},{10,11... | collective-permute-start | bytes 61448 | tf_op jit(solution)/shard_map/ppermute | solution.py:460
  87.3 3.9 %all-to-all-start.2 = ((f32[32,32,128]{2,1,0:T(8,128)}), f32[32,32,128]{2,1,0:T(8,128)S(1)}, u32[]{:S(2)}, u32[]{:S(2)}) async-start(f32[32,32,128]{2,1,0:T(8,128)} %bitcast.24), calls=%async_computation.2 | async-start | bytes 1048576 | tf_op jit(solution)/shard_map/all_to_all | solution.py:471
  91.9 3.7 %collective-permute-start.16 = (f32[48,128]{1,0:T(8,128)S(1)}, f32[48,128]{1,0:T(8,128)S(1)}, u32[]{:S(2)}, u32[]{:S(2)}) collective-permute-start(f32[48,128]{1,0:T(8,128)S(1)} %get-tuple-element.70), channel_id=1, source_target_pairs={{0,16},{16,0},{32,48},{48,32},{1,17},{17,1},{33,49},{49,33},{2,18}... | collective-permute-start | bytes 73736 | tf_op jit(solution)/shard_map/ppermute | solution.py:476
  96.8 3.0 %collective-permute-start.15 = (f32[32,128]{1,0:T(8,128)S(1)}, f32[32,128]{1,0:T(8,128)S(1)}, u32[]{:S(2)}, u32[]{:S(2)}) collective-permute-start(f32[32,128]{1,0:T(8,128)S(1)} %get-tuple-element.69), channel_id=1, source_target_pairs={{1,2},{2,1},{3,4},{4,3},{5,6},{6,5},{7,8},{8,7},{9,10},{10,9},{11,... | collective-permute-start | bytes 49160 | tf_op jit(solution)/shard_map/ppermute | solution.py:475
  99.8 2.3 %collective-permute-done.15.refs_2_ = f32[32,128]{1,0:T(8,128)S(1)} collective-permute-done((f32[32,128]{1,0:T(8,128)S(1)}, f32[32,128]{1,0:T(8,128)S(1)}, u32[]{:S(2)}, u32[]{:S(2)}) %collective-permute-start.15) | collective-permute-done | bytes 16416 | tf_op jit(solution)/shard_map/ppermute | solution.py:475
  102.9 6.6 %shard_map.80 = (f32[1536,128]{1,0:T(8,128)S(1)}, f32[40,128]{1,0:T(8,128)S(1)}, f32[32,128]{1,0:T(8,128)S(1)}, f32[32,128]{1,0:T(8,128)S(1)}, f32[48,128]{1,0:T(8,128)S(1)}) custom-call(f32[1536,128]{1,0:T(8,128)S(1)} %get-tuple-element.63.refs_0_.refs_1_, f32[32,128]{1,0:T(8,128)S(1)} %collective-permute-done.14.refs_1_, ...), custom_call_target="tpu_custom_call" | custom-call | tf_op jit(solution)/shard_map/pallas_call | solution.py:489
  109.5 2.5 %collective-permute-start.18 = (f32[40,128]{1,0:T(8,128)S(1)}, f32[40,128]{1,0:T(8,128)S(1)}, u32[]{:S(2)}, u32[]{:S(2)}) collective-permute-start(f32[40,128]{1,0:T(8,128)S(1)} %get-tuple-element.73), channel_id=1, source_target_pairs={{0,64},{64,0},{1,65},{65,1},{2,66},{66,2},{3,67},{67,3},{4,68},{68... | collective-permute-start | bytes 61448 | tf_op jit(solution)/shard_map/ppermute | solution.py:459
  112.0 1.7 %collective-permute-done.18.message_a = f32[40,128]{1,0:T(8,128)S(1)} collective-permute-done((f32[40,128]{1,0:T(8,128)S(1)}, f32[40,128]{1,0:T(8,128)S(1)}, u32[]{:S(2)}, u32[]{:S(2)}) %collective-permute-start.18) | collective-permute-done | bytes 20512 | tf_op jit(solution)/shard_map/ppermute | solution.py:459
  113.7 3.0 %collective-permute-start.19 = (f32[40,128]{1,0:T(8,128)S(1)}, f32[40,128]{1,0:T(8,128)S(1)}, u32[]{:S(2)}, u32[]{:S(2)}) collective-permute-start(f32[40,128]{1,0:T(8,128)S(1)} %collective-permute-done.18.message_a), channel_id=1, source_target_pairs={{0,1},{1,0},{2,3},{3,2},{4,5},{5,4},{6,7},{7,6},{8,9},{9,8},{10,11... | collective-permute-start | bytes 61448 | tf_op jit(solution)/shard_map/ppermute | solution.py:460
  118.9 3.9 %all-to-all-start.3 = ((f32[32,32,128]{2,1,0:T(8,128)}), f32[32,32,128]{2,1,0:T(8,128)S(1)}, u32[]{:S(2)}, u32[]{:S(2)}) async-start(f32[32,32,128]{2,1,0:T(8,128)} %bitcast.26), calls=%async_computation.3 | async-start | bytes 1048576 | tf_op jit(solution)/shard_map/all_to_all | solution.py:471
  123.4 3.7 %collective-permute-start.22 = (f32[48,128]{1,0:T(8,128)S(1)}, f32[48,128]{1,0:T(8,128)S(1)}, u32[]{:S(2)}, u32[]{:S(2)}) collective-permute-start(f32[48,128]{1,0:T(8,128)S(1)} %get-tuple-element.79), channel_id=1, source_target_pairs={{0,16},{16,0},{32,48},{48,32},{1,17},{17,1},{33,49},{49,33},{2,18}... | collective-permute-start | bytes 73736 | tf_op jit(solution)/shard_map/ppermute | solution.py:476
  128.3 3.0 %collective-permute-start.21 = (f32[32,128]{1,0:T(8,128)S(1)}, f32[32,128]{1,0:T(8,128)S(1)}, u32[]{:S(2)}, u32[]{:S(2)}) collective-permute-start(f32[32,128]{1,0:T(8,128)S(1)} %get-tuple-element.78), channel_id=1, source_target_pairs={{1,2},{2,1},{3,4},{4,3},{5,6},{6,5},{7,8},{8,7},{9,10},{10,9},{11,... | collective-permute-start | bytes 49160 | tf_op jit(solution)/shard_map/ppermute | solution.py:475
  131.3 2.3 %collective-permute-done.21.refs_3_ = f32[32,128]{1,0:T(8,128)S(1)} collective-permute-done((f32[32,128]{1,0:T(8,128)S(1)}, f32[32,128]{1,0:T(8,128)S(1)}, u32[]{:S(2)}, u32[]{:S(2)}) %collective-permute-start.21) | collective-permute-done | bytes 16416 | tf_op jit(solution)/shard_map/ppermute | solution.py:475
  134.5 4.9 %shard_map.82 = f32[1536,128]{1,0:T(8,128)} custom-call(f32[1536,128]{1,0:T(8,128)S(1)} %get-tuple-element.72.refs_0_, f32[1536,128]{1,0:T(8,128)S(1)} %get-tuple-element.63.refs_0_.refs_1_, f32[32,128]{1,0:T(8,128)S(1)} %collective-permute-done.20.refs_2_, f32[32,128]{1,0:T(8,128)S(1)} %collective-permute-done.21.refs_3_, ...), custom_call_target="tpu_custom_call" | custom-call | tf_op jit(solution)/shard_map/pallas_call | solution.py:489
  (73 shorter events, 25.6 us)
Async XLA Ops:
  1.5 0.7 copy-start.3
  3.0 1.1 copy-start
  9.2 4.8 %collective-permute-start = (f32[40,128]{1,0:T(8,128)S(1)}, f32[40,128]{1,0:T(8,128)S(1)}, u32[]{:S(2)}, u32[]{:S(2)}) collective-permute-start(f32[40,128]{1,0:T(8,128)S(1)} %get-tuple-element.44), channel_id=1, source_target_pairs={{0,64},{64,0},{1,65},{65,1},{2,66},{66,2},{3,67},{67,3},{4,68},{68... | collective-permute-start | bytes 61448 | tf_op jit(solution)/shard_map/ppermute | solution.py:459
  14.0 2.8 %collective-permute-start.1 = (f32[40,128]{1,0:T(8,128)S(1)}, f32[40,128]{1,0:T(8,128)S(1)}, u32[]{:S(2)}, u32[]{:S(2)}) collective-permute-start(f32[40,128]{1,0:T(8,128)S(1)} %collective-permute-done.message_a), channel_id=1, source_target_pairs={{0,1},{1,0},{2,3},{3,2},{4,5},{5,4},{6,7},{7,6},{8,9},{9,8},{10,11... | collective-permute-start | bytes 61448 | tf_op jit(solution)/shard_map/ppermute | solution.py:460
  18.9 9.1 %copy-start.2 = (s32[1,1,1,896]{3,2,1,0:T(1,128)S(1)}, s32[1,1,1,896]{3,2,1,0:T(1,128)}, u32[]{:S(2)}) copy-start(s32[1,1,1,896]{3,2,1,0:T(1,128)} %param.13) | copy-start | bytes 10756
  18.9 20.6 %all-to-all-start = ((f32[32,32,128]{2,1,0:T(8,128)}), f32[32,32,128]{2,1,0:T(8,128)S(1)}, u32[]{:S(2)}, u32[]{:S(2)}) async-start(f32[32,32,128]{2,1,0:T(8,128)} %bitcast.19), calls=%async_computation | async-start | bytes 1048576 | tf_op jit(solution)/shard_map/all_to_all | solution.py:471
  28.1 9.0 %slice-start = ((s32[1,1,1,896]{3,2,1,0:T(1,128)}), s32[1,1,1,512]{3,2,1,0:T(1,128)S(1)}, s32[]{:S(2)}) async-start(s32[1,1,1,896]{3,2,1,0:T(1,128)} %param.13), calls=%async_computation.4 | async-start | bytes 4096 | tf_op jit(solution)/shard_map/slice | solution.py:427
  28.2 11.4 %collective-permute-start.5 = (f32[48,128]{1,0:T(8,128)S(1)}, f32[48,128]{1,0:T(8,128)S(1)}, u32[]{:S(2)}, u32[]{:S(2)}) collective-permute-start(f32[48,128]{1,0:T(8,128)S(1)} %get-tuple-element.50), channel_id=1, source_target_pairs={{16,32},{32,16},{17,33},{33,17},{18,34},{34,18},{19,35},{35,19},{2... | collective-permute-start | bytes 73736 | tf_op jit(solution)/shard_map/ppermute | solution.py:477
  29.0 10.6 %collective-permute-start.4 = (f32[48,128]{1,0:T(8,128)S(1)}, f32[48,128]{1,0:T(8,128)S(1)}, u32[]{:S(2)}, u32[]{:S(2)}) collective-permute-start(f32[48,128]{1,0:T(8,128)S(1)} %get-tuple-element.50), channel_id=1, source_target_pairs={{0,16},{16,0},{32,48},{48,32},{1,17},{17,1},{33,49},{49,33},{2,18}... | collective-permute-start | bytes 73736 | tf_op jit(solution)/shard_map/ppermute | solution.py:476
  32.7 5.0 %collective-permute-start.2 = (f32[32,128]{1,0:T(8,128)S(1)}, f32[32,128]{1,0:T(8,128)S(1)}, u32[]{:S(2)}, u32[]{:S(2)}) collective-permute-start(f32[32,128]{1,0:T(8,128)S(1)} %get-tuple-element.48), channel_id=1, source_target_pairs={{0,1},{1,0},{2,3},{3,2},{4,5},{5,4},{6,7},{7,6},{8,9},{9,8},{10,11... | collective-permute-start | bytes 49160 | tf_op jit(solution)/shard_map/ppermute | solution.py:474
  34.2 5.3 %collective-permute-start.3 = (f32[32,128]{1,0:T(8,128)S(1)}, f32[32,128]{1,0:T(8,128)S(1)}, u32[]{:S(2)}, u32[]{:S(2)}) collective-permute-start(f32[32,128]{1,0:T(8,128)S(1)} %get-tuple-element.49), channel_id=1, source_target_pairs={{1,2},{2,1},{3,4},{4,3},{5,6},{6,5},{7,8},{8,7},{9,10},{10,9},{11,... | collective-permute-start | bytes 49160 | tf_op jit(solution)/shard_map/ppermute | solution.py:475
  46.1 4.2 %collective-permute-start.6 = (f32[40,128]{1,0:T(8,128)S(1)}, f32[40,128]{1,0:T(8,128)S(1)}, u32[]{:S(2)}, u32[]{:S(2)}) collective-permute-start(f32[40,128]{1,0:T(8,128)S(1)} %get-tuple-element.55), channel_id=1, source_target_pairs={{0,64},{64,0},{1,65},{65,1},{2,66},{66,2},{3,67},{67,3},{4,68},{68... | collective-permute-start | bytes 61448 | tf_op jit(solution)/shard_map/ppermute | solution.py:459
  50.3 4.0 %collective-permute-start.7 = (f32[40,128]{1,0:T(8,128)S(1)}, f32[40,128]{1,0:T(8,128)S(1)}, u32[]{:S(2)}, u32[]{:S(2)}) collective-permute-start(f32[40,128]{1,0:T(8,128)S(1)} %collective-permute-done.6.message_a), channel_id=1, source_target_pairs={{0,1},{1,0},{2,3},{3,2},{4,5},{5,4},{6,7},{7,6},{8,9},{9,8},{10,11... | collective-permute-start | bytes 61448 | tf_op jit(solution)/shard_map/ppermute | solution.py:460
  55.7 15.6 %all-to-all-start.1 = ((f32[32,32,128]{2,1,0:T(8,128)}), f32[32,32,128]{2,1,0:T(8,128)S(1)}, u32[]{:S(2)}, u32[]{:S(2)}) async-start(f32[32,32,128]{2,1,0:T(8,128)} %bitcast.22), calls=%async_computation.1 | async-start | bytes 1048576 | tf_op jit(solution)/shard_map/all_to_all | solution.py:471
  59.6 10.9 %collective-permute-start.11 = (f32[48,128]{1,0:T(8,128)S(1)}, f32[48,128]{1,0:T(8,128)S(1)}, u32[]{:S(2)}, u32[]{:S(2)}) collective-permute-start(f32[48,128]{1,0:T(8,128)S(1)} %get-tuple-element.61), channel_id=1, source_target_pairs={{16,32},{32,16},{17,33},{33,17},{18,34},{34,18},{19,35},{35,19},{2... | collective-permute-start | bytes 73736 | tf_op jit(solution)/shard_map/ppermute | solution.py:477
  60.2 10.3 %collective-permute-start.10 = (f32[48,128]{1,0:T(8,128)S(1)}, f32[48,128]{1,0:T(8,128)S(1)}, u32[]{:S(2)}, u32[]{:S(2)}) collective-permute-start(f32[48,128]{1,0:T(8,128)S(1)} %get-tuple-element.61), channel_id=1, source_target_pairs={{0,16},{16,0},{32,48},{48,32},{1,17},{17,1},{33,49},{49,33},{2,18}... | collective-permute-start | bytes 73736 | tf_op jit(solution)/shard_map/ppermute | solution.py:476
  64.0 4.2 %collective-permute-start.8 = (f32[32,128]{1,0:T(8,128)S(1)}, f32[32,128]{1,0:T(8,128)S(1)}, u32[]{:S(2)}, u32[]{:S(2)}) collective-permute-start(f32[32,128]{1,0:T(8,128)S(1)} %get-tuple-element.59), channel_id=1, source_target_pairs={{0,1},{1,0},{2,3},{3,2},{4,5},{5,4},{6,7},{7,6},{8,9},{9,8},{10,11... | collective-permute-start | bytes 49160 | tf_op jit(solution)/shard_map/ppermute | solution.py:474
  65.2 5.3 %collective-permute-start.9 = (f32[32,128]{1,0:T(8,128)S(1)}, f32[32,128]{1,0:T(8,128)S(1)}, u32[]{:S(2)}, u32[]{:S(2)}) collective-permute-start(f32[32,128]{1,0:T(8,128)S(1)} %get-tuple-element.60), channel_id=1, source_target_pairs={{1,2},{2,1},{3,4},{4,3},{5,6},{6,5},{7,8},{8,7},{9,10},{10,9},{11,... | collective-permute-start | bytes 49160 | tf_op jit(solution)/shard_map/ppermute | solution.py:475
  78.0 4.2 %collective-permute-start.12 = (f32[40,128]{1,0:T(8,128)S(1)}, f32[40,128]{1,0:T(8,128)S(1)}, u32[]{:S(2)}, u32[]{:S(2)}) collective-permute-start(f32[40,128]{1,0:T(8,128)S(1)} %get-tuple-element.64), channel_id=1, source_target_pairs={{0,64},{64,0},{1,65},{65,1},{2,66},{66,2},{3,67},{67,3},{4,68},{68... | collective-permute-start | bytes 61448 | tf_op jit(solution)/shard_map/ppermute | solution.py:459
  82.2 3.8 %collective-permute-start.13 = (f32[40,128]{1,0:T(8,128)S(1)}, f32[40,128]{1,0:T(8,128)S(1)}, u32[]{:S(2)}, u32[]{:S(2)}) collective-permute-start(f32[40,128]{1,0:T(8,128)S(1)} %collective-permute-done.12.message_a), channel_id=1, source_target_pairs={{0,1},{1,0},{2,3},{3,2},{4,5},{5,4},{6,7},{7,6},{8,9},{9,8},{10,11... | collective-permute-start | bytes 61448 | tf_op jit(solution)/shard_map/ppermute | solution.py:460
  87.3 15.6 %all-to-all-start.2 = ((f32[32,32,128]{2,1,0:T(8,128)}), f32[32,32,128]{2,1,0:T(8,128)S(1)}, u32[]{:S(2)}, u32[]{:S(2)}) async-start(f32[32,32,128]{2,1,0:T(8,128)} %bitcast.24), calls=%async_computation.2 | async-start | bytes 1048576 | tf_op jit(solution)/shard_map/all_to_all | solution.py:471
  91.2 10.9 %collective-permute-start.17 = (f32[48,128]{1,0:T(8,128)S(1)}, f32[48,128]{1,0:T(8,128)S(1)}, u32[]{:S(2)}, u32[]{:S(2)}) collective-permute-start(f32[48,128]{1,0:T(8,128)S(1)} %get-tuple-element.70), channel_id=1, source_target_pairs={{16,32},{32,16},{17,33},{33,17},{18,34},{34,18},{19,35},{35,19},{2... | collective-permute-start | bytes 73736 | tf_op jit(solution)/shard_map/ppermute | solution.py:477
  91.9 10.3 %collective-permute-start.16 = (f32[48,128]{1,0:T(8,128)S(1)}, f32[48,128]{1,0:T(8,128)S(1)}, u32[]{:S(2)}, u32[]{:S(2)}) collective-permute-start(f32[48,128]{1,0:T(8,128)S(1)} %get-tuple-element.70), channel_id=1, source_target_pairs={{0,16},{16,0},{32,48},{48,32},{1,17},{17,1},{33,49},{49,33},{2,18}... | collective-permute-start | bytes 73736 | tf_op jit(solution)/shard_map/ppermute | solution.py:476
  95.6 4.2 %collective-permute-start.14 = (f32[32,128]{1,0:T(8,128)S(1)}, f32[32,128]{1,0:T(8,128)S(1)}, u32[]{:S(2)}, u32[]{:S(2)}) collective-permute-start(f32[32,128]{1,0:T(8,128)S(1)} %get-tuple-element.68), channel_id=1, source_target_pairs={{0,1},{1,0},{2,3},{3,2},{4,5},{5,4},{6,7},{7,6},{8,9},{9,8},{10,11... | collective-permute-start | bytes 49160 | tf_op jit(solution)/shard_map/ppermute | solution.py:474
  96.8 5.3 %collective-permute-start.15 = (f32[32,128]{1,0:T(8,128)S(1)}, f32[32,128]{1,0:T(8,128)S(1)}, u32[]{:S(2)}, u32[]{:S(2)}) collective-permute-start(f32[32,128]{1,0:T(8,128)S(1)} %get-tuple-element.69), channel_id=1, source_target_pairs={{1,2},{2,1},{3,4},{4,3},{5,6},{6,5},{7,8},{8,7},{9,10},{10,9},{11,... | collective-permute-start | bytes 49160 | tf_op jit(solution)/shard_map/ppermute | solution.py:475
  109.5 4.2 %collective-permute-start.18 = (f32[40,128]{1,0:T(8,128)S(1)}, f32[40,128]{1,0:T(8,128)S(1)}, u32[]{:S(2)}, u32[]{:S(2)}) collective-permute-start(f32[40,128]{1,0:T(8,128)S(1)} %get-tuple-element.73), channel_id=1, source_target_pairs={{0,64},{64,0},{1,65},{65,1},{2,66},{66,2},{3,67},{67,3},{4,68},{68... | collective-permute-start | bytes 61448 | tf_op jit(solution)/shard_map/ppermute | solution.py:459
  113.7 3.8 %collective-permute-start.19 = (f32[40,128]{1,0:T(8,128)S(1)}, f32[40,128]{1,0:T(8,128)S(1)}, u32[]{:S(2)}, u32[]{:S(2)}) collective-permute-start(f32[40,128]{1,0:T(8,128)S(1)} %collective-permute-done.18.message_a), channel_id=1, source_target_pairs={{0,1},{1,0},{2,3},{3,2},{4,5},{5,4},{6,7},{7,6},{8,9},{9,8},{10,11... | collective-permute-start | bytes 61448 | tf_op jit(solution)/shard_map/ppermute | solution.py:460
  118.9 15.6 %all-to-all-start.3 = ((f32[32,32,128]{2,1,0:T(8,128)}), f32[32,32,128]{2,1,0:T(8,128)S(1)}, u32[]{:S(2)}, u32[]{:S(2)}) async-start(f32[32,32,128]{2,1,0:T(8,128)} %bitcast.26), calls=%async_computation.3 | async-start | bytes 1048576 | tf_op jit(solution)/shard_map/all_to_all | solution.py:471
  122.8 10.9 %collective-permute-start.23 = (f32[48,128]{1,0:T(8,128)S(1)}, f32[48,128]{1,0:T(8,128)S(1)}, u32[]{:S(2)}, u32[]{:S(2)}) collective-permute-start(f32[48,128]{1,0:T(8,128)S(1)} %get-tuple-element.79), channel_id=1, source_target_pairs={{16,32},{32,16},{17,33},{33,17},{18,34},{34,18},{19,35},{35,19},{2... | collective-permute-start | bytes 73736 | tf_op jit(solution)/shard_map/ppermute | solution.py:477
  123.4 10.3 %collective-permute-start.22 = (f32[48,128]{1,0:T(8,128)S(1)}, f32[48,128]{1,0:T(8,128)S(1)}, u32[]{:S(2)}, u32[]{:S(2)}) collective-permute-start(f32[48,128]{1,0:T(8,128)S(1)} %get-tuple-element.79), channel_id=1, source_target_pairs={{0,16},{16,0},{32,48},{48,32},{1,17},{17,1},{33,49},{49,33},{2,18}... | collective-permute-start | bytes 73736 | tf_op jit(solution)/shard_map/ppermute | solution.py:476
  127.2 4.2 %collective-permute-start.20 = (f32[32,128]{1,0:T(8,128)S(1)}, f32[32,128]{1,0:T(8,128)S(1)}, u32[]{:S(2)}, u32[]{:S(2)}) collective-permute-start(f32[32,128]{1,0:T(8,128)S(1)} %get-tuple-element.77), channel_id=1, source_target_pairs={{0,1},{1,0},{2,3},{3,2},{4,5},{5,4},{6,7},{7,6},{8,9},{9,8},{10,11... | collective-permute-start | bytes 49160 | tf_op jit(solution)/shard_map/ppermute | solution.py:474
  128.3 5.3 %collective-permute-start.21 = (f32[32,128]{1,0:T(8,128)S(1)}, f32[32,128]{1,0:T(8,128)S(1)}, u32[]{:S(2)}, u32[]{:S(2)}) collective-permute-start(f32[32,128]{1,0:T(8,128)S(1)} %get-tuple-element.78), channel_id=1, source_target_pairs={{1,2},{2,1},{3,4},{4,3},{5,6},{6,5},{7,8},{8,7},{9,10},{10,9},{11,... | collective-permute-start | bytes 49160 | tf_op jit(solution)/shard_map/ppermute | solution.py:475
  (4 other events, 2.7 us)

commit v3 on v2

--- a/solution.py
+++ b/solution.py
@@ -56,25 +56,59 @@
     return ref[rows_of(u), :]
 
 
-def gather_rows(field, src, table, sent):
+def pick(field, src, at, m, slot, accs):
     lane = lane_ids(2 * ROWS)
-
-    def one(slot, m, accs):
-        cell = src[slot * LANES + m]
+    cell = src[at]
+    lon = lax.shift_right_logical(cell, 7)
+    lat = lax.bitwise_and(cell, LANES - 1)
+    both = field[pl.ds(pl.multiple_of(lon * ROWS, ROWS), 2 * ROWS), :]
+    both = pltpu.roll(both, lax.bitwise_and(m - lat + LANES, LANES - 1), 1)
+    here = lane == m
+    beside = lane == lax.bitwise_and(m + 1, LANES - 1)
+    accs = list(accs)
+    for number in range(2):
+        if isinstance(slot, int) and slot != number:
+            continue
+        ours, next_to = here, beside
+        if not isinstance(slot, int):
+            shown = jnp.where(slot == number, m, 2 * LANES)
+            ours = lane == shown
+            next_to = jnp.logical_and(beside, slot == number)
+        accs[2 * number] = jnp.where(ours, both, accs[2 * number])
+        accs[2 * number + 1] = jnp.where(next_to, both, accs[2 * number + 1])
+    return tuple(accs)
+
+
+def gather_all(field, src, lon_cells=0, listed=None):
+    def note(at, count):
+        if listed is None:
+            return count
+        cell = src[at]
         lon = lax.shift_right_logical(cell, 7)
         lat = lax.bitwise_and(cell, LANES - 1)
-        both = field[pl.ds(pl.multiple_of(lon * ROWS, ROWS), 2 * ROWS), :]
-        both = pltpu.roll(both, lax.bitwise_and(m - lat + LANES, LANES - 1), 1)
-        near, far = accs
-        near = jnp.where(lane == m, both, near)
-        far = jnp.where(lane == lax.bitwise_and(m + 1, LANES - 1), both, far)
-        return near, far
-
-    def body(m, accs):
-        return one(0, m, accs[0:2]) + one(1, m, accs[2:4])
+        low = jnp.logical_or(lat < 2, lon < 2)
+        high = jnp.logical_or(lat >= LANES - 3, lon >= lon_cells - 3)
+        listed[count] = at
+        return count + jnp.logical_or(low, high).astype(jnp.int32)
+
+    def body(m, carry):
+        count, accs = carry
+        accs = pick(field, src, m, m, 0, accs)
+        count = note(m, count)
+        accs = pick(field, src, LANES + m, m, 1, accs)
+        count = note(LANES + m, count)
+        return count, accs
 
     zero = jnp.zeros((2 * ROWS, LANES), jnp.float32)
-    accs = lax.fori_loop(0, LANES, body, (zero, zero, zero, zero), unroll=8)
+    count, accs = lax.fori_loop(0, LANES, body, (jnp.int32(0), (zero, zero, zero, zero)), unroll=8)
+    if listed is not None:
+        for k in range(4):
+            listed[count + k] = 0
+        listed[listed.shape[0] - 1] = count
+    return accs
+
+
+def finish_rows(accs, table, sent):
     sub = sub_ids()
     for slot in range(2):
         near, far = accs[2 * slot], accs[2 * slot + 1]
@@ -106,23 +140,53 @@
     return pltpu.roll(value, 4 * col + 2, 1)
 
 
-def start_kernel(lon_cells, state, src, table, flag, field, sent, edge_a, edge_b, strips):
+def start_kernel(
+    lon_cells, state, src, counts, names, weights, turn, flag,
+    field, edge_a, edge_b, strips, buffer, sent, table, listed, parts, zeros, sems
+):
+    blocks = lon_cells // 32
+    loads = []
+    for block in range(blocks):
+        copy = pltpu.make_async_copy(state.at[:, pl.ds(32 * block, 32), :], parts.at[block], sems.at[block])
+        copy.start()
+        loads.append(copy)
+    zeros[...] = jnp.zeros(zeros.shape, jnp.float32)
+    count = zeros.shape[0]
+    clears = []
+    for number in range(buffer.shape[0] // count):
+        copy = pltpu.make_async_copy(zeros, buffer.at[pl.ds(number * count, count), :], sems.at[blocks + number])
+        copy.start()
+        clears.append(copy)
     lane = lane_ids(ROWS)
     quad = lax.shift_right_logical(lane, 2)
-    for block in range(lon_cells // 32):
-
-        def body(col, acc, block=block):
-            u = block * 32 + col
-            low = state[pl.ds(u, 8, stride=lon_cells), :]
-            high = state[pl.ds(u + 8 * lon_cells, 8, stride=lon_cells), :]
+    for block in range(blocks):
+        loads[block].wait()
+        rows = parts.at[block].reshape(32 * ROWS, LANES)
+
+        def body(col, acc, block=block, rows=rows):
+            low = rows[pl.ds(col, 8, stride=32), :]
+            high = rows[pl.ds(col + 8 * 32, 8, stride=32), :]
             value = jnp.concatenate([low, high], axis=0)
-            field[pl.ds(pl.multiple_of(u * ROWS, ROWS), ROWS), :] = value
+            field[rows_of(block * 32 + col), :] = value
             return jnp.where(quad == col, strip_of(value, col), acc)
 
-        acc = lax.fori_loop(0, 32, body, jnp.zeros((ROWS, LANES), jnp.float32), unroll=4)
+        acc = lax.fori_loop(0, 32, body, jnp.zeros((ROWS, LANES), jnp.float32), unroll=8)
         strips[block * ROWS : (block + 1) * ROWS, :] = acc
     put_edges(field, flag, lon_cells, edge_a, edge_b)
-    gather_rows(field, src, table, sent)
+    row = lane_ids(1)
+    table[...] = jnp.zeros(table.shape, jnp.float32)
+    angle = turn[...]
+    cosine, sine = jnp.cos(angle), jnp.sin(angle)
+    for slot in range(2):
+        for corner in range(4):
+            value = weights[2 * corner + slot : 2 * corner + slot + 1, :]
+            table[8 * slot + corner : 8 * slot + corner + 1, :] = jnp.where(row < counts[slot], value, 0.0)
+        table[8 * slot + 4 : 8 * slot + 5, :] = cosine[slot : slot + 1]
+        table[8 * slot + 5 : 8 * slot + 6, :] = sine[slot : slot + 1]
+        table[16 + slot : 17 + slot, :] = jnp.full((1, LANES), names[slot], jnp.int32).astype(jnp.float32)
+    finish_rows(gather_all(field, src, lon_cells, listed), table, sent)
+    for copy in clears:
+        copy.wait()
 
 
 def key_kernel(slots, keys, listed):
@@ -142,36 +206,42 @@
         now = jnp.min(jnp.where(key > last, key, NO_KEY), axis=1, keepdims=True)
         now = jnp.broadcast_to(now, (8, LANES))
         hit = now < NO_KEY
-        found = jnp.where(lane == count, jnp.where(hit, now, 0.0), found)
-        total = total + jnp.where(hit, 1.0, 0.0)
         more = (jnp.min(now) < NO_KEY).astype(jnp.int32)
+        found = jnp.where(lane == count, jnp.where(hit, now, -1.0), found)
+        total = total + more.astype(jnp.float32)
         return count + 1, more, now, found, total
 
     zero = jnp.zeros((8, LANES), jnp.float32)
-    out = lax.while_loop(cond, body, (jnp.int32(0), jnp.int32(1), zero - 1.0, zero, zero))
+    out = lax.while_loop(cond, body, (jnp.int32(0), jnp.int32(1), zero - 1.0, zero - 1.0, zero))
     listed[0:8, :] = out[3].astype(jnp.int32)
     listed[8:16, :] = out[4].astype(jnp.int32)
 
 
 def fill_ghosts(received, keys, listed, ghosts):
-    for row in range(8):
-        wanted = keys[row : row + 1, :]
-
-        def body(i, acc, row=row, wanted=wanted):
+    def body(i, accs):
+        out = []
+        for row in range(4):
             key = listed[row, i]
-            peer = lax.shift_right_logical(key, 7)
-            shift = lax.bitwise_and(key, LANES - 1)
+            known = jnp.maximum(key, 0)
+            peer = lax.shift_right_logical(known, 7)
+            shift = lax.bitwise_and(known, LANES - 1)
             value = pltpu.roll(tile(received, peer), lax.bitwise_and(LANES - shift, LANES - 1), 1)
-            return jnp.where(wanted == key.astype(jnp.float32), value, acc)
-
-        acc = lax.fori_loop(0, listed[8 + row, 0], body, jnp.zeros((ROWS, LANES), jnp.float32))
-        ghosts[row * ROWS : (row + 1) * ROWS, :] = acc
+            out.append(jnp.where(keys[row : row + 1, :] == key.astype(jnp.float32), value, accs[row]))
+        return tuple(out)
+
+    zero = jnp.zeros((ROWS, LANES), jnp.float32)
+    accs = lax.fori_loop(0, listed[8, 0], body, (zero, zero, zero, zero))
+    for row in range(4):
+        ghosts[row * ROWS : (row + 1) * ROWS, :] = accs[row]
 
 
 def merge_strips(strip_a, strip_b, flag, ghosts, merged, blocks):
     lane = lane_ids(8)
     part = lax.bitwise_and(lane, 3)
     odd = flag[1] > 0
+    north = flag[2] > 0
+    first = part == jnp.where(north, 1, 2)
+    second = part == jnp.where(north, 0, 3)
     for block in range(blocks):
         spread = lax.shift_right_logical(lane, 2) + 32 * block
         for half in range(2):
@@ -179,24 +249,17 @@
             a = strip_a[at : at + 8, :]
             b = strip_b[at : at + 8, :]
             value = jnp.where(part < 2, jnp.where(odd, a, b), jnp.where(odd, b, a))
-            extra = jnp.zeros((8, LANES), jnp.float32)
-            for row, where in ((0, 1), (1, 0), (2, 2), (3, 3)):
-                source = ghosts[row * ROWS + half * 8 : row * ROWS + half * 8 + 8, :]
-                wide = jnp.take_along_axis(source, spread, axis=1)
-                extra = jnp.where(part == where, wide, extra)
-            merged[at : at + 8, :] = value + extra
-
-
-def coefficients(geo, lon_cells, consts, coef):
+            wide0 = jnp.take_along_axis(ghosts[half * 8 : half * 8 + 8, :], spread, axis=1)
+            wide1 = jnp.take_along_axis(ghosts[ROWS + half * 8 : ROWS + half * 8 + 8, :], spread, axis=1)
+            merged[at : at + 8, :] = value + jnp.where(first, wide0, jnp.where(second, wide1, 0.0))
+
+
+def coefficients(sin_t, cos_t, yang, consts):
     d_theta, d_phi, step, kappa, viscous, omega, buoyancy, radial = consts
     sub = sub_ids()
     low = sub < 4
     level = lax.bitwise_and(sub, 3).astype(jnp.float32)
     inverse = 1.0 / (level * radial + R_LOW)
-    base = 2 * lon_cells
-    sin_t = geo[base : base + 8, :]
-    cos_t = geo[base + 8 : base + 16, :]
-    yang = geo[base + 16 : base + 24, :]
     keep = 1.0 - yang
     over_sin = 1.0 / sin_t
     square = inverse * inverse
@@ -226,37 +289,19 @@
         jnp.where(low, zero, twice * cos_t),
         jnp.where(low, -twice, 0.0) + zero,
     ]
-    for i, value in enumerate(values):
-        coef[8 * i : 8 * i + 8, :] = value
-
-
-def stage_kernel(
-    second, final, lon_cells, consts, *refs
-):
+    return values
+
+
+def inner_kernel(second, lon_cells, consts, *refs):
     refs = list(refs)
     field = refs.pop(0)
     origin = refs.pop(0) if second else None
-    lon_a, lon_b, strip_a, strip_b, received, keys, listed, flag, geo, src, table = refs[:11]
-    refs = refs[11:]
-    if final:
-        result = refs.pop(0)
-    else:
-        result, sent, edge_a, edge_b, strips = refs[:5]
-        refs = refs[5:]
-    ghosts, merged, coef, sides = refs
-
+    geo, result, strips, coef = refs
+    base = 2 * lon_cells
+    sin_t, cos_t, yang = (geo[base + 8 * i : base + 8 * i + 8, :] for i in range(3))
+    for i, value in enumerate(coefficients(sin_t, cos_t, yang, consts)):
+        coef[8 * i : 8 * i + 8, :] = value
     radial = consts[7]
-    coefficients(geo, lon_cells, consts, coef)
-    fill_ghosts(received, keys, listed, ghosts)
-    merge_strips(strip_a, strip_b, flag, ghosts, merged, lon_cells // 32)
-    odd = flag[0] > 0
-    before = jnp.where(odd, lon_a[...], lon_b[...])
-    after = jnp.where(odd, lon_b[...], lon_a[...])
-    sides[0:ROWS, :] = before[0:ROWS] + ghosts[5 * ROWS : 6 * ROWS, :]
-    sides[ROWS : 2 * ROWS, :] = before[ROWS:] + ghosts[4 * ROWS : 5 * ROWS, :]
-    sides[2 * ROWS : 3 * ROWS, :] = after[0:ROWS] + ghosts[6 * ROWS : 7 * ROWS, :]
-    sides[3 * ROWS : 4 * ROWS, :] = after[ROWS:] + ghosts[7 * ROWS : 8 * ROWS, :]
-
     lane16 = lane_ids(ROWS)
     quad = lax.shift_right_logical(lane16, 2)
     sub = sub_ids()
@@ -269,12 +314,11 @@
     def c(i):
         return coef[8 * i : 8 * i + 8, :]
 
-    def update(u, block, col, down2, down1, here, up1, up2):
-        border = pltpu.roll(tile(merged, block), lax.bitwise_and(LANES - 2 - 4 * col, LANES - 1), 1)
-        south1 = pltpu.roll(jnp.where(lane16 == LANES - 1, border, here), 1, 1)
-        south2 = pltpu.roll(jnp.where(lane16 >= LANES - 2, border, here), 2, 1)
-        north1 = pltpu.roll(jnp.where(lane16 == 0, border, here), LANES - 1, 1)
-        north2 = pltpu.roll(jnp.where(lane16 < 2, border, here), LANES - 2, 1)
+    def update(u, down2, down1, here, up1, up2):
+        south1 = jnp.where(lane16 >= 1, pltpu.roll(here, 1, 1), 0.0)
+        south2 = jnp.where(lane16 >= 2, pltpu.roll(here, 2, 1), 0.0)
+        north1 = jnp.where(lane16 < LANES - 1, pltpu.roll(here, LANES - 1, 1), 0.0)
+        north2 = jnp.where(lane16 < LANES - 2, pltpu.roll(here, LANES - 2, 1), 0.0)
         lat_odd = 8.0 * (north1 - south1) - (north2 - south2)
         lat_even = 16.0 * (north1 + south1) - (north2 + south2)
         lon_odd = 8.0 * (up1 - down1) - (up2 - down2)
@@ -313,6 +357,104 @@
             new = 0.5 * (tile(origin, u) + new)
         return new
 
+    def at(u):
+        if u < 0 or u >= lon_cells:
+            return jnp.zeros((ROWS, LANES), jnp.float32)
+        return tile(field, u)
+
+    def group(index, block, col, tiles):
+        acc = jnp.zeros((ROWS, LANES), jnp.float32)
+        for k in range(GROUP):
+            new = update(index + k, *tiles[k : k + 5])
+            result[rows_of(index + k), :] = new
+            acc = jnp.where(quad == col + k, strip_of(new, col + k), acc)
+        rows = rows_of(block)
+        mine = jnp.logical_and(quad >= col, quad < col + GROUP)
+        strips[rows, :] = jnp.where(mine, acc, strips[rows, :])
+
+    strips[...] = jnp.zeros(strips.shape, jnp.float32)
+    for index in (0, lon_cells - GROUP):
+        group(index, index // 32, index % 32, [at(u) for u in range(index - 2, index + GROUP + 2)])
+
+    def body(number, carry):
+        index = number * GROUP
+        tiles = [tile(field, index + k) for k in range(-2, GROUP + 2)]
+        group(index, lax.shift_right_logical(index, 5), lax.bitwise_and(index, 31), tiles)
+        return carry
+
+    lax.fori_loop(1, lon_cells // GROUP - 1, body, 0)
+
+
+def rows_kernel(field, src, corners):
+    for i, value in enumerate(gather_all(field, src)):
+        corners[2 * i * ROWS : 2 * (i + 1) * ROWS, :] = value
+
+
+def outer_kernel(second, final, lon_cells, consts, *refs):
+    refs = list(refs)
+    part, part_strips, own_a, own_b, own_strips, lon_a, lon_b, strip_a, strip_b, received, keys, listed, flag, geo = refs[:14]
+    refs = refs[14:]
+    if final:
+        result = refs.pop(0)
+    else:
+        corners, again, src, table, result, sent, edge_a, edge_b, strips = refs[:9]
+        refs = refs[9:]
+    ghosts, merged, fixes, sides = refs
+    blocks = lon_cells // 32
+    fill_ghosts(received, keys, listed, ghosts)
+    merge_strips(strip_a, strip_b, flag, ghosts, merged, blocks)
+
+    base = 2 * lon_cells
+    sin_t, cos_t, yang, strip_sin, strip_cos = (geo[base + 8 * i : base + 8 * i + 8, :] for i in range(5))
+    low = sub_ids() < 4
+    lane = lane_ids(8)
+    scale = 0.5 if second else 1.0
+
+    values = coefficients(strip_sin, strip_cos, yang, consts)
+    quarter = lax.bitwise_and(lane, 3)
+    for block in range(blocks):
+        at = block * ROWS
+        v1 = own_strips[at + 8 : at + 16, :]
+        along = jnp.where(low, v1, pltpu.roll(v1, 4, 0)) * values[0]
+        for half in range(2):
+            rows = slice(at + 8 * half, at + 8 * half + 8)
+            outside = merged[rows, :]
+            left1, left2 = pltpu.roll(outside, LANES - 1, 1), pltpu.roll(outside, LANES - 2, 1)
+            right1, right2 = pltpu.roll(outside, 1, 1), pltpu.roll(outside, 2, 1)
+            near = jnp.where(quarter == 1, left1, jnp.where(quarter == 2, right1, 0.0))
+            far = jnp.where(quarter < 2, left2, right2)
+            first = jnp.where(quarter < 2, 8.0 * near - far, far - 8.0 * near)
+            twice = 16.0 * near - far
+            fixes[rows, :] = scale * ((values[3 + 6 * half] + along) * first + values[2 + 6 * half] * twice)
+
+    values = coefficients(sin_t, cos_t, yang, consts)
+    odd = flag[0] > 0
+    west = flag[3] > 0
+    for i, row in enumerate((3, 2, 2, 3)):
+        came = jnp.where(odd, lon_a[...], lon_b[...]) if i < 2 else jnp.where(odd, lon_b[...], lon_a[...])
+        ghost = jnp.where(west if i < 2 else jnp.logical_not(west), ghosts[rows_of(row), :], 0.0)
+        sides[rows_of(i), :] = came[rows_of(i % 2)] + ghost
+    before2, before1, after1, after2 = (sides[rows_of(i), :] for i in range(4))
+    for i, (near, far, sign) in enumerate(
+        ((before1, before2, -1.0), (None, before1, -1.0), (None, after1, 1.0), (after1, after2, 1.0))
+    ):
+        own = jnp.where(odd, own_a[...], own_b[...]) if i < 2 else jnp.where(odd, own_b[...], own_a[...])
+        v1 = own[rows_of(i % 2)][8:]
+        along = jnp.where(low, pltpu.roll(v1, 4, 0), v1) * values[1]
+        first = -far if near is None else 8.0 * near - far
+        twice = -far if near is None else 16.0 * near - far
+        for half in range(2):
+            rows = slice(8 * half, 8 * half + 8)
+            change = sign * along * first[rows] + values[4 + 6 * half] * twice[rows]
+            sides[i * ROWS + 8 * half : i * ROWS + 8 * half + 8, :] = scale * change
+
+    lane16 = lane_ids(ROWS)
+    rim = jnp.logical_or(lane16 < 2, lane16 >= LANES - 2)
+
+    def corrected(u, block, col):
+        moved = pltpu.roll(tile(fixes, block), lax.bitwise_and(LANES - 2 - 4 * col, LANES - 1), 1)
+        return tile(part, u) + jnp.where(rim, moved, 0.0)
+
     def store(u, new):
         if final:
             result[pl.ds(u, 8, stride=lon_cells), :] = new[:8]
@@ -320,40 +462,37 @@
         else:
             result[rows_of(u), :] = new
 
-    def at(u):
-        if u < 0:
-            return sides[(u + 2) * ROWS : (u + 3) * ROWS, :]
-        if u >= lon_cells:
-            return sides[(u - lon_cells + 2) * ROWS : (u - lon_cells + 3) * ROWS, :]
-        return field[u * ROWS : (u + 1) * ROWS, :]
-
-    def group(index, block, col, tiles):
-        acc = jnp.zeros((ROWS, LANES), jnp.float32)
-        for k in range(GROUP):
-            new = update(index + k, block, col + k, *tiles[k : k + 5])
-            store(index + k, new)
-            if not final:
-                acc = jnp.where(quad == col + k, strip_of(new, col + k), acc)
-        if not final:
-            rows = rows_of(block)
-            mine = jnp.logical_and(quad >= col, quad < col + GROUP)
-            strips[rows, :] = jnp.where(mine, acc, strips[rows, :])
-
-    if not final:
-        strips[...] = jnp.zeros(strips.shape, jnp.float32)
-    for index in (0, lon_cells - GROUP):
-        group(index, index // 32, index % 32, [at(u) for u in range(index - 2, index + GROUP + 2)])
-
     def body(number, carry):
         index = number * GROUP
-        tiles = [tile(field, index + k) for k in range(-2, GROUP + 2)]
-        group(index, lax.shift_right_logical(index, 5), lax.bitwise_and(index, 31), tiles)
+        block = lax.shift_right_logical(index, 5)
+        col = lax.bitwise_and(index, 31)
+        for new, k in [(corrected(index + k, block, col + k), k) for k in range(GROUP)]:
+            store(index + k, new)
         return carry
 
-    lax.fori_loop(1, lon_cells // GROUP - 1, body, 0)
+    lax.fori_loop(0, lon_cells // GROUP, body, 0)
     if not final:
-        put_edges(result, flag, lon_cells, edge_a, edge_b)
-        gather_rows(result, src, table, sent)
+        strips[...] = part_strips[...] + fixes[...]
+    quad = lax.shift_right_logical(lane16, 2)
+    for i, u in enumerate((0, 1, lon_cells - 2, lon_cells - 1)):
+        block, col = divmod(u, 32)
+        change = sides[rows_of(i), :]
+        store(u, corrected(u, block, col) + change)
+        if not final:
+            strips[rows_of(block), :] += jnp.where(quad == col, strip_of(change, col), 0.0)
+    if final:
+        return
+    put_edges(result, flag, lon_cells, edge_a, edge_b)
+
+    def repeat(step, accs):
+        for k in range(4):
+            at = again[4 * step + k]
+            accs = pick(result, src, at, lax.bitwise_and(at, LANES - 1), lax.shift_right_logical(at, 7), accs)
+        return accs
+
+    accs = tuple(corners[2 * i * ROWS : 2 * (i + 1) * ROWS, :] for i in range(4))
+    steps = lax.shift_right_logical(again[again.shape[0] - 1] + 3, 2)
+    finish_rows(lax.fori_loop(0, steps, repeat, accs), table, sent)
 
 
 def pack_kernel(message_a, message_b, flag, _, buffer, staged, sems):
@@ -400,18 +539,12 @@
     colat = lax.axis_index("colat")
     lon = lax.axis_index(lon_axes)
     yang = lax.axis_index("panel").astype(jnp.float32)
-    flag = jnp.stack([lon % 2, colat % 2]).astype(jnp.int32)
-
-    live = jnp.arange(LANES, dtype=jnp.int32)[None, :] < send_counts[0, 0, 0][:, None]
-    turn = turn_angles[0, 0, 0].reshape(2, LANES)
-    wts = jnp.where(live[None], weights[:, 0, 0, 0].reshape(4, 2, LANES), 0.0)
-    named = jnp.broadcast_to(partners[0, 0, 0].astype(jnp.float32)[:, None], (2, LANES))
-    blank = jnp.zeros((2, LANES), jnp.float32)
-    table = jnp.stack([wts[0], wts[1], wts[2], wts[3], jnp.cos(turn), jnp.sin(turn), blank, blank], axis=1)
-    table = jnp.concatenate([table.reshape(16, LANES), named, jnp.zeros((6, LANES), jnp.float32)])
+    flag = jnp.stack([lon % 2, colat % 2, colat == 0, lon == 0]).astype(jnp.int32)
+
     src = source_cells[0, 0, 0]
-
     theta = ((colat * lat_cells + jnp.arange(lat_cells, dtype=jnp.int32)).astype(jnp.float32) + 0.5) * consts[0] + 0.25 * math.pi
+    rim_lat = (jnp.arange(LANES, dtype=jnp.int32) + 2) % 4 + jnp.where(jnp.arange(LANES, dtype=jnp.int32) % 4 < 2, lat_cells - 4, 0)
+    rim_theta = ((colat * lat_cells + rim_lat).astype(jnp.float32) + 0.5) * consts[0] + 0.25 * math.pi
     phi = ((lon * lon_cells + jnp.arange(lon_cells, dtype=jnp.int32)).astype(jnp.float32) + 0.5) * consts[1] - 0.75 * math.pi
     geo = jnp.concatenate(
         [
@@ -420,11 +553,15 @@
             jnp.broadcast_to(jnp.sin(theta)[None], (8, LANES)),
             jnp.broadcast_to(jnp.cos(theta)[None], (8, LANES)),
             jnp.broadcast_to(yang, (8, LANES)),
+            jnp.broadcast_to(jnp.sin(rim_theta)[None], (8, LANES)),
+            jnp.broadcast_to(jnp.cos(rim_theta)[None], (8, LANES)),
         ]
     )
     slot = ghost_slots[0, 0, 0]
-    poles = jnp.pad(slot[: 4 * lon_cells].reshape(4, lon_cells), ((0, 0), (0, LANES - lon_cells)), constant_values=-1)
-    slots = jnp.concatenate([poles, slot[4 * lon_cells :].reshape(4, LANES)])
+    pole = slot[: 4 * lon_cells].reshape(2, 2, lon_cells)
+    pole = jnp.pad(jnp.maximum(pole[0], pole[1]), ((0, 0), (0, LANES - lon_cells)), constant_values=-1)
+    side = slot[4 * lon_cells :].reshape(2, 2, LANES)
+    slots = jnp.concatenate([pole, jnp.maximum(side[0], side[1]), jnp.full((4, LANES), -1, jnp.int32)])
 
     vmem = pl.BlockSpec(memory_space=pltpu.VMEM)
     smem = pl.BlockSpec(memory_space=pltpu.SMEM)
@@ -445,18 +582,45 @@
         compiler_params=params,
     )(slots)
 
-    field, sent, edge_a, edge_b, strips = pl.pallas_call(
+    hbm = pl.BlockSpec(memory_space=pltpu.HBM)
+    field, edge_a, edge_b, strips, buffer, sent, table, again = pl.pallas_call(
         functools.partial(start_kernel, lon_cells),
-        out_shape=moving,
-        in_specs=[vmem, smem, vmem, smem],
-        out_specs=[vmem] * 5,
+        out_shape=[moving[0], moving[2], moving[3], moving[4], f32(peers * ROWS, LANES), moving[1], f32(24, LANES)]
+        + [jax.ShapeDtypeStruct((2 * LANES + 8,), jnp.int32)],
+        in_specs=[hbm, smem, smem, smem, vmem, vmem, smem],
+        out_specs=[vmem] * 4 + [hbm] + [vmem] * 2 + [smem],
+        scratch_shapes=[
+            pltpu.VMEM((lon_cells // 32, ROWS, 32, LANES), jnp.float32),
+            pltpu.VMEM((LANES, LANES), jnp.float32),
+            pltpu.SemaphoreType.DMA((lon_cells // 32 + peers * ROWS // LANES,)),
+        ],
         compiler_params=params,
-    )(state.reshape(cells, LANES), src, table, flag)
-
-    hbm = pl.BlockSpec(memory_space=pl.ANY)
-
-    def exchange(buffer, sent, edge_a, edge_b, strips):
+    )(
+        state.reshape(ROWS, lon_cells, LANES),
+        src,
+        send_counts[0, 0, 0],
+        partners[0, 0, 0],
+        weights.reshape(8, LANES),
+        turn_angles.reshape(2, LANES),
+        flag,
+    )
+
+    origin = field
+    for number in range(2 * STEPS):
+        second = number % 2 == 1
+        final = number == 2 * STEPS - 1
         over = lax.ppermute(sent, "panel", SWAP)
+        operands = [field] + ([origin] if second else []) + [geo]
+        part, part_strips = pl.pallas_call(
+            functools.partial(inner_kernel, second, lon_cells, consts),
+            out_shape=[moving[0], moving[4]],
+            in_specs=[vmem] * len(operands),
+            out_specs=[vmem, vmem],
+            scratch_shapes=[pltpu.VMEM((8 * 23, LANES), jnp.float32)],
+            compiler_params=params,
+            cost_estimate=pl.CostEstimate(flops=20_000_000, bytes_accessed=1 << 23, transcendentals=0),
+        )(*operands)
+        over, part, part_strips = lax.optimization_barrier((over, part, part_strips))
         mate = lax.ppermute(over, "core", SWAP)
         buffer = pl.pallas_call(
             pack_kernel,
@@ -467,34 +631,37 @@
             input_output_aliases={3: 0},
             compiler_params=params,
         )(over, mate, flag, buffer)
-        buffer, edge_a, edge_b, strips = lax.optimization_barrier((buffer, edge_a, edge_b, strips))
+        buffer, own_a, own_b, own_strips, part = lax.optimization_barrier((buffer, edge_a, edge_b, strips, part))
         received = lax.all_to_all(
             buffer.reshape(peers // 2, 2 * ROWS, LANES), ("colat", "lon_hi"), split_axis=0, concat_axis=0, tiled=True
-        )
-        lon_a = lax.ppermute(edge_a, lon_axes, pairs(lon_blocks, 0))
-        lon_b = lax.ppermute(edge_b, lon_axes, pairs(lon_blocks, 1))
-        strip_a = lax.ppermute(strips, "colat", pairs(lat_blocks, 0))
-        strip_b = lax.ppermute(strips, "colat", pairs(lat_blocks, 1))
-        return buffer, lon_a, lon_b, strip_a, strip_b, received.reshape(peers * ROWS, LANES)
-
-    origin = field
-    buffer = jnp.zeros((peers * ROWS, LANES), jnp.float32)
-    for number in range(2 * STEPS):
-        second = number % 2 == 1
-        final = number == 2 * STEPS - 1
-        buffer, lon_a, lon_b, strip_a, strip_b, received = exchange(buffer, sent, edge_a, edge_b, strips)
-        operands = [field] + ([origin] if second else [])
-        specs = [vmem] * len(operands) + [vmem] * 5 + [vmem, smem, smem, vmem, smem, vmem]
-        operands += [lon_a, lon_b, strip_a, strip_b, received, keys, listed, flag, geo, src, table]
+        ).reshape(peers * ROWS, LANES)
+        if not final:
+            corners = pl.pallas_call(
+                rows_kernel,
+                out_shape=f32(8 * ROWS, LANES),
+                in_specs=[vmem, smem],
+                out_specs=vmem,
+                compiler_params=params,
+                cost_estimate=pl.CostEstimate(flops=8_000_000, bytes_accessed=1 << 22, transcendentals=0),
+            )(part, src)
+        lon_a = lax.ppermute(own_a, lon_axes, pairs(lon_blocks, 0))
+        lon_b = lax.ppermute(own_b, lon_axes, pairs(lon_blocks, 1))
+        strip_a = lax.ppermute(own_strips, "colat", pairs(lat_blocks, 0))
+        strip_b = lax.ppermute(own_strips, "colat", pairs(lat_blocks, 1))
+        operands = [part, part_strips, own_a, own_b, own_strips, lon_a, lon_b, strip_a, strip_b, received, keys, listed, flag, geo]
+        specs = [vmem] * 11 + [smem, smem, vmem]
+        if not final:
+            operands += [corners, again, src, table]
+            specs += [vmem, smem, smem, vmem]
         out = pl.pallas_call(
-            functools.partial(stage_kernel, second, final, lon_cells, consts),
+            functools.partial(outer_kernel, second, final, lon_cells, consts),
             out_shape=moving[:1] if final else moving,
             in_specs=specs,
             out_specs=[vmem] * (1 if final else 5),
             scratch_shapes=[
-                pltpu.VMEM((8 * ROWS, LANES), jnp.float32),
+                pltpu.VMEM((4 * ROWS, LANES), jnp.float32),
                 pltpu.VMEM((strip_rows, LANES), jnp.float32),
-                pltpu.VMEM((8 * 23, LANES), jnp.float32),
+                pltpu.VMEM((strip_rows, LANES), jnp.float32),
                 pltpu.VMEM((4 * ROWS, LANES), jnp.float32),
             ],
             compiler_params=params,

time: 141 us -> 125 us (0.89)
  waiting for transfers between devices: 20.7 us -> 5.87 us
  Pallas kernels: 35.5 us -> 41.7 us
  starting transfers between devices: 77.7 us -> 73 us
  local copies, waits for them, and re-layouts: 5.01 us -> 2.19 us
    ppermute x24, waiting for transfers between devices: 18.3 us -> 5.7 us  [the longest x4 3.3 us: on_device(): mate = lax.ppermute(over, 'core', SWAP)]
    pallas_call x9 -> x16, Pallas kernels: 35 us -> 41.2 us  [the longest x4 12.3 us: on_device(): pl.pallas_call(functools.partial(outer_kernel, second, final, lon_cells,...]
    ppermute x24, starting transfers between devices: 56.9 us -> 52 us  [the longest x4 15 us: on_device(): strip_a = lax.ppermute(own_strips, 'colat', pairs(lat_blocks, 0))]
    all_to_all x4, waiting for transfers between devices: 2.37 us -> 0.17 us  [on_device(): lax.all_to_all(buffer.reshape(peers // 2, 2 * ROWS, LANES), ('colat', 'lo...]
    unnamed x18 -> x20, local copies, waits for them, and re-layouts: 3.84 us -> 2.02 us
  transfers between devices with their start and end apart: 28 -> 28, of which waited for: 15 -> 6; matrix products, arithmetic and copies ran while one was open for 0% -> 1% of each run, Pallas kernels for 0% -> 15%
where the time goes in v3:
time: 125 us; the launch traced here: 124 us
  starting transfers between devices  73 us (58%)
  Pallas kernels  41.7 us (33%)
  waiting for transfers between devices  5.87 us (5%)
  local copies, waits for them, and re-layouts  2.19 us (2%)
    all_to_all x4, starting transfers between devices, on_device(): lax.all_to_all(buffer.reshape(peers // 2, 2 * ROWS, LANES), ('colat', 'lo...  21.1 us
    ppermute x4, starting transfers between devices, on_device(): strip_a = lax.ppermute(own_strips, 'colat', pairs(lat_blocks, 0))  15 us
    pallas_call x4, Pallas kernels, on_device(): pl.pallas_call(functools.partial(outer_kernel, second, final, lon_cells,...  12.3 us
    ppermute x4, starting transfers between devices, on_device(): lon_b = lax.ppermute(own_b, lon_axes, pairs(lon_blocks, 1))  11.9 us
    ppermute x4, starting transfers between devices, on_device(): over = lax.ppermute(sent, 'panel', SWAP)  10.5 us
    pallas_call x4, Pallas kernels, on_device(): pl.pallas_call(functools.partial(inner_kernel, second, lon_cells, consts)...  10.3 us
    pallas_call x3, Pallas kernels, on_device(): pl.pallas_call(rows_kernel, out_shape=f32(8 * ROWS, LANES), in_specs=[vme...  8.12 us
    ppermute x4, starting transfers between devices, on_device(): mate = lax.ppermute(over, 'core', SWAP)  6.08 us
  transfers between devices with their start and end apart: 28, of which 6 were waited for; matrix products, arithmetic and copies ran while one was open for 1% of the time, Pallas kernels for 15%

profile of v3, /device:TPU:1, one launch (start us, length us, event | category | flops | bytes accessed | tf_op | source)
XLA Modules:
  0.0 123.6 jit_solution(5408112856245354008)
XLA Ops:
  1.9 5.2 %shard_map.73 = (f32[1536,128]{1,0:T(8,128)S(1)}, f32[32,128]{1,0:T(8,128)S(1)}, f32[32,128]{1,0:T(8,128)S(1)}, f32[48,128]{1,0:T(8,128)S(1)}, f32[1024,128]{1,0...) custom-call(f32[16,96,128]{2,1,0:T(8,128)S(1)} %bitcast.26, s32[256]{0:T(256)S(1)} %bitcast.27, ...), custom_call_target="tpu_custom_call" | custom-call | tf_op jit(solution)/shard_map/pallas_call | solution.py:586
  7.2 3.7 %collective-permute-start = (f32[40,128]{1,0:T(8,128)S(1)}, f32[40,128]{1,0:T(8,128)S(1)}, u32[]{:S(2)}, u32[]{:S(2)}) collective-permute-start(f32[40,128]{1,0:T(8,128)S(1)} %get-tuple-element.70), channel_id=1, source_target_pairs={{0,64},{64,0},{1,65},{65,1},{2,66},{66,2},{3,67},{67,3},{4,68},{68... | collective-permute-start | bytes 61448 | tf_op jit(solution)/shard_map/ppermute | solution.py:612
  11.2 2.6 %shard_map.74 = (f32[1536,128]{1,0:T(8,128)S(1)}, f32[48,128]{1,0:T(8,128)S(1)}) custom-call(f32[1536,128]{1,0:T(8,128)S(1)} %get-tuple-element.71.refs_0_.refs_1_, f32[232,128]{1,0:T(8,128)S(1)} %constant_dynamic-update-slice_fusion.refs_1_.refs_13_.refs_2_), custom_call_target="tpu_custom_call" | custom-call | flops 20000000 | bytes 8388608 | tf_op jit(solution)/shard_map/pallas_call | solution.py:614
  17.0 8.2 %all-to-all-start = ((f32[32,32,128]{2,1,0:T(8,128)}), f32[32,32,128]{2,1,0:T(8,128)S(1)}, u32[]{:S(2)}, u32[]{:S(2)}) async-start(f32[32,32,128]{2,1,0:T(8,128)} %bitcast.10), calls=%async_computation | async-start | bytes 1048576 | tf_op jit(solution)/shard_map/all_to_all | solution.py:635
  26.1 3.7 %collective-permute-start.4 = (f32[48,128]{1,0:T(8,128)S(1)}, f32[48,128]{1,0:T(8,128)S(1)}, u32[]{:S(2)}, u32[]{:S(2)}) collective-permute-start(f32[48,128]{1,0:T(8,128)S(1)} %get-tuple-element.84.refs_4_), channel_id=1, source_target_pairs={{0,16},{16,0},{32,48},{48,32},{1,17},{17,1},{33,49},{49,33},{2,18}... | collective-permute-start | bytes 73736 | tf_op jit(solution)/shard_map/ppermute | solution.py:649
  31.3 3.0 %collective-permute-start.3 = (f32[32,128]{1,0:T(8,128)S(1)}, f32[32,128]{1,0:T(8,128)S(1)}, u32[]{:S(2)}, u32[]{:S(2)}) collective-permute-start(f32[32,128]{1,0:T(8,128)S(1)} %get-tuple-element.83.refs_3_), channel_id=1, source_target_pairs={{1,2},{2,1},{3,4},{4,3},{5,6},{6,5},{7,8},{8,7},{9,10},{10,9},{11,... | collective-permute-start | bytes 49160 | tf_op jit(solution)/shard_map/ppermute | solution.py:648
  34.8 2.7 %shard_map.77.refs_14_ = f32[128,128]{1,0:T(8,128)S(1)} custom-call(f32[1536,128]{1,0:T(8,128)S(1)} %get-tuple-element.80.field.refs_0_, s32[256]{0:T(256)S(1)} %bitcast.28), custom_call_target="tpu_custom_call" | custom-call | flops 8000000 | bytes 4194304 | tf_op jit(solution)/shard_map/pallas_call | solution.py:639
  37.6 2.9 %shard_map.78 = (f32[1536,128]{1,0:T(8,128)S(1)}, f32[40,128]{1,0:T(8,128)S(1)}, f32[32,128]{1,0:T(8,128)S(1)}, f32[32,128]{1,0:T(8,128)S(1)}, f32[48,128]{1,0:T(8,128)S(1)}) custom-call(f32[1536,128]{1,0:T(8,128)S(1)} %get-tuple-element.80.field.refs_0_, f32[48,128]{1,0:T(8,128)S(1)} %get-tuple-element.81.refs_1_, f32[32,128]{1,0:T(8,128)S(1)} %get-tuple-element.82.refs_2_, ...), custom_call_target="tpu_custom_call" | custom-call | tf_op jit(solution)/shard_map/pallas_call | solution.py:656
  40.5 2.4 %collective-permute-start.6 = (f32[40,128]{1,0:T(8,128)S(1)}, f32[40,128]{1,0:T(8,128)S(1)}, u32[]{:S(2)}, u32[]{:S(2)}) collective-permute-start(f32[40,128]{1,0:T(8,128)S(1)} %get-tuple-element.90), channel_id=1, source_target_pairs={{0,64},{64,0},{1,65},{65,1},{2,66},{66,2},{3,67},{67,3},{4,68},{68... | collective-permute-start | bytes 61448 | tf_op jit(solution)/shard_map/ppermute | solution.py:612
  42.9 2.6 %shard_map.79 = (f32[1536,128]{1,0:T(8,128)S(1)}, f32[48,128]{1,0:T(8,128)S(1)}) custom-call(f32[1536,128]{1,0:T(8,128)S(1)} %get-tuple-element.91.refs_0_, f32[1536,128]{1,0:T(8,128)S(1)} %get-tuple-element.71.refs_0_.refs_1_, f32[232,128]{1,0:T(8,128)S(1)} %constant_dynamic-update-slice_fusion.refs_1_.refs_13_.refs_2_), custom_call_target="tpu_custom_call" | custom-call | flops 20000000 | bytes 8388608 | tf_op jit(solution)/shard_map/pallas_call | solution.py:614
  48.8 4.8 %all-to-all-start.1 = ((f32[32,32,128]{2,1,0:T(8,128)}), f32[32,32,128]{2,1,0:T(8,128)S(1)}, u32[]{:S(2)}, u32[]{:S(2)}) async-start(f32[32,32,128]{2,1,0:T(8,128)} %bitcast.13), calls=%async_computation.1 | async-start | bytes 1048576 | tf_op jit(solution)/shard_map/all_to_all | solution.py:635
  54.2 3.7 %collective-permute-start.10 = (f32[48,128]{1,0:T(8,128)S(1)}, f32[48,128]{1,0:T(8,128)S(1)}, u32[]{:S(2)}, u32[]{:S(2)}) collective-permute-start(f32[48,128]{1,0:T(8,128)S(1)} %get-tuple-element.103.refs_4_), channel_id=1, source_target_pairs={{0,16},{16,0},{32,48},{48,32},{1,17},{17,1},{33,49},{49,33},{2,18}... | collective-permute-start | bytes 73736 | tf_op jit(solution)/shard_map/ppermute | solution.py:649
  59.5 3.0 %collective-permute-start.9 = (f32[32,128]{1,0:T(8,128)S(1)}, f32[32,128]{1,0:T(8,128)S(1)}, u32[]{:S(2)}, u32[]{:S(2)}) collective-permute-start(f32[32,128]{1,0:T(8,128)S(1)} %get-tuple-element.102.refs_3_), channel_id=1, source_target_pairs={{1,2},{2,1},{3,4},{4,3},{5,6},{6,5},{7,8},{8,7},{9,10},{10,9},{11,... | collective-permute-start | bytes 49160 | tf_op jit(solution)/shard_map/ppermute | solution.py:648
  62.4 2.7 %shard_map.81.refs_14_ = f32[128,128]{1,0:T(8,128)S(1)} custom-call(f32[1536,128]{1,0:T(8,128)S(1)} %get-tuple-element.99.field.refs_0_, s32[256]{0:T(256)S(1)} %bitcast.30), custom_call_target="tpu_custom_call" | custom-call | flops 8000000 | bytes 4194304 | tf_op jit(solution)/shard_map/pallas_call | solution.py:639
  65.2 2.9 %shard_map.82 = (f32[1536,128]{1,0:T(8,128)S(1)}, f32[40,128]{1,0:T(8,128)S(1)}, f32[32,128]{1,0:T(8,128)S(1)}, f32[32,128]{1,0:T(8,128)S(1)}, f32[48,128]{1,0:T(8,128)S(1)}) custom-call(f32[1536,128]{1,0:T(8,128)S(1)} %get-tuple-element.99.field.refs_0_, f32[48,128]{1,0:T(8,128)S(1)} %get-tuple-element.100.refs_1_, ...), custom_call_target="tpu_custom_call" | custom-call | tf_op jit(solution)/shard_map/pallas_call | solution.py:656
  68.1 2.2 %collective-permute-start.12 = (f32[40,128]{1,0:T(8,128)S(1)}, f32[40,128]{1,0:T(8,128)S(1)}, u32[]{:S(2)}, u32[]{:S(2)}) collective-permute-start(f32[40,128]{1,0:T(8,128)S(1)} %get-tuple-element.105), channel_id=1, source_target_pairs={{0,64},{64,0},{1,65},{65,1},{2,66},{66,2},{3,67},{67,3},{4,68},{68... | collective-permute-start | bytes 61448 | tf_op jit(solution)/shard_map/ppermute | solution.py:612
  70.4 2.6 %shard_map.83 = (f32[1536,128]{1,0:T(8,128)S(1)}, f32[48,128]{1,0:T(8,128)S(1)}) custom-call(f32[1536,128]{1,0:T(8,128)S(1)} %get-tuple-element.106.refs_0_.refs_1_, f32[232,128]{1,0:T(8,128)S(1)} %constant_dynamic-update-slice_fusion.refs_1_.refs_13_.refs_2_), custom_call_target="tpu_custom_call" | custom-call | flops 20000000 | bytes 8388608 | tf_op jit(solution)/shard_map/pallas_call | solution.py:614
  73.0 2.0 %collective-permute-start.13 = (f32[40,128]{1,0:T(8,128)S(1)}, f32[40,128]{1,0:T(8,128)S(1)}, u32[]{:S(2)}, u32[]{:S(2)}) collective-permute-start(f32[40,128]{1,0:T(8,128)S(1)} %collective-permute-done.12.message_a), channel_id=1, source_target_pairs={{0,1},{1,0},{2,3},{3,2},{4,5},{5,4},{6,7},{7,6},{8,9},{9,8},{10,11... | collective-permute-start | bytes 61448 | tf_op jit(solution)/shard_map/ppermute | solution.py:624
  77.1 4.0 %all-to-all-start.2 = ((f32[32,32,128]{2,1,0:T(8,128)}), f32[32,32,128]{2,1,0:T(8,128)S(1)}, u32[]{:S(2)}, u32[]{:S(2)}) async-start(f32[32,32,128]{2,1,0:T(8,128)} %bitcast.15), calls=%async_computation.2 | async-start | bytes 1048576 | tf_op jit(solution)/shard_map/all_to_all | solution.py:635
  81.8 3.7 %collective-permute-start.16 = (f32[48,128]{1,0:T(8,128)S(1)}, f32[48,128]{1,0:T(8,128)S(1)}, u32[]{:S(2)}, u32[]{:S(2)}) collective-permute-start(f32[48,128]{1,0:T(8,128)S(1)} %get-tuple-element.118.refs_4_), channel_id=1, source_target_pairs={{0,16},{16,0},{32,48},{48,32},{1,17},{17,1},{33,49},{49,33},{2,18}... | collective-permute-start | bytes 73736 | tf_op jit(solution)/shard_map/ppermute | solution.py:649
  85.5 1.5 %collective-permute-start.14 = (f32[32,128]{1,0:T(8,128)S(1)}, f32[32,128]{1,0:T(8,128)S(1)}, u32[]{:S(2)}, u32[]{:S(2)}) collective-permute-start(f32[32,128]{1,0:T(8,128)S(1)} %get-tuple-element.116.refs_2_), channel_id=1, source_target_pairs={{0,1},{1,0},{2,3},{3,2},{4,5},{5,4},{6,7},{7,6},{8,9},{9,8},{10,11... | collective-permute-start | bytes 49160 | tf_op jit(solution)/shard_map/ppermute | solution.py:647
  87.0 3.0 %collective-permute-start.15 = (f32[32,128]{1,0:T(8,128)S(1)}, f32[32,128]{1,0:T(8,128)S(1)}, u32[]{:S(2)}, u32[]{:S(2)}) collective-permute-start(f32[32,128]{1,0:T(8,128)S(1)} %get-tuple-element.117.refs_3_), channel_id=1, source_target_pairs={{1,2},{2,1},{3,4},{4,3},{5,6},{6,5},{7,8},{8,7},{9,10},{10,9},{11,... | collective-permute-start | bytes 49160 | tf_op jit(solution)/shard_map/ppermute | solution.py:648
  90.0 2.7 %shard_map.85.refs_14_ = f32[128,128]{1,0:T(8,128)S(1)} custom-call(f32[1536,128]{1,0:T(8,128)S(1)} %get-tuple-element.114.field.refs_0_, s32[256]{0:T(256)S(1)} %bitcast.32), custom_call_target="tpu_custom_call" | custom-call | flops 8000000 | bytes 4194304 | tf_op jit(solution)/shard_map/pallas_call | solution.py:639
  92.7 2.9 %shard_map.86 = (f32[1536,128]{1,0:T(8,128)S(1)}, f32[40,128]{1,0:T(8,128)S(1)}, f32[32,128]{1,0:T(8,128)S(1)}, f32[32,128]{1,0:T(8,128)S(1)}, f32[48,128]{1,0:T(8,128)S(1)}) custom-call(f32[1536,128]{1,0:T(8,128)S(1)} %get-tuple-element.114.field.refs_0_, f32[48,128]{1,0:T(8,128)S(1)} %get-tuple-element.115.refs_1_, ...), custom_call_target="tpu_custom_call" | custom-call | tf_op jit(solution)/shard_map/pallas_call | solution.py:656
  95.7 2.3 %collective-permute-start.18 = (f32[40,128]{1,0:T(8,128)S(1)}, f32[40,128]{1,0:T(8,128)S(1)}, u32[]{:S(2)}, u32[]{:S(2)}) collective-permute-start(f32[40,128]{1,0:T(8,128)S(1)} %get-tuple-element.120), channel_id=1, source_target_pairs={{0,64},{64,0},{1,65},{65,1},{2,66},{66,2},{3,67},{67,3},{4,68},{68... | collective-permute-start | bytes 61448 | tf_op jit(solution)/shard_map/ppermute | solution.py:612
  98.0 2.6 %shard_map.87 = (f32[1536,128]{1,0:T(8,128)S(1)}, f32[48,128]{1,0:T(8,128)S(1)}) custom-call(f32[1536,128]{1,0:T(8,128)S(1)} %get-tuple-element.121.refs_0_, f32[1536,128]{1,0:T(8,128)S(1)} %get-tuple-element.106.refs_0_.refs_1_, f32[232,128]{1,0:T(8,128)S(1)} %constant_dynamic-update-slice_fusion.refs_1_.refs_13_.refs_2_), custom_call_target="tpu_custom_call" | custom-call | flops 20000000 | bytes 8388608 | tf_op jit(solution)/shard_map/pallas_call | solution.py:614
  100.6 1.9 %collective-permute-start.19 = (f32[40,128]{1,0:T(8,128)S(1)}, f32[40,128]{1,0:T(8,128)S(1)}, u32[]{:S(2)}, u32[]{:S(2)}) collective-permute-start(f32[40,128]{1,0:T(8,128)S(1)} %collective-permute-done.18.message_a), channel_id=1, source_target_pairs={{0,1},{1,0},{2,3},{3,2},{4,5},{5,4},{6,7},{7,6},{8,9},{9,8},{10,11... | collective-permute-start | bytes 61448 | tf_op jit(solution)/shard_map/ppermute | solution.py:624
  104.7 4.1 %all-to-all-start.3 = ((f32[32,32,128]{2,1,0:T(8,128)}), f32[32,32,128]{2,1,0:T(8,128)S(1)}, u32[]{:S(2)}, u32[]{:S(2)}) async-start(f32[32,32,128]{2,1,0:T(8,128)} %bitcast.17), calls=%async_computation.3 | async-start | bytes 1048576 | tf_op jit(solution)/shard_map/all_to_all | solution.py:635
  109.4 3.7 %collective-permute-start.22 = (f32[48,128]{1,0:T(8,128)S(1)}, f32[48,128]{1,0:T(8,128)S(1)}, u32[]{:S(2)}, u32[]{:S(2)}) collective-permute-start(f32[48,128]{1,0:T(8,128)S(1)} %get-tuple-element.133.refs_4_), channel_id=1, source_target_pairs={{0,16},{16,0},{32,48},{48,32},{1,17},{17,1},{33,49},{49,33},{2,18}... | collective-permute-start | bytes 73736 | tf_op jit(solution)/shard_map/ppermute | solution.py:649
  114.6 3.0 %collective-permute-start.21 = (f32[32,128]{1,0:T(8,128)S(1)}, f32[32,128]{1,0:T(8,128)S(1)}, u32[]{:S(2)}, u32[]{:S(2)}) collective-permute-start(f32[32,128]{1,0:T(8,128)S(1)} %get-tuple-element.132.refs_3_), channel_id=1, source_target_pairs={{1,2},{2,1},{3,4},{4,3},{5,6},{6,5},{7,8},{8,7},{9,10},{10,9},{11,... | collective-permute-start | bytes 49160 | tf_op jit(solution)/shard_map/ppermute | solution.py:648
  117.6 2.4 %collective-permute-done.21.refs_6_ = f32[32,128]{1,0:T(8,128)S(1)} collective-permute-done((f32[32,128]{1,0:T(8,128)S(1)}, f32[32,128]{1,0:T(8,128)S(1)}, u32[]{:S(2)}, u32[]{:S(2)}) %collective-permute-start.21) | collective-permute-done | bytes 16416 | tf_op jit(solution)/shard_map/ppermute | solution.py:648
  120.1 3.5 %shard_map.89 = f32[1536,128]{1,0:T(8,128)} custom-call(f32[1536,128]{1,0:T(8,128)S(1)} %get-tuple-element.129.refs_0_, f32[48,128]{1,0:T(8,128)S(1)} %get-tuple-element.130.refs_1_, f32[32,128]{1,0:T(8,128)S(1)} %get-tuple-element.131.refs_2_, f32[32,128]{1,0:T(8,128)S(1)} %get-tuple-element.132.refs_3_, f32[48,128]{1,0:T(8,128)S(1)} %get-tuple-element.133.refs_4_, ...), custom_call_target="tpu_custom_call" | custom-call | tf_op jit(solution)/shard_map/pallas_call | solution.py:656
  (73 shorter events, 21.0 us)
Async XLA Ops:
  0.1 0.7 copy-start.1
  0.1 0.7 copy-start.4
  0.8 1.1 copy-start
  7.2 6.6 %collective-permute-start = (f32[40,128]{1,0:T(8,128)S(1)}, f32[40,128]{1,0:T(8,128)S(1)}, u32[]{:S(2)}, u32[]{:S(2)}) collective-permute-start(f32[40,128]{1,0:T(8,128)S(1)} %get-tuple-element.70), channel_id=1, source_target_pairs={{0,64},{64,0},{1,65},{65,1},{2,66},{66,2},{3,67},{67,3},{4,68},{68... | collective-permute-start | bytes 61448 | tf_op jit(solution)/shard_map/ppermute | solution.py:612
  13.8 1.9 %collective-permute-start.1 = (f32[40,128]{1,0:T(8,128)S(1)}, f32[40,128]{1,0:T(8,128)S(1)}, u32[]{:S(2)}, u32[]{:S(2)}) collective-permute-start(f32[40,128]{1,0:T(8,128)S(1)} %collective-permute-done.message_a), channel_id=1, source_target_pairs={{0,1},{1,0},{2,3},{3,2},{4,5},{5,4},{6,7},{7,6},{8,9},{9,8},{10,11... | collective-permute-start | bytes 61448 | tf_op jit(solution)/shard_map/ppermute | solution.py:624
  17.0 8.2 %copy-start.6 = (s32[1,1,1,896]{3,2,1,0:T(1,128)S(1)}, s32[1,1,1,896]{3,2,1,0:T(1,128)}, u32[]{:S(2)}) copy-start(s32[1,1,1,896]{3,2,1,0:T(1,128)} %param.13) | copy-start | bytes 10756
  17.0 20.6 %all-to-all-start = ((f32[32,32,128]{2,1,0:T(8,128)}), f32[32,32,128]{2,1,0:T(8,128)S(1)}, u32[]{:S(2)}, u32[]{:S(2)}) async-start(f32[32,32,128]{2,1,0:T(8,128)} %bitcast.10), calls=%async_computation | async-start | bytes 1048576 | tf_op jit(solution)/shard_map/all_to_all | solution.py:635
  25.4 12.2 %collective-permute-start.5 = (f32[48,128]{1,0:T(8,128)S(1)}, f32[48,128]{1,0:T(8,128)S(1)}, u32[]{:S(2)}, u32[]{:S(2)}) collective-permute-start(f32[48,128]{1,0:T(8,128)S(1)} %get-tuple-element.84.refs_4_), channel_id=1, source_target_pairs={{16,32},{32,16},{17,33},{33,17},{18,34},{34,18},{19,35},{35,19},{2... | collective-permute-start | bytes 73736 | tf_op jit(solution)/shard_map/ppermute | solution.py:650
  26.1 11.5 %collective-permute-start.4 = (f32[48,128]{1,0:T(8,128)S(1)}, f32[48,128]{1,0:T(8,128)S(1)}, u32[]{:S(2)}, u32[]{:S(2)}) collective-permute-start(f32[48,128]{1,0:T(8,128)S(1)} %get-tuple-element.84.refs_4_), channel_id=1, source_target_pairs={{0,16},{16,0},{32,48},{48,32},{1,17},{17,1},{33,49},{49,33},{2,18}... | collective-permute-start | bytes 73736 | tf_op jit(solution)/shard_map/ppermute | solution.py:649
  29.8 7.7 %collective-permute-start.2 = (f32[32,128]{1,0:T(8,128)S(1)}, f32[32,128]{1,0:T(8,128)S(1)}, u32[]{:S(2)}, u32[]{:S(2)}) collective-permute-start(f32[32,128]{1,0:T(8,128)S(1)} %get-tuple-element.82.refs_2_), channel_id=1, source_target_pairs={{0,1},{1,0},{2,3},{3,2},{4,5},{5,4},{6,7},{7,6},{8,9},{9,8},{10,11... | collective-permute-start | bytes 49160 | tf_op jit(solution)/shard_map/ppermute | solution.py:647
  31.3 6.3 %collective-permute-start.3 = (f32[32,128]{1,0:T(8,128)S(1)}, f32[32,128]{1,0:T(8,128)S(1)}, u32[]{:S(2)}, u32[]{:S(2)}) collective-permute-start(f32[32,128]{1,0:T(8,128)S(1)} %get-tuple-element.83.refs_3_), channel_id=1, source_target_pairs={{1,2},{2,1},{3,4},{4,3},{5,6},{6,5},{7,8},{8,7},{9,10},{10,9},{11,... | collective-permute-start | bytes 49160 | tf_op jit(solution)/shard_map/ppermute | solution.py:648
  40.5 5.0 %collective-permute-start.6 = (f32[40,128]{1,0:T(8,128)S(1)}, f32[40,128]{1,0:T(8,128)S(1)}, u32[]{:S(2)}, u32[]{:S(2)}) collective-permute-start(f32[40,128]{1,0:T(8,128)S(1)} %get-tuple-element.90), channel_id=1, source_target_pairs={{0,64},{64,0},{1,65},{65,1},{2,66},{66,2},{3,67},{67,3},{4,68},{68... | collective-permute-start | bytes 61448 | tf_op jit(solution)/shard_map/ppermute | solution.py:612
  45.5 2.0 %collective-permute-start.7 = (f32[40,128]{1,0:T(8,128)S(1)}, f32[40,128]{1,0:T(8,128)S(1)}, u32[]{:S(2)}, u32[]{:S(2)}) collective-permute-start(f32[40,128]{1,0:T(8,128)S(1)} %collective-permute-done.6.message_a), channel_id=1, source_target_pairs={{0,1},{1,0},{2,3},{3,2},{4,5},{5,4},{6,7},{7,6},{8,9},{9,8},{10,11... | collective-permute-start | bytes 61448 | tf_op jit(solution)/shard_map/ppermute | solution.py:624
  48.8 16.4 %all-to-all-start.1 = ((f32[32,32,128]{2,1,0:T(8,128)}), f32[32,32,128]{2,1,0:T(8,128)S(1)}, u32[]{:S(2)}, u32[]{:S(2)}) async-start(f32[32,32,128]{2,1,0:T(8,128)} %bitcast.13), calls=%async_computation.1 | async-start | bytes 1048576 | tf_op jit(solution)/shard_map/all_to_all | solution.py:635
  53.6 11.6 %collective-permute-start.11 = (f32[48,128]{1,0:T(8,128)S(1)}, f32[48,128]{1,0:T(8,128)S(1)}, u32[]{:S(2)}, u32[]{:S(2)}) collective-permute-start(f32[48,128]{1,0:T(8,128)S(1)} %get-tuple-element.103.refs_4_), channel_id=1, source_target_pairs={{16,32},{32,16},{17,33},{33,17},{18,34},{34,18},{19,35},{35,19},{2... | collective-permute-start | bytes 73736 | tf_op jit(solution)/shard_map/ppermute | solution.py:650
  54.2 10.9 %collective-permute-start.10 = (f32[48,128]{1,0:T(8,128)S(1)}, f32[48,128]{1,0:T(8,128)S(1)}, u32[]{:S(2)}, u32[]{:S(2)}) collective-permute-start(f32[48,128]{1,0:T(8,128)S(1)} %get-tuple-element.103.refs_4_), channel_id=1, source_target_pairs={{0,16},{16,0},{32,48},{48,32},{1,17},{17,1},{33,49},{49,33},{2,18}... | collective-permute-start | bytes 73736 | tf_op jit(solution)/shard_map/ppermute | solution.py:649
  58.0 7.2 %collective-permute-start.8 = (f32[32,128]{1,0:T(8,128)S(1)}, f32[32,128]{1,0:T(8,128)S(1)}, u32[]{:S(2)}, u32[]{:S(2)}) collective-permute-start(f32[32,128]{1,0:T(8,128)S(1)} %get-tuple-element.101.refs_2_), channel_id=1, source_target_pairs={{0,1},{1,0},{2,3},{3,2},{4,5},{5,4},{6,7},{7,6},{8,9},{9,8},{10,11... | collective-permute-start | bytes 49160 | tf_op jit(solution)/shard_map/ppermute | solution.py:647
  59.5 5.7 %collective-permute-start.9 = (f32[32,128]{1,0:T(8,128)S(1)}, f32[32,128]{1,0:T(8,128)S(1)}, u32[]{:S(2)}, u32[]{:S(2)}) collective-permute-start(f32[32,128]{1,0:T(8,128)S(1)} %get-tuple-element.102.refs_3_), channel_id=1, source_target_pairs={{1,2},{2,1},{3,4},{4,3},{5,6},{6,5},{7,8},{8,7},{9,10},{10,9},{11,... | collective-permute-start | bytes 49160 | tf_op jit(solution)/shard_map/ppermute | solution.py:648
  68.1 4.8 %collective-permute-start.12 = (f32[40,128]{1,0:T(8,128)S(1)}, f32[40,128]{1,0:T(8,128)S(1)}, u32[]{:S(2)}, u32[]{:S(2)}) collective-permute-start(f32[40,128]{1,0:T(8,128)S(1)} %get-tuple-element.105), channel_id=1, source_target_pairs={{0,64},{64,0},{1,65},{65,1},{2,66},{66,2},{3,67},{67,3},{4,68},{68... | collective-permute-start | bytes 61448 | tf_op jit(solution)/shard_map/ppermute | solution.py:612
  73.0 2.8 %collective-permute-start.13 = (f32[40,128]{1,0:T(8,128)S(1)}, f32[40,128]{1,0:T(8,128)S(1)}, u32[]{:S(2)}, u32[]{:S(2)}) collective-permute-start(f32[40,128]{1,0:T(8,128)S(1)} %collective-permute-done.12.message_a), channel_id=1, source_target_pairs={{0,1},{1,0},{2,3},{3,2},{4,5},{5,4},{6,7},{7,6},{8,9},{9,8},{10,11... | collective-permute-start | bytes 61448 | tf_op jit(solution)/shard_map/ppermute | solution.py:624
  77.1 15.6 %all-to-all-start.2 = ((f32[32,32,128]{2,1,0:T(8,128)}), f32[32,32,128]{2,1,0:T(8,128)S(1)}, u32[]{:S(2)}, u32[]{:S(2)}) async-start(f32[32,32,128]{2,1,0:T(8,128)} %bitcast.15), calls=%async_computation.2 | async-start | bytes 1048576 | tf_op jit(solution)/shard_map/all_to_all | solution.py:635
  81.1 11.6 %collective-permute-start.17 = (f32[48,128]{1,0:T(8,128)S(1)}, f32[48,128]{1,0:T(8,128)S(1)}, u32[]{:S(2)}, u32[]{:S(2)}) collective-permute-start(f32[48,128]{1,0:T(8,128)S(1)} %get-tuple-element.118.refs_4_), channel_id=1, source_target_pairs={{16,32},{32,16},{17,33},{33,17},{18,34},{34,18},{19,35},{35,19},{2... | collective-permute-start | bytes 73736 | tf_op jit(solution)/shard_map/ppermute | solution.py:650
  81.8 10.9 %collective-permute-start.16 = (f32[48,128]{1,0:T(8,128)S(1)}, f32[48,128]{1,0:T(8,128)S(1)}, u32[]{:S(2)}, u32[]{:S(2)}) collective-permute-start(f32[48,128]{1,0:T(8,128)S(1)} %get-tuple-element.118.refs_4_), channel_id=1, source_target_pairs={{0,16},{16,0},{32,48},{48,32},{1,17},{17,1},{33,49},{49,33},{2,18}... | collective-permute-start | bytes 73736 | tf_op jit(solution)/shard_map/ppermute | solution.py:649
  85.5 7.2 %collective-permute-start.14 = (f32[32,128]{1,0:T(8,128)S(1)}, f32[32,128]{1,0:T(8,128)S(1)}, u32[]{:S(2)}, u32[]{:S(2)}) collective-permute-start(f32[32,128]{1,0:T(8,128)S(1)} %get-tuple-element.116.refs_2_), channel_id=1, source_target_pairs={{0,1},{1,0},{2,3},{3,2},{4,5},{5,4},{6,7},{7,6},{8,9},{9,8},{10,11... | collective-permute-start | bytes 49160 | tf_op jit(solution)/shard_map/ppermute | solution.py:647
  87.0 5.7 %collective-permute-start.15 = (f32[32,128]{1,0:T(8,128)S(1)}, f32[32,128]{1,0:T(8,128)S(1)}, u32[]{:S(2)}, u32[]{:S(2)}) collective-permute-start(f32[32,128]{1,0:T(8,128)S(1)} %get-tuple-element.117.refs_3_), channel_id=1, source_target_pairs={{1,2},{2,1},{3,4},{4,3},{5,6},{6,5},{7,8},{8,7},{9,10},{10,9},{11,... | collective-permute-start | bytes 49160 | tf_op jit(solution)/shard_map/ppermute | solution.py:648
  95.7 4.9 %collective-permute-start.18 = (f32[40,128]{1,0:T(8,128)S(1)}, f32[40,128]{1,0:T(8,128)S(1)}, u32[]{:S(2)}, u32[]{:S(2)}) collective-permute-start(f32[40,128]{1,0:T(8,128)S(1)} %get-tuple-element.120), channel_id=1, source_target_pairs={{0,64},{64,0},{1,65},{65,1},{2,66},{66,2},{3,67},{67,3},{4,68},{68... | collective-permute-start | bytes 61448 | tf_op jit(solution)/shard_map/ppermute | solution.py:612
  100.6 2.8 %collective-permute-start.19 = (f32[40,128]{1,0:T(8,128)S(1)}, f32[40,128]{1,0:T(8,128)S(1)}, u32[]{:S(2)}, u32[]{:S(2)}) collective-permute-start(f32[40,128]{1,0:T(8,128)S(1)} %collective-permute-done.18.message_a), channel_id=1, source_target_pairs={{0,1},{1,0},{2,3},{3,2},{4,5},{5,4},{6,7},{7,6},{8,9},{9,8},{10,11... | collective-permute-start | bytes 61448 | tf_op jit(solution)/shard_map/ppermute | solution.py:624
  104.7 15.5 %all-to-all-start.3 = ((f32[32,32,128]{2,1,0:T(8,128)}), f32[32,32,128]{2,1,0:T(8,128)S(1)}, u32[]{:S(2)}, u32[]{:S(2)}) async-start(f32[32,32,128]{2,1,0:T(8,128)} %bitcast.17), calls=%async_computation.3 | async-start | bytes 1048576 | tf_op jit(solution)/shard_map/all_to_all | solution.py:635
  108.7 11.2 %collective-permute-start.23 = (f32[48,128]{1,0:T(8,128)S(1)}, f32[48,128]{1,0:T(8,128)S(1)}, u32[]{:S(2)}, u32[]{:S(2)}) collective-permute-start(f32[48,128]{1,0:T(8,128)S(1)} %get-tuple-element.133.refs_4_), channel_id=1, source_target_pairs={{16,32},{32,16},{17,33},{33,17},{18,34},{34,18},{19,35},{35,19},{2... | collective-permute-start | bytes 73736 | tf_op jit(solution)/shard_map/ppermute | solution.py:650
  109.4 10.6 %collective-permute-start.22 = (f32[48,128]{1,0:T(8,128)S(1)}, f32[48,128]{1,0:T(8,128)S(1)}, u32[]{:S(2)}, u32[]{:S(2)}) collective-permute-start(f32[48,128]{1,0:T(8,128)S(1)} %get-tuple-element.133.refs_4_), channel_id=1, source_target_pairs={{0,16},{16,0},{32,48},{48,32},{1,17},{17,1},{33,49},{49,33},{2,18}... | collective-permute-start | bytes 73736 | tf_op jit(solution)/shard_map/ppermute | solution.py:649
  113.1 4.4 %collective-permute-start.20 = (f32[32,128]{1,0:T(8,128)S(1)}, f32[32,128]{1,0:T(8,128)S(1)}, u32[]{:S(2)}, u32[]{:S(2)}) collective-permute-start(f32[32,128]{1,0:T(8,128)S(1)} %get-tuple-element.131.refs_2_), channel_id=1, source_target_pairs={{0,1},{1,0},{2,3},{3,2},{4,5},{5,4},{6,7},{7,6},{8,9},{9,8},{10,11... | collective-permute-start | bytes 49160 | tf_op jit(solution)/shard_map/ppermute | solution.py:647
  114.6 5.3 %collective-permute-start.21 = (f32[32,128]{1,0:T(8,128)S(1)}, f32[32,128]{1,0:T(8,128)S(1)}, u32[]{:S(2)}, u32[]{:S(2)}) collective-permute-start(f32[32,128]{1,0:T(8,128)S(1)} %get-tuple-element.132.refs_3_), channel_id=1, source_target_pairs={{1,2},{2,1},{3,4},{4,3},{5,6},{6,5},{7,8},{8,7},{9,10},{10,9},{11,... | collective-permute-start | bytes 49160 | tf_op jit(solution)/shard_map/ppermute | solution.py:648
  (3 other events, 2.1 us)

commit v4 on v3

--- a/solution.py
+++ b/solution.py
@@ -15,8 +15,9 @@
 LANES = 128
 ROWS = 16
 NO_KEY = 1.0e9
+AGAIN = 8
 GROUP = 8
-SWAP = [(0, 1), (1, 0)]
+CROSS = [(0, 3), (3, 0), (1, 2), (2, 1)]
 
 
 def constants(lat_total, lon_total):
@@ -57,25 +58,25 @@
 
 
 def pick(field, src, at, m, slot, accs):
-    lane = lane_ids(2 * ROWS)
+    lane = lane_ids(8)
     cell = src[at]
     lon = lax.shift_right_logical(cell, 7)
     lat = lax.bitwise_and(cell, LANES - 1)
     both = field[pl.ds(pl.multiple_of(lon * ROWS, ROWS), 2 * ROWS), :]
-    both = pltpu.roll(both, lax.bitwise_and(m - lat + LANES, LANES - 1), 1)
-    here = lane == m
-    beside = lane == lax.bitwise_and(m + 1, LANES - 1)
+    near = pltpu.roll(both, lax.bitwise_and(m - lat + LANES, LANES - 1), 1)
     accs = list(accs)
-    for number in range(2):
-        if isinstance(slot, int) and slot != number:
-            continue
-        ours, next_to = here, beside
-        if not isinstance(slot, int):
-            shown = jnp.where(slot == number, m, 2 * LANES)
-            ours = lane == shown
-            next_to = jnp.logical_and(beside, slot == number)
-        accs[2 * number] = jnp.where(ours, both, accs[2 * number])
-        accs[2 * number + 1] = jnp.where(next_to, both, accs[2 * number + 1])
+    if isinstance(slot, int):
+        columns = [(2 * slot, near, lane == m), (2 * slot + 1, near, lane == lax.bitwise_and(m + 1, LANES - 1))]
+    else:
+        far = pltpu.roll(both, lax.bitwise_and(m - lat + LANES - 1, LANES - 1), 1)
+        columns = []
+        for number in range(2):
+            mask = lane == jnp.where(slot == number, m, 2 * LANES)
+            columns += [(2 * number, near, mask), (2 * number + 1, far, mask)]
+    for number, column, mask in columns:
+        old = accs[number]
+        rows = [jnp.where(mask, column[8 * i : 8 * i + 8], old[8 * i : 8 * i + 8]) for i in range(4)]
+        accs[number] = jnp.concatenate(rows, axis=0)
     return tuple(accs)
 
 
@@ -100,19 +101,19 @@
         return count, accs
 
     zero = jnp.zeros((2 * ROWS, LANES), jnp.float32)
-    count, accs = lax.fori_loop(0, LANES, body, (jnp.int32(0), (zero, zero, zero, zero)), unroll=8)
+    count, accs = lax.fori_loop(0, LANES, body, (jnp.int32(0), (zero, zero, zero, zero)), unroll=32)
     if listed is not None:
-        for k in range(4):
+        for k in range(AGAIN):
             listed[count + k] = 0
         listed[listed.shape[0] - 1] = count
-    return accs
+    near0, far0, near1, far1 = accs
+    return near0, pltpu.roll(far0, LANES - 1, 1), near1, pltpu.roll(far1, LANES - 1, 1)
 
 
 def finish_rows(accs, table, sent):
     sub = sub_ids()
     for slot in range(2):
         near, far = accs[2 * slot], accs[2 * slot + 1]
-        far = pltpu.roll(far, LANES - 1, 1)
         base = slot * 8
         w0 = table[base : base + 1, :]
         w1 = table[base + 1 : base + 2, :]
@@ -192,7 +193,7 @@
 def key_kernel(slots, keys, listed):
     lane = lane_ids(8)
     slot = slots[...]
-    peer = lax.shift_right_arithmetic(slot, 7)
+    peer = lax.bitwise_xor(lax.shift_right_arithmetic(slot, 7), 1)
     shift = lax.bitwise_and(slot - lane, LANES - 1)
     key = jnp.where(slot >= 0, (peer * LANES + shift).astype(jnp.float32), NO_KEY)
     keys[...] = key
@@ -462,15 +463,13 @@
         else:
             result[rows_of(u), :] = new
 
-    def body(number, carry):
-        index = number * GROUP
-        block = lax.shift_right_logical(index, 5)
-        col = lax.bitwise_and(index, 31)
-        for new, k in [(corrected(index + k, block, col + k), k) for k in range(GROUP)]:
-            store(index + k, new)
+    def body(block, carry):
+        for col in range(32):
+            u = block * 32 + col
+            store(u, corrected(u, block, col))
         return carry
 
-    lax.fori_loop(0, lon_cells // GROUP, body, 0)
+    lax.fori_loop(0, blocks, body, 0)
     if not final:
         strips[...] = part_strips[...] + fixes[...]
     quad = lax.shift_right_logical(lane16, 2)
@@ -485,40 +484,35 @@
     put_edges(result, flag, lon_cells, edge_a, edge_b)
 
     def repeat(step, accs):
-        for k in range(4):
-            at = again[4 * step + k]
+        for k in range(AGAIN):
+            at = again[AGAIN * step + k]
             accs = pick(result, src, at, lax.bitwise_and(at, LANES - 1), lax.shift_right_logical(at, 7), accs)
         return accs
 
     accs = tuple(corners[2 * i * ROWS : 2 * (i + 1) * ROWS, :] for i in range(4))
-    steps = lax.shift_right_logical(again[again.shape[0] - 1] + 3, 2)
+    steps = (again[again.shape[0] - 1] + AGAIN - 1) // AGAIN
     finish_rows(lax.fori_loop(0, steps, repeat, accs), table, sent)
 
 
-def pack_kernel(message_a, message_b, flag, _, buffer, staged, sems):
-    core = flag[0]
-    copies = []
-    for number, (message, own) in enumerate(((message_a, core), (message_b, 1 - core))):
-        target0 = jnp.max(message[32:33, :]).astype(jnp.int32)
-        target1 = jnp.max(message[33:34, :]).astype(jnp.int32)
-        same = target0 == target1
-        slot0, slot1 = message[0:ROWS, :], message[ROWS : 2 * ROWS, :]
-        staged[2 * number * ROWS : (2 * number + 1) * ROWS, :] = jnp.where(same, slot0 + slot1, slot0)
-        staged[(2 * number + 1) * ROWS : (2 * number + 2) * ROWS, :] = slot1
-        for slot, target in ((0, target0), (1, target1)):
-            wanted = lax.bitwise_and(target, 1) == core
-            if slot == 1:
-                wanted = jnp.logical_and(wanted, jnp.logical_not(same))
-            place = pl.multiple_of((target - core + own) * ROWS, ROWS)
-            at = 2 * number + slot
-            copy = pltpu.make_async_copy(
-                staged.at[pl.ds(at * ROWS, ROWS), :], buffer.at[pl.ds(place, ROWS), :], sems.at[at]
-            )
-            copies.append((wanted, copy))
-    for wanted, copy in copies:
-        pl.when(wanted)(copy.start)
-    for wanted, copy in copies:
-        pl.when(wanted)(copy.wait)
+def pack_kernel(message, _, buffer, staged, sems):
+    target0 = jnp.max(message[32:33, :]).astype(jnp.int32)
+    target1 = jnp.max(message[33:34, :]).astype(jnp.int32)
+    same = target0 == target1
+    slot0, slot1 = message[0:ROWS, :], message[ROWS : 2 * ROWS, :]
+    staged[0:ROWS, :] = jnp.where(same, slot0 + slot1, slot0)
+    staged[ROWS : 2 * ROWS, :] = slot1
+    copies = [
+        pltpu.make_async_copy(
+            staged.at[pl.ds(at * ROWS, ROWS), :],
+            buffer.at[pl.ds(pl.multiple_of(target * ROWS, ROWS), ROWS), :],
+            sems.at[at],
+        )
+        for at, target in enumerate((target0, target1))
+    ]
+    copies[0].start()
+    pl.when(jnp.logical_not(same))(copies[1].start)
+    copies[0].wait()
+    pl.when(jnp.logical_not(same))(copies[1].wait)
 
 
 def pairs(count, first):
@@ -586,7 +580,7 @@
     field, edge_a, edge_b, strips, buffer, sent, table, again = pl.pallas_call(
         functools.partial(start_kernel, lon_cells),
         out_shape=[moving[0], moving[2], moving[3], moving[4], f32(peers * ROWS, LANES), moving[1], f32(24, LANES)]
-        + [jax.ShapeDtypeStruct((2 * LANES + 8,), jnp.int32)],
+        + [jax.ShapeDtypeStruct((2 * LANES + 16,), jnp.int32)],
         in_specs=[hbm, smem, smem, smem, vmem, vmem, smem],
         out_specs=[vmem] * 4 + [hbm] + [vmem] * 2 + [smem],
         scratch_shapes=[
@@ -609,7 +603,7 @@
     for number in range(2 * STEPS):
         second = number % 2 == 1
         final = number == 2 * STEPS - 1
-        over = lax.ppermute(sent, "panel", SWAP)
+        over = lax.ppermute(sent, ("panel", "core"), CROSS)
         operands = [field] + ([origin] if second else []) + [geo]
         part, part_strips = pl.pallas_call(
             functools.partial(inner_kernel, second, lon_cells, consts),
@@ -620,20 +614,20 @@
             compiler_params=params,
             cost_estimate=pl.CostEstimate(flops=20_000_000, bytes_accessed=1 << 23, transcendentals=0),
         )(*operands)
-        over, part, part_strips = lax.optimization_barrier((over, part, part_strips))
-        mate = lax.ppermute(over, "core", SWAP)
+        lon_a = lax.ppermute(edge_a, lon_axes, pairs(lon_blocks, 0))
+        over, part, part_strips, lon_a = lax.optimization_barrier((over, part, part_strips, lon_a))
         buffer = pl.pallas_call(
             pack_kernel,
             out_shape=f32(peers * ROWS, LANES),
-            in_specs=[vmem, vmem, smem, hbm],
+            in_specs=[vmem, hbm],
             out_specs=hbm,
-            scratch_shapes=[pltpu.VMEM((4 * ROWS, LANES), jnp.float32), pltpu.SemaphoreType.DMA((4,))],
-            input_output_aliases={3: 0},
+            scratch_shapes=[pltpu.VMEM((2 * ROWS, LANES), jnp.float32), pltpu.SemaphoreType.DMA((2,))],
+            input_output_aliases={1: 0},
             compiler_params=params,
-        )(over, mate, flag, buffer)
+        )(over, buffer)
         buffer, own_a, own_b, own_strips, part = lax.optimization_barrier((buffer, edge_a, edge_b, strips, part))
         received = lax.all_to_all(
-            buffer.reshape(peers // 2, 2 * ROWS, LANES), ("colat", "lon_hi"), split_axis=0, concat_axis=0, tiled=True
+            buffer.reshape(peers, ROWS, LANES), ("colat", "lon_hi", "core"), split_axis=0, concat_axis=0, tiled=True
         ).reshape(peers * ROWS, LANES)
         if not final:
             corners = pl.pallas_call(
@@ -644,7 +638,6 @@
                 compiler_params=params,
                 cost_estimate=pl.CostEstimate(flops=8_000_000, bytes_accessed=1 << 22, transcendentals=0),
             )(part, src)
-        lon_a = lax.ppermute(own_a, lon_axes, pairs(lon_blocks, 0))
         lon_b = lax.ppermute(own_b, lon_axes, pairs(lon_blocks, 1))
         strip_a = lax.ppermute(own_strips, "colat", pairs(lat_blocks, 0))
         strip_b = lax.ppermute(own_strips, "colat", pairs(lat_blocks, 1))

time: 125 us -> 115 us (0.920)
  Pallas kernels: 41.7 us -> 32.9 us
  waiting for transfers between devices: 5.87 us -> 10.6 us
  starting transfers between devices: 73 us -> 68.3 us
    ppermute x12 -> x8, starting transfers between devices: 22.5 us -> 11.3 us  [the longest x4 9.68 us: on_device(): over = lax.ppermute(sent, ('panel', 'core'), CROSS)]
    all_to_all x4, waiting for transfers between devices: 0.17 us -> 8.46 us  [on_device(): lax.all_to_all(buffer.reshape(peers, ROWS, LANES), ('colat', 'lon_hi', 'c...]
    ppermute x4, starting transfers between devices: 11.9 us -> 15.6 us  [on_device(): lon_b = lax.ppermute(own_b, lon_axes, pairs(lon_blocks, 1))]
    pallas_call x4, Pallas kernels: 12.3 us -> 8.66 us  [on_device(): pl.pallas_call(functools.partial(outer_kernel, second, final, lon_cells,...]
    ppermute x12 -> x8, waiting for transfers between devices: 3.32 us -> 0.42 us  [the longest x4 0.41 us: on_device(): over = lax.ppermute(sent, ('panel', 'core'), CROSS)]
    pallas_call x4, Pallas kernels: 5.22 us -> 2.98 us  [on_device(): pl.pallas_call(pack_kernel, out_shape=f32(peers * ROWS, LANES), in_specs=...]
    pallas_call x3, Pallas kernels: 8.12 us -> 5.99 us  [on_device(): pl.pallas_call(rows_kernel, out_shape=f32(8 * ROWS, LANES), in_specs=[vme...]
    all_to_all x4, starting transfers between devices: 21.1 us -> 22.5 us  [on_device(): lax.all_to_all(buffer.reshape(peers, ROWS, LANES), ('colat', 'lon_hi', 'c...]
  transfers between devices with their start and end apart: 28 -> 24, of which waited for: 6 -> 7; matrix products, arithmetic and copies ran while one was open for 1% -> 1% of each run, Pallas kernels for 15% -> 15%
where the time goes in v4:
time: 115 us
  starting transfers between devices  68.3 us (59%)
  Pallas kernels  32.9 us (29%)
  waiting for transfers between devices  10.6 us (9%)
  local copies, waits for them, and re-layouts  2.19 us (2%)
    all_to_all x4, starting transfers between devices, on_device(): lax.all_to_all(buffer.reshape(peers, ROWS, LANES), ('colat', 'lon_hi', 'c...  22.5 us
    ppermute x4, starting transfers between devices, on_device(): strip_a = lax.ppermute(own_strips, 'colat', pairs(lat_blocks, 0))  16.3 us
    ppermute x4, starting transfers between devices, on_device(): lon_b = lax.ppermute(own_b, lon_axes, pairs(lon_blocks, 1))  15.6 us
    pallas_call x4, Pallas kernels, on_device(): pl.pallas_call(functools.partial(inner_kernel, second, lon_cells, consts)...  10.3 us
    ppermute x4, starting transfers between devices, on_device(): over = lax.ppermute(sent, ('panel', 'core'), CROSS)  9.68 us
    pallas_call x4, Pallas kernels, on_device(): pl.pallas_call(functools.partial(outer_kernel, second, final, lon_cells,...  8.66 us
    all_to_all x4, waiting for transfers between devices, on_device(): lax.all_to_all(buffer.reshape(peers, ROWS, LANES), ('colat', 'lon_hi', 'c...  8.46 us
    pallas_call x3, Pallas kernels, on_device(): pl.pallas_call(rows_kernel, out_shape=f32(8 * ROWS, LANES), in_specs=[vme...  5.99 us
  transfers between devices with their start and end apart: 24, of which 7 were waited for; matrix products, arithmetic and copies ran while one was open for 1% of the time, Pallas kernels for 15%

profile of v4, /device:TPU:1, one launch (start us, length us, event | category | flops | bytes accessed | tf_op | source)
XLA Modules:
  0.0 114.8 jit_solution(2462306085857059794)
XLA Ops:
  1.9 4.6 %shard_map.73 = (f32[1536,128]{1,0:T(8,128)S(1)}, f32[32,128]{1,0:T(8,128)S(1)}, f32[32,128]{1,0:T(8,128)S(1)}, f32[48,128]{1,0:T(8,128)S(1)}, f32[1024,128]{1,0...) custom-call(f32[16,96,128]{2,1,0:T(8,128)S(1)} %bitcast.26, s32[256]{0:T(256)S(1)} %bitcast.27, ...), custom_call_target="tpu_custom_call" | custom-call | tf_op jit(solution)/shard_map/pallas_call | solution.py:580
  8.0 2.8 %collective-permute-start = (f32[40,128]{1,0:T(8,128)S(1)}, f32[40,128]{1,0:T(8,128)S(1)}, u32[]{:S(2)}, u32[]{:S(2)}) collective-permute-start(f32[40,128]{1,0:T(8,128)S(1)} %get-tuple-element.74), channel_id=1, source_target_pairs={{0,65},{65,0},{1,64},{64,1},{2,67},{67,2},{3,66},{66,3},{4,69},{69... | collective-permute-start | bytes 61448 | tf_op jit(solution)/shard_map/ppermute | solution.py:606
  11.3 2.6 %shard_map.74 = (f32[1536,128]{1,0:T(8,128)S(1)}, f32[48,128]{1,0:T(8,128)S(1)}) custom-call(f32[1536,128]{1,0:T(8,128)S(1)} %get-tuple-element.75.refs_0_.refs_1_, f32[232,128]{1,0:T(8,128)S(1)} %constant_dynamic-update-slice_fusion.refs_1_.refs_13_.refs_2_), custom_call_target="tpu_custom_call" | custom-call | flops 20000000 | bytes 8388608 | tf_op jit(solution)/shard_map/pallas_call | solution.py:608
  14.7 9.0 %all-to-all-start = ((f32[64,16,128]{2,1,0:T(8,128)}), f32[64,16,128]{2,1,0:T(8,128)S(1)}, u32[]{:S(2)}, u32[]{:S(2)}) async-start(f32[64,16,128]{2,1,0:T(8,128)} %bitcast.10), calls=%async_computation | async-start | bytes 1048576 | tf_op jit(solution)/shard_map/all_to_all | solution.py:629
  24.5 4.0 %collective-permute-start.3 = (f32[48,128]{1,0:T(8,128)S(1)}, f32[48,128]{1,0:T(8,128)S(1)}, u32[]{:S(2)}, u32[]{:S(2)}) collective-permute-start(f32[48,128]{1,0:T(8,128)S(1)} %get-tuple-element.88.refs_4_), channel_id=1, source_target_pairs={{0,16},{16,0},{32,48},{48,32},{1,17},{17,1},{33,49},{49,33},{2,18}... | collective-permute-start | bytes 73736 | tf_op jit(solution)/shard_map/ppermute | solution.py:642
  28.5 3.9 %collective-permute-start.2 = (f32[32,128]{1,0:T(8,128)S(1)}, f32[32,128]{1,0:T(8,128)S(1)}, u32[]{:S(2)}, u32[]{:S(2)}) collective-permute-start(f32[32,128]{1,0:T(8,128)S(1)} %get-tuple-element.87.refs_3_), channel_id=1, source_target_pairs={{1,2},{2,1},{3,4},{4,3},{5,6},{6,5},{7,8},{8,7},{9,10},{10,9},{11,... | collective-permute-start | bytes 49160 | tf_op jit(solution)/shard_map/ppermute | solution.py:641
  32.9 2.0 %shard_map.77.refs_14_ = f32[128,128]{1,0:T(8,128)S(1)} custom-call(f32[1536,128]{1,0:T(8,128)S(1)} %get-tuple-element.84.field.refs_0_, s32[256]{0:T(256)S(1)} %bitcast.28), custom_call_target="tpu_custom_call" | custom-call | flops 8000000 | bytes 4194304 | tf_op jit(solution)/shard_map/pallas_call | solution.py:633
  36.5 1.9 %shard_map.78 = (f32[1536,128]{1,0:T(8,128)S(1)}, f32[40,128]{1,0:T(8,128)S(1)}, f32[32,128]{1,0:T(8,128)S(1)}, f32[32,128]{1,0:T(8,128)S(1)}, f32[48,128]{1,0:T(8,128)S(1)}) custom-call(f32[1536,128]{1,0:T(8,128)S(1)} %get-tuple-element.84.field.refs_0_, f32[48,128]{1,0:T(8,128)S(1)} %get-tuple-element.85.refs_1_, f32[32,128]{1,0:T(8,128)S(1)} %get-tuple-element.86.refs_2_, ...), custom_call_target="tpu_custom_call" | custom-call | tf_op jit(solution)/shard_map/pallas_call | solution.py:649
  38.4 2.5 %collective-permute-start.5 = (f32[40,128]{1,0:T(8,128)S(1)}, f32[40,128]{1,0:T(8,128)S(1)}, u32[]{:S(2)}, u32[]{:S(2)}) collective-permute-start(f32[40,128]{1,0:T(8,128)S(1)} %get-tuple-element.95), channel_id=1, source_target_pairs={{0,65},{65,0},{1,64},{64,1},{2,67},{67,2},{3,66},{66,3},{4,69},{69... | collective-permute-start | bytes 61448 | tf_op jit(solution)/shard_map/ppermute | solution.py:606
  40.9 2.6 %shard_map.79 = (f32[1536,128]{1,0:T(8,128)S(1)}, f32[48,128]{1,0:T(8,128)S(1)}) custom-call(f32[1536,128]{1,0:T(8,128)S(1)} %get-tuple-element.96.refs_0_, f32[1536,128]{1,0:T(8,128)S(1)} %get-tuple-element.75.refs_0_.refs_1_, f32[232,128]{1,0:T(8,128)S(1)} %constant_dynamic-update-slice_fusion.refs_1_.refs_13_.refs_2_), custom_call_target="tpu_custom_call" | custom-call | flops 20000000 | bytes 8388608 | tf_op jit(solution)/shard_map/pallas_call | solution.py:608
  44.3 4.6 %all-to-all-start.1 = ((f32[64,16,128]{2,1,0:T(8,128)}), f32[64,16,128]{2,1,0:T(8,128)S(1)}, u32[]{:S(2)}, u32[]{:S(2)}) async-start(f32[64,16,128]{2,1,0:T(8,128)} %bitcast.13), calls=%async_computation.1 | async-start | bytes 1048576 | tf_op jit(solution)/shard_map/all_to_all | solution.py:629
  49.5 4.1 %collective-permute-start.8 = (f32[48,128]{1,0:T(8,128)S(1)}, f32[48,128]{1,0:T(8,128)S(1)}, u32[]{:S(2)}, u32[]{:S(2)}) collective-permute-start(f32[48,128]{1,0:T(8,128)S(1)} %get-tuple-element.108.refs_4_), channel_id=1, source_target_pairs={{0,16},{16,0},{32,48},{48,32},{1,17},{17,1},{33,49},{49,33},{2,18}... | collective-permute-start | bytes 73736 | tf_op jit(solution)/shard_map/ppermute | solution.py:642
  53.6 3.9 %collective-permute-start.7 = (f32[32,128]{1,0:T(8,128)S(1)}, f32[32,128]{1,0:T(8,128)S(1)}, u32[]{:S(2)}, u32[]{:S(2)}) collective-permute-start(f32[32,128]{1,0:T(8,128)S(1)} %get-tuple-element.107.refs_3_), channel_id=1, source_target_pairs={{1,2},{2,1},{3,4},{4,3},{5,6},{6,5},{7,8},{8,7},{9,10},{10,9},{11,... | collective-permute-start | bytes 49160 | tf_op jit(solution)/shard_map/ppermute | solution.py:641
  57.5 2.0 %shard_map.81.refs_14_ = f32[128,128]{1,0:T(8,128)S(1)} custom-call(f32[1536,128]{1,0:T(8,128)S(1)} %get-tuple-element.104.field.refs_0_, s32[256]{0:T(256)S(1)} %bitcast.30), custom_call_target="tpu_custom_call" | custom-call | flops 8000000 | bytes 4194304 | tf_op jit(solution)/shard_map/pallas_call | solution.py:633
  59.6 2.2 %all-to-all-done.1 = f32[64,16,128]{2,1,0:T(8,128)S(1)} async-done(((f32[64,16,128]{2,1,0:T(8,128)}), f32[64,16,128]{2,1,0:T(8,128)S(1)}, u32[]{:S(2)}, u32[]{:S(2)}) %all-to-all-start.1) | async-done | bytes 524320 | tf_op jit(solution)/shard_map/all_to_all | solution.py:629
  61.8 1.9 %shard_map.82 = (f32[1536,128]{1,0:T(8,128)S(1)}, f32[40,128]{1,0:T(8,128)S(1)}, f32[32,128]{1,0:T(8,128)S(1)}, f32[32,128]{1,0:T(8,128)S(1)}, f32[48,128]{1,0:T(8,128)S(1)}) custom-call(f32[1536,128]{1,0:T(8,128)S(1)} %get-tuple-element.104.field.refs_0_, f32[48,128]{1,0:T(8,128)S(1)} %get-tuple-element.105.refs_1_, ...), custom_call_target="tpu_custom_call" | custom-call | tf_op jit(solution)/shard_map/pallas_call | solution.py:649
  63.7 2.2 %collective-permute-start.10 = (f32[40,128]{1,0:T(8,128)S(1)}, f32[40,128]{1,0:T(8,128)S(1)}, u32[]{:S(2)}, u32[]{:S(2)}) collective-permute-start(f32[40,128]{1,0:T(8,128)S(1)} %get-tuple-element.111), channel_id=1, source_target_pairs={{0,65},{65,0},{1,64},{64,1},{2,67},{67,2},{3,66},{66,3},{4,69},{69... | collective-permute-start | bytes 61448 | tf_op jit(solution)/shard_map/ppermute | solution.py:606
  66.0 2.6 %shard_map.83 = (f32[1536,128]{1,0:T(8,128)S(1)}, f32[48,128]{1,0:T(8,128)S(1)}) custom-call(f32[1536,128]{1,0:T(8,128)S(1)} %get-tuple-element.112.refs_0_.refs_1_, f32[232,128]{1,0:T(8,128)S(1)} %constant_dynamic-update-slice_fusion.refs_1_.refs_13_.refs_2_), custom_call_target="tpu_custom_call" | custom-call | flops 20000000 | bytes 8388608 | tf_op jit(solution)/shard_map/pallas_call | solution.py:608
  69.5 4.5 %all-to-all-start.2 = ((f32[64,16,128]{2,1,0:T(8,128)}), f32[64,16,128]{2,1,0:T(8,128)S(1)}, u32[]{:S(2)}, u32[]{:S(2)}) async-start(f32[64,16,128]{2,1,0:T(8,128)} %bitcast.15), calls=%async_computation.2 | async-start | bytes 1048576 | tf_op jit(solution)/shard_map/all_to_all | solution.py:629
  74.6 4.1 %collective-permute-start.13 = (f32[48,128]{1,0:T(8,128)S(1)}, f32[48,128]{1,0:T(8,128)S(1)}, u32[]{:S(2)}, u32[]{:S(2)}) collective-permute-start(f32[48,128]{1,0:T(8,128)S(1)} %get-tuple-element.124.refs_4_), channel_id=1, source_target_pairs={{0,16},{16,0},{32,48},{48,32},{1,17},{17,1},{33,49},{49,33},{2,18}... | collective-permute-start | bytes 73736 | tf_op jit(solution)/shard_map/ppermute | solution.py:642
  78.7 3.9 %collective-permute-start.12 = (f32[32,128]{1,0:T(8,128)S(1)}, f32[32,128]{1,0:T(8,128)S(1)}, u32[]{:S(2)}, u32[]{:S(2)}) collective-permute-start(f32[32,128]{1,0:T(8,128)S(1)} %get-tuple-element.123.refs_3_), channel_id=1, source_target_pairs={{1,2},{2,1},{3,4},{4,3},{5,6},{6,5},{7,8},{8,7},{9,10},{10,9},{11,... | collective-permute-start | bytes 49160 | tf_op jit(solution)/shard_map/ppermute | solution.py:641
  82.7 2.0 %shard_map.85.refs_14_ = f32[128,128]{1,0:T(8,128)S(1)} custom-call(f32[1536,128]{1,0:T(8,128)S(1)} %get-tuple-element.120.field.refs_0_, s32[256]{0:T(256)S(1)} %bitcast.32), custom_call_target="tpu_custom_call" | custom-call | flops 8000000 | bytes 4194304 | tf_op jit(solution)/shard_map/pallas_call | solution.py:633
  84.7 2.2 %all-to-all-done.2 = f32[64,16,128]{2,1,0:T(8,128)S(1)} async-done(((f32[64,16,128]{2,1,0:T(8,128)}), f32[64,16,128]{2,1,0:T(8,128)S(1)}, u32[]{:S(2)}, u32[]{:S(2)}) %all-to-all-start.2) | async-done | bytes 524320 | tf_op jit(solution)/shard_map/all_to_all | solution.py:629
  86.9 1.9 %shard_map.86 = (f32[1536,128]{1,0:T(8,128)S(1)}, f32[40,128]{1,0:T(8,128)S(1)}, f32[32,128]{1,0:T(8,128)S(1)}, f32[32,128]{1,0:T(8,128)S(1)}, f32[48,128]{1,0:T(8,128)S(1)}) custom-call(f32[1536,128]{1,0:T(8,128)S(1)} %get-tuple-element.120.field.refs_0_, f32[48,128]{1,0:T(8,128)S(1)} %get-tuple-element.121.refs_1_, ...), custom_call_target="tpu_custom_call" | custom-call | tf_op jit(solution)/shard_map/pallas_call | solution.py:649
  88.8 2.2 %collective-permute-start.15 = (f32[40,128]{1,0:T(8,128)S(1)}, f32[40,128]{1,0:T(8,128)S(1)}, u32[]{:S(2)}, u32[]{:S(2)}) collective-permute-start(f32[40,128]{1,0:T(8,128)S(1)} %get-tuple-element.127), channel_id=1, source_target_pairs={{0,65},{65,0},{1,64},{64,1},{2,67},{67,2},{3,66},{66,3},{4,69},{69... | collective-permute-start | bytes 61448 | tf_op jit(solution)/shard_map/ppermute | solution.py:606
  91.0 2.6 %shard_map.87 = (f32[1536,128]{1,0:T(8,128)S(1)}, f32[48,128]{1,0:T(8,128)S(1)}) custom-call(f32[1536,128]{1,0:T(8,128)S(1)} %get-tuple-element.128.refs_0_, f32[1536,128]{1,0:T(8,128)S(1)} %get-tuple-element.112.refs_0_.refs_1_, f32[232,128]{1,0:T(8,128)S(1)} %constant_dynamic-update-slice_fusion.refs_1_.refs_13_.refs_2_), custom_call_target="tpu_custom_call" | custom-call | flops 20000000 | bytes 8388608 | tf_op jit(solution)/shard_map/pallas_call | solution.py:608
  94.6 4.5 %all-to-all-start.3 = ((f32[64,16,128]{2,1,0:T(8,128)}), f32[64,16,128]{2,1,0:T(8,128)S(1)}, u32[]{:S(2)}, u32[]{:S(2)}) async-start(f32[64,16,128]{2,1,0:T(8,128)} %bitcast.17), calls=%async_computation.3 | async-start | bytes 1048576 | tf_op jit(solution)/shard_map/all_to_all | solution.py:629
  99.8 4.1 %collective-permute-start.18 = (f32[48,128]{1,0:T(8,128)S(1)}, f32[48,128]{1,0:T(8,128)S(1)}, u32[]{:S(2)}, u32[]{:S(2)}) collective-permute-start(f32[48,128]{1,0:T(8,128)S(1)} %get-tuple-element.140.refs_4_), channel_id=1, source_target_pairs={{0,16},{16,0},{32,48},{48,32},{1,17},{17,1},{33,49},{49,33},{2,18}... | collective-permute-start | bytes 73736 | tf_op jit(solution)/shard_map/ppermute | solution.py:642
  103.9 3.9 %collective-permute-start.17 = (f32[32,128]{1,0:T(8,128)S(1)}, f32[32,128]{1,0:T(8,128)S(1)}, u32[]{:S(2)}, u32[]{:S(2)}) collective-permute-start(f32[32,128]{1,0:T(8,128)S(1)} %get-tuple-element.139.refs_3_), channel_id=1, source_target_pairs={{1,2},{2,1},{3,4},{4,3},{5,6},{6,5},{7,8},{8,7},{9,10},{10,9},{11,... | collective-permute-start | bytes 49160 | tf_op jit(solution)/shard_map/ppermute | solution.py:641
  107.8 1.7 %collective-permute-done.17.refs_6_ = f32[32,128]{1,0:T(8,128)S(1)} collective-permute-done((f32[32,128]{1,0:T(8,128)S(1)}, f32[32,128]{1,0:T(8,128)S(1)}, u32[]{:S(2)}, u32[]{:S(2)}) %collective-permute-start.17) | collective-permute-done | bytes 16416 | tf_op jit(solution)/shard_map/ppermute | solution.py:641
  109.5 2.5 %all-to-all-done.3 = f32[64,16,128]{2,1,0:T(8,128)S(1)} async-done(((f32[64,16,128]{2,1,0:T(8,128)}), f32[64,16,128]{2,1,0:T(8,128)S(1)}, u32[]{:S(2)}, u32[]{:S(2)}) %all-to-all-start.3) | async-done | bytes 524320 | tf_op jit(solution)/shard_map/all_to_all | solution.py:629
  112.0 2.8 %shard_map.89 = f32[1536,128]{1,0:T(8,128)} custom-call(f32[1536,128]{1,0:T(8,128)S(1)} %get-tuple-element.136.refs_0_, f32[48,128]{1,0:T(8,128)S(1)} %get-tuple-element.137.refs_1_, f32[32,128]{1,0:T(8,128)S(1)} %get-tuple-element.138.refs_2_, f32[32,128]{1,0:T(8,128)S(1)} %get-tuple-element.139.refs_3_, f32[48,128]{1,0:T(8,128)S(1)} %get-tuple-element.140.refs_4_, ...), custom_call_target="tpu_custom_call" | custom-call | tf_op jit(solution)/shard_map/pallas_call | solution.py:649
  (65 shorter events, 12.2 us)
Async XLA Ops:
  0.1 0.7 copy-start.2
  0.1 0.7 copy-start.3
  0.1 0.7 copy-start.5
  0.1 0.7 copy-start.1
  0.1 0.7 copy-start.4
  0.8 1.1 copy-start
  6.5 7.4 %collective-permute-start.1 = (f32[32,128]{1,0:T(8,128)S(1)}, f32[32,128]{1,0:T(8,128)S(1)}, u32[]{:S(2)}, u32[]{:S(2)}) collective-permute-start(f32[32,128]{1,0:T(8,128)S(1)} %get-tuple-element.86.refs_2_), channel_id=1, source_target_pairs={{0,1},{1,0},{2,3},{3,2},{4,5},{5,4},{6,7},{7,6},{8,9},{9,8},{10,11... | collective-permute-start | bytes 49160 | tf_op jit(solution)/shard_map/ppermute | solution.py:617
  8.0 5.9 %collective-permute-start = (f32[40,128]{1,0:T(8,128)S(1)}, f32[40,128]{1,0:T(8,128)S(1)}, u32[]{:S(2)}, u32[]{:S(2)}) collective-permute-start(f32[40,128]{1,0:T(8,128)S(1)} %get-tuple-element.74), channel_id=1, source_target_pairs={{0,65},{65,0},{1,64},{64,1},{2,67},{67,2},{3,66},{66,3},{4,69},{69... | collective-permute-start | bytes 61448 | tf_op jit(solution)/shard_map/ppermute | solution.py:606
  14.7 9.0 %copy-start.6 = (s32[1,1,1,896]{3,2,1,0:T(1,128)S(1)}, s32[1,1,1,896]{3,2,1,0:T(1,128)}, u32[]{:S(2)}) copy-start(s32[1,1,1,896]{3,2,1,0:T(1,128)} %param.13) | copy-start | bytes 10756
  14.7 21.8 %all-to-all-start = ((f32[64,16,128]{2,1,0:T(8,128)}), f32[64,16,128]{2,1,0:T(8,128)S(1)}, u32[]{:S(2)}, u32[]{:S(2)}) async-start(f32[64,16,128]{2,1,0:T(8,128)} %bitcast.10), calls=%async_computation | async-start | bytes 1048576 | tf_op jit(solution)/shard_map/all_to_all | solution.py:629
  23.9 11.0 %collective-permute-start.4 = (f32[48,128]{1,0:T(8,128)S(1)}, f32[48,128]{1,0:T(8,128)S(1)}, u32[]{:S(2)}, u32[]{:S(2)}) collective-permute-start(f32[48,128]{1,0:T(8,128)S(1)} %get-tuple-element.88.refs_4_), channel_id=1, source_target_pairs={{16,32},{32,16},{17,33},{33,17},{18,34},{34,18},{19,35},{35,19},{2... | collective-permute-start | bytes 73736 | tf_op jit(solution)/shard_map/ppermute | solution.py:643
  24.5 10.4 %collective-permute-start.3 = (f32[48,128]{1,0:T(8,128)S(1)}, f32[48,128]{1,0:T(8,128)S(1)}, u32[]{:S(2)}, u32[]{:S(2)}) collective-permute-start(f32[48,128]{1,0:T(8,128)S(1)} %get-tuple-element.88.refs_4_), channel_id=1, source_target_pairs={{0,16},{16,0},{32,48},{48,32},{1,17},{17,1},{33,49},{49,33},{2,18}... | collective-permute-start | bytes 73736 | tf_op jit(solution)/shard_map/ppermute | solution.py:642
  28.5 6.4 %collective-permute-start.2 = (f32[32,128]{1,0:T(8,128)S(1)}, f32[32,128]{1,0:T(8,128)S(1)}, u32[]{:S(2)}, u32[]{:S(2)}) collective-permute-start(f32[32,128]{1,0:T(8,128)S(1)} %get-tuple-element.87.refs_3_), channel_id=1, source_target_pairs={{1,2},{2,1},{3,4},{4,3},{5,6},{6,5},{7,8},{8,7},{9,10},{10,9},{11,... | collective-permute-start | bytes 49160 | tf_op jit(solution)/shard_map/ppermute | solution.py:641
  38.4 5.1 %collective-permute-start.5 = (f32[40,128]{1,0:T(8,128)S(1)}, f32[40,128]{1,0:T(8,128)S(1)}, u32[]{:S(2)}, u32[]{:S(2)}) collective-permute-start(f32[40,128]{1,0:T(8,128)S(1)} %get-tuple-element.95), channel_id=1, source_target_pairs={{0,65},{65,0},{1,64},{64,1},{2,67},{67,2},{3,66},{66,3},{4,69},{69... | collective-permute-start | bytes 61448 | tf_op jit(solution)/shard_map/ppermute | solution.py:606
  40.9 2.6 %collective-permute-start.6 = (f32[32,128]{1,0:T(8,128)S(1)}, f32[32,128]{1,0:T(8,128)S(1)}, u32[]{:S(2)}, u32[]{:S(2)}) collective-permute-start(f32[32,128]{1,0:T(8,128)S(1)} %get-tuple-element.106.refs_2_), channel_id=1, source_target_pairs={{0,1},{1,0},{2,3},{3,2},{4,5},{5,4},{6,7},{7,6},{8,9},{9,8},{10,11... | collective-permute-start | bytes 49160 | tf_op jit(solution)/shard_map/ppermute | solution.py:617
  44.3 17.5 %all-to-all-start.1 = ((f32[64,16,128]{2,1,0:T(8,128)}), f32[64,16,128]{2,1,0:T(8,128)S(1)}, u32[]{:S(2)}, u32[]{:S(2)}) async-start(f32[64,16,128]{2,1,0:T(8,128)} %bitcast.13), calls=%async_computation.1 | async-start | bytes 1048576 | tf_op jit(solution)/shard_map/all_to_all | solution.py:629
  48.9 10.7 %collective-permute-start.9 = (f32[48,128]{1,0:T(8,128)S(1)}, f32[48,128]{1,0:T(8,128)S(1)}, u32[]{:S(2)}, u32[]{:S(2)}) collective-permute-start(f32[48,128]{1,0:T(8,128)S(1)} %get-tuple-element.108.refs_4_), channel_id=1, source_target_pairs={{16,32},{32,16},{17,33},{33,17},{18,34},{34,18},{19,35},{35,19},{2... | collective-permute-start | bytes 73736 | tf_op jit(solution)/shard_map/ppermute | solution.py:643
  49.5 10.0 %collective-permute-start.8 = (f32[48,128]{1,0:T(8,128)S(1)}, f32[48,128]{1,0:T(8,128)S(1)}, u32[]{:S(2)}, u32[]{:S(2)}) collective-permute-start(f32[48,128]{1,0:T(8,128)S(1)} %get-tuple-element.108.refs_4_), channel_id=1, source_target_pairs={{0,16},{16,0},{32,48},{48,32},{1,17},{17,1},{33,49},{49,33},{2,18}... | collective-permute-start | bytes 73736 | tf_op jit(solution)/shard_map/ppermute | solution.py:642
  53.6 5.9 %collective-permute-start.7 = (f32[32,128]{1,0:T(8,128)S(1)}, f32[32,128]{1,0:T(8,128)S(1)}, u32[]{:S(2)}, u32[]{:S(2)}) collective-permute-start(f32[32,128]{1,0:T(8,128)S(1)} %get-tuple-element.107.refs_3_), channel_id=1, source_target_pairs={{1,2},{2,1},{3,4},{4,3},{5,6},{6,5},{7,8},{8,7},{9,10},{10,9},{11,... | collective-permute-start | bytes 49160 | tf_op jit(solution)/shard_map/ppermute | solution.py:641
  63.7 5.0 %collective-permute-start.10 = (f32[40,128]{1,0:T(8,128)S(1)}, f32[40,128]{1,0:T(8,128)S(1)}, u32[]{:S(2)}, u32[]{:S(2)}) collective-permute-start(f32[40,128]{1,0:T(8,128)S(1)} %get-tuple-element.111), channel_id=1, source_target_pairs={{0,65},{65,0},{1,64},{64,1},{2,67},{67,2},{3,66},{66,3},{4,69},{69... | collective-permute-start | bytes 61448 | tf_op jit(solution)/shard_map/ppermute | solution.py:606
  66.0 2.6 %collective-permute-start.11 = (f32[32,128]{1,0:T(8,128)S(1)}, f32[32,128]{1,0:T(8,128)S(1)}, u32[]{:S(2)}, u32[]{:S(2)}) collective-permute-start(f32[32,128]{1,0:T(8,128)S(1)} %get-tuple-element.122.refs_2_), channel_id=1, source_target_pairs={{0,1},{1,0},{2,3},{3,2},{4,5},{5,4},{6,7},{7,6},{8,9},{9,8},{10,11... | collective-permute-start | bytes 49160 | tf_op jit(solution)/shard_map/ppermute | solution.py:617
  69.5 17.4 %all-to-all-start.2 = ((f32[64,16,128]{2,1,0:T(8,128)}), f32[64,16,128]{2,1,0:T(8,128)S(1)}, u32[]{:S(2)}, u32[]{:S(2)}) async-start(f32[64,16,128]{2,1,0:T(8,128)} %bitcast.15), calls=%async_computation.2 | async-start | bytes 1048576 | tf_op jit(solution)/shard_map/all_to_all | solution.py:629
  74.0 10.7 %collective-permute-start.14 = (f32[48,128]{1,0:T(8,128)S(1)}, f32[48,128]{1,0:T(8,128)S(1)}, u32[]{:S(2)}, u32[]{:S(2)}) collective-permute-start(f32[48,128]{1,0:T(8,128)S(1)} %get-tuple-element.124.refs_4_), channel_id=1, source_target_pairs={{16,32},{32,16},{17,33},{33,17},{18,34},{34,18},{19,35},{35,19},{2... | collective-permute-start | bytes 73736 | tf_op jit(solution)/shard_map/ppermute | solution.py:643
  74.6 10.0 %collective-permute-start.13 = (f32[48,128]{1,0:T(8,128)S(1)}, f32[48,128]{1,0:T(8,128)S(1)}, u32[]{:S(2)}, u32[]{:S(2)}) collective-permute-start(f32[48,128]{1,0:T(8,128)S(1)} %get-tuple-element.124.refs_4_), channel_id=1, source_target_pairs={{0,16},{16,0},{32,48},{48,32},{1,17},{17,1},{33,49},{49,33},{2,18}... | collective-permute-start | bytes 73736 | tf_op jit(solution)/shard_map/ppermute | solution.py:642
  78.7 5.9 %collective-permute-start.12 = (f32[32,128]{1,0:T(8,128)S(1)}, f32[32,128]{1,0:T(8,128)S(1)}, u32[]{:S(2)}, u32[]{:S(2)}) collective-permute-start(f32[32,128]{1,0:T(8,128)S(1)} %get-tuple-element.123.refs_3_), channel_id=1, source_target_pairs={{1,2},{2,1},{3,4},{4,3},{5,6},{6,5},{7,8},{8,7},{9,10},{10,9},{11,... | collective-permute-start | bytes 49160 | tf_op jit(solution)/shard_map/ppermute | solution.py:641
  88.8 5.0 %collective-permute-start.15 = (f32[40,128]{1,0:T(8,128)S(1)}, f32[40,128]{1,0:T(8,128)S(1)}, u32[]{:S(2)}, u32[]{:S(2)}) collective-permute-start(f32[40,128]{1,0:T(8,128)S(1)} %get-tuple-element.127), channel_id=1, source_target_pairs={{0,65},{65,0},{1,64},{64,1},{2,67},{67,2},{3,66},{66,3},{4,69},{69... | collective-permute-start | bytes 61448 | tf_op jit(solution)/shard_map/ppermute | solution.py:606
  91.0 2.6 %collective-permute-start.16 = (f32[32,128]{1,0:T(8,128)S(1)}, f32[32,128]{1,0:T(8,128)S(1)}, u32[]{:S(2)}, u32[]{:S(2)}) collective-permute-start(f32[32,128]{1,0:T(8,128)S(1)} %get-tuple-element.138.refs_2_), channel_id=1, source_target_pairs={{0,1},{1,0},{2,3},{3,2},{4,5},{5,4},{6,7},{7,6},{8,9},{9,8},{10,11... | collective-permute-start | bytes 49160 | tf_op jit(solution)/shard_map/ppermute | solution.py:617
  94.6 17.4 %all-to-all-start.3 = ((f32[64,16,128]{2,1,0:T(8,128)}), f32[64,16,128]{2,1,0:T(8,128)S(1)}, u32[]{:S(2)}, u32[]{:S(2)}) async-start(f32[64,16,128]{2,1,0:T(8,128)} %bitcast.17), calls=%async_computation.3 | async-start | bytes 1048576 | tf_op jit(solution)/shard_map/all_to_all | solution.py:629
  99.1 10.4 %collective-permute-start.19 = (f32[48,128]{1,0:T(8,128)S(1)}, f32[48,128]{1,0:T(8,128)S(1)}, u32[]{:S(2)}, u32[]{:S(2)}) collective-permute-start(f32[48,128]{1,0:T(8,128)S(1)} %get-tuple-element.140.refs_4_), channel_id=1, source_target_pairs={{16,32},{32,16},{17,33},{33,17},{18,34},{34,18},{19,35},{35,19},{2... | collective-permute-start | bytes 73736 | tf_op jit(solution)/shard_map/ppermute | solution.py:643
  99.8 9.7 %collective-permute-start.18 = (f32[48,128]{1,0:T(8,128)S(1)}, f32[48,128]{1,0:T(8,128)S(1)}, u32[]{:S(2)}, u32[]{:S(2)}) collective-permute-start(f32[48,128]{1,0:T(8,128)S(1)} %get-tuple-element.140.refs_4_), channel_id=1, source_target_pairs={{0,16},{16,0},{32,48},{48,32},{1,17},{17,1},{33,49},{49,33},{2,18}... | collective-permute-start | bytes 73736 | tf_op jit(solution)/shard_map/ppermute | solution.py:642
  103.9 5.6 %collective-permute-start.17 = (f32[32,128]{1,0:T(8,128)S(1)}, f32[32,128]{1,0:T(8,128)S(1)}, u32[]{:S(2)}, u32[]{:S(2)}) collective-permute-start(f32[32,128]{1,0:T(8,128)S(1)} %get-tuple-element.139.refs_3_), channel_id=1, source_target_pairs={{1,2},{2,1},{3,4},{4,3},{5,6},{6,5},{7,8},{8,7},{9,10},{10,9},{11,... | collective-permute-start | bytes 49160 | tf_op jit(solution)/shard_map/ppermute | solution.py:641

commit v5 on v4

--- a/solution.py
+++ b/solution.py
@@ -15,9 +15,9 @@
 LANES = 128
 ROWS = 16
 NO_KEY = 1.0e9
-AGAIN = 8
+AGAIN = 16
 GROUP = 8
-CROSS = [(0, 3), (3, 0), (1, 2), (2, 1)]
+FLIP = 3
 
 
 def constants(lat_total, lon_total):
@@ -143,35 +143,27 @@
 
 def start_kernel(
     lon_cells, state, src, counts, names, weights, turn, flag,
-    field, edge_a, edge_b, strips, buffer, sent, table, listed, parts, zeros, sems
+    field, edge_a, edge_b, strips, buffer, sent, table, listed, zeros, sems
 ):
     blocks = lon_cells // 32
-    loads = []
-    for block in range(blocks):
-        copy = pltpu.make_async_copy(state.at[:, pl.ds(32 * block, 32), :], parts.at[block], sems.at[block])
-        copy.start()
-        loads.append(copy)
     zeros[...] = jnp.zeros(zeros.shape, jnp.float32)
     count = zeros.shape[0]
     clears = []
     for number in range(buffer.shape[0] // count):
-        copy = pltpu.make_async_copy(zeros, buffer.at[pl.ds(number * count, count), :], sems.at[blocks + number])
+        copy = pltpu.make_async_copy(zeros, buffer.at[pl.ds(number * count, count), :], sems.at[number])
         copy.start()
         clears.append(copy)
     lane = lane_ids(ROWS)
     quad = lax.shift_right_logical(lane, 2)
     for block in range(blocks):
-        loads[block].wait()
-        rows = parts.at[block].reshape(32 * ROWS, LANES)
-
-        def body(col, acc, block=block, rows=rows):
-            low = rows[pl.ds(col, 8, stride=32), :]
-            high = rows[pl.ds(col + 8 * 32, 8, stride=32), :]
+        acc = jnp.zeros((ROWS, LANES), jnp.float32)
+        for col in range(32):
+            u = block * 32 + col
+            low = state[pl.ds(u, 8, stride=lon_cells), :]
+            high = state[pl.ds(u + 8 * lon_cells, 8, stride=lon_cells), :]
             value = jnp.concatenate([low, high], axis=0)
-            field[rows_of(block * 32 + col), :] = value
-            return jnp.where(quad == col, strip_of(value, col), acc)
-
-        acc = lax.fori_loop(0, 32, body, jnp.zeros((ROWS, LANES), jnp.float32), unroll=8)
+            field[rows_of(u), :] = value
+            acc = jnp.where(quad == col, strip_of(value, col), acc)
         strips[block * ROWS : (block + 1) * ROWS, :] = acc
     put_edges(field, flag, lon_cells, edge_a, edge_b)
     row = lane_ids(1)
@@ -193,7 +185,7 @@
 def key_kernel(slots, keys, listed):
     lane = lane_ids(8)
     slot = slots[...]
-    peer = lax.bitwise_xor(lax.shift_right_arithmetic(slot, 7), 1)
+    peer = lax.bitwise_xor(lax.shift_right_arithmetic(slot, 7), FLIP)
     shift = lax.bitwise_and(slot - lane, LANES - 1)
     key = jnp.where(slot >= 0, (peer * LANES + shift).astype(jnp.float32), NO_KEY)
     keys[...] = key
@@ -219,19 +211,20 @@
 
 
 def fill_ghosts(received, keys, listed, ghosts):
-    def body(i, accs):
-        out = []
+    def body(step, accs):
+        accs = list(accs)
         for row in range(4):
-            key = listed[row, i]
-            known = jnp.maximum(key, 0)
-            peer = lax.shift_right_logical(known, 7)
-            shift = lax.bitwise_and(known, LANES - 1)
-            value = pltpu.roll(tile(received, peer), lax.bitwise_and(LANES - shift, LANES - 1), 1)
-            out.append(jnp.where(keys[row : row + 1, :] == key.astype(jnp.float32), value, accs[row]))
-        return tuple(out)
+            for i in (2 * step, 2 * step + 1):
+                key = listed[row, i]
+                known = jnp.maximum(key, 0)
+                peer = lax.shift_right_logical(known, 7)
+                shift = lax.bitwise_and(known, LANES - 1)
+                value = pltpu.roll(tile(received, peer), lax.bitwise_and(LANES - shift, LANES - 1), 1)
+                accs[row] = jnp.where(keys[row : row + 1, :] == key.astype(jnp.float32), value, accs[row])
+        return tuple(accs)
 
     zero = jnp.zeros((ROWS, LANES), jnp.float32)
-    accs = lax.fori_loop(0, listed[8, 0], body, (zero, zero, zero, zero))
+    accs = lax.fori_loop(0, lax.shift_right_logical(listed[8, 0] + 1, 1), body, (zero, zero, zero, zero))
     for row in range(4):
         ghosts[row * ROWS : (row + 1) * ROWS, :] = accs[row]
 
@@ -515,6 +508,10 @@
     pl.when(jnp.logical_not(same))(copies[1].wait)
 
 
+def crossing(count):
+    return [(here, (here ^ FLIP) + count) for here in range(count)] + [(here + count, here ^ FLIP) for here in range(count)]
+
+
 def pairs(count, first):
     route = []
     for low in range(first, count - 1, 2):
@@ -581,16 +578,15 @@
         functools.partial(start_kernel, lon_cells),
         out_shape=[moving[0], moving[2], moving[3], moving[4], f32(peers * ROWS, LANES), moving[1], f32(24, LANES)]
         + [jax.ShapeDtypeStruct((2 * LANES + 16,), jnp.int32)],
-        in_specs=[hbm, smem, smem, smem, vmem, vmem, smem],
+        in_specs=[vmem, smem, smem, smem, vmem, vmem, smem],
         out_specs=[vmem] * 4 + [hbm] + [vmem] * 2 + [smem],
         scratch_shapes=[
-            pltpu.VMEM((lon_cells // 32, ROWS, 32, LANES), jnp.float32),
             pltpu.VMEM((LANES, LANES), jnp.float32),
-            pltpu.SemaphoreType.DMA((lon_cells // 32 + peers * ROWS // LANES,)),
+            pltpu.SemaphoreType.DMA((peers * ROWS // LANES,)),
         ],
         compiler_params=params,
     )(
-        state.reshape(ROWS, lon_cells, LANES),
+        state.reshape(cells, LANES),
         src,
         send_counts[0, 0, 0],
         partners[0, 0, 0],
@@ -603,7 +599,7 @@
     for number in range(2 * STEPS):
         second = number % 2 == 1
         final = number == 2 * STEPS - 1
-        over = lax.ppermute(sent, ("panel", "core"), CROSS)
+        over = lax.ppermute(sent, ("panel",) + lon_axes, crossing(lon_blocks))
         operands = [field] + ([origin] if second else []) + [geo]
         part, part_strips = pl.pallas_call(
             functools.partial(inner_kernel, second, lon_cells, consts),

time: 115 us -> 113 us (0.983)
  starting transfers between devices: 68.3 us -> 63.7 us
  waiting for transfers between devices: 10.6 us -> 13.3 us
    ppermute x4, starting transfers between devices: 9.68 us -> 5.3 us  [on_device(): over = lax.ppermute(sent, ('panel',) + lon_axes, crossing(lon_blocks))]
    ppermute x4, waiting for transfers between devices: 0.41 us -> 3.18 us  [on_device(): over = lax.ppermute(sent, ('panel',) + lon_axes, crossing(lon_blocks))]
  transfers between devices with their start and end apart: 24 -> 24, of which waited for: 7 -> 8; matrix products, arithmetic and copies ran while one was open for 1% -> 1% of each run, Pallas kernels for 15% -> 15%
where the time goes in v5:
time: 113 us; the launch traced here: 112 us
  starting transfers between devices  63.7 us (56%)
  Pallas kernels  32.2 us (28%)
  waiting for transfers between devices  13.3 us (12%)
  local copies, waits for them, and re-layouts  2.19 us (2%)
    all_to_all x4, starting transfers between devices, on_device(): lax.all_to_all(buffer.reshape(peers, ROWS, LANES), ('colat', 'lon_hi', 'c...  22.4 us
    ppermute x4, starting transfers between devices, on_device(): strip_a = lax.ppermute(own_strips, 'colat', pairs(lat_blocks, 0))  16.3 us
    ppermute x4, starting transfers between devices, on_device(): lon_b = lax.ppermute(own_b, lon_axes, pairs(lon_blocks, 1))  15.6 us
    pallas_call x4, Pallas kernels, on_device(): pl.pallas_call(functools.partial(inner_kernel, second, lon_cells, consts)...  10.3 us
    pallas_call x4, Pallas kernels, on_device(): pl.pallas_call(functools.partial(outer_kernel, second, final, lon_cells,...  8.79 us
    all_to_all x4, waiting for transfers between devices, on_device(): lax.all_to_all(buffer.reshape(peers, ROWS, LANES), ('colat', 'lon_hi', 'c...  8.33 us
    pallas_call x3, Pallas kernels, on_device(): pl.pallas_call(rows_kernel, out_shape=f32(8 * ROWS, LANES), in_specs=[vme...  5.99 us
    ppermute x4, starting transfers between devices, on_device(): over = lax.ppermute(sent, ('panel',) + lon_axes, crossing(lon_blocks))  5.3 us
  transfers between devices with their start and end apart: 24, of which 8 were waited for; matrix products, arithmetic and copies ran while one was open for 1% of the time, Pallas kernels for 15%

profile of v5, /device:TPU:1, one launch (start us, length us, event | category | flops | bytes accessed | tf_op | source)
XLA Modules:
  0.0 112.2 jit_solution(7601604479159645714)
XLA Ops:
  1.9 3.7 %shard_map.73 = (f32[1536,128]{1,0:T(8,128)S(1)}, f32[32,128]{1,0:T(8,128)S(1)}, f32[32,128]{1,0:T(8,128)S(1)}, f32[48,128]{1,0:T(8,128)S(1)}, f32[1024,128]{1,0...) custom-call(f32[1536,128]{1,0:T(8,128)S(1)} %bitcast.26, s32[256]{0:T(256)S(1)} %bitcast.27, ...), custom_call_target="tpu_custom_call" | custom-call | tf_op jit(solution)/shard_map/pallas_call | solution.py:577
  5.6 1.5 %collective-permute-start.1 = (f32[32,128]{1,0:T(8,128)S(1)}, f32[32,128]{1,0:T(8,128)S(1)}, u32[]{:S(2)}, u32[]{:S(2)}) collective-permute-start(f32[32,128]{1,0:T(8,128)S(1)} %get-tuple-element.86.refs_2_), channel_id=1, source_target_pairs={{0,1},{1,0},{2,3},{3,2},{4,5},{5,4},{6,7},{7,6},{8,9},{9,8},{10,11... | collective-permute-start | bytes 49160 | tf_op jit(solution)/shard_map/ppermute | solution.py:613
  7.1 2.5 %collective-permute-start = (f32[40,128]{1,0:T(8,128)S(1)}, f32[40,128]{1,0:T(8,128)S(1)}, u32[]{:S(2)}, u32[]{:S(2)}) collective-permute-start(f32[40,128]{1,0:T(8,128)S(1)} %get-tuple-element.74), channel_id=1, source_target_pairs={{0,67},{1,66},{2,65},{3,64},{4,71},{5,70},{6,69},{7,68},{8,75},{9,... | collective-permute-start | bytes 61448 | tf_op jit(solution)/shard_map/ppermute | solution.py:602
  10.1 2.6 %shard_map.74 = (f32[1536,128]{1,0:T(8,128)S(1)}, f32[48,128]{1,0:T(8,128)S(1)}) custom-call(f32[1536,128]{1,0:T(8,128)S(1)} %get-tuple-element.75.refs_0_.refs_1_, f32[232,128]{1,0:T(8,128)S(1)} %constant_dynamic-update-slice_fusion.refs_1_.refs_13_.refs_2_), custom_call_target="tpu_custom_call" | custom-call | flops 20000000 | bytes 8388608 | tf_op jit(solution)/shard_map/pallas_call | solution.py:604
  13.5 8.9 %all-to-all-start = ((f32[64,16,128]{2,1,0:T(8,128)}), f32[64,16,128]{2,1,0:T(8,128)S(1)}, u32[]{:S(2)}, u32[]{:S(2)}) async-start(f32[64,16,128]{2,1,0:T(8,128)} %bitcast.10), calls=%async_computation | async-start | bytes 1048576 | tf_op jit(solution)/shard_map/all_to_all | solution.py:625
  23.3 4.0 %collective-permute-start.3 = (f32[48,128]{1,0:T(8,128)S(1)}, f32[48,128]{1,0:T(8,128)S(1)}, u32[]{:S(2)}, u32[]{:S(2)}) collective-permute-start(f32[48,128]{1,0:T(8,128)S(1)} %get-tuple-element.88.refs_4_), channel_id=1, source_target_pairs={{0,16},{16,0},{32,48},{48,32},{1,17},{17,1},{33,49},{49,33},{2,18}... | collective-permute-start | bytes 73736 | tf_op jit(solution)/shard_map/ppermute | solution.py:638
  27.3 3.9 %collective-permute-start.2 = (f32[32,128]{1,0:T(8,128)S(1)}, f32[32,128]{1,0:T(8,128)S(1)}, u32[]{:S(2)}, u32[]{:S(2)}) collective-permute-start(f32[32,128]{1,0:T(8,128)S(1)} %get-tuple-element.87.refs_3_), channel_id=1, source_target_pairs={{1,2},{2,1},{3,4},{4,3},{5,6},{6,5},{7,8},{8,7},{9,10},{10,9},{11,... | collective-permute-start | bytes 49160 | tf_op jit(solution)/shard_map/ppermute | solution.py:637
  31.8 2.0 %shard_map.77.refs_14_ = f32[128,128]{1,0:T(8,128)S(1)} custom-call(f32[1536,128]{1,0:T(8,128)S(1)} %get-tuple-element.84.field.refs_0_, s32[256]{0:T(256)S(1)} %bitcast.28), custom_call_target="tpu_custom_call" | custom-call | flops 8000000 | bytes 4194304 | tf_op jit(solution)/shard_map/pallas_call | solution.py:629
  33.8 1.4 %all-to-all-done = f32[64,16,128]{2,1,0:T(8,128)S(1)} async-done(((f32[64,16,128]{2,1,0:T(8,128)}), f32[64,16,128]{2,1,0:T(8,128)S(1)}, u32[]{:S(2)}, u32[]{:S(2)}) %all-to-all-start) | async-done | bytes 524320 | tf_op jit(solution)/shard_map/all_to_all | solution.py:625
  35.2 2.0 %shard_map.78 = (f32[1536,128]{1,0:T(8,128)S(1)}, f32[40,128]{1,0:T(8,128)S(1)}, f32[32,128]{1,0:T(8,128)S(1)}, f32[32,128]{1,0:T(8,128)S(1)}, f32[48,128]{1,0:T(8,128)S(1)}) custom-call(f32[1536,128]{1,0:T(8,128)S(1)} %get-tuple-element.84.field.refs_0_, f32[48,128]{1,0:T(8,128)S(1)} %get-tuple-element.85.refs_1_, f32[32,128]{1,0:T(8,128)S(1)} %get-tuple-element.86.refs_2_, ...), custom_call_target="tpu_custom_call" | custom-call | tf_op jit(solution)/shard_map/pallas_call | solution.py:645
  38.4 2.6 %shard_map.79 = (f32[1536,128]{1,0:T(8,128)S(1)}, f32[48,128]{1,0:T(8,128)S(1)}) custom-call(f32[1536,128]{1,0:T(8,128)S(1)} %get-tuple-element.96.refs_0_, f32[1536,128]{1,0:T(8,128)S(1)} %get-tuple-element.75.refs_0_.refs_1_, f32[232,128]{1,0:T(8,128)S(1)} %constant_dynamic-update-slice_fusion.refs_1_.refs_13_.refs_2_), custom_call_target="tpu_custom_call" | custom-call | flops 20000000 | bytes 8388608 | tf_op jit(solution)/shard_map/pallas_call | solution.py:604
  42.5 4.5 %all-to-all-start.1 = ((f32[64,16,128]{2,1,0:T(8,128)}), f32[64,16,128]{2,1,0:T(8,128)S(1)}, u32[]{:S(2)}, u32[]{:S(2)}) async-start(f32[64,16,128]{2,1,0:T(8,128)} %bitcast.13), calls=%async_computation.1 | async-start | bytes 1048576 | tf_op jit(solution)/shard_map/all_to_all | solution.py:625
  47.7 4.1 %collective-permute-start.8 = (f32[48,128]{1,0:T(8,128)S(1)}, f32[48,128]{1,0:T(8,128)S(1)}, u32[]{:S(2)}, u32[]{:S(2)}) collective-permute-start(f32[48,128]{1,0:T(8,128)S(1)} %get-tuple-element.108.refs_4_), channel_id=1, source_target_pairs={{0,16},{16,0},{32,48},{48,32},{1,17},{17,1},{33,49},{49,33},{2,18}... | collective-permute-start | bytes 73736 | tf_op jit(solution)/shard_map/ppermute | solution.py:638
  51.8 3.9 %collective-permute-start.7 = (f32[32,128]{1,0:T(8,128)S(1)}, f32[32,128]{1,0:T(8,128)S(1)}, u32[]{:S(2)}, u32[]{:S(2)}) collective-permute-start(f32[32,128]{1,0:T(8,128)S(1)} %get-tuple-element.107.refs_3_), channel_id=1, source_target_pairs={{1,2},{2,1},{3,4},{4,3},{5,6},{6,5},{7,8},{8,7},{9,10},{10,9},{11,... | collective-permute-start | bytes 49160 | tf_op jit(solution)/shard_map/ppermute | solution.py:637
  55.7 2.0 %shard_map.81.refs_14_ = f32[128,128]{1,0:T(8,128)S(1)} custom-call(f32[1536,128]{1,0:T(8,128)S(1)} %get-tuple-element.104.field.refs_0_, s32[256]{0:T(256)S(1)} %bitcast.30), custom_call_target="tpu_custom_call" | custom-call | flops 8000000 | bytes 4194304 | tf_op jit(solution)/shard_map/pallas_call | solution.py:629
  57.7 2.2 %all-to-all-done.1 = f32[64,16,128]{2,1,0:T(8,128)S(1)} async-done(((f32[64,16,128]{2,1,0:T(8,128)}), f32[64,16,128]{2,1,0:T(8,128)S(1)}, u32[]{:S(2)}, u32[]{:S(2)}) %all-to-all-start.1) | async-done | bytes 524320 | tf_op jit(solution)/shard_map/all_to_all | solution.py:625
  59.9 2.0 %shard_map.82 = (f32[1536,128]{1,0:T(8,128)S(1)}, f32[40,128]{1,0:T(8,128)S(1)}, f32[32,128]{1,0:T(8,128)S(1)}, f32[32,128]{1,0:T(8,128)S(1)}, f32[48,128]{1,0:T(8,128)S(1)}) custom-call(f32[1536,128]{1,0:T(8,128)S(1)} %get-tuple-element.104.field.refs_0_, f32[48,128]{1,0:T(8,128)S(1)} %get-tuple-element.105.refs_1_, ...), custom_call_target="tpu_custom_call" | custom-call | tf_op jit(solution)/shard_map/pallas_call | solution.py:645
  62.9 2.6 %shard_map.83 = (f32[1536,128]{1,0:T(8,128)S(1)}, f32[48,128]{1,0:T(8,128)S(1)}) custom-call(f32[1536,128]{1,0:T(8,128)S(1)} %get-tuple-element.112.refs_0_.refs_1_, f32[232,128]{1,0:T(8,128)S(1)} %constant_dynamic-update-slice_fusion.refs_1_.refs_13_.refs_2_), custom_call_target="tpu_custom_call" | custom-call | flops 20000000 | bytes 8388608 | tf_op jit(solution)/shard_map/pallas_call | solution.py:604
  67.3 4.5 %all-to-all-start.2 = ((f32[64,16,128]{2,1,0:T(8,128)}), f32[64,16,128]{2,1,0:T(8,128)S(1)}, u32[]{:S(2)}, u32[]{:S(2)}) async-start(f32[64,16,128]{2,1,0:T(8,128)} %bitcast.15), calls=%async_computation.2 | async-start | bytes 1048576 | tf_op jit(solution)/shard_map/all_to_all | solution.py:625
  72.4 4.1 %collective-permute-start.13 = (f32[48,128]{1,0:T(8,128)S(1)}, f32[48,128]{1,0:T(8,128)S(1)}, u32[]{:S(2)}, u32[]{:S(2)}) collective-permute-start(f32[48,128]{1,0:T(8,128)S(1)} %get-tuple-element.124.refs_4_), channel_id=1, source_target_pairs={{0,16},{16,0},{32,48},{48,32},{1,17},{17,1},{33,49},{49,33},{2,18}... | collective-permute-start | bytes 73736 | tf_op jit(solution)/shard_map/ppermute | solution.py:638
  76.5 3.9 %collective-permute-start.12 = (f32[32,128]{1,0:T(8,128)S(1)}, f32[32,128]{1,0:T(8,128)S(1)}, u32[]{:S(2)}, u32[]{:S(2)}) collective-permute-start(f32[32,128]{1,0:T(8,128)S(1)} %get-tuple-element.123.refs_3_), channel_id=1, source_target_pairs={{1,2},{2,1},{3,4},{4,3},{5,6},{6,5},{7,8},{8,7},{9,10},{10,9},{11,... | collective-permute-start | bytes 49160 | tf_op jit(solution)/shard_map/ppermute | solution.py:637
  80.4 2.0 %shard_map.85.refs_14_ = f32[128,128]{1,0:T(8,128)S(1)} custom-call(f32[1536,128]{1,0:T(8,128)S(1)} %get-tuple-element.120.field.refs_0_, s32[256]{0:T(256)S(1)} %bitcast.32), custom_call_target="tpu_custom_call" | custom-call | flops 8000000 | bytes 4194304 | tf_op jit(solution)/shard_map/pallas_call | solution.py:629
  82.4 2.2 %all-to-all-done.2 = f32[64,16,128]{2,1,0:T(8,128)S(1)} async-done(((f32[64,16,128]{2,1,0:T(8,128)}), f32[64,16,128]{2,1,0:T(8,128)S(1)}, u32[]{:S(2)}, u32[]{:S(2)}) %all-to-all-start.2) | async-done | bytes 524320 | tf_op jit(solution)/shard_map/all_to_all | solution.py:625
  84.6 2.0 %shard_map.86 = (f32[1536,128]{1,0:T(8,128)S(1)}, f32[40,128]{1,0:T(8,128)S(1)}, f32[32,128]{1,0:T(8,128)S(1)}, f32[32,128]{1,0:T(8,128)S(1)}, f32[48,128]{1,0:T(8,128)S(1)}) custom-call(f32[1536,128]{1,0:T(8,128)S(1)} %get-tuple-element.120.field.refs_0_, f32[48,128]{1,0:T(8,128)S(1)} %get-tuple-element.121.refs_1_, ...), custom_call_target="tpu_custom_call" | custom-call | tf_op jit(solution)/shard_map/pallas_call | solution.py:645
  87.3 2.6 %shard_map.87 = (f32[1536,128]{1,0:T(8,128)S(1)}, f32[48,128]{1,0:T(8,128)S(1)}) custom-call(f32[1536,128]{1,0:T(8,128)S(1)} %get-tuple-element.128.refs_0_, f32[1536,128]{1,0:T(8,128)S(1)} %get-tuple-element.112.refs_0_.refs_1_, f32[232,128]{1,0:T(8,128)S(1)} %constant_dynamic-update-slice_fusion.refs_1_.refs_13_.refs_2_), custom_call_target="tpu_custom_call" | custom-call | flops 20000000 | bytes 8388608 | tf_op jit(solution)/shard_map/pallas_call | solution.py:604
  89.9 1.3 %collective-permute-done.15.message = f32[40,128]{1,0:T(8,128)S(1)} collective-permute-done((f32[40,128]{1,0:T(8,128)S(1)}, f32[40,128]{1,0:T(8,128)S(1)}, u32[]{:S(2)}, u32[]{:S(2)}) %collective-permute-start.15) | collective-permute-done | bytes 20512 | tf_op jit(solution)/shard_map/ppermute | solution.py:602
  92.0 4.5 %all-to-all-start.3 = ((f32[64,16,128]{2,1,0:T(8,128)}), f32[64,16,128]{2,1,0:T(8,128)S(1)}, u32[]{:S(2)}, u32[]{:S(2)}) async-start(f32[64,16,128]{2,1,0:T(8,128)} %bitcast.17), calls=%async_computation.3 | async-start | bytes 1048576 | tf_op jit(solution)/shard_map/all_to_all | solution.py:625
  97.1 4.1 %collective-permute-start.18 = (f32[48,128]{1,0:T(8,128)S(1)}, f32[48,128]{1,0:T(8,128)S(1)}, u32[]{:S(2)}, u32[]{:S(2)}) collective-permute-start(f32[48,128]{1,0:T(8,128)S(1)} %get-tuple-element.140.refs_4_), channel_id=1, source_target_pairs={{0,16},{16,0},{32,48},{48,32},{1,17},{17,1},{33,49},{49,33},{2,18}... | collective-permute-start | bytes 73736 | tf_op jit(solution)/shard_map/ppermute | solution.py:638
  101.2 3.9 %collective-permute-start.17 = (f32[32,128]{1,0:T(8,128)S(1)}, f32[32,128]{1,0:T(8,128)S(1)}, u32[]{:S(2)}, u32[]{:S(2)}) collective-permute-start(f32[32,128]{1,0:T(8,128)S(1)} %get-tuple-element.139.refs_3_), channel_id=1, source_target_pairs={{1,2},{2,1},{3,4},{4,3},{5,6},{6,5},{7,8},{8,7},{9,10},{10,9},{11,... | collective-permute-start | bytes 49160 | tf_op jit(solution)/shard_map/ppermute | solution.py:637
  105.1 1.7 %collective-permute-done.17.refs_6_ = f32[32,128]{1,0:T(8,128)S(1)} collective-permute-done((f32[32,128]{1,0:T(8,128)S(1)}, f32[32,128]{1,0:T(8,128)S(1)}, u32[]{:S(2)}, u32[]{:S(2)}) %collective-permute-start.17) | collective-permute-done | bytes 16416 | tf_op jit(solution)/shard_map/ppermute | solution.py:637
  106.8 2.5 %all-to-all-done.3 = f32[64,16,128]{2,1,0:T(8,128)S(1)} async-done(((f32[64,16,128]{2,1,0:T(8,128)}), f32[64,16,128]{2,1,0:T(8,128)S(1)}, u32[]{:S(2)}, u32[]{:S(2)}) %all-to-all-start.3) | async-done | bytes 524320 | tf_op jit(solution)/shard_map/all_to_all | solution.py:625
  109.3 2.8 %shard_map.89 = f32[1536,128]{1,0:T(8,128)} custom-call(f32[1536,128]{1,0:T(8,128)S(1)} %get-tuple-element.136.refs_0_, f32[48,128]{1,0:T(8,128)S(1)} %get-tuple-element.137.refs_1_, f32[32,128]{1,0:T(8,128)S(1)} %get-tuple-element.138.refs_2_, f32[32,128]{1,0:T(8,128)S(1)} %get-tuple-element.139.refs_3_, f32[48,128]{1,0:T(8,128)S(1)} %get-tuple-element.140.refs_4_, ...), custom_call_target="tpu_custom_call" | custom-call | tf_op jit(solution)/shard_map/pallas_call | solution.py:645
  (65 shorter events, 13.4 us)
Async XLA Ops:
  0.1 0.7 copy-start.2
  0.1 0.7 copy-start.3
  0.1 0.7 copy-start.5
  0.1 0.7 copy-start.1
  0.1 0.7 copy-start.4
  0.8 1.1 %copy-start = (f32[4,1,4,96,128]{4,3,2,1,0:T(8,128)S(1)}, f32[4,1,4,96,128]{4,3,2,1,0:T(8,128)}, u32[]{:S(2)}) copy-start(f32[4,1,4,96,128]{4,3,2,1,0:T(8,128)} %param.7) | copy-start | bytes 2359300
  5.6 7.1 %collective-permute-start.1 = (f32[32,128]{1,0:T(8,128)S(1)}, f32[32,128]{1,0:T(8,128)S(1)}, u32[]{:S(2)}, u32[]{:S(2)}) collective-permute-start(f32[32,128]{1,0:T(8,128)S(1)} %get-tuple-element.86.refs_2_), channel_id=1, source_target_pairs={{0,1},{1,0},{2,3},{3,2},{4,5},{5,4},{6,7},{7,6},{8,9},{9,8},{10,11... | collective-permute-start | bytes 49160 | tf_op jit(solution)/shard_map/ppermute | solution.py:613
  7.1 5.6 %collective-permute-start = (f32[40,128]{1,0:T(8,128)S(1)}, f32[40,128]{1,0:T(8,128)S(1)}, u32[]{:S(2)}, u32[]{:S(2)}) collective-permute-start(f32[40,128]{1,0:T(8,128)S(1)} %get-tuple-element.74), channel_id=1, source_target_pairs={{0,67},{1,66},{2,65},{3,64},{4,71},{5,70},{6,69},{7,68},{8,75},{9,... | collective-permute-start | bytes 61448 | tf_op jit(solution)/shard_map/ppermute | solution.py:602
  13.5 9.0 %copy-start.6 = (s32[1,1,1,896]{3,2,1,0:T(1,128)S(1)}, s32[1,1,1,896]{3,2,1,0:T(1,128)}, u32[]{:S(2)}) copy-start(s32[1,1,1,896]{3,2,1,0:T(1,128)} %param.13) | copy-start | bytes 10756
  13.5 21.7 %all-to-all-start = ((f32[64,16,128]{2,1,0:T(8,128)}), f32[64,16,128]{2,1,0:T(8,128)S(1)}, u32[]{:S(2)}, u32[]{:S(2)}) async-start(f32[64,16,128]{2,1,0:T(8,128)} %bitcast.10), calls=%async_computation | async-start | bytes 1048576 | tf_op jit(solution)/shard_map/all_to_all | solution.py:625
  22.6 11.1 %collective-permute-start.4 = (f32[48,128]{1,0:T(8,128)S(1)}, f32[48,128]{1,0:T(8,128)S(1)}, u32[]{:S(2)}, u32[]{:S(2)}) collective-permute-start(f32[48,128]{1,0:T(8,128)S(1)} %get-tuple-element.88.refs_4_), channel_id=1, source_target_pairs={{16,32},{32,16},{17,33},{33,17},{18,34},{34,18},{19,35},{35,19},{2... | collective-permute-start | bytes 73736 | tf_op jit(solution)/shard_map/ppermute | solution.py:639
  23.3 10.5 %collective-permute-start.3 = (f32[48,128]{1,0:T(8,128)S(1)}, f32[48,128]{1,0:T(8,128)S(1)}, u32[]{:S(2)}, u32[]{:S(2)}) collective-permute-start(f32[48,128]{1,0:T(8,128)S(1)} %get-tuple-element.88.refs_4_), channel_id=1, source_target_pairs={{0,16},{16,0},{32,48},{48,32},{1,17},{17,1},{33,49},{49,33},{2,18}... | collective-permute-start | bytes 73736 | tf_op jit(solution)/shard_map/ppermute | solution.py:638
  27.3 6.5 %collective-permute-start.2 = (f32[32,128]{1,0:T(8,128)S(1)}, f32[32,128]{1,0:T(8,128)S(1)}, u32[]{:S(2)}, u32[]{:S(2)}) collective-permute-start(f32[32,128]{1,0:T(8,128)S(1)} %get-tuple-element.87.refs_3_), channel_id=1, source_target_pairs={{1,2},{2,1},{3,4},{4,3},{5,6},{6,5},{7,8},{8,7},{9,10},{10,9},{11,... | collective-permute-start | bytes 49160 | tf_op jit(solution)/shard_map/ppermute | solution.py:637
  37.2 4.6 %collective-permute-start.5 = (f32[40,128]{1,0:T(8,128)S(1)}, f32[40,128]{1,0:T(8,128)S(1)}, u32[]{:S(2)}, u32[]{:S(2)}) collective-permute-start(f32[40,128]{1,0:T(8,128)S(1)} %get-tuple-element.95), channel_id=1, source_target_pairs={{0,67},{1,66},{2,65},{3,64},{4,71},{5,70},{6,69},{7,68},{8,75},{9,... | collective-permute-start | bytes 61448 | tf_op jit(solution)/shard_map/ppermute | solution.py:602
  38.4 2.6 %collective-permute-start.6 = (f32[32,128]{1,0:T(8,128)S(1)}, f32[32,128]{1,0:T(8,128)S(1)}, u32[]{:S(2)}, u32[]{:S(2)}) collective-permute-start(f32[32,128]{1,0:T(8,128)S(1)} %get-tuple-element.106.refs_2_), channel_id=1, source_target_pairs={{0,1},{1,0},{2,3},{3,2},{4,5},{5,4},{6,7},{7,6},{8,9},{9,8},{10,11... | collective-permute-start | bytes 49160 | tf_op jit(solution)/shard_map/ppermute | solution.py:613
  42.5 17.4 %all-to-all-start.1 = ((f32[64,16,128]{2,1,0:T(8,128)}), f32[64,16,128]{2,1,0:T(8,128)S(1)}, u32[]{:S(2)}, u32[]{:S(2)}) async-start(f32[64,16,128]{2,1,0:T(8,128)} %bitcast.13), calls=%async_computation.1 | async-start | bytes 1048576 | tf_op jit(solution)/shard_map/all_to_all | solution.py:625
  47.0 10.7 %collective-permute-start.9 = (f32[48,128]{1,0:T(8,128)S(1)}, f32[48,128]{1,0:T(8,128)S(1)}, u32[]{:S(2)}, u32[]{:S(2)}) collective-permute-start(f32[48,128]{1,0:T(8,128)S(1)} %get-tuple-element.108.refs_4_), channel_id=1, source_target_pairs={{16,32},{32,16},{17,33},{33,17},{18,34},{34,18},{19,35},{35,19},{2... | collective-permute-start | bytes 73736 | tf_op jit(solution)/shard_map/ppermute | solution.py:639
  47.7 10.0 %collective-permute-start.8 = (f32[48,128]{1,0:T(8,128)S(1)}, f32[48,128]{1,0:T(8,128)S(1)}, u32[]{:S(2)}, u32[]{:S(2)}) collective-permute-start(f32[48,128]{1,0:T(8,128)S(1)} %get-tuple-element.108.refs_4_), channel_id=1, source_target_pairs={{0,16},{16,0},{32,48},{48,32},{1,17},{17,1},{33,49},{49,33},{2,18}... | collective-permute-start | bytes 73736 | tf_op jit(solution)/shard_map/ppermute | solution.py:638
  51.8 5.9 %collective-permute-start.7 = (f32[32,128]{1,0:T(8,128)S(1)}, f32[32,128]{1,0:T(8,128)S(1)}, u32[]{:S(2)}, u32[]{:S(2)}) collective-permute-start(f32[32,128]{1,0:T(8,128)S(1)} %get-tuple-element.107.refs_3_), channel_id=1, source_target_pairs={{1,2},{2,1},{3,4},{4,3},{5,6},{6,5},{7,8},{8,7},{9,10},{10,9},{11,... | collective-permute-start | bytes 49160 | tf_op jit(solution)/shard_map/ppermute | solution.py:637
  61.9 4.6 %collective-permute-start.10 = (f32[40,128]{1,0:T(8,128)S(1)}, f32[40,128]{1,0:T(8,128)S(1)}, u32[]{:S(2)}, u32[]{:S(2)}) collective-permute-start(f32[40,128]{1,0:T(8,128)S(1)} %get-tuple-element.111), channel_id=1, source_target_pairs={{0,67},{1,66},{2,65},{3,64},{4,71},{5,70},{6,69},{7,68},{8,75},{9,... | collective-permute-start | bytes 61448 | tf_op jit(solution)/shard_map/ppermute | solution.py:602
  62.9 2.6 %collective-permute-start.11 = (f32[32,128]{1,0:T(8,128)S(1)}, f32[32,128]{1,0:T(8,128)S(1)}, u32[]{:S(2)}, u32[]{:S(2)}) collective-permute-start(f32[32,128]{1,0:T(8,128)S(1)} %get-tuple-element.122.refs_2_), channel_id=1, source_target_pairs={{0,1},{1,0},{2,3},{3,2},{4,5},{5,4},{6,7},{7,6},{8,9},{9,8},{10,11... | collective-permute-start | bytes 49160 | tf_op jit(solution)/shard_map/ppermute | solution.py:613
  67.3 17.4 %all-to-all-start.2 = ((f32[64,16,128]{2,1,0:T(8,128)}), f32[64,16,128]{2,1,0:T(8,128)S(1)}, u32[]{:S(2)}, u32[]{:S(2)}) async-start(f32[64,16,128]{2,1,0:T(8,128)} %bitcast.15), calls=%async_computation.2 | async-start | bytes 1048576 | tf_op jit(solution)/shard_map/all_to_all | solution.py:625
  71.7 10.7 %collective-permute-start.14 = (f32[48,128]{1,0:T(8,128)S(1)}, f32[48,128]{1,0:T(8,128)S(1)}, u32[]{:S(2)}, u32[]{:S(2)}) collective-permute-start(f32[48,128]{1,0:T(8,128)S(1)} %get-tuple-element.124.refs_4_), channel_id=1, source_target_pairs={{16,32},{32,16},{17,33},{33,17},{18,34},{34,18},{19,35},{35,19},{2... | collective-permute-start | bytes 73736 | tf_op jit(solution)/shard_map/ppermute | solution.py:639
  72.4 10.0 %collective-permute-start.13 = (f32[48,128]{1,0:T(8,128)S(1)}, f32[48,128]{1,0:T(8,128)S(1)}, u32[]{:S(2)}, u32[]{:S(2)}) collective-permute-start(f32[48,128]{1,0:T(8,128)S(1)} %get-tuple-element.124.refs_4_), channel_id=1, source_target_pairs={{0,16},{16,0},{32,48},{48,32},{1,17},{17,1},{33,49},{49,33},{2,18}... | collective-permute-start | bytes 73736 | tf_op jit(solution)/shard_map/ppermute | solution.py:638
  76.5 5.9 %collective-permute-start.12 = (f32[32,128]{1,0:T(8,128)S(1)}, f32[32,128]{1,0:T(8,128)S(1)}, u32[]{:S(2)}, u32[]{:S(2)}) collective-permute-start(f32[32,128]{1,0:T(8,128)S(1)} %get-tuple-element.123.refs_3_), channel_id=1, source_target_pairs={{1,2},{2,1},{3,4},{4,3},{5,6},{6,5},{7,8},{8,7},{9,10},{10,9},{11,... | collective-permute-start | bytes 49160 | tf_op jit(solution)/shard_map/ppermute | solution.py:637
  86.6 4.6 %collective-permute-start.15 = (f32[40,128]{1,0:T(8,128)S(1)}, f32[40,128]{1,0:T(8,128)S(1)}, u32[]{:S(2)}, u32[]{:S(2)}) collective-permute-start(f32[40,128]{1,0:T(8,128)S(1)} %get-tuple-element.127), channel_id=1, source_target_pairs={{0,67},{1,66},{2,65},{3,64},{4,71},{5,70},{6,69},{7,68},{8,75},{9,... | collective-permute-start | bytes 61448 | tf_op jit(solution)/shard_map/ppermute | solution.py:602
  87.3 2.6 %collective-permute-start.16 = (f32[32,128]{1,0:T(8,128)S(1)}, f32[32,128]{1,0:T(8,128)S(1)}, u32[]{:S(2)}, u32[]{:S(2)}) collective-permute-start(f32[32,128]{1,0:T(8,128)S(1)} %get-tuple-element.138.refs_2_), channel_id=1, source_target_pairs={{0,1},{1,0},{2,3},{3,2},{4,5},{5,4},{6,7},{7,6},{8,9},{9,8},{10,11... | collective-permute-start | bytes 49160 | tf_op jit(solution)/shard_map/ppermute | solution.py:613
  92.0 17.4 %all-to-all-start.3 = ((f32[64,16,128]{2,1,0:T(8,128)}), f32[64,16,128]{2,1,0:T(8,128)S(1)}, u32[]{:S(2)}, u32[]{:S(2)}) async-start(f32[64,16,128]{2,1,0:T(8,128)} %bitcast.17), calls=%async_computation.3 | async-start | bytes 1048576 | tf_op jit(solution)/shard_map/all_to_all | solution.py:625
  96.4 10.4 %collective-permute-start.19 = (f32[48,128]{1,0:T(8,128)S(1)}, f32[48,128]{1,0:T(8,128)S(1)}, u32[]{:S(2)}, u32[]{:S(2)}) collective-permute-start(f32[48,128]{1,0:T(8,128)S(1)} %get-tuple-element.140.refs_4_), channel_id=1, source_target_pairs={{16,32},{32,16},{17,33},{33,17},{18,34},{34,18},{19,35},{35,19},{2... | collective-permute-start | bytes 73736 | tf_op jit(solution)/shard_map/ppermute | solution.py:639
  97.1 9.7 %collective-permute-start.18 = (f32[48,128]{1,0:T(8,128)S(1)}, f32[48,128]{1,0:T(8,128)S(1)}, u32[]{:S(2)}, u32[]{:S(2)}) collective-permute-start(f32[48,128]{1,0:T(8,128)S(1)} %get-tuple-element.140.refs_4_), channel_id=1, source_target_pairs={{0,16},{16,0},{32,48},{48,32},{1,17},{17,1},{33,49},{49,33},{2,18}... | collective-permute-start | bytes 73736 | tf_op jit(solution)/shard_map/ppermute | solution.py:638
  101.2 5.6 %collective-permute-start.17 = (f32[32,128]{1,0:T(8,128)S(1)}, f32[32,128]{1,0:T(8,128)S(1)}, u32[]{:S(2)}, u32[]{:S(2)}) collective-permute-start(f32[32,128]{1,0:T(8,128)S(1)} %get-tuple-element.139.refs_3_), channel_id=1, source_target_pairs={{1,2},{2,1},{3,4},{4,3},{5,6},{6,5},{7,8},{8,7},{9,10},{10,9},{11,... | collective-permute-start | bytes 49160 | tf_op jit(solution)/shard_map/ppermute | solution.py:637

commit v6 on v5

--- a/solution.py
+++ b/solution.py
@@ -185,7 +185,7 @@
 def key_kernel(slots, keys, listed):
     lane = lane_ids(8)
     slot = slots[...]
-    peer = lax.bitwise_xor(lax.shift_right_arithmetic(slot, 7), FLIP)
+    peer = seat(lax.bitwise_xor(lax.shift_right_logical(jnp.maximum(slot, 0), 7), FLIP))
     shift = lax.bitwise_and(slot - lane, LANES - 1)
     key = jnp.where(slot >= 0, (peer * LANES + shift).astype(jnp.float32), NO_KEY)
     keys[...] = key
@@ -487,6 +487,10 @@
     finish_rows(lax.fori_loop(0, steps, repeat, accs), table, sent)
 
 
+def seat(block):
+    return lax.bitwise_and(block, 15) * 4 + lax.shift_right_logical(block, 4)
+
+
 def pack_kernel(message, _, buffer, staged, sems):
     target0 = jnp.max(message[32:33, :]).astype(jnp.int32)
     target1 = jnp.max(message[33:34, :]).astype(jnp.int32)
@@ -497,7 +501,7 @@
     copies = [
         pltpu.make_async_copy(
             staged.at[pl.ds(at * ROWS, ROWS), :],
-            buffer.at[pl.ds(pl.multiple_of(target * ROWS, ROWS), ROWS), :],
+            buffer.at[pl.ds(pl.multiple_of(seat(target) * ROWS, ROWS), ROWS), :],
             sems.at[at],
         )
         for at, target in enumerate((target0, target1))
@@ -623,7 +627,7 @@
         )(over, buffer)
         buffer, own_a, own_b, own_strips, part = lax.optimization_barrier((buffer, edge_a, edge_b, strips, part))
         received = lax.all_to_all(
-            buffer.reshape(peers, ROWS, LANES), ("colat", "lon_hi", "core"), split_axis=0, concat_axis=0, tiled=True
+            buffer.reshape(peers, ROWS, LANES), ("lon_hi", "core", "colat"), split_axis=0, concat_axis=0, tiled=True
         ).reshape(peers * ROWS, LANES)
         if not final:
             corners = pl.pallas_call(

time: 113 us -> 111 us (0.982)
  waiting for transfers between devices: 13.3 us -> 7.12 us
  starting transfers between devices: 63.7 us -> 68.5 us
    ppermute x4, waiting for transfers between devices: 3.18 us -> 0.02 us  [on_device(): over = lax.ppermute(sent, ('panel',) + lon_axes, crossing(lon_blocks))]
    ppermute x4, starting transfers between devices: 5.3 us -> 8.31 us  [on_device(): over = lax.ppermute(sent, ('panel',) + lon_axes, crossing(lon_blocks))]
    all_to_all x4, waiting for transfers between devices: 8.33 us -> 5.35 us  [on_device(): lax.all_to_all(buffer.reshape(peers, ROWS, LANES), ('lon_hi', 'core', 'co...]
    all_to_all x4, starting transfers between devices: 22.4 us -> 24.8 us  [on_device(): lax.all_to_all(buffer.reshape(peers, ROWS, LANES), ('lon_hi', 'core', 'co...]
  transfers between devices with their start and end apart: 24 -> 24, of which waited for: 8 -> 5; matrix products, arithmetic and copies ran while one was open for 1% -> 1% of each run, Pallas kernels for 15% -> 15%
where the time goes in v6:
time: 111 us
  starting transfers between devices  68.5 us (62%)
  Pallas kernels  32.3 us (29%)
  waiting for transfers between devices  7.12 us (6%)
  local copies, waits for them, and re-layouts  2.19 us (2%)
    all_to_all x4, starting transfers between devices, on_device(): lax.all_to_all(buffer.reshape(peers, ROWS, LANES), ('lon_hi', 'core', 'co...  24.8 us
    ppermute x4, starting transfers between devices, on_device(): lon_b = lax.ppermute(own_b, lon_axes, pairs(lon_blocks, 1))  15.7 us
    ppermute x4, starting transfers between devices, on_device(): strip_a = lax.ppermute(own_strips, 'colat', pairs(lat_blocks, 0))  15.6 us
    pallas_call x4, Pallas kernels, on_device(): pl.pallas_call(functools.partial(inner_kernel, second, lon_cells, consts)...  10.3 us
    pallas_call x4, Pallas kernels, on_device(): pl.pallas_call(functools.partial(outer_kernel, second, final, lon_cells,...  8.79 us
    ppermute x4, starting transfers between devices, on_device(): over = lax.ppermute(sent, ('panel',) + lon_axes, crossing(lon_blocks))  8.31 us
    pallas_call x3, Pallas kernels, on_device(): pl.pallas_call(rows_kernel, out_shape=f32(8 * ROWS, LANES), in_specs=[vme...  5.99 us
    all_to_all x4, waiting for transfers between devices, on_device(): lax.all_to_all(buffer.reshape(peers, ROWS, LANES), ('lon_hi', 'core', 'co...  5.35 us
  transfers between devices with their start and end apart: 24, of which 5 were waited for; matrix products, arithmetic and copies ran while one was open for 1% of the time, Pallas kernels for 15%

profile of v6, /device:TPU:1, one launch (start us, length us, event | category | flops | bytes accessed | tf_op | source)
XLA Modules:
  0.0 110.8 jit_solution(9006366509596949274)
XLA Ops:
  1.9 3.7 %shard_map.73 = (f32[1536,128]{1,0:T(8,128)S(1)}, f32[32,128]{1,0:T(8,128)S(1)}, f32[32,128]{1,0:T(8,128)S(1)}, f32[48,128]{1,0:T(8,128)S(1)}, f32[1024,128]{1,0...) custom-call(f32[1536,128]{1,0:T(8,128)S(1)} %bitcast.26, s32[256]{0:T(256)S(1)} %bitcast.27, ...), custom_call_target="tpu_custom_call" | custom-call | tf_op jit(solution)/shard_map/pallas_call | solution.py:581
  5.6 1.5 %collective-permute-start.1 = (f32[32,128]{1,0:T(8,128)S(1)}, f32[32,128]{1,0:T(8,128)S(1)}, u32[]{:S(2)}, u32[]{:S(2)}) collective-permute-start(f32[32,128]{1,0:T(8,128)S(1)} %get-tuple-element.86.refs_2_), channel_id=1, source_target_pairs={{0,1},{1,0},{2,3},{3,2},{4,5},{5,4},{6,7},{7,6},{8,9},{9,8},{10,11... | collective-permute-start | bytes 49160 | tf_op jit(solution)/shard_map/ppermute | solution.py:617
  7.1 2.5 %collective-permute-start = (f32[40,128]{1,0:T(8,128)S(1)}, f32[40,128]{1,0:T(8,128)S(1)}, u32[]{:S(2)}, u32[]{:S(2)}) collective-permute-start(f32[40,128]{1,0:T(8,128)S(1)} %get-tuple-element.74), channel_id=1, source_target_pairs={{0,67},{1,66},{2,65},{3,64},{4,71},{5,70},{6,69},{7,68},{8,75},{9,... | collective-permute-start | bytes 61448 | tf_op jit(solution)/shard_map/ppermute | solution.py:606
  10.1 2.6 %shard_map.74 = (f32[1536,128]{1,0:T(8,128)S(1)}, f32[48,128]{1,0:T(8,128)S(1)}) custom-call(f32[1536,128]{1,0:T(8,128)S(1)} %get-tuple-element.75.refs_0_.refs_1_, f32[232,128]{1,0:T(8,128)S(1)} %constant_dynamic-update-slice_fusion.refs_1_.refs_13_.refs_2_), custom_call_target="tpu_custom_call" | custom-call | flops 20000000 | bytes 8388608 | tf_op jit(solution)/shard_map/pallas_call | solution.py:608
  13.5 8.9 %all-to-all-start = ((f32[64,16,128]{2,1,0:T(8,128)}), f32[64,16,128]{2,1,0:T(8,128)S(1)}, u32[]{:S(2)}, u32[]{:S(2)}) async-start(f32[64,16,128]{2,1,0:T(8,128)} %bitcast.10), calls=%async_computation | async-start | bytes 1048576 | tf_op jit(solution)/shard_map/all_to_all | solution.py:629
  23.3 3.9 %collective-permute-start.3 = (f32[48,128]{1,0:T(8,128)S(1)}, f32[48,128]{1,0:T(8,128)S(1)}, u32[]{:S(2)}, u32[]{:S(2)}) collective-permute-start(f32[48,128]{1,0:T(8,128)S(1)} %get-tuple-element.88.refs_4_), channel_id=1, source_target_pairs={{0,16},{16,0},{32,48},{48,32},{1,17},{17,1},{33,49},{49,33},{2,18}... | collective-permute-start | bytes 73736 | tf_op jit(solution)/shard_map/ppermute | solution.py:642
  27.2 3.9 %collective-permute-start.2 = (f32[32,128]{1,0:T(8,128)S(1)}, f32[32,128]{1,0:T(8,128)S(1)}, u32[]{:S(2)}, u32[]{:S(2)}) collective-permute-start(f32[32,128]{1,0:T(8,128)S(1)} %get-tuple-element.87.refs_3_), channel_id=1, source_target_pairs={{1,2},{2,1},{3,4},{4,3},{5,6},{6,5},{7,8},{8,7},{9,10},{10,9},{11,... | collective-permute-start | bytes 49160 | tf_op jit(solution)/shard_map/ppermute | solution.py:641
  31.7 2.0 %shard_map.77.refs_14_ = f32[128,128]{1,0:T(8,128)S(1)} custom-call(f32[1536,128]{1,0:T(8,128)S(1)} %get-tuple-element.84.field.refs_0_, s32[256]{0:T(256)S(1)} %bitcast.28), custom_call_target="tpu_custom_call" | custom-call | flops 8000000 | bytes 4194304 | tf_op jit(solution)/shard_map/pallas_call | solution.py:633
  34.3 2.0 %shard_map.78 = (f32[1536,128]{1,0:T(8,128)S(1)}, f32[40,128]{1,0:T(8,128)S(1)}, f32[32,128]{1,0:T(8,128)S(1)}, f32[32,128]{1,0:T(8,128)S(1)}, f32[48,128]{1,0:T(8,128)S(1)}) custom-call(f32[1536,128]{1,0:T(8,128)S(1)} %get-tuple-element.84.field.refs_0_, f32[48,128]{1,0:T(8,128)S(1)} %get-tuple-element.85.refs_1_, f32[32,128]{1,0:T(8,128)S(1)} %get-tuple-element.86.refs_2_, ...), custom_call_target="tpu_custom_call" | custom-call | tf_op jit(solution)/shard_map/pallas_call | solution.py:649
  36.3 1.9 %collective-permute-start.5 = (f32[40,128]{1,0:T(8,128)S(1)}, f32[40,128]{1,0:T(8,128)S(1)}, u32[]{:S(2)}, u32[]{:S(2)}) collective-permute-start(f32[40,128]{1,0:T(8,128)S(1)} %get-tuple-element.95), channel_id=1, source_target_pairs={{0,67},{1,66},{2,65},{3,64},{4,71},{5,70},{6,69},{7,68},{8,75},{9,... | collective-permute-start | bytes 61448 | tf_op jit(solution)/shard_map/ppermute | solution.py:606
  38.2 2.6 %shard_map.79 = (f32[1536,128]{1,0:T(8,128)S(1)}, f32[48,128]{1,0:T(8,128)S(1)}) custom-call(f32[1536,128]{1,0:T(8,128)S(1)} %get-tuple-element.96.refs_0_, f32[1536,128]{1,0:T(8,128)S(1)} %get-tuple-element.75.refs_0_.refs_1_, f32[232,128]{1,0:T(8,128)S(1)} %constant_dynamic-update-slice_fusion.refs_1_.refs_13_.refs_2_), custom_call_target="tpu_custom_call" | custom-call | flops 20000000 | bytes 8388608 | tf_op jit(solution)/shard_map/pallas_call | solution.py:608
  41.6 5.3 %all-to-all-start.1 = ((f32[64,16,128]{2,1,0:T(8,128)}), f32[64,16,128]{2,1,0:T(8,128)S(1)}, u32[]{:S(2)}, u32[]{:S(2)}) async-start(f32[64,16,128]{2,1,0:T(8,128)} %bitcast.13), calls=%async_computation.1 | async-start | bytes 1048576 | tf_op jit(solution)/shard_map/all_to_all | solution.py:629
  47.6 3.9 %collective-permute-start.8 = (f32[48,128]{1,0:T(8,128)S(1)}, f32[48,128]{1,0:T(8,128)S(1)}, u32[]{:S(2)}, u32[]{:S(2)}) collective-permute-start(f32[48,128]{1,0:T(8,128)S(1)} %get-tuple-element.108.refs_4_), channel_id=1, source_target_pairs={{0,16},{16,0},{32,48},{48,32},{1,17},{17,1},{33,49},{49,33},{2,18}... | collective-permute-start | bytes 73736 | tf_op jit(solution)/shard_map/ppermute | solution.py:642
  51.5 3.9 %collective-permute-start.7 = (f32[32,128]{1,0:T(8,128)S(1)}, f32[32,128]{1,0:T(8,128)S(1)}, u32[]{:S(2)}, u32[]{:S(2)}) collective-permute-start(f32[32,128]{1,0:T(8,128)S(1)} %get-tuple-element.107.refs_3_), channel_id=1, source_target_pairs={{1,2},{2,1},{3,4},{4,3},{5,6},{6,5},{7,8},{8,7},{9,10},{10,9},{11,... | collective-permute-start | bytes 49160 | tf_op jit(solution)/shard_map/ppermute | solution.py:641
  55.4 2.0 %shard_map.81.refs_14_ = f32[128,128]{1,0:T(8,128)S(1)} custom-call(f32[1536,128]{1,0:T(8,128)S(1)} %get-tuple-element.104.field.refs_0_, s32[256]{0:T(256)S(1)} %bitcast.30), custom_call_target="tpu_custom_call" | custom-call | flops 8000000 | bytes 4194304 | tf_op jit(solution)/shard_map/pallas_call | solution.py:633
  57.4 1.5 %all-to-all-done.1 = f32[64,16,128]{2,1,0:T(8,128)S(1)} async-done(((f32[64,16,128]{2,1,0:T(8,128)}), f32[64,16,128]{2,1,0:T(8,128)S(1)}, u32[]{:S(2)}, u32[]{:S(2)}) %all-to-all-start.1) | async-done | bytes 524320 | tf_op jit(solution)/shard_map/all_to_all | solution.py:629
  58.9 2.0 %shard_map.82 = (f32[1536,128]{1,0:T(8,128)S(1)}, f32[40,128]{1,0:T(8,128)S(1)}, f32[32,128]{1,0:T(8,128)S(1)}, f32[32,128]{1,0:T(8,128)S(1)}, f32[48,128]{1,0:T(8,128)S(1)}) custom-call(f32[1536,128]{1,0:T(8,128)S(1)} %get-tuple-element.104.field.refs_0_, f32[48,128]{1,0:T(8,128)S(1)} %get-tuple-element.105.refs_1_, ...), custom_call_target="tpu_custom_call" | custom-call | tf_op jit(solution)/shard_map/pallas_call | solution.py:649
  60.9 2.0 %collective-permute-start.10 = (f32[40,128]{1,0:T(8,128)S(1)}, f32[40,128]{1,0:T(8,128)S(1)}, u32[]{:S(2)}, u32[]{:S(2)}) collective-permute-start(f32[40,128]{1,0:T(8,128)S(1)} %get-tuple-element.111), channel_id=1, source_target_pairs={{0,67},{1,66},{2,65},{3,64},{4,71},{5,70},{6,69},{7,68},{8,75},{9,... | collective-permute-start | bytes 61448 | tf_op jit(solution)/shard_map/ppermute | solution.py:606
  62.9 2.6 %shard_map.83 = (f32[1536,128]{1,0:T(8,128)S(1)}, f32[48,128]{1,0:T(8,128)S(1)}) custom-call(f32[1536,128]{1,0:T(8,128)S(1)} %get-tuple-element.112.refs_0_.refs_1_, f32[232,128]{1,0:T(8,128)S(1)} %constant_dynamic-update-slice_fusion.refs_1_.refs_13_.refs_2_), custom_call_target="tpu_custom_call" | custom-call | flops 20000000 | bytes 8388608 | tf_op jit(solution)/shard_map/pallas_call | solution.py:608
  66.2 5.2 %all-to-all-start.2 = ((f32[64,16,128]{2,1,0:T(8,128)}), f32[64,16,128]{2,1,0:T(8,128)S(1)}, u32[]{:S(2)}, u32[]{:S(2)}) async-start(f32[64,16,128]{2,1,0:T(8,128)} %bitcast.15), calls=%async_computation.2 | async-start | bytes 1048576 | tf_op jit(solution)/shard_map/all_to_all | solution.py:629
  72.1 3.9 %collective-permute-start.13 = (f32[48,128]{1,0:T(8,128)S(1)}, f32[48,128]{1,0:T(8,128)S(1)}, u32[]{:S(2)}, u32[]{:S(2)}) collective-permute-start(f32[48,128]{1,0:T(8,128)S(1)} %get-tuple-element.124.refs_4_), channel_id=1, source_target_pairs={{0,16},{16,0},{32,48},{48,32},{1,17},{17,1},{33,49},{49,33},{2,18}... | collective-permute-start | bytes 73736 | tf_op jit(solution)/shard_map/ppermute | solution.py:642
  76.0 3.9 %collective-permute-start.12 = (f32[32,128]{1,0:T(8,128)S(1)}, f32[32,128]{1,0:T(8,128)S(1)}, u32[]{:S(2)}, u32[]{:S(2)}) collective-permute-start(f32[32,128]{1,0:T(8,128)S(1)} %get-tuple-element.123.refs_3_), channel_id=1, source_target_pairs={{1,2},{2,1},{3,4},{4,3},{5,6},{6,5},{7,8},{8,7},{9,10},{10,9},{11,... | collective-permute-start | bytes 49160 | tf_op jit(solution)/shard_map/ppermute | solution.py:641
  79.9 2.0 %shard_map.85.refs_14_ = f32[128,128]{1,0:T(8,128)S(1)} custom-call(f32[1536,128]{1,0:T(8,128)S(1)} %get-tuple-element.120.field.refs_0_, s32[256]{0:T(256)S(1)} %bitcast.32), custom_call_target="tpu_custom_call" | custom-call | flops 8000000 | bytes 4194304 | tf_op jit(solution)/shard_map/pallas_call | solution.py:633
  83.4 2.0 %shard_map.86 = (f32[1536,128]{1,0:T(8,128)S(1)}, f32[40,128]{1,0:T(8,128)S(1)}, f32[32,128]{1,0:T(8,128)S(1)}, f32[32,128]{1,0:T(8,128)S(1)}, f32[48,128]{1,0:T(8,128)S(1)}) custom-call(f32[1536,128]{1,0:T(8,128)S(1)} %get-tuple-element.120.field.refs_0_, f32[48,128]{1,0:T(8,128)S(1)} %get-tuple-element.121.refs_1_, ...), custom_call_target="tpu_custom_call" | custom-call | tf_op jit(solution)/shard_map/pallas_call | solution.py:649
  85.4 1.9 %collective-permute-start.15 = (f32[40,128]{1,0:T(8,128)S(1)}, f32[40,128]{1,0:T(8,128)S(1)}, u32[]{:S(2)}, u32[]{:S(2)}) collective-permute-start(f32[40,128]{1,0:T(8,128)S(1)} %get-tuple-element.127), channel_id=1, source_target_pairs={{0,67},{1,66},{2,65},{3,64},{4,71},{5,70},{6,69},{7,68},{8,75},{9,... | collective-permute-start | bytes 61448 | tf_op jit(solution)/shard_map/ppermute | solution.py:606
  87.3 2.6 %shard_map.87 = (f32[1536,128]{1,0:T(8,128)S(1)}, f32[48,128]{1,0:T(8,128)S(1)}) custom-call(f32[1536,128]{1,0:T(8,128)S(1)} %get-tuple-element.128.refs_0_, f32[1536,128]{1,0:T(8,128)S(1)} %get-tuple-element.112.refs_0_.refs_1_, f32[232,128]{1,0:T(8,128)S(1)} %constant_dynamic-update-slice_fusion.refs_1_.refs_13_.refs_2_), custom_call_target="tpu_custom_call" | custom-call | flops 20000000 | bytes 8388608 | tf_op jit(solution)/shard_map/pallas_call | solution.py:608
  90.7 5.3 %all-to-all-start.3 = ((f32[64,16,128]{2,1,0:T(8,128)}), f32[64,16,128]{2,1,0:T(8,128)S(1)}, u32[]{:S(2)}, u32[]{:S(2)}) async-start(f32[64,16,128]{2,1,0:T(8,128)} %bitcast.17), calls=%async_computation.3 | async-start | bytes 1048576 | tf_op jit(solution)/shard_map/all_to_all | solution.py:629
  96.7 3.9 %collective-permute-start.18 = (f32[48,128]{1,0:T(8,128)S(1)}, f32[48,128]{1,0:T(8,128)S(1)}, u32[]{:S(2)}, u32[]{:S(2)}) collective-permute-start(f32[48,128]{1,0:T(8,128)S(1)} %get-tuple-element.140.refs_4_), channel_id=1, source_target_pairs={{0,16},{16,0},{32,48},{48,32},{1,17},{17,1},{33,49},{49,33},{2,18}... | collective-permute-start | bytes 73736 | tf_op jit(solution)/shard_map/ppermute | solution.py:642
  100.5 3.9 %collective-permute-start.17 = (f32[32,128]{1,0:T(8,128)S(1)}, f32[32,128]{1,0:T(8,128)S(1)}, u32[]{:S(2)}, u32[]{:S(2)}) collective-permute-start(f32[32,128]{1,0:T(8,128)S(1)} %get-tuple-element.139.refs_3_), channel_id=1, source_target_pairs={{1,2},{2,1},{3,4},{4,3},{5,6},{6,5},{7,8},{8,7},{9,10},{10,9},{11,... | collective-permute-start | bytes 49160 | tf_op jit(solution)/shard_map/ppermute | solution.py:641
  104.5 1.7 %collective-permute-done.17.refs_6_ = f32[32,128]{1,0:T(8,128)S(1)} collective-permute-done((f32[32,128]{1,0:T(8,128)S(1)}, f32[32,128]{1,0:T(8,128)S(1)}, u32[]{:S(2)}, u32[]{:S(2)}) %collective-permute-start.17) | collective-permute-done | bytes 16416 | tf_op jit(solution)/shard_map/ppermute | solution.py:641
  106.2 1.8 %all-to-all-done.3 = f32[64,16,128]{2,1,0:T(8,128)S(1)} async-done(((f32[64,16,128]{2,1,0:T(8,128)}), f32[64,16,128]{2,1,0:T(8,128)S(1)}, u32[]{:S(2)}, u32[]{:S(2)}) %all-to-all-start.3) | async-done | bytes 524320 | tf_op jit(solution)/shard_map/all_to_all | solution.py:629
  108.0 2.8 %shard_map.89 = f32[1536,128]{1,0:T(8,128)} custom-call(f32[1536,128]{1,0:T(8,128)S(1)} %get-tuple-element.136.refs_0_, f32[48,128]{1,0:T(8,128)S(1)} %get-tuple-element.137.refs_1_, f32[32,128]{1,0:T(8,128)S(1)} %get-tuple-element.138.refs_2_, f32[32,128]{1,0:T(8,128)S(1)} %get-tuple-element.139.refs_3_, f32[48,128]{1,0:T(8,128)S(1)} %get-tuple-element.140.refs_4_, ...), custom_call_target="tpu_custom_call" | custom-call | tf_op jit(solution)/shard_map/pallas_call | solution.py:649
  (65 shorter events, 10.9 us)
Async XLA Ops:
  0.1 0.7 copy-start.2
  0.1 0.7 copy-start.3
  0.1 0.7 copy-start.5
  0.1 0.7 copy-start.1
  0.1 0.7 copy-start.4
  0.8 1.1 %copy-start = (f32[4,1,4,96,128]{4,3,2,1,0:T(8,128)S(1)}, f32[4,1,4,96,128]{4,3,2,1,0:T(8,128)}, u32[]{:S(2)}) copy-start(f32[4,1,4,96,128]{4,3,2,1,0:T(8,128)} %param.7) | copy-start | bytes 2359300
  5.6 7.1 %collective-permute-start.1 = (f32[32,128]{1,0:T(8,128)S(1)}, f32[32,128]{1,0:T(8,128)S(1)}, u32[]{:S(2)}, u32[]{:S(2)}) collective-permute-start(f32[32,128]{1,0:T(8,128)S(1)} %get-tuple-element.86.refs_2_), channel_id=1, source_target_pairs={{0,1},{1,0},{2,3},{3,2},{4,5},{5,4},{6,7},{7,6},{8,9},{9,8},{10,11... | collective-permute-start | bytes 49160 | tf_op jit(solution)/shard_map/ppermute | solution.py:617
  7.1 5.6 %collective-permute-start = (f32[40,128]{1,0:T(8,128)S(1)}, f32[40,128]{1,0:T(8,128)S(1)}, u32[]{:S(2)}, u32[]{:S(2)}) collective-permute-start(f32[40,128]{1,0:T(8,128)S(1)} %get-tuple-element.74), channel_id=1, source_target_pairs={{0,67},{1,66},{2,65},{3,64},{4,71},{5,70},{6,69},{7,68},{8,75},{9,... | collective-permute-start | bytes 61448 | tf_op jit(solution)/shard_map/ppermute | solution.py:606
  13.5 9.0 %copy-start.6 = (s32[1,1,1,896]{3,2,1,0:T(1,128)S(1)}, s32[1,1,1,896]{3,2,1,0:T(1,128)}, u32[]{:S(2)}) copy-start(s32[1,1,1,896]{3,2,1,0:T(1,128)} %param.13) | copy-start | bytes 10756
  13.5 20.8 %all-to-all-start = ((f32[64,16,128]{2,1,0:T(8,128)}), f32[64,16,128]{2,1,0:T(8,128)S(1)}, u32[]{:S(2)}, u32[]{:S(2)}) async-start(f32[64,16,128]{2,1,0:T(8,128)} %bitcast.10), calls=%async_computation | async-start | bytes 1048576 | tf_op jit(solution)/shard_map/all_to_all | solution.py:629
  22.6 11.0 %collective-permute-start.4 = (f32[48,128]{1,0:T(8,128)S(1)}, f32[48,128]{1,0:T(8,128)S(1)}, u32[]{:S(2)}, u32[]{:S(2)}) collective-permute-start(f32[48,128]{1,0:T(8,128)S(1)} %get-tuple-element.88.refs_4_), channel_id=1, source_target_pairs={{16,32},{32,16},{17,33},{33,17},{18,34},{34,18},{19,35},{35,19},{2... | collective-permute-start | bytes 73736 | tf_op jit(solution)/shard_map/ppermute | solution.py:643
  23.3 10.4 %collective-permute-start.3 = (f32[48,128]{1,0:T(8,128)S(1)}, f32[48,128]{1,0:T(8,128)S(1)}, u32[]{:S(2)}, u32[]{:S(2)}) collective-permute-start(f32[48,128]{1,0:T(8,128)S(1)} %get-tuple-element.88.refs_4_), channel_id=1, source_target_pairs={{0,16},{16,0},{32,48},{48,32},{1,17},{17,1},{33,49},{49,33},{2,18}... | collective-permute-start | bytes 73736 | tf_op jit(solution)/shard_map/ppermute | solution.py:642
  27.2 6.5 %collective-permute-start.2 = (f32[32,128]{1,0:T(8,128)S(1)}, f32[32,128]{1,0:T(8,128)S(1)}, u32[]{:S(2)}, u32[]{:S(2)}) collective-permute-start(f32[32,128]{1,0:T(8,128)S(1)} %get-tuple-element.87.refs_3_), channel_id=1, source_target_pairs={{1,2},{2,1},{3,4},{4,3},{5,6},{6,5},{7,8},{8,7},{9,10},{10,9},{11,... | collective-permute-start | bytes 49160 | tf_op jit(solution)/shard_map/ppermute | solution.py:641
  36.3 4.5 %collective-permute-start.5 = (f32[40,128]{1,0:T(8,128)S(1)}, f32[40,128]{1,0:T(8,128)S(1)}, u32[]{:S(2)}, u32[]{:S(2)}) collective-permute-start(f32[40,128]{1,0:T(8,128)S(1)} %get-tuple-element.95), channel_id=1, source_target_pairs={{0,67},{1,66},{2,65},{3,64},{4,71},{5,70},{6,69},{7,68},{8,75},{9,... | collective-permute-start | bytes 61448 | tf_op jit(solution)/shard_map/ppermute | solution.py:606
  38.2 2.6 %collective-permute-start.6 = (f32[32,128]{1,0:T(8,128)S(1)}, f32[32,128]{1,0:T(8,128)S(1)}, u32[]{:S(2)}, u32[]{:S(2)}) collective-permute-start(f32[32,128]{1,0:T(8,128)S(1)} %get-tuple-element.106.refs_2_), channel_id=1, source_target_pairs={{0,1},{1,0},{2,3},{3,2},{4,5},{5,4},{6,7},{7,6},{8,9},{9,8},{10,11... | collective-permute-start | bytes 49160 | tf_op jit(solution)/shard_map/ppermute | solution.py:617
  41.6 17.3 %all-to-all-start.1 = ((f32[64,16,128]{2,1,0:T(8,128)}), f32[64,16,128]{2,1,0:T(8,128)S(1)}, u32[]{:S(2)}, u32[]{:S(2)}) async-start(f32[64,16,128]{2,1,0:T(8,128)} %bitcast.13), calls=%async_computation.1 | async-start | bytes 1048576 | tf_op jit(solution)/shard_map/all_to_all | solution.py:629
  46.9 10.5 %collective-permute-start.9 = (f32[48,128]{1,0:T(8,128)S(1)}, f32[48,128]{1,0:T(8,128)S(1)}, u32[]{:S(2)}, u32[]{:S(2)}) collective-permute-start(f32[48,128]{1,0:T(8,128)S(1)} %get-tuple-element.108.refs_4_), channel_id=1, source_target_pairs={{16,32},{32,16},{17,33},{33,17},{18,34},{34,18},{19,35},{35,19},{2... | collective-permute-start | bytes 73736 | tf_op jit(solution)/shard_map/ppermute | solution.py:643
  47.6 9.8 %collective-permute-start.8 = (f32[48,128]{1,0:T(8,128)S(1)}, f32[48,128]{1,0:T(8,128)S(1)}, u32[]{:S(2)}, u32[]{:S(2)}) collective-permute-start(f32[48,128]{1,0:T(8,128)S(1)} %get-tuple-element.108.refs_4_), channel_id=1, source_target_pairs={{0,16},{16,0},{32,48},{48,32},{1,17},{17,1},{33,49},{49,33},{2,18}... | collective-permute-start | bytes 73736 | tf_op jit(solution)/shard_map/ppermute | solution.py:642
  51.5 5.9 %collective-permute-start.7 = (f32[32,128]{1,0:T(8,128)S(1)}, f32[32,128]{1,0:T(8,128)S(1)}, u32[]{:S(2)}, u32[]{:S(2)}) collective-permute-start(f32[32,128]{1,0:T(8,128)S(1)} %get-tuple-element.107.refs_3_), channel_id=1, source_target_pairs={{1,2},{2,1},{3,4},{4,3},{5,6},{6,5},{7,8},{8,7},{9,10},{10,9},{11,... | collective-permute-start | bytes 49160 | tf_op jit(solution)/shard_map/ppermute | solution.py:641
  60.9 4.6 %collective-permute-start.10 = (f32[40,128]{1,0:T(8,128)S(1)}, f32[40,128]{1,0:T(8,128)S(1)}, u32[]{:S(2)}, u32[]{:S(2)}) collective-permute-start(f32[40,128]{1,0:T(8,128)S(1)} %get-tuple-element.111), channel_id=1, source_target_pairs={{0,67},{1,66},{2,65},{3,64},{4,71},{5,70},{6,69},{7,68},{8,75},{9,... | collective-permute-start | bytes 61448 | tf_op jit(solution)/shard_map/ppermute | solution.py:606
  62.9 2.6 %collective-permute-start.11 = (f32[32,128]{1,0:T(8,128)S(1)}, f32[32,128]{1,0:T(8,128)S(1)}, u32[]{:S(2)}, u32[]{:S(2)}) collective-permute-start(f32[32,128]{1,0:T(8,128)S(1)} %get-tuple-element.122.refs_2_), channel_id=1, source_target_pairs={{0,1},{1,0},{2,3},{3,2},{4,5},{5,4},{6,7},{7,6},{8,9},{9,8},{10,11... | collective-permute-start | bytes 49160 | tf_op jit(solution)/shard_map/ppermute | solution.py:617
  66.2 17.2 %all-to-all-start.2 = ((f32[64,16,128]{2,1,0:T(8,128)}), f32[64,16,128]{2,1,0:T(8,128)S(1)}, u32[]{:S(2)}, u32[]{:S(2)}) async-start(f32[64,16,128]{2,1,0:T(8,128)} %bitcast.15), calls=%async_computation.2 | async-start | bytes 1048576 | tf_op jit(solution)/shard_map/all_to_all | solution.py:629
  71.4 10.5 %collective-permute-start.14 = (f32[48,128]{1,0:T(8,128)S(1)}, f32[48,128]{1,0:T(8,128)S(1)}, u32[]{:S(2)}, u32[]{:S(2)}) collective-permute-start(f32[48,128]{1,0:T(8,128)S(1)} %get-tuple-element.124.refs_4_), channel_id=1, source_target_pairs={{16,32},{32,16},{17,33},{33,17},{18,34},{34,18},{19,35},{35,19},{2... | collective-permute-start | bytes 73736 | tf_op jit(solution)/shard_map/ppermute | solution.py:643
  72.1 9.8 %collective-permute-start.13 = (f32[48,128]{1,0:T(8,128)S(1)}, f32[48,128]{1,0:T(8,128)S(1)}, u32[]{:S(2)}, u32[]{:S(2)}) collective-permute-start(f32[48,128]{1,0:T(8,128)S(1)} %get-tuple-element.124.refs_4_), channel_id=1, source_target_pairs={{0,16},{16,0},{32,48},{48,32},{1,17},{17,1},{33,49},{49,33},{2,18}... | collective-permute-start | bytes 73736 | tf_op jit(solution)/shard_map/ppermute | solution.py:642
  76.0 5.9 %collective-permute-start.12 = (f32[32,128]{1,0:T(8,128)S(1)}, f32[32,128]{1,0:T(8,128)S(1)}, u32[]{:S(2)}, u32[]{:S(2)}) collective-permute-start(f32[32,128]{1,0:T(8,128)S(1)} %get-tuple-element.123.refs_3_), channel_id=1, source_target_pairs={{1,2},{2,1},{3,4},{4,3},{5,6},{6,5},{7,8},{8,7},{9,10},{10,9},{11,... | collective-permute-start | bytes 49160 | tf_op jit(solution)/shard_map/ppermute | solution.py:641
  85.4 4.5 %collective-permute-start.15 = (f32[40,128]{1,0:T(8,128)S(1)}, f32[40,128]{1,0:T(8,128)S(1)}, u32[]{:S(2)}, u32[]{:S(2)}) collective-permute-start(f32[40,128]{1,0:T(8,128)S(1)} %get-tuple-element.127), channel_id=1, source_target_pairs={{0,67},{1,66},{2,65},{3,64},{4,71},{5,70},{6,69},{7,68},{8,75},{9,... | collective-permute-start | bytes 61448 | tf_op jit(solution)/shard_map/ppermute | solution.py:606
  87.3 2.6 %collective-permute-start.16 = (f32[32,128]{1,0:T(8,128)S(1)}, f32[32,128]{1,0:T(8,128)S(1)}, u32[]{:S(2)}, u32[]{:S(2)}) collective-permute-start(f32[32,128]{1,0:T(8,128)S(1)} %get-tuple-element.138.refs_2_), channel_id=1, source_target_pairs={{0,1},{1,0},{2,3},{3,2},{4,5},{5,4},{6,7},{7,6},{8,9},{9,8},{10,11... | collective-permute-start | bytes 49160 | tf_op jit(solution)/shard_map/ppermute | solution.py:617
  90.7 17.3 %all-to-all-start.3 = ((f32[64,16,128]{2,1,0:T(8,128)}), f32[64,16,128]{2,1,0:T(8,128)S(1)}, u32[]{:S(2)}, u32[]{:S(2)}) async-start(f32[64,16,128]{2,1,0:T(8,128)} %bitcast.17), calls=%async_computation.3 | async-start | bytes 1048576 | tf_op jit(solution)/shard_map/all_to_all | solution.py:629
  96.0 10.2 %collective-permute-start.19 = (f32[48,128]{1,0:T(8,128)S(1)}, f32[48,128]{1,0:T(8,128)S(1)}, u32[]{:S(2)}, u32[]{:S(2)}) collective-permute-start(f32[48,128]{1,0:T(8,128)S(1)} %get-tuple-element.140.refs_4_), channel_id=1, source_target_pairs={{16,32},{32,16},{17,33},{33,17},{18,34},{34,18},{19,35},{35,19},{2... | collective-permute-start | bytes 73736 | tf_op jit(solution)/shard_map/ppermute | solution.py:643
  96.7 9.5 %collective-permute-start.18 = (f32[48,128]{1,0:T(8,128)S(1)}, f32[48,128]{1,0:T(8,128)S(1)}, u32[]{:S(2)}, u32[]{:S(2)}) collective-permute-start(f32[48,128]{1,0:T(8,128)S(1)} %get-tuple-element.140.refs_4_), channel_id=1, source_target_pairs={{0,16},{16,0},{32,48},{48,32},{1,17},{17,1},{33,49},{49,33},{2,18}... | collective-permute-start | bytes 73736 | tf_op jit(solution)/shard_map/ppermute | solution.py:642
  100.5 5.6 %collective-permute-start.17 = (f32[32,128]{1,0:T(8,128)S(1)}, f32[32,128]{1,0:T(8,128)S(1)}, u32[]{:S(2)}, u32[]{:S(2)}) collective-permute-start(f32[32,128]{1,0:T(8,128)S(1)} %get-tuple-element.139.refs_3_), channel_id=1, source_target_pairs={{1,2},{2,1},{3,4},{4,3},{5,6},{6,5},{7,8},{8,7},{9,10},{10,9},{11,... | collective-permute-start | bytes 49160 | tf_op jit(solution)/shard_map/ppermute | solution.py:641

commit v7 on v6

--- a/solution.py
+++ b/solution.py
@@ -488,7 +488,7 @@
 
 
 def seat(block):
-    return lax.bitwise_and(block, 15) * 4 + lax.shift_right_logical(block, 4)
+    return lax.bitwise_and(block, 1) * 32 + lax.bitwise_and(lax.shift_right_logical(block, 1), 7) * 4 + lax.shift_right_logical(block, 4)
 
 
 def pack_kernel(message, _, buffer, staged, sems):
@@ -627,7 +627,7 @@
         )(over, buffer)
         buffer, own_a, own_b, own_strips, part = lax.optimization_barrier((buffer, edge_a, edge_b, strips, part))
         received = lax.all_to_all(
-            buffer.reshape(peers, ROWS, LANES), ("lon_hi", "core", "colat"), split_axis=0, concat_axis=0, tiled=True
+            buffer.reshape(peers, ROWS, LANES), ("core", "lon_hi", "colat"), split_axis=0, concat_axis=0, tiled=True
         ).reshape(peers * ROWS, LANES)
         if not final:
             corners = pl.pallas_call(

time: 111 us -> 111 us (level)
  no operation moved by 1% of the time
where the time goes in v7:
time: 111 us; the launch traced here: 110 us
  starting transfers between devices  68.6 us (62%)
  Pallas kernels  32.3 us (29%)
  waiting for transfers between devices  6.24 us (6%)
  local copies, waits for them, and re-layouts  2.19 us (2%)
    all_to_all x4, starting transfers between devices, on_device(): lax.all_to_all(buffer.reshape(peers, ROWS, LANES), ('core', 'lon_hi', 'co...  23.8 us
    ppermute x4, starting transfers between devices, on_device(): strip_a = lax.ppermute(own_strips, 'colat', pairs(lat_blocks, 0))  15.5 us
    ppermute x4, starting transfers between devices, on_device(): lon_b = lax.ppermute(own_b, lon_axes, pairs(lon_blocks, 1))  15.1 us
    pallas_call x4, Pallas kernels, on_device(): pl.pallas_call(functools.partial(inner_kernel, second, lon_cells, consts)...  10.3 us
    ppermute x4, starting transfers between devices, on_device(): over = lax.ppermute(sent, ('panel',) + lon_axes, crossing(lon_blocks))  9.05 us
    pallas_call x4, Pallas kernels, on_device(): pl.pallas_call(functools.partial(outer_kernel, second, final, lon_cells,...  8.79 us
    pallas_call x3, Pallas kernels, on_device(): pl.pallas_call(rows_kernel, out_shape=f32(8 * ROWS, LANES), in_specs=[vme...  5.99 us
    all_to_all x4, waiting for transfers between devices, on_device(): lax.all_to_all(buffer.reshape(peers, ROWS, LANES), ('core', 'lon_hi', 'co...  4.49 us
  transfers between devices with their start and end apart: 24, of which 5 were waited for; matrix products, arithmetic and copies ran while one was open for 1% of the time, Pallas kernels for 15%

profile of v7, /device:TPU:1, one launch (start us, length us, event | category | flops | bytes accessed | tf_op | source)
XLA Modules:
  0.0 110.1 jit_solution(14602526783154686348)
XLA Ops:
  1.9 3.7 %shard_map.73 = (f32[1536,128]{1,0:T(8,128)S(1)}, f32[32,128]{1,0:T(8,128)S(1)}, f32[32,128]{1,0:T(8,128)S(1)}, f32[48,128]{1,0:T(8,128)S(1)}, f32[1024,128]{1,0...) custom-call(f32[1536,128]{1,0:T(8,128)S(1)} %bitcast.26, s32[256]{0:T(256)S(1)} %bitcast.27, ...), custom_call_target="tpu_custom_call" | custom-call | tf_op jit(solution)/shard_map/pallas_call | solution.py:581
  5.6 1.5 %collective-permute-start.1 = (f32[32,128]{1,0:T(8,128)S(1)}, f32[32,128]{1,0:T(8,128)S(1)}, u32[]{:S(2)}, u32[]{:S(2)}) collective-permute-start(f32[32,128]{1,0:T(8,128)S(1)} %get-tuple-element.86.refs_2_), channel_id=1, source_target_pairs={{0,1},{1,0},{2,3},{3,2},{4,5},{5,4},{6,7},{7,6},{8,9},{9,8},{10,11... | collective-permute-start | bytes 49160 | tf_op jit(solution)/shard_map/ppermute | solution.py:617
  7.1 2.5 %collective-permute-start = (f32[40,128]{1,0:T(8,128)S(1)}, f32[40,128]{1,0:T(8,128)S(1)}, u32[]{:S(2)}, u32[]{:S(2)}) collective-permute-start(f32[40,128]{1,0:T(8,128)S(1)} %get-tuple-element.74), channel_id=1, source_target_pairs={{0,67},{1,66},{2,65},{3,64},{4,71},{5,70},{6,69},{7,68},{8,75},{9,... | collective-permute-start | bytes 61448 | tf_op jit(solution)/shard_map/ppermute | solution.py:606
  10.1 2.6 %shard_map.74 = (f32[1536,128]{1,0:T(8,128)S(1)}, f32[48,128]{1,0:T(8,128)S(1)}) custom-call(f32[1536,128]{1,0:T(8,128)S(1)} %get-tuple-element.75.refs_0_.refs_1_, f32[232,128]{1,0:T(8,128)S(1)} %constant_dynamic-update-slice_fusion.refs_1_.refs_13_.refs_2_), custom_call_target="tpu_custom_call" | custom-call | flops 20000000 | bytes 8388608 | tf_op jit(solution)/shard_map/pallas_call | solution.py:608
  13.5 9.0 %all-to-all-start = ((f32[64,16,128]{2,1,0:T(8,128)}), f32[64,16,128]{2,1,0:T(8,128)S(1)}, u32[]{:S(2)}, u32[]{:S(2)}) async-start(f32[64,16,128]{2,1,0:T(8,128)} %bitcast.10), calls=%async_computation | async-start | bytes 1048576 | tf_op jit(solution)/shard_map/all_to_all | solution.py:629
  23.4 3.9 %collective-permute-start.3 = (f32[48,128]{1,0:T(8,128)S(1)}, f32[48,128]{1,0:T(8,128)S(1)}, u32[]{:S(2)}, u32[]{:S(2)}) collective-permute-start(f32[48,128]{1,0:T(8,128)S(1)} %get-tuple-element.88.refs_4_), channel_id=1, source_target_pairs={{0,16},{16,0},{32,48},{48,32},{1,17},{17,1},{33,49},{49,33},{2,18}... | collective-permute-start | bytes 73736 | tf_op jit(solution)/shard_map/ppermute | solution.py:642
  27.3 3.8 %collective-permute-start.2 = (f32[32,128]{1,0:T(8,128)S(1)}, f32[32,128]{1,0:T(8,128)S(1)}, u32[]{:S(2)}, u32[]{:S(2)}) collective-permute-start(f32[32,128]{1,0:T(8,128)S(1)} %get-tuple-element.87.refs_3_), channel_id=1, source_target_pairs={{1,2},{2,1},{3,4},{4,3},{5,6},{6,5},{7,8},{8,7},{9,10},{10,9},{11,... | collective-permute-start | bytes 49160 | tf_op jit(solution)/shard_map/ppermute | solution.py:641
  31.7 2.0 %shard_map.77.refs_14_ = f32[128,128]{1,0:T(8,128)S(1)} custom-call(f32[1536,128]{1,0:T(8,128)S(1)} %get-tuple-element.84.field.refs_0_, s32[256]{0:T(256)S(1)} %bitcast.28), custom_call_target="tpu_custom_call" | custom-call | flops 8000000 | bytes 4194304 | tf_op jit(solution)/shard_map/pallas_call | solution.py:633
  34.1 2.0 %shard_map.78 = (f32[1536,128]{1,0:T(8,128)S(1)}, f32[40,128]{1,0:T(8,128)S(1)}, f32[32,128]{1,0:T(8,128)S(1)}, f32[32,128]{1,0:T(8,128)S(1)}, f32[48,128]{1,0:T(8,128)S(1)}) custom-call(f32[1536,128]{1,0:T(8,128)S(1)} %get-tuple-element.84.field.refs_0_, f32[48,128]{1,0:T(8,128)S(1)} %get-tuple-element.85.refs_1_, f32[32,128]{1,0:T(8,128)S(1)} %get-tuple-element.86.refs_2_, ...), custom_call_target="tpu_custom_call" | custom-call | tf_op jit(solution)/shard_map/pallas_call | solution.py:649
  36.1 2.1 %collective-permute-start.5 = (f32[40,128]{1,0:T(8,128)S(1)}, f32[40,128]{1,0:T(8,128)S(1)}, u32[]{:S(2)}, u32[]{:S(2)}) collective-permute-start(f32[40,128]{1,0:T(8,128)S(1)} %get-tuple-element.95), channel_id=1, source_target_pairs={{0,67},{1,66},{2,65},{3,64},{4,71},{5,70},{6,69},{7,68},{8,75},{9,... | collective-permute-start | bytes 61448 | tf_op jit(solution)/shard_map/ppermute | solution.py:606
  38.6 2.6 %shard_map.79 = (f32[1536,128]{1,0:T(8,128)S(1)}, f32[48,128]{1,0:T(8,128)S(1)}) custom-call(f32[1536,128]{1,0:T(8,128)S(1)} %get-tuple-element.96.refs_0_, f32[1536,128]{1,0:T(8,128)S(1)} %get-tuple-element.75.refs_0_.refs_1_, f32[232,128]{1,0:T(8,128)S(1)} %constant_dynamic-update-slice_fusion.refs_1_.refs_13_.refs_2_), custom_call_target="tpu_custom_call" | custom-call | flops 20000000 | bytes 8388608 | tf_op jit(solution)/shard_map/pallas_call | solution.py:608
  42.0 5.0 %all-to-all-start.1 = ((f32[64,16,128]{2,1,0:T(8,128)}), f32[64,16,128]{2,1,0:T(8,128)S(1)}, u32[]{:S(2)}, u32[]{:S(2)}) async-start(f32[64,16,128]{2,1,0:T(8,128)} %bitcast.13), calls=%async_computation.1 | async-start | bytes 1048576 | tf_op jit(solution)/shard_map/all_to_all | solution.py:629
  47.7 3.9 %collective-permute-start.8 = (f32[48,128]{1,0:T(8,128)S(1)}, f32[48,128]{1,0:T(8,128)S(1)}, u32[]{:S(2)}, u32[]{:S(2)}) collective-permute-start(f32[48,128]{1,0:T(8,128)S(1)} %get-tuple-element.108.refs_4_), channel_id=1, source_target_pairs={{0,16},{16,0},{32,48},{48,32},{1,17},{17,1},{33,49},{49,33},{2,18}... | collective-permute-start | bytes 73736 | tf_op jit(solution)/shard_map/ppermute | solution.py:642
  51.5 3.8 %collective-permute-start.7 = (f32[32,128]{1,0:T(8,128)S(1)}, f32[32,128]{1,0:T(8,128)S(1)}, u32[]{:S(2)}, u32[]{:S(2)}) collective-permute-start(f32[32,128]{1,0:T(8,128)S(1)} %get-tuple-element.107.refs_3_), channel_id=1, source_target_pairs={{1,2},{2,1},{3,4},{4,3},{5,6},{6,5},{7,8},{8,7},{9,10},{10,9},{11,... | collective-permute-start | bytes 49160 | tf_op jit(solution)/shard_map/ppermute | solution.py:641
  55.4 2.0 %shard_map.81.refs_14_ = f32[128,128]{1,0:T(8,128)S(1)} custom-call(f32[1536,128]{1,0:T(8,128)S(1)} %get-tuple-element.104.field.refs_0_, s32[256]{0:T(256)S(1)} %bitcast.30), custom_call_target="tpu_custom_call" | custom-call | flops 8000000 | bytes 4194304 | tf_op jit(solution)/shard_map/pallas_call | solution.py:633
  58.6 2.0 %shard_map.82 = (f32[1536,128]{1,0:T(8,128)S(1)}, f32[40,128]{1,0:T(8,128)S(1)}, f32[32,128]{1,0:T(8,128)S(1)}, f32[32,128]{1,0:T(8,128)S(1)}, f32[48,128]{1,0:T(8,128)S(1)}) custom-call(f32[1536,128]{1,0:T(8,128)S(1)} %get-tuple-element.104.field.refs_0_, f32[48,128]{1,0:T(8,128)S(1)} %get-tuple-element.105.refs_1_, ...), custom_call_target="tpu_custom_call" | custom-call | tf_op jit(solution)/shard_map/pallas_call | solution.py:649
  60.6 2.2 %collective-permute-start.10 = (f32[40,128]{1,0:T(8,128)S(1)}, f32[40,128]{1,0:T(8,128)S(1)}, u32[]{:S(2)}, u32[]{:S(2)}) collective-permute-start(f32[40,128]{1,0:T(8,128)S(1)} %get-tuple-element.111), channel_id=1, source_target_pairs={{0,67},{1,66},{2,65},{3,64},{4,71},{5,70},{6,69},{7,68},{8,75},{9,... | collective-permute-start | bytes 61448 | tf_op jit(solution)/shard_map/ppermute | solution.py:606
  63.1 2.6 %shard_map.83 = (f32[1536,128]{1,0:T(8,128)S(1)}, f32[48,128]{1,0:T(8,128)S(1)}) custom-call(f32[1536,128]{1,0:T(8,128)S(1)} %get-tuple-element.112.refs_0_.refs_1_, f32[232,128]{1,0:T(8,128)S(1)} %constant_dynamic-update-slice_fusion.refs_1_.refs_13_.refs_2_), custom_call_target="tpu_custom_call" | custom-call | flops 20000000 | bytes 8388608 | tf_op jit(solution)/shard_map/pallas_call | solution.py:608
  66.5 4.8 %all-to-all-start.2 = ((f32[64,16,128]{2,1,0:T(8,128)}), f32[64,16,128]{2,1,0:T(8,128)S(1)}, u32[]{:S(2)}, u32[]{:S(2)}) async-start(f32[64,16,128]{2,1,0:T(8,128)} %bitcast.15), calls=%async_computation.2 | async-start | bytes 1048576 | tf_op jit(solution)/shard_map/all_to_all | solution.py:629
  72.0 3.9 %collective-permute-start.13 = (f32[48,128]{1,0:T(8,128)S(1)}, f32[48,128]{1,0:T(8,128)S(1)}, u32[]{:S(2)}, u32[]{:S(2)}) collective-permute-start(f32[48,128]{1,0:T(8,128)S(1)} %get-tuple-element.124.refs_4_), channel_id=1, source_target_pairs={{0,16},{16,0},{32,48},{48,32},{1,17},{17,1},{33,49},{49,33},{2,18}... | collective-permute-start | bytes 73736 | tf_op jit(solution)/shard_map/ppermute | solution.py:642
  75.9 3.7 %collective-permute-start.12 = (f32[32,128]{1,0:T(8,128)S(1)}, f32[32,128]{1,0:T(8,128)S(1)}, u32[]{:S(2)}, u32[]{:S(2)}) collective-permute-start(f32[32,128]{1,0:T(8,128)S(1)} %get-tuple-element.123.refs_3_), channel_id=1, source_target_pairs={{1,2},{2,1},{3,4},{4,3},{5,6},{6,5},{7,8},{8,7},{9,10},{10,9},{11,... | collective-permute-start | bytes 49160 | tf_op jit(solution)/shard_map/ppermute | solution.py:641
  79.6 2.0 %shard_map.85.refs_14_ = f32[128,128]{1,0:T(8,128)S(1)} custom-call(f32[1536,128]{1,0:T(8,128)S(1)} %get-tuple-element.120.field.refs_0_, s32[256]{0:T(256)S(1)} %bitcast.32), custom_call_target="tpu_custom_call" | custom-call | flops 8000000 | bytes 4194304 | tf_op jit(solution)/shard_map/pallas_call | solution.py:633
  81.6 1.3 %all-to-all-done.2 = f32[64,16,128]{2,1,0:T(8,128)S(1)} async-done(((f32[64,16,128]{2,1,0:T(8,128)}), f32[64,16,128]{2,1,0:T(8,128)S(1)}, u32[]{:S(2)}, u32[]{:S(2)}) %all-to-all-start.2) | async-done | bytes 524320 | tf_op jit(solution)/shard_map/all_to_all | solution.py:629
  82.9 2.0 %shard_map.86 = (f32[1536,128]{1,0:T(8,128)S(1)}, f32[40,128]{1,0:T(8,128)S(1)}, f32[32,128]{1,0:T(8,128)S(1)}, f32[32,128]{1,0:T(8,128)S(1)}, f32[48,128]{1,0:T(8,128)S(1)}) custom-call(f32[1536,128]{1,0:T(8,128)S(1)} %get-tuple-element.120.field.refs_0_, f32[48,128]{1,0:T(8,128)S(1)} %get-tuple-element.121.refs_1_, ...), custom_call_target="tpu_custom_call" | custom-call | tf_op jit(solution)/shard_map/pallas_call | solution.py:649
  84.9 2.1 %collective-permute-start.15 = (f32[40,128]{1,0:T(8,128)S(1)}, f32[40,128]{1,0:T(8,128)S(1)}, u32[]{:S(2)}, u32[]{:S(2)}) collective-permute-start(f32[40,128]{1,0:T(8,128)S(1)} %get-tuple-element.127), channel_id=1, source_target_pairs={{0,67},{1,66},{2,65},{3,64},{4,71},{5,70},{6,69},{7,68},{8,75},{9,... | collective-permute-start | bytes 61448 | tf_op jit(solution)/shard_map/ppermute | solution.py:606
  87.4 2.6 %shard_map.87 = (f32[1536,128]{1,0:T(8,128)S(1)}, f32[48,128]{1,0:T(8,128)S(1)}) custom-call(f32[1536,128]{1,0:T(8,128)S(1)} %get-tuple-element.128.refs_0_, f32[1536,128]{1,0:T(8,128)S(1)} %get-tuple-element.112.refs_0_.refs_1_, f32[232,128]{1,0:T(8,128)S(1)} %constant_dynamic-update-slice_fusion.refs_1_.refs_13_.refs_2_), custom_call_target="tpu_custom_call" | custom-call | flops 20000000 | bytes 8388608 | tf_op jit(solution)/shard_map/pallas_call | solution.py:608
  90.7 4.9 %all-to-all-start.3 = ((f32[64,16,128]{2,1,0:T(8,128)}), f32[64,16,128]{2,1,0:T(8,128)S(1)}, u32[]{:S(2)}, u32[]{:S(2)}) async-start(f32[64,16,128]{2,1,0:T(8,128)} %bitcast.17), calls=%async_computation.3 | async-start | bytes 1048576 | tf_op jit(solution)/shard_map/all_to_all | solution.py:629
  96.3 3.9 %collective-permute-start.18 = (f32[48,128]{1,0:T(8,128)S(1)}, f32[48,128]{1,0:T(8,128)S(1)}, u32[]{:S(2)}, u32[]{:S(2)}) collective-permute-start(f32[48,128]{1,0:T(8,128)S(1)} %get-tuple-element.140.refs_4_), channel_id=1, source_target_pairs={{0,16},{16,0},{32,48},{48,32},{1,17},{17,1},{33,49},{49,33},{2,18}... | collective-permute-start | bytes 73736 | tf_op jit(solution)/shard_map/ppermute | solution.py:642
  100.2 3.7 %collective-permute-start.17 = (f32[32,128]{1,0:T(8,128)S(1)}, f32[32,128]{1,0:T(8,128)S(1)}, u32[]{:S(2)}, u32[]{:S(2)}) collective-permute-start(f32[32,128]{1,0:T(8,128)S(1)} %get-tuple-element.139.refs_3_), channel_id=1, source_target_pairs={{1,2},{2,1},{3,4},{4,3},{5,6},{6,5},{7,8},{8,7},{9,10},{10,9},{11,... | collective-permute-start | bytes 49160 | tf_op jit(solution)/shard_map/ppermute | solution.py:641
  103.9 1.7 %collective-permute-done.17.refs_6_ = f32[32,128]{1,0:T(8,128)S(1)} collective-permute-done((f32[32,128]{1,0:T(8,128)S(1)}, f32[32,128]{1,0:T(8,128)S(1)}, u32[]{:S(2)}, u32[]{:S(2)}) %collective-permute-start.17) | collective-permute-done | bytes 16416 | tf_op jit(solution)/shard_map/ppermute | solution.py:641
  105.6 1.6 %all-to-all-done.3 = f32[64,16,128]{2,1,0:T(8,128)S(1)} async-done(((f32[64,16,128]{2,1,0:T(8,128)}), f32[64,16,128]{2,1,0:T(8,128)S(1)}, u32[]{:S(2)}, u32[]{:S(2)}) %all-to-all-start.3) | async-done | bytes 524320 | tf_op jit(solution)/shard_map/all_to_all | solution.py:629
  107.2 2.8 %shard_map.89 = f32[1536,128]{1,0:T(8,128)} custom-call(f32[1536,128]{1,0:T(8,128)S(1)} %get-tuple-element.136.refs_0_, f32[48,128]{1,0:T(8,128)S(1)} %get-tuple-element.137.refs_1_, f32[32,128]{1,0:T(8,128)S(1)} %get-tuple-element.138.refs_2_, f32[32,128]{1,0:T(8,128)S(1)} %get-tuple-element.139.refs_3_, f32[48,128]{1,0:T(8,128)S(1)} %get-tuple-element.140.refs_4_, ...), custom_call_target="tpu_custom_call" | custom-call | tf_op jit(solution)/shard_map/pallas_call | solution.py:649
  (65 shorter events, 11.5 us)
Async XLA Ops:
  0.1 0.7 copy-start.2
  0.1 0.7 copy-start.3
  0.1 0.7 copy-start.5
  0.1 0.7 copy-start.1
  0.1 0.7 copy-start.4
  0.8 1.1 %copy-start = (f32[4,1,4,96,128]{4,3,2,1,0:T(8,128)S(1)}, f32[4,1,4,96,128]{4,3,2,1,0:T(8,128)}, u32[]{:S(2)}) copy-start(f32[4,1,4,96,128]{4,3,2,1,0:T(8,128)} %param.7) | copy-start | bytes 2359300
  5.6 7.1 %collective-permute-start.1 = (f32[32,128]{1,0:T(8,128)S(1)}, f32[32,128]{1,0:T(8,128)S(1)}, u32[]{:S(2)}, u32[]{:S(2)}) collective-permute-start(f32[32,128]{1,0:T(8,128)S(1)} %get-tuple-element.86.refs_2_), channel_id=1, source_target_pairs={{0,1},{1,0},{2,3},{3,2},{4,5},{5,4},{6,7},{7,6},{8,9},{9,8},{10,11... | collective-permute-start | bytes 49160 | tf_op jit(solution)/shard_map/ppermute | solution.py:617
  7.1 5.6 %collective-permute-start = (f32[40,128]{1,0:T(8,128)S(1)}, f32[40,128]{1,0:T(8,128)S(1)}, u32[]{:S(2)}, u32[]{:S(2)}) collective-permute-start(f32[40,128]{1,0:T(8,128)S(1)} %get-tuple-element.74), channel_id=1, source_target_pairs={{0,67},{1,66},{2,65},{3,64},{4,71},{5,70},{6,69},{7,68},{8,75},{9,... | collective-permute-start | bytes 61448 | tf_op jit(solution)/shard_map/ppermute | solution.py:606
  13.5 9.1 %copy-start.6 = (s32[1,1,1,896]{3,2,1,0:T(1,128)S(1)}, s32[1,1,1,896]{3,2,1,0:T(1,128)}, u32[]{:S(2)}) copy-start(s32[1,1,1,896]{3,2,1,0:T(1,128)} %param.13) | copy-start | bytes 10756
  13.5 20.6 %all-to-all-start = ((f32[64,16,128]{2,1,0:T(8,128)}), f32[64,16,128]{2,1,0:T(8,128)S(1)}, u32[]{:S(2)}, u32[]{:S(2)}) async-start(f32[64,16,128]{2,1,0:T(8,128)} %bitcast.10), calls=%async_computation | async-start | bytes 1048576 | tf_op jit(solution)/shard_map/all_to_all | solution.py:629
  22.7 10.9 %collective-permute-start.4 = (f32[48,128]{1,0:T(8,128)S(1)}, f32[48,128]{1,0:T(8,128)S(1)}, u32[]{:S(2)}, u32[]{:S(2)}) collective-permute-start(f32[48,128]{1,0:T(8,128)S(1)} %get-tuple-element.88.refs_4_), channel_id=1, source_target_pairs={{16,32},{32,16},{17,33},{33,17},{18,34},{34,18},{19,35},{35,19},{2... | collective-permute-start | bytes 73736 | tf_op jit(solution)/shard_map/ppermute | solution.py:643
  23.4 10.3 %collective-permute-start.3 = (f32[48,128]{1,0:T(8,128)S(1)}, f32[48,128]{1,0:T(8,128)S(1)}, u32[]{:S(2)}, u32[]{:S(2)}) collective-permute-start(f32[48,128]{1,0:T(8,128)S(1)} %get-tuple-element.88.refs_4_), channel_id=1, source_target_pairs={{0,16},{16,0},{32,48},{48,32},{1,17},{17,1},{33,49},{49,33},{2,18}... | collective-permute-start | bytes 73736 | tf_op jit(solution)/shard_map/ppermute | solution.py:642
  27.3 6.4 %collective-permute-start.2 = (f32[32,128]{1,0:T(8,128)S(1)}, f32[32,128]{1,0:T(8,128)S(1)}, u32[]{:S(2)}, u32[]{:S(2)}) collective-permute-start(f32[32,128]{1,0:T(8,128)S(1)} %get-tuple-element.87.refs_3_), channel_id=1, source_target_pairs={{1,2},{2,1},{3,4},{4,3},{5,6},{6,5},{7,8},{8,7},{9,10},{10,9},{11,... | collective-permute-start | bytes 49160 | tf_op jit(solution)/shard_map/ppermute | solution.py:641
  36.1 5.1 %collective-permute-start.5 = (f32[40,128]{1,0:T(8,128)S(1)}, f32[40,128]{1,0:T(8,128)S(1)}, u32[]{:S(2)}, u32[]{:S(2)}) collective-permute-start(f32[40,128]{1,0:T(8,128)S(1)} %get-tuple-element.95), channel_id=1, source_target_pairs={{0,67},{1,66},{2,65},{3,64},{4,71},{5,70},{6,69},{7,68},{8,75},{9,... | collective-permute-start | bytes 61448 | tf_op jit(solution)/shard_map/ppermute | solution.py:606
  38.3 2.9 %collective-permute-start.6 = (f32[32,128]{1,0:T(8,128)S(1)}, f32[32,128]{1,0:T(8,128)S(1)}, u32[]{:S(2)}, u32[]{:S(2)}) collective-permute-start(f32[32,128]{1,0:T(8,128)S(1)} %get-tuple-element.106.refs_2_), channel_id=1, source_target_pairs={{0,1},{1,0},{2,3},{3,2},{4,5},{5,4},{6,7},{7,6},{8,9},{9,8},{10,11... | collective-permute-start | bytes 49160 | tf_op jit(solution)/shard_map/ppermute | solution.py:617
  42.0 16.6 %all-to-all-start.1 = ((f32[64,16,128]{2,1,0:T(8,128)}), f32[64,16,128]{2,1,0:T(8,128)S(1)}, u32[]{:S(2)}, u32[]{:S(2)}) async-start(f32[64,16,128]{2,1,0:T(8,128)} %bitcast.13), calls=%async_computation.1 | async-start | bytes 1048576 | tf_op jit(solution)/shard_map/all_to_all | solution.py:629
  47.0 10.4 %collective-permute-start.9 = (f32[48,128]{1,0:T(8,128)S(1)}, f32[48,128]{1,0:T(8,128)S(1)}, u32[]{:S(2)}, u32[]{:S(2)}) collective-permute-start(f32[48,128]{1,0:T(8,128)S(1)} %get-tuple-element.108.refs_4_), channel_id=1, source_target_pairs={{16,32},{32,16},{17,33},{33,17},{18,34},{34,18},{19,35},{35,19},{2... | collective-permute-start | bytes 73736 | tf_op jit(solution)/shard_map/ppermute | solution.py:643
  47.7 9.7 %collective-permute-start.8 = (f32[48,128]{1,0:T(8,128)S(1)}, f32[48,128]{1,0:T(8,128)S(1)}, u32[]{:S(2)}, u32[]{:S(2)}) collective-permute-start(f32[48,128]{1,0:T(8,128)S(1)} %get-tuple-element.108.refs_4_), channel_id=1, source_target_pairs={{0,16},{16,0},{32,48},{48,32},{1,17},{17,1},{33,49},{49,33},{2,18}... | collective-permute-start | bytes 73736 | tf_op jit(solution)/shard_map/ppermute | solution.py:642
  51.5 5.8 %collective-permute-start.7 = (f32[32,128]{1,0:T(8,128)S(1)}, f32[32,128]{1,0:T(8,128)S(1)}, u32[]{:S(2)}, u32[]{:S(2)}) collective-permute-start(f32[32,128]{1,0:T(8,128)S(1)} %get-tuple-element.107.refs_3_), channel_id=1, source_target_pairs={{1,2},{2,1},{3,4},{4,3},{5,6},{6,5},{7,8},{8,7},{9,10},{10,9},{11,... | collective-permute-start | bytes 49160 | tf_op jit(solution)/shard_map/ppermute | solution.py:641
  60.6 5.1 %collective-permute-start.10 = (f32[40,128]{1,0:T(8,128)S(1)}, f32[40,128]{1,0:T(8,128)S(1)}, u32[]{:S(2)}, u32[]{:S(2)}) collective-permute-start(f32[40,128]{1,0:T(8,128)S(1)} %get-tuple-element.111), channel_id=1, source_target_pairs={{0,67},{1,66},{2,65},{3,64},{4,71},{5,70},{6,69},{7,68},{8,75},{9,... | collective-permute-start | bytes 61448 | tf_op jit(solution)/shard_map/ppermute | solution.py:606
  62.8 2.9 %collective-permute-start.11 = (f32[32,128]{1,0:T(8,128)S(1)}, f32[32,128]{1,0:T(8,128)S(1)}, u32[]{:S(2)}, u32[]{:S(2)}) collective-permute-start(f32[32,128]{1,0:T(8,128)S(1)} %get-tuple-element.122.refs_2_), channel_id=1, source_target_pairs={{0,1},{1,0},{2,3},{3,2},{4,5},{5,4},{6,7},{7,6},{8,9},{9,8},{10,11... | collective-permute-start | bytes 49160 | tf_op jit(solution)/shard_map/ppermute | solution.py:617
  66.5 16.4 %all-to-all-start.2 = ((f32[64,16,128]{2,1,0:T(8,128)}), f32[64,16,128]{2,1,0:T(8,128)S(1)}, u32[]{:S(2)}, u32[]{:S(2)}) async-start(f32[64,16,128]{2,1,0:T(8,128)} %bitcast.15), calls=%async_computation.2 | async-start | bytes 1048576 | tf_op jit(solution)/shard_map/all_to_all | solution.py:629
  71.3 10.3 %collective-permute-start.14 = (f32[48,128]{1,0:T(8,128)S(1)}, f32[48,128]{1,0:T(8,128)S(1)}, u32[]{:S(2)}, u32[]{:S(2)}) collective-permute-start(f32[48,128]{1,0:T(8,128)S(1)} %get-tuple-element.124.refs_4_), channel_id=1, source_target_pairs={{16,32},{32,16},{17,33},{33,17},{18,34},{34,18},{19,35},{35,19},{2... | collective-permute-start | bytes 73736 | tf_op jit(solution)/shard_map/ppermute | solution.py:643
  72.0 9.6 %collective-permute-start.13 = (f32[48,128]{1,0:T(8,128)S(1)}, f32[48,128]{1,0:T(8,128)S(1)}, u32[]{:S(2)}, u32[]{:S(2)}) collective-permute-start(f32[48,128]{1,0:T(8,128)S(1)} %get-tuple-element.124.refs_4_), channel_id=1, source_target_pairs={{0,16},{16,0},{32,48},{48,32},{1,17},{17,1},{33,49},{49,33},{2,18}... | collective-permute-start | bytes 73736 | tf_op jit(solution)/shard_map/ppermute | solution.py:642
  75.9 5.7 %collective-permute-start.12 = (f32[32,128]{1,0:T(8,128)S(1)}, f32[32,128]{1,0:T(8,128)S(1)}, u32[]{:S(2)}, u32[]{:S(2)}) collective-permute-start(f32[32,128]{1,0:T(8,128)S(1)} %get-tuple-element.123.refs_3_), channel_id=1, source_target_pairs={{1,2},{2,1},{3,4},{4,3},{5,6},{6,5},{7,8},{8,7},{9,10},{10,9},{11,... | collective-permute-start | bytes 49160 | tf_op jit(solution)/shard_map/ppermute | solution.py:641
  84.9 5.1 %collective-permute-start.15 = (f32[40,128]{1,0:T(8,128)S(1)}, f32[40,128]{1,0:T(8,128)S(1)}, u32[]{:S(2)}, u32[]{:S(2)}) collective-permute-start(f32[40,128]{1,0:T(8,128)S(1)} %get-tuple-element.127), channel_id=1, source_target_pairs={{0,67},{1,66},{2,65},{3,64},{4,71},{5,70},{6,69},{7,68},{8,75},{9,... | collective-permute-start | bytes 61448 | tf_op jit(solution)/shard_map/ppermute | solution.py:606
  87.0 2.9 %collective-permute-start.16 = (f32[32,128]{1,0:T(8,128)S(1)}, f32[32,128]{1,0:T(8,128)S(1)}, u32[]{:S(2)}, u32[]{:S(2)}) collective-permute-start(f32[32,128]{1,0:T(8,128)S(1)} %get-tuple-element.138.refs_2_), channel_id=1, source_target_pairs={{0,1},{1,0},{2,3},{3,2},{4,5},{5,4},{6,7},{7,6},{8,9},{9,8},{10,11... | collective-permute-start | bytes 49160 | tf_op jit(solution)/shard_map/ppermute | solution.py:617
  90.7 16.5 %all-to-all-start.3 = ((f32[64,16,128]{2,1,0:T(8,128)}), f32[64,16,128]{2,1,0:T(8,128)S(1)}, u32[]{:S(2)}, u32[]{:S(2)}) async-start(f32[64,16,128]{2,1,0:T(8,128)} %bitcast.17), calls=%async_computation.3 | async-start | bytes 1048576 | tf_op jit(solution)/shard_map/all_to_all | solution.py:629
  95.6 10.0 %collective-permute-start.19 = (f32[48,128]{1,0:T(8,128)S(1)}, f32[48,128]{1,0:T(8,128)S(1)}, u32[]{:S(2)}, u32[]{:S(2)}) collective-permute-start(f32[48,128]{1,0:T(8,128)S(1)} %get-tuple-element.140.refs_4_), channel_id=1, source_target_pairs={{16,32},{32,16},{17,33},{33,17},{18,34},{34,18},{19,35},{35,19},{2... | collective-permute-start | bytes 73736 | tf_op jit(solution)/shard_map/ppermute | solution.py:643
  96.3 9.3 %collective-permute-start.18 = (f32[48,128]{1,0:T(8,128)S(1)}, f32[48,128]{1,0:T(8,128)S(1)}, u32[]{:S(2)}, u32[]{:S(2)}) collective-permute-start(f32[48,128]{1,0:T(8,128)S(1)} %get-tuple-element.140.refs_4_), channel_id=1, source_target_pairs={{0,16},{16,0},{32,48},{48,32},{1,17},{17,1},{33,49},{49,33},{2,18}... | collective-permute-start | bytes 73736 | tf_op jit(solution)/shard_map/ppermute | solution.py:642
  100.2 5.4 %collective-permute-start.17 = (f32[32,128]{1,0:T(8,128)S(1)}, f32[32,128]{1,0:T(8,128)S(1)}, u32[]{:S(2)}, u32[]{:S(2)}) collective-permute-start(f32[32,128]{1,0:T(8,128)S(1)} %get-tuple-element.139.refs_3_), channel_id=1, source_target_pairs={{1,2},{2,1},{3,4},{4,3},{5,6},{6,5},{7,8},{8,7},{9,10},{10,9},{11,... | collective-permute-start | bytes 49160 | tf_op jit(solution)/shard_map/ppermute | solution.py:641

commit v8 on v7

--- a/solution.py
+++ b/solution.py
@@ -614,8 +614,7 @@
             compiler_params=params,
             cost_estimate=pl.CostEstimate(flops=20_000_000, bytes_accessed=1 << 23, transcendentals=0),
         )(*operands)
-        lon_a = lax.ppermute(edge_a, lon_axes, pairs(lon_blocks, 0))
-        over, part, part_strips, lon_a = lax.optimization_barrier((over, part, part_strips, lon_a))
+        over, part, part_strips = lax.optimization_barrier((over, part, part_strips))
         buffer = pl.pallas_call(
             pack_kernel,
             out_shape=f32(peers * ROWS, LANES),
@@ -638,6 +637,7 @@
                 compiler_params=params,
                 cost_estimate=pl.CostEstimate(flops=8_000_000, bytes_accessed=1 << 22, transcendentals=0),
             )(part, src)
+        lon_a = lax.ppermute(own_a, lon_axes, pairs(lon_blocks, 0))
         lon_b = lax.ppermute(own_b, lon_axes, pairs(lon_blocks, 1))
         strip_a = lax.ppermute(own_strips, "colat", pairs(lat_blocks, 0))
         strip_b = lax.ppermute(own_strips, "colat", pairs(lat_blocks, 1))

time: 111 us -> 113 us (1.018)
  starting transfers between devices: 68.6 us -> 71.7 us
    ppermute x4, starting transfers between devices: 9.05 us -> 12.6 us  [on_device(): over = lax.ppermute(sent, ('panel',) + lon_axes, crossing(lon_blocks))]
    ppermute x4, starting transfers between devices: 15.1 us -> 11.9 us  [on_device(): lon_b = lax.ppermute(own_b, lon_axes, pairs(lon_blocks, 1))]
    all_to_all x4, starting transfers between devices: 23.8 us -> 25.8 us  [on_device(): lax.all_to_all(buffer.reshape(peers, ROWS, LANES), ('core', 'lon_hi', 'co...]
    all_to_all x4, waiting for transfers between devices: 4.49 us -> 2.96 us  [on_device(): lax.all_to_all(buffer.reshape(peers, ROWS, LANES), ('core', 'lon_hi', 'co...]
    ppermute x4, waiting for transfers between devices: 1.71 us -> 3.07 us  [on_device(): lon_b = lax.ppermute(own_b, lon_axes, pairs(lon_blocks, 1))]
  transfers between devices with their start and end apart: 24 -> 24, of which waited for: 5 -> 7; matrix products, arithmetic and copies ran while one was open for 1% -> 1% of each run, Pallas kernels for 15% -> 15%
where the time goes in v8:
time: 113 us; the launch traced here: 112 us
  starting transfers between devices  71.7 us (63%)
  Pallas kernels  31.6 us (28%)
  waiting for transfers between devices  6.07 us (5%)
  local copies, waits for them, and re-layouts  2.19 us (2%)
    all_to_all x4, starting transfers between devices, on_device(): lax.all_to_all(buffer.reshape(peers, ROWS, LANES), ('core', 'lon_hi', 'co...  25.8 us
    ppermute x4, starting transfers between devices, on_device(): strip_a = lax.ppermute(own_strips, 'colat', pairs(lat_blocks, 0))  15.5 us
    ppermute x4, starting transfers between devices, on_device(): over = lax.ppermute(sent, ('panel',) + lon_axes, crossing(lon_blocks))  12.6 us
    ppermute x4, starting transfers between devices, on_device(): lon_b = lax.ppermute(own_b, lon_axes, pairs(lon_blocks, 1))  11.9 us
    pallas_call x4, Pallas kernels, on_device(): pl.pallas_call(functools.partial(inner_kernel, second, lon_cells, consts)...  10.3 us
    pallas_call x4, Pallas kernels, on_device(): pl.pallas_call(functools.partial(outer_kernel, second, final, lon_cells,...  8.17 us
    pallas_call x3, Pallas kernels, on_device(): pl.pallas_call(rows_kernel, out_shape=f32(8 * ROWS, LANES), in_specs=[vme...  5.99 us
    pallas_call x1, Pallas kernels, on_device(): pl.pallas_call(functools.partial(start_kernel, lon_cells), out_shape=[mov...  3.65 us
  transfers between devices with their start and end apart: 24, of which 7 were waited for; matrix products, arithmetic and copies ran while one was open for 1% of the time, Pallas kernels for 15%

profile of v8, /device:TPU:1, one launch (start us, length us, event | category | flops | bytes accessed | tf_op | source)
XLA Modules:
  0.0 112.4 jit_solution(6594388837484164185)
XLA Ops:
  0.8 1.1 %copy-done = f32[4,1,4,96,128]{4,3,2,1,0:T(8,128)S(1)} copy-done((f32[4,1,4,96,128]{4,3,2,1,0:T(8,128)S(1)}, f32[4,1,4,96,128]{4,3,2,1,0:T(8,128)}, u32[]{:S(2)}) %copy-start) | copy-done | bytes 786456
  1.9 3.7 %shard_map.73 = (f32[1536,128]{1,0:T(8,128)S(1)}, f32[32,128]{1,0:T(8,128)S(1)}, f32[32,128]{1,0:T(8,128)S(1)}, f32[48,128]{1,0:T(8,128)S(1)}, f32[1024,128]{1,0...) custom-call(f32[1536,128]{1,0:T(8,128)S(1)} %bitcast.26, s32[256]{0:T(256)S(1)} %bitcast.27, ...), custom_call_target="tpu_custom_call" | custom-call | tf_op jit(solution)/shard_map/pallas_call | solution.py:581
  5.6 3.9 %collective-permute-start = (f32[40,128]{1,0:T(8,128)S(1)}, f32[40,128]{1,0:T(8,128)S(1)}, u32[]{:S(2)}, u32[]{:S(2)}) collective-permute-start(f32[40,128]{1,0:T(8,128)S(1)} %get-tuple-element.70), channel_id=1, source_target_pairs={{0,67},{1,66},{2,65},{3,64},{4,71},{5,70},{6,69},{7,68},{8,75},{9,... | collective-permute-start | bytes 61448 | tf_op jit(solution)/shard_map/ppermute | solution.py:606
  10.1 2.6 %shard_map.74 = (f32[1536,128]{1,0:T(8,128)S(1)}, f32[48,128]{1,0:T(8,128)S(1)}) custom-call(f32[1536,128]{1,0:T(8,128)S(1)} %get-tuple-element.71.refs_0_.refs_1_, f32[232,128]{1,0:T(8,128)S(1)} %constant_dynamic-update-slice_fusion.refs_1_.refs_13_.refs_2_), custom_call_target="tpu_custom_call" | custom-call | flops 20000000 | bytes 8388608 | tf_op jit(solution)/shard_map/pallas_call | solution.py:608
  13.4 8.7 %all-to-all-start = ((f32[64,16,128]{2,1,0:T(8,128)}), f32[64,16,128]{2,1,0:T(8,128)S(1)}, u32[]{:S(2)}, u32[]{:S(2)}) async-start(f32[64,16,128]{2,1,0:T(8,128)} %bitcast.10), calls=%async_computation | async-start | bytes 1048576 | tf_op jit(solution)/shard_map/all_to_all | solution.py:628
  23.0 3.9 %collective-permute-start.3 = (f32[48,128]{1,0:T(8,128)S(1)}, f32[48,128]{1,0:T(8,128)S(1)}, u32[]{:S(2)}, u32[]{:S(2)}) collective-permute-start(f32[48,128]{1,0:T(8,128)S(1)} %get-tuple-element.84.refs_4_), channel_id=1, source_target_pairs={{0,16},{16,0},{32,48},{48,32},{1,17},{17,1},{33,49},{49,33},{2,18}... | collective-permute-start | bytes 73736 | tf_op jit(solution)/shard_map/ppermute | solution.py:642
  27.7 3.0 %collective-permute-start.2 = (f32[32,128]{1,0:T(8,128)S(1)}, f32[32,128]{1,0:T(8,128)S(1)}, u32[]{:S(2)}, u32[]{:S(2)}) collective-permute-start(f32[32,128]{1,0:T(8,128)S(1)} %get-tuple-element.83.refs_3_), channel_id=1, source_target_pairs={{1,2},{2,1},{3,4},{4,3},{5,6},{6,5},{7,8},{8,7},{9,10},{10,9},{11,... | collective-permute-start | bytes 49160 | tf_op jit(solution)/shard_map/ppermute | solution.py:641
  31.3 2.0 %shard_map.77.refs_14_ = f32[128,128]{1,0:T(8,128)S(1)} custom-call(f32[1536,128]{1,0:T(8,128)S(1)} %get-tuple-element.80.field.refs_0_, s32[256]{0:T(256)S(1)} %bitcast.28), custom_call_target="tpu_custom_call" | custom-call | flops 8000000 | bytes 4194304 | tf_op jit(solution)/shard_map/pallas_call | solution.py:632
  33.7 1.8 %shard_map.78 = (f32[1536,128]{1,0:T(8,128)S(1)}, f32[40,128]{1,0:T(8,128)S(1)}, f32[32,128]{1,0:T(8,128)S(1)}, f32[32,128]{1,0:T(8,128)S(1)}, f32[48,128]{1,0:T(8,128)S(1)}) custom-call(f32[1536,128]{1,0:T(8,128)S(1)} %get-tuple-element.80.field.refs_0_, f32[48,128]{1,0:T(8,128)S(1)} %get-tuple-element.81.refs_1_, f32[32,128]{1,0:T(8,128)S(1)} %get-tuple-element.82.refs_2_, ...), custom_call_target="tpu_custom_call" | custom-call | tf_op jit(solution)/shard_map/pallas_call | solution.py:649
  35.5 2.8 %collective-permute-start.5 = (f32[40,128]{1,0:T(8,128)S(1)}, f32[40,128]{1,0:T(8,128)S(1)}, u32[]{:S(2)}, u32[]{:S(2)}) collective-permute-start(f32[40,128]{1,0:T(8,128)S(1)} %get-tuple-element.90), channel_id=1, source_target_pairs={{0,67},{1,66},{2,65},{3,64},{4,71},{5,70},{6,69},{7,68},{8,75},{9,... | collective-permute-start | bytes 61448 | tf_op jit(solution)/shard_map/ppermute | solution.py:606
  38.3 2.6 %shard_map.79 = (f32[1536,128]{1,0:T(8,128)S(1)}, f32[48,128]{1,0:T(8,128)S(1)}) custom-call(f32[1536,128]{1,0:T(8,128)S(1)} %get-tuple-element.91.refs_0_, f32[1536,128]{1,0:T(8,128)S(1)} %get-tuple-element.71.refs_0_.refs_1_, f32[232,128]{1,0:T(8,128)S(1)} %constant_dynamic-update-slice_fusion.refs_1_.refs_13_.refs_2_), custom_call_target="tpu_custom_call" | custom-call | flops 20000000 | bytes 8388608 | tf_op jit(solution)/shard_map/pallas_call | solution.py:608
  41.7 5.8 %all-to-all-start.1 = ((f32[64,16,128]{2,1,0:T(8,128)}), f32[64,16,128]{2,1,0:T(8,128)S(1)}, u32[]{:S(2)}, u32[]{:S(2)}) async-start(f32[64,16,128]{2,1,0:T(8,128)} %bitcast.13), calls=%async_computation.1 | async-start | bytes 1048576 | tf_op jit(solution)/shard_map/all_to_all | solution.py:628
  48.1 3.9 %collective-permute-start.8 = (f32[48,128]{1,0:T(8,128)S(1)}, f32[48,128]{1,0:T(8,128)S(1)}, u32[]{:S(2)}, u32[]{:S(2)}) collective-permute-start(f32[48,128]{1,0:T(8,128)S(1)} %get-tuple-element.103.refs_4_), channel_id=1, source_target_pairs={{0,16},{16,0},{32,48},{48,32},{1,17},{17,1},{33,49},{49,33},{2,18}... | collective-permute-start | bytes 73736 | tf_op jit(solution)/shard_map/ppermute | solution.py:642
  52.9 3.0 %collective-permute-start.7 = (f32[32,128]{1,0:T(8,128)S(1)}, f32[32,128]{1,0:T(8,128)S(1)}, u32[]{:S(2)}, u32[]{:S(2)}) collective-permute-start(f32[32,128]{1,0:T(8,128)S(1)} %get-tuple-element.102.refs_3_), channel_id=1, source_target_pairs={{1,2},{2,1},{3,4},{4,3},{5,6},{6,5},{7,8},{8,7},{9,10},{10,9},{11,... | collective-permute-start | bytes 49160 | tf_op jit(solution)/shard_map/ppermute | solution.py:641
  55.8 2.0 %shard_map.81.refs_14_ = f32[128,128]{1,0:T(8,128)S(1)} custom-call(f32[1536,128]{1,0:T(8,128)S(1)} %get-tuple-element.99.field.refs_0_, s32[256]{0:T(256)S(1)} %bitcast.30), custom_call_target="tpu_custom_call" | custom-call | flops 8000000 | bytes 4194304 | tf_op jit(solution)/shard_map/pallas_call | solution.py:632
  58.2 0.8 all-to-all-done.1
  59.1 1.8 %shard_map.82 = (f32[1536,128]{1,0:T(8,128)S(1)}, f32[40,128]{1,0:T(8,128)S(1)}, f32[32,128]{1,0:T(8,128)S(1)}, f32[32,128]{1,0:T(8,128)S(1)}, f32[48,128]{1,0:T(8,128)S(1)}) custom-call(f32[1536,128]{1,0:T(8,128)S(1)} %get-tuple-element.99.field.refs_0_, f32[48,128]{1,0:T(8,128)S(1)} %get-tuple-element.100.refs_1_, ...), custom_call_target="tpu_custom_call" | custom-call | tf_op jit(solution)/shard_map/pallas_call | solution.py:649
  60.8 2.8 %collective-permute-start.10 = (f32[40,128]{1,0:T(8,128)S(1)}, f32[40,128]{1,0:T(8,128)S(1)}, u32[]{:S(2)}, u32[]{:S(2)}) collective-permute-start(f32[40,128]{1,0:T(8,128)S(1)} %get-tuple-element.105), channel_id=1, source_target_pairs={{0,67},{1,66},{2,65},{3,64},{4,71},{5,70},{6,69},{7,68},{8,75},{9,... | collective-permute-start | bytes 61448 | tf_op jit(solution)/shard_map/ppermute | solution.py:606
  63.7 2.6 %shard_map.83 = (f32[1536,128]{1,0:T(8,128)S(1)}, f32[48,128]{1,0:T(8,128)S(1)}) custom-call(f32[1536,128]{1,0:T(8,128)S(1)} %get-tuple-element.106.refs_0_.refs_1_, f32[232,128]{1,0:T(8,128)S(1)} %constant_dynamic-update-slice_fusion.refs_1_.refs_13_.refs_2_), custom_call_target="tpu_custom_call" | custom-call | flops 20000000 | bytes 8388608 | tf_op jit(solution)/shard_map/pallas_call | solution.py:608
  67.0 5.6 %all-to-all-start.2 = ((f32[64,16,128]{2,1,0:T(8,128)}), f32[64,16,128]{2,1,0:T(8,128)S(1)}, u32[]{:S(2)}, u32[]{:S(2)}) async-start(f32[64,16,128]{2,1,0:T(8,128)} %bitcast.15), calls=%async_computation.2 | async-start | bytes 1048576 | tf_op jit(solution)/shard_map/all_to_all | solution.py:628
  73.3 3.9 %collective-permute-start.13 = (f32[48,128]{1,0:T(8,128)S(1)}, f32[48,128]{1,0:T(8,128)S(1)}, u32[]{:S(2)}, u32[]{:S(2)}) collective-permute-start(f32[48,128]{1,0:T(8,128)S(1)} %get-tuple-element.118.refs_4_), channel_id=1, source_target_pairs={{0,16},{16,0},{32,48},{48,32},{1,17},{17,1},{33,49},{49,33},{2,18}... | collective-permute-start | bytes 73736 | tf_op jit(solution)/shard_map/ppermute | solution.py:642
  78.0 3.0 %collective-permute-start.12 = (f32[32,128]{1,0:T(8,128)S(1)}, f32[32,128]{1,0:T(8,128)S(1)}, u32[]{:S(2)}, u32[]{:S(2)}) collective-permute-start(f32[32,128]{1,0:T(8,128)S(1)} %get-tuple-element.117.refs_3_), channel_id=1, source_target_pairs={{1,2},{2,1},{3,4},{4,3},{5,6},{6,5},{7,8},{8,7},{9,10},{10,9},{11,... | collective-permute-start | bytes 49160 | tf_op jit(solution)/shard_map/ppermute | solution.py:641
  81.0 2.0 %shard_map.85.refs_14_ = f32[128,128]{1,0:T(8,128)S(1)} custom-call(f32[1536,128]{1,0:T(8,128)S(1)} %get-tuple-element.114.field.refs_0_, s32[256]{0:T(256)S(1)} %bitcast.32), custom_call_target="tpu_custom_call" | custom-call | flops 8000000 | bytes 4194304 | tf_op jit(solution)/shard_map/pallas_call | solution.py:632
  83.3 0.8 all-to-all-done.2
  84.2 1.8 %shard_map.86 = (f32[1536,128]{1,0:T(8,128)S(1)}, f32[40,128]{1,0:T(8,128)S(1)}, f32[32,128]{1,0:T(8,128)S(1)}, f32[32,128]{1,0:T(8,128)S(1)}, f32[48,128]{1,0:T(8,128)S(1)}) custom-call(f32[1536,128]{1,0:T(8,128)S(1)} %get-tuple-element.114.field.refs_0_, f32[48,128]{1,0:T(8,128)S(1)} %get-tuple-element.115.refs_1_, ...), custom_call_target="tpu_custom_call" | custom-call | tf_op jit(solution)/shard_map/pallas_call | solution.py:649
  86.0 3.0 %collective-permute-start.15 = (f32[40,128]{1,0:T(8,128)S(1)}, f32[40,128]{1,0:T(8,128)S(1)}, u32[]{:S(2)}, u32[]{:S(2)}) collective-permute-start(f32[40,128]{1,0:T(8,128)S(1)} %get-tuple-element.120), channel_id=1, source_target_pairs={{0,67},{1,66},{2,65},{3,64},{4,71},{5,70},{6,69},{7,68},{8,75},{9,... | collective-permute-start | bytes 61448 | tf_op jit(solution)/shard_map/ppermute | solution.py:606
  89.0 2.6 %shard_map.87 = (f32[1536,128]{1,0:T(8,128)S(1)}, f32[48,128]{1,0:T(8,128)S(1)}) custom-call(f32[1536,128]{1,0:T(8,128)S(1)} %get-tuple-element.121.refs_0_, f32[1536,128]{1,0:T(8,128)S(1)} %get-tuple-element.106.refs_0_.refs_1_, f32[232,128]{1,0:T(8,128)S(1)} %constant_dynamic-update-slice_fusion.refs_1_.refs_13_.refs_2_), custom_call_target="tpu_custom_call" | custom-call | flops 20000000 | bytes 8388608 | tf_op jit(solution)/shard_map/pallas_call | solution.py:608
  92.3 5.6 %all-to-all-start.3 = ((f32[64,16,128]{2,1,0:T(8,128)}), f32[64,16,128]{2,1,0:T(8,128)S(1)}, u32[]{:S(2)}, u32[]{:S(2)}) async-start(f32[64,16,128]{2,1,0:T(8,128)} %bitcast.17), calls=%async_computation.3 | async-start | bytes 1048576 | tf_op jit(solution)/shard_map/all_to_all | solution.py:628
  98.6 3.9 %collective-permute-start.18 = (f32[48,128]{1,0:T(8,128)S(1)}, f32[48,128]{1,0:T(8,128)S(1)}, u32[]{:S(2)}, u32[]{:S(2)}) collective-permute-start(f32[48,128]{1,0:T(8,128)S(1)} %get-tuple-element.133.refs_4_), channel_id=1, source_target_pairs={{0,16},{16,0},{32,48},{48,32},{1,17},{17,1},{33,49},{49,33},{2,18}... | collective-permute-start | bytes 73736 | tf_op jit(solution)/shard_map/ppermute | solution.py:642
  103.4 3.0 %collective-permute-start.17 = (f32[32,128]{1,0:T(8,128)S(1)}, f32[32,128]{1,0:T(8,128)S(1)}, u32[]{:S(2)}, u32[]{:S(2)}) collective-permute-start(f32[32,128]{1,0:T(8,128)S(1)} %get-tuple-element.132.refs_3_), channel_id=1, source_target_pairs={{1,2},{2,1},{3,4},{4,3},{5,6},{6,5},{7,8},{8,7},{9,10},{10,9},{11,... | collective-permute-start | bytes 49160 | tf_op jit(solution)/shard_map/ppermute | solution.py:641
  106.3 2.4 %collective-permute-done.17.refs_6_ = f32[32,128]{1,0:T(8,128)S(1)} collective-permute-done((f32[32,128]{1,0:T(8,128)S(1)}, f32[32,128]{1,0:T(8,128)S(1)}, u32[]{:S(2)}, u32[]{:S(2)}) %collective-permute-start.17) | collective-permute-done | bytes 16416 | tf_op jit(solution)/shard_map/ppermute | solution.py:641
  109.6 2.8 %shard_map.89 = f32[1536,128]{1,0:T(8,128)} custom-call(f32[1536,128]{1,0:T(8,128)S(1)} %get-tuple-element.129.refs_0_, f32[48,128]{1,0:T(8,128)S(1)} %get-tuple-element.130.refs_1_, f32[32,128]{1,0:T(8,128)S(1)} %get-tuple-element.131.refs_2_, f32[32,128]{1,0:T(8,128)S(1)} %get-tuple-element.132.refs_3_, f32[48,128]{1,0:T(8,128)S(1)} %get-tuple-element.133.refs_4_, ...), custom_call_target="tpu_custom_call" | custom-call | tf_op jit(solution)/shard_map/pallas_call | solution.py:649
  (65 shorter events, 13.0 us)
Async XLA Ops:
  0.1 0.7 copy-start.2
  0.1 0.7 copy-start.3
  0.1 0.7 copy-start.5
  0.1 0.7 copy-start.1
  0.1 0.7 copy-start.4
  0.8 1.1 %copy-start = (f32[4,1,4,96,128]{4,3,2,1,0:T(8,128)S(1)}, f32[4,1,4,96,128]{4,3,2,1,0:T(8,128)}, u32[]{:S(2)}) copy-start(f32[4,1,4,96,128]{4,3,2,1,0:T(8,128)} %param.7) | copy-start | bytes 2359300
  5.6 7.0 %collective-permute-start = (f32[40,128]{1,0:T(8,128)S(1)}, f32[40,128]{1,0:T(8,128)S(1)}, u32[]{:S(2)}, u32[]{:S(2)}) collective-permute-start(f32[40,128]{1,0:T(8,128)S(1)} %get-tuple-element.70), channel_id=1, source_target_pairs={{0,67},{1,66},{2,65},{3,64},{4,71},{5,70},{6,69},{7,68},{8,75},{9,... | collective-permute-start | bytes 61448 | tf_op jit(solution)/shard_map/ppermute | solution.py:606
  13.4 8.7 %copy-start.6 = (s32[1,1,1,896]{3,2,1,0:T(1,128)S(1)}, s32[1,1,1,896]{3,2,1,0:T(1,128)}, u32[]{:S(2)}) copy-start(s32[1,1,1,896]{3,2,1,0:T(1,128)} %param.13) | copy-start | bytes 10756
  13.4 20.3 %all-to-all-start = ((f32[64,16,128]{2,1,0:T(8,128)}), f32[64,16,128]{2,1,0:T(8,128)S(1)}, u32[]{:S(2)}, u32[]{:S(2)}) async-start(f32[64,16,128]{2,1,0:T(8,128)} %bitcast.10), calls=%async_computation | async-start | bytes 1048576 | tf_op jit(solution)/shard_map/all_to_all | solution.py:628
  22.3 11.0 %collective-permute-start.4 = (f32[48,128]{1,0:T(8,128)S(1)}, f32[48,128]{1,0:T(8,128)S(1)}, u32[]{:S(2)}, u32[]{:S(2)}) collective-permute-start(f32[48,128]{1,0:T(8,128)S(1)} %get-tuple-element.84.refs_4_), channel_id=1, source_target_pairs={{16,32},{32,16},{17,33},{33,17},{18,34},{34,18},{19,35},{35,19},{2... | collective-permute-start | bytes 73736 | tf_op jit(solution)/shard_map/ppermute | solution.py:643
  23.0 10.3 %collective-permute-start.3 = (f32[48,128]{1,0:T(8,128)S(1)}, f32[48,128]{1,0:T(8,128)S(1)}, u32[]{:S(2)}, u32[]{:S(2)}) collective-permute-start(f32[48,128]{1,0:T(8,128)S(1)} %get-tuple-element.84.refs_4_), channel_id=1, source_target_pairs={{0,16},{16,0},{32,48},{48,32},{1,17},{17,1},{33,49},{49,33},{2,18}... | collective-permute-start | bytes 73736 | tf_op jit(solution)/shard_map/ppermute | solution.py:642
  26.8 6.4 %collective-permute-start.1 = (f32[32,128]{1,0:T(8,128)S(1)}, f32[32,128]{1,0:T(8,128)S(1)}, u32[]{:S(2)}, u32[]{:S(2)}) collective-permute-start(f32[32,128]{1,0:T(8,128)S(1)} %get-tuple-element.82.refs_2_), channel_id=1, source_target_pairs={{0,1},{1,0},{2,3},{3,2},{4,5},{5,4},{6,7},{7,6},{8,9},{9,8},{10,11... | collective-permute-start | bytes 49160 | tf_op jit(solution)/shard_map/ppermute | solution.py:640
  27.7 5.6 %collective-permute-start.2 = (f32[32,128]{1,0:T(8,128)S(1)}, f32[32,128]{1,0:T(8,128)S(1)}, u32[]{:S(2)}, u32[]{:S(2)}) collective-permute-start(f32[32,128]{1,0:T(8,128)S(1)} %get-tuple-element.83.refs_3_), channel_id=1, source_target_pairs={{1,2},{2,1},{3,4},{4,3},{5,6},{6,5},{7,8},{8,7},{9,10},{10,9},{11,... | collective-permute-start | bytes 49160 | tf_op jit(solution)/shard_map/ppermute | solution.py:641
  35.5 5.4 %collective-permute-start.5 = (f32[40,128]{1,0:T(8,128)S(1)}, f32[40,128]{1,0:T(8,128)S(1)}, u32[]{:S(2)}, u32[]{:S(2)}) collective-permute-start(f32[40,128]{1,0:T(8,128)S(1)} %get-tuple-element.90), channel_id=1, source_target_pairs={{0,67},{1,66},{2,65},{3,64},{4,71},{5,70},{6,69},{7,68},{8,75},{9,... | collective-permute-start | bytes 61448 | tf_op jit(solution)/shard_map/ppermute | solution.py:606
  41.7 17.4 %all-to-all-start.1 = ((f32[64,16,128]{2,1,0:T(8,128)}), f32[64,16,128]{2,1,0:T(8,128)S(1)}, u32[]{:S(2)}, u32[]{:S(2)}) async-start(f32[64,16,128]{2,1,0:T(8,128)} %bitcast.13), calls=%async_computation.1 | async-start | bytes 1048576 | tf_op jit(solution)/shard_map/all_to_all | solution.py:628
  47.5 10.7 %collective-permute-start.9 = (f32[48,128]{1,0:T(8,128)S(1)}, f32[48,128]{1,0:T(8,128)S(1)}, u32[]{:S(2)}, u32[]{:S(2)}) collective-permute-start(f32[48,128]{1,0:T(8,128)S(1)} %get-tuple-element.103.refs_4_), channel_id=1, source_target_pairs={{16,32},{32,16},{17,33},{33,17},{18,34},{34,18},{19,35},{35,19},{2... | collective-permute-start | bytes 73736 | tf_op jit(solution)/shard_map/ppermute | solution.py:643
  48.1 10.1 %collective-permute-start.8 = (f32[48,128]{1,0:T(8,128)S(1)}, f32[48,128]{1,0:T(8,128)S(1)}, u32[]{:S(2)}, u32[]{:S(2)}) collective-permute-start(f32[48,128]{1,0:T(8,128)S(1)} %get-tuple-element.103.refs_4_), channel_id=1, source_target_pairs={{0,16},{16,0},{32,48},{48,32},{1,17},{17,1},{33,49},{49,33},{2,18}... | collective-permute-start | bytes 73736 | tf_op jit(solution)/shard_map/ppermute | solution.py:642
  52.0 5.8 %collective-permute-start.6 = (f32[32,128]{1,0:T(8,128)S(1)}, f32[32,128]{1,0:T(8,128)S(1)}, u32[]{:S(2)}, u32[]{:S(2)}) collective-permute-start(f32[32,128]{1,0:T(8,128)S(1)} %get-tuple-element.101.refs_2_), channel_id=1, source_target_pairs={{0,1},{1,0},{2,3},{3,2},{4,5},{5,4},{6,7},{7,6},{8,9},{9,8},{10,11... | collective-permute-start | bytes 49160 | tf_op jit(solution)/shard_map/ppermute | solution.py:640
  52.9 5.3 %collective-permute-start.7 = (f32[32,128]{1,0:T(8,128)S(1)}, f32[32,128]{1,0:T(8,128)S(1)}, u32[]{:S(2)}, u32[]{:S(2)}) collective-permute-start(f32[32,128]{1,0:T(8,128)S(1)} %get-tuple-element.102.refs_3_), channel_id=1, source_target_pairs={{1,2},{2,1},{3,4},{4,3},{5,6},{6,5},{7,8},{8,7},{9,10},{10,9},{11,... | collective-permute-start | bytes 49160 | tf_op jit(solution)/shard_map/ppermute | solution.py:641
  60.8 5.4 %collective-permute-start.10 = (f32[40,128]{1,0:T(8,128)S(1)}, f32[40,128]{1,0:T(8,128)S(1)}, u32[]{:S(2)}, u32[]{:S(2)}) collective-permute-start(f32[40,128]{1,0:T(8,128)S(1)} %get-tuple-element.105), channel_id=1, source_target_pairs={{0,67},{1,66},{2,65},{3,64},{4,71},{5,70},{6,69},{7,68},{8,75},{9,... | collective-permute-start | bytes 61448 | tf_op jit(solution)/shard_map/ppermute | solution.py:606
  67.0 17.2 %all-to-all-start.2 = ((f32[64,16,128]{2,1,0:T(8,128)}), f32[64,16,128]{2,1,0:T(8,128)S(1)}, u32[]{:S(2)}, u32[]{:S(2)}) async-start(f32[64,16,128]{2,1,0:T(8,128)} %bitcast.15), calls=%async_computation.2 | async-start | bytes 1048576 | tf_op jit(solution)/shard_map/all_to_all | solution.py:628
  72.6 10.7 %collective-permute-start.14 = (f32[48,128]{1,0:T(8,128)S(1)}, f32[48,128]{1,0:T(8,128)S(1)}, u32[]{:S(2)}, u32[]{:S(2)}) collective-permute-start(f32[48,128]{1,0:T(8,128)S(1)} %get-tuple-element.118.refs_4_), channel_id=1, source_target_pairs={{16,32},{32,16},{17,33},{33,17},{18,34},{34,18},{19,35},{35,19},{2... | collective-permute-start | bytes 73736 | tf_op jit(solution)/shard_map/ppermute | solution.py:643
  73.3 10.1 %collective-permute-start.13 = (f32[48,128]{1,0:T(8,128)S(1)}, f32[48,128]{1,0:T(8,128)S(1)}, u32[]{:S(2)}, u32[]{:S(2)}) collective-permute-start(f32[48,128]{1,0:T(8,128)S(1)} %get-tuple-element.118.refs_4_), channel_id=1, source_target_pairs={{0,16},{16,0},{32,48},{48,32},{1,17},{17,1},{33,49},{49,33},{2,18}... | collective-permute-start | bytes 73736 | tf_op jit(solution)/shard_map/ppermute | solution.py:642
  77.2 5.8 %collective-permute-start.11 = (f32[32,128]{1,0:T(8,128)S(1)}, f32[32,128]{1,0:T(8,128)S(1)}, u32[]{:S(2)}, u32[]{:S(2)}) collective-permute-start(f32[32,128]{1,0:T(8,128)S(1)} %get-tuple-element.116.refs_2_), channel_id=1, source_target_pairs={{0,1},{1,0},{2,3},{3,2},{4,5},{5,4},{6,7},{7,6},{8,9},{9,8},{10,11... | collective-permute-start | bytes 49160 | tf_op jit(solution)/shard_map/ppermute | solution.py:640
  78.0 5.3 %collective-permute-start.12 = (f32[32,128]{1,0:T(8,128)S(1)}, f32[32,128]{1,0:T(8,128)S(1)}, u32[]{:S(2)}, u32[]{:S(2)}) collective-permute-start(f32[32,128]{1,0:T(8,128)S(1)} %get-tuple-element.117.refs_3_), channel_id=1, source_target_pairs={{1,2},{2,1},{3,4},{4,3},{5,6},{6,5},{7,8},{8,7},{9,10},{10,9},{11,... | collective-permute-start | bytes 49160 | tf_op jit(solution)/shard_map/ppermute | solution.py:641
  86.0 5.6 %collective-permute-start.15 = (f32[40,128]{1,0:T(8,128)S(1)}, f32[40,128]{1,0:T(8,128)S(1)}, u32[]{:S(2)}, u32[]{:S(2)}) collective-permute-start(f32[40,128]{1,0:T(8,128)S(1)} %get-tuple-element.120), channel_id=1, source_target_pairs={{0,67},{1,66},{2,65},{3,64},{4,71},{5,70},{6,69},{7,68},{8,75},{9,... | collective-permute-start | bytes 61448 | tf_op jit(solution)/shard_map/ppermute | solution.py:606
  92.3 17.2 %all-to-all-start.3 = ((f32[64,16,128]{2,1,0:T(8,128)}), f32[64,16,128]{2,1,0:T(8,128)S(1)}, u32[]{:S(2)}, u32[]{:S(2)}) async-start(f32[64,16,128]{2,1,0:T(8,128)} %bitcast.17), calls=%async_computation.3 | async-start | bytes 1048576 | tf_op jit(solution)/shard_map/all_to_all | solution.py:628
  98.0 10.7 %collective-permute-start.19 = (f32[48,128]{1,0:T(8,128)S(1)}, f32[48,128]{1,0:T(8,128)S(1)}, u32[]{:S(2)}, u32[]{:S(2)}) collective-permute-start(f32[48,128]{1,0:T(8,128)S(1)} %get-tuple-element.133.refs_4_), channel_id=1, source_target_pairs={{16,32},{32,16},{17,33},{33,17},{18,34},{34,18},{19,35},{35,19},{2... | collective-permute-start | bytes 73736 | tf_op jit(solution)/shard_map/ppermute | solution.py:643
  98.6 10.1 %collective-permute-start.18 = (f32[48,128]{1,0:T(8,128)S(1)}, f32[48,128]{1,0:T(8,128)S(1)}, u32[]{:S(2)}, u32[]{:S(2)}) collective-permute-start(f32[48,128]{1,0:T(8,128)S(1)} %get-tuple-element.133.refs_4_), channel_id=1, source_target_pairs={{0,16},{16,0},{32,48},{48,32},{1,17},{17,1},{33,49},{49,33},{2,18}... | collective-permute-start | bytes 73736 | tf_op jit(solution)/shard_map/ppermute | solution.py:642
  102.5 3.8 %collective-permute-start.16 = (f32[32,128]{1,0:T(8,128)S(1)}, f32[32,128]{1,0:T(8,128)S(1)}, u32[]{:S(2)}, u32[]{:S(2)}) collective-permute-start(f32[32,128]{1,0:T(8,128)S(1)} %get-tuple-element.131.refs_2_), channel_id=1, source_target_pairs={{0,1},{1,0},{2,3},{3,2},{4,5},{5,4},{6,7},{7,6},{8,9},{9,8},{10,11... | collective-permute-start | bytes 49160 | tf_op jit(solution)/shard_map/ppermute | solution.py:640
  103.4 5.3 %collective-permute-start.17 = (f32[32,128]{1,0:T(8,128)S(1)}, f32[32,128]{1,0:T(8,128)S(1)}, u32[]{:S(2)}, u32[]{:S(2)}) collective-permute-start(f32[32,128]{1,0:T(8,128)S(1)} %get-tuple-element.132.refs_3_), channel_id=1, source_target_pairs={{1,2},{2,1},{3,4},{4,3},{5,6},{6,5},{7,8},{8,7},{9,10},{10,9},{11,... | collective-permute-start | bytes 49160 | tf_op jit(solution)/shard_map/ppermute | solution.py:641
